TPU v7x, 32 devices: a whole 2x2x4 slice. The times are simulated.
32 devices in a mesh: rep: 2 (over y), row: 16 (over z, x, core).
Axes of the slice: x: 2, y: 2, z: 4, core: 2. Of those that a mesh axis runs over, the one named last changes fastest.
Arguments:
- states: float32 [2, 128, 16384], P('rep', None, 'row'), parts along dimension 0, may hold values from -6 to 6
- weights: bfloat16 [32768, 16384], P(('rep', 'row')), parts along dimension 0, may hold values from -0.0625 to 0.0625
- pert_table: float32 [32, 16384], P('rep', 'row'), parts along dimension 0, may hold values from -6 to 6
- eps_gain: float32 [32768], P(('rep', 'row')), parts along dimension 0, may hold values from 0.5 to 2
- decay: float32 [32768], P(('rep', 'row')), parts along dimension 0, may hold values from 0.1 to 1
- perts: int32 [2], P('rep'), parts along dimension 0, may hold values from 0 to 15
Outputs:
- grad_w: bfloat16 [32768, 16384], P(('rep', 'row')), parts along dimension 0
- grad_x: float32 [2, 128, 16384], P('rep', None, 'row'), parts along dimension 0
- grad_table: float32 [32, 16384], P('rep', 'row'), parts along dimension 0
- grad_eps: float32 [32768], P(('rep', 'row')), parts along dimension 0
- grad_decay: float32 [32768], P(('rep', 'row')), parts along dimension 0
There are 2 independent parts, one for each index of `rep`. A program takes and returns all parts, laid end to end along the dimension named above; each array names one. Nothing has to cross between parts.
All inputs are finite; a program needn't handle non-finite values.
Results may differ from a plain program's by a relative error of at most 0.0074.
Values may be sent and summed in bfloat16 or wider, within the bound.
No kernel may reach another device: no remote copies, remote signals or barrier semaphores. Data moves between devices by JAX's collectives and lax.ppermute only.
A program may use at most 320 MiB of HBM per device.

v0:
```python
import jax
import jax.numpy as jnp
from jax import lax
from jax.sharding import PartitionSpec as P


def cheb_matrix(count):
    index = jnp.arange(count)
    points = jnp.cos(jnp.pi * index.astype(jnp.float32) / (count - 1))
    signs = jnp.where(index % 2 == 0, 1.0, -1.0).astype(jnp.float32)
    ends = jnp.where((index == 0) | (index == count - 1), 2.0, 1.0).astype(jnp.float32)
    weight_c = signs * ends
    same = index[:, None] == index[None, :]
    spread = points[:, None] - points[None, :]
    spread = jnp.where(same, 1.0, spread)
    off = jnp.where(same, 0.0, weight_c[:, None] / weight_c[None, :] / spread)
    return off - jnp.diag(jnp.sum(off, axis=1))


def contract_last(left, right):
    return lax.dot_general(
        left, right, (((1,), (1,)), ((), ())), preferred_element_type=jnp.float32
    )


def contract_first(left, right):
    return lax.dot_general(
        left, right, (((0,), (0,)), ((), ())), preferred_element_type=jnp.float32
    )


def contract_cross(left, right):
    return lax.dot_general(
        left, right, (((0,), (1,)), ((), ())), preferred_element_type=jnp.float32
    )


def body(states, weights, pert_table, eps_gain, decay, perts):
    scale = 2.0 / 1024.0
    traj, nodes, slab = states.shape
    total_rows = traj * nodes
    cheb = cheb_matrix(nodes)
    xb = states.astype(jnp.bfloat16).reshape(total_rows, slab)
    full_state = lax.all_gather(xb, "row", axis=1, tiled=True)
    pre = contract_last(full_state, weights)
    onehot = (perts[:, None] == jnp.arange(pert_table.shape[0], dtype=jnp.int32)[None, :]).astype(
        jnp.float32
    )
    drive = jnp.dot(onehot, pert_table, precision=lax.Precision.HIGHEST)
    pre = pre.reshape(traj, nodes, slab) + drive[:, None, :]
    act = jnp.tanh(pre)
    deriv = scale * jnp.einsum("kl,clg->ckg", cheb, states, precision=lax.Precision.HIGHEST)
    resid = deriv - (eps_gain * act - decay * states)
    delta = (-eps_gain * (1.0 - act * act) * resid).astype(jnp.bfloat16)
    dflat = delta.reshape(total_rows, slab)
    grad_w = contract_first(dflat, full_state).astype(jnp.bfloat16)
    back = lax.psum_scatter(
        contract_cross(weights, dflat), "row", scatter_dimension=0, tiled=True
    ).T
    back = back.reshape(traj, nodes, slab)
    grad_x = (
        scale * jnp.einsum("lk,clg->ckg", cheb, resid, precision=lax.Precision.HIGHEST)
        + decay * resid
        + back
    )
    node_sums = jnp.sum(delta.astype(jnp.float32), axis=1)
    grad_table = jnp.dot(onehot.T, node_sums, precision=lax.Precision.HIGHEST)
    grad_eps = -jnp.sum(act * resid, axis=(0, 1))
    grad_decay = jnp.sum(states * resid, axis=(0, 1))
    return (grad_w, grad_x, grad_table, grad_eps, grad_decay)


def solution(mesh):
    in_specs = (
        P("rep", None, "row"),
        P(("rep", "row"), None),
        P("rep", "row"),
        P(("rep", "row")),
        P(("rep", "row")),
        P("rep"),
    )
    out_specs = (
        P(("rep", "row"), None),
        P("rep", None, "row"),
        P("rep", "row"),
        P(("rep", "row")),
        P(("rep", "row")),
    )
    return jax.shard_map(body, mesh=mesh, in_specs=in_specs, out_specs=out_specs, check_vma=False)
```

profile of v0, /device:TPU:0, one launch (start us, length us, event | category | flops | bytes accessed | tf_op | source)
XLA Modules:
  0.0 214.0 jit_solution(14643508128186551390)
XLA Ops:
  7.2 0.0 copy-start
  7.2 0.0 copy-start.2
  7.2 0.0 copy-start.4
  7.2 0.0 copy-start.3
  7.2 0.0 all-gather.3.cloned.1.call-start
  7.3 1.8 convert_element_type.26
  9.1 0.0 all-gather.3.cloned.1.call-update
  9.1 0.0 reduce-scatter.2.cloned.1.call-start
  9.8 0.7 neg.6
  10.6 0.2 fusion.24
  10.7 0.0 copy-done
  10.8 0.1 fusion.25
  10.9 53.2 %all-gather.3.cloned.1.call-done = bf16[1,128,16384]{2,1,0:T(8,128)(2,1)} async-done(((bf16[1,128,1024]{2,1,0:T(8,128)(2,1)}), bf16[1,128,16384]{2,1,0:T(8,128)(2,1)}) %all-gather.3.cloned.1.call-update) | async-done | bytes 4194320 | tf_op jit(solution)/shard_map/all_gather | solution.py:44
  64.1 16.9 %fusion.11 = f32[128,1024]{1,0:T(8,128)S(1)} fusion(bf16[1024,16384]{1,0:T(8,128)(2,1)} %param.7, bf16[1,128,16384]{2,1,0:T(8,128)(2,1)} %all-gather.3.cloned.1.call-done, f32[1024]{0:T(1024)S(1)} %bitcast.67), kind=kOutput, calls=%fused_computation.13 | convolution fusion | flops 4295098368 | bytes 38277120 | tf_op jit(solution)/shard_map/dot_general | solution.py:21
  81.1 0.0 copy-done.2
  81.1 0.0 copy-done.4
  81.1 0.0 copy-done.3
  81.1 1.5 multiply_reduce_fusion
  82.6 0.0 copy-start.1
  82.6 18.3 %convolution_bitcast_fusion = f32[16384,128]{0,1:T(8,128)} fusion(bf16[1024,16384]{1,0:T(8,128)(2,1)} %param.7, bf16[1,128,1024]{2,1,0:T(8,128)(2,1)S(1)} %get-tuple-element.10), kind=kOutput, calls=%fused_computation.1 | convolution fusion | flops 4294967296 | bytes 42205184 | tf_op jit(solution)/shard_map/dot_general | solution.py:33
  100.9 0.0 reduce-scatter.2.cloned.1.call-update
  101.0 0.6 neg.7
  101.6 0.7 broadcast_multiply_fusion
  102.3 18.4 %convolution_convert_fusion = bf16[1024,16384]{1,0:T(8,128)(2,1)} fusion(bf16[1,128,16384]{2,1,0:T(8,128)(2,1)} %all-gather.3.cloned.1.call-done, bf16[1,128,1024]{2,1,0:T(8,128)(2,1)S(1)} %get-tuple-element.10), kind=kOutput, calls=%fused_computation | convolution fusion | flops 4311744512 | bytes 38010880 | tf_op jit(solution)/shard_map/dot_general | solution.py:27
  120.7 83.8 %reduce-scatter.2.cloned.1.call-done = f32[1024,128]{0,1:T(8,128)} async-done(((f32[16384,128]{0,1:T(8,128)}), f32[1024,128]{0,1:T(8,128)}) %reduce-scatter.2.cloned.1.call-update) | async-done | bytes 524304 | tf_op jit(solution)/shard_map/reduce_scatter | solution.py:57
  204.6 2.6 %fusion.7 = f32[1,128,1024]{2,1,0:T(8,128)} fusion(f32[1024,128]{0,1:T(8,128)} %reduce-scatter.2.cloned.1.call-done, f32[1,128,1024]{2,1,0:T(8,128)S(1)} %get-tuple-element.11, f32[1024]{0:T(1024)S(1)} %copy-done.3, f32[128]{0:T(128)S(1)} %fusion.24, f32[128]{0:T(128)S(1)} %get-tuple-element.13, f32[128]{0:T(128)S(1)} %get-tuple-element.12), kind=kOutput, calls=%fused_computation.11 | convolution fusion | flops 201981952 | bytes 1578496 | tf_op jit(solution)/shard_map/lk,clg->ckg/dot_general | solution.py:62
  207.1 0.0 copy-done.1
  (2 shorter events, 0.0 us)
Async XLA Ops:
  7.2 3.6 %copy-start = (f32[16,1024]{1,0:T(8,128)S(1)}, f32[16,1024]{1,0:T(8,128)}, u32[]{:S(2)}) copy-start(f32[16,1024]{1,0:T(8,128)} %param.8) | copy-start | bytes 196612
  7.2 73.9 %copy-start.2 = (f32[1,128,1024]{2,1,0:T(8,128)S(1)}, f32[1,128,1024]{2,1,0:T(8,128)}, u32[]{:S(2)}) copy-start(f32[1,128,1024]{2,1,0:T(8,128)} %param.6) | copy-start | bytes 1572868
  7.2 73.9 %copy-start.4 = (f32[1024]{0:T(1024)S(1)}, f32[1024]{0:T(1024)}, u32[]{:S(2)}) copy-start(f32[1024]{0:T(1024)} %param.9) | copy-start | bytes 12292
  7.2 73.9 %copy-start.3 = (f32[1024]{0:T(1024)S(1)}, f32[1024]{0:T(1024)}, u32[]{:S(2)}) copy-start(f32[1024]{0:T(1024)} %param.10) | copy-start | bytes 12292
  7.2 56.9 %all-gather.3.cloned.1.call-start = ((), (), s32[]{:S(2)}) async-start(), calls=%async_computation.2 | async-start | bytes 4456448 | tf_op jit(solution)/shard_map/all_gather | solution.py:44
  9.1 195.4 %reduce-scatter.2.cloned.1.call-start = ((), (), s32[]{:S(2)}) async-start(), calls=%async_computation.1 | async-start | bytes 8912896 | tf_op jit(solution)/shard_map/reduce_scatter | solution.py:57
  82.6 124.5 %copy-start.1 = (f32[16,1024]{1,0:T(8,128)S(1)}, f32[16,1024]{1,0:T(8,128)}, u32[]{:S(2)}) copy-start(f32[16,1024]{1,0:T(8,128)} %param.8) | copy-start | bytes 196612
Sparse Core Ops, SparseCore 0:
  10.8 53.2 all-gather.2
  101.1 103.4 reduce-scatter.1
where the time goes:
time: 214 us
  waiting for transfers between devices  137 us (64%)
  matrix products  57.9 us (27%)
  between operations  14.8 us (7%)
  other arithmetic  4.05 us (2%)
    reduce_scatter x1, waiting for transfers between devices, body(): lax.psum_scatter(contract_cross(weights, dflat), 'row', scatter_dimension...  83.8 us
    all_gather x1, waiting for transfers between devices, body(): full_state = lax.all_gather(xb, 'row', axis=1, tiled=True)  53.2 us
    dot_general x1, matrix products, contract_first(): lax.dot_general(left, right, (((0,), (0,)), ((), ())), preferred_element_...  18.4 us
    dot_general x1, matrix products, contract_cross(): lax.dot_general(left, right, (((0,), (1,)), ((), ())), preferred_element_...  18.3 us
    dot_general x1, matrix products, contract_last(): lax.dot_general(left, right, (((1,), (1,)), ((), ())), preferred_element_...  16.9 us
  transfers between devices with their start and end apart: 2, of which 2 were waited for; matrix products, arithmetic and copies ran while one was open for 10% of the time, Pallas kernels for 0%

commit v1 on v0

v1 whole, which is shorter than its diff:
```python
import functools

import jax
import jax.numpy as jnp
import numpy as np
from jax import lax
from jax.experimental import pallas as pl
from jax.experimental.pallas import tpu as pltpu
from jax.sharding import PartitionSpec as P

SCALE = 2.0 / 1024.0
VMEM_LIMIT = 24 * 2**20
LONGEST_RING = 16


def cheb_matrix(count):
    index = np.arange(count)
    points = np.cos(np.pi * index / (count - 1))
    signs = np.where(index % 2 == 0, 1.0, -1.0)
    weight_c = signs * np.where((index == 0) | (index == count - 1), 2.0, 1.0)
    same = index[:, None] == index[None, :]
    spread = np.where(same, 1.0, points[:, None] - points[None, :])
    off = np.where(same, 0.0, weight_c[:, None] / weight_c[None, :] / spread)
    return jnp.asarray((off - np.diag(np.sum(off, axis=1))).astype(np.float32))


def chip_ring(chips):
    rows = 4
    cols = chips // rows
    cells = [(0, col) for col in range(cols)]
    for row in range(1, rows):
        span = range(1, cols)
        cells += [(row, col) for col in (reversed(span) if row % 2 else span)]
    cells += [(row, 0) for row in range(rows - 1, 0, -1)]
    return [row * cols + col for row, col in cells]


def whole(shape):
    return pl.BlockSpec(shape, lambda *_: (0,) * len(shape))


def cost(products, nodes, slab, rows):
    return pl.CostEstimate(
        flops=2 * products * nodes * slab * rows // 16,
        bytes_accessed=2 * products * slab * rows // 16,
        transcendentals=0,
    )


def pre_kernel(count, first, *refs):
    xs, (w_ref, *acc_ref), out_ref = refs[1 : 1 + count], refs[1 + count : -1], refs[-1]
    block, tile = pl.program_id(0), w_ref.shape[0]
    here = pl.ds(pl.multiple_of(pl.program_id(1) * tile, tile), tile)
    for at in range(count):

        @pl.when(block == at)
        def _():
            part = lax.dot_general(
                w_ref[...], xs[at][...], (((1,), (1,)), ((), ())),
                preferred_element_type=jnp.float32,
            )
            if at > 0:
                part += out_ref[here, :]
            elif not first:
                part += acc_ref[0][here, :]
            out_ref[here, :] = part


def add_products(offs, base, xs, weights, acc):
    nodes, slab = xs[0].shape
    rows, count = weights.shape[0], len(xs)
    tile = rows // 2
    first = acc is None
    return pl.pallas_call(
        functools.partial(pre_kernel, count, first),
        out_shape=jax.ShapeDtypeStruct((rows, nodes), jnp.float32),
        grid_spec=pltpu.PrefetchScalarGridSpec(
            num_scalar_prefetch=1,
            grid=(count, rows // tile),
            in_specs=[whole((nodes, slab))] * count
            + [pl.BlockSpec((tile, slab), lambda b, t, offs: (t, offs[base + b]))]
            + ([] if first else [whole((rows, nodes))]),
            out_specs=whole((rows, nodes)),
        ),
        compiler_params=pltpu.CompilerParams(vmem_limit_bytes=VMEM_LIMIT),
        cost_estimate=cost(count, nodes, slab, rows),
    )(offs, *xs, weights, *([] if first else [acc]))


def middle_kernel(
    offs, x_ref, w_ref, acc_ref, deriv_ref, states_ref, drive_ref, eps_ref, decay_ref,
    resid_ref, delta_ref, delta_t_ref, sums_ref,
):
    part = acc_ref[...] + lax.dot_general(
        w_ref[...], x_ref[...], (((1,), (1,)), ((), ())),
        preferred_element_type=jnp.float32,
    )
    states = states_ref[...]
    act = jnp.tanh(part.T + drive_ref[...])
    eps = eps_ref[...]
    resid = deriv_ref[...] - (eps * act - decay_ref[...] * states)
    delta = (-eps * (1.0 - act * act) * resid).astype(jnp.bfloat16)
    wide = delta.astype(jnp.float32)
    resid_ref[...] = resid
    delta_ref[...] = delta
    delta_t_ref[...] = wide.T.astype(jnp.bfloat16)
    sums_ref[0:1, :] = jnp.sum(wide, axis=0, keepdims=True)
    sums_ref[1:2, :] = -jnp.sum(act * resid, axis=0, keepdims=True)
    sums_ref[2:3, :] = jnp.sum(states * resid, axis=0, keepdims=True)


def middle(offs, base, x, weights, acc, deriv, states, drive, eps, decay):
    nodes, slab = x.shape
    rows = weights.shape[0]
    tile = max(rows // 4, 128)
    by_gene = pl.BlockSpec((nodes, tile), lambda t, offs: (0, t))
    row = pl.BlockSpec((1, tile), lambda t, offs: (0, t))
    turned = pl.BlockSpec((tile, nodes), lambda t, offs: (t, 0))
    return pl.pallas_call(
        middle_kernel,
        out_shape=(
            jax.ShapeDtypeStruct((nodes, rows), jnp.float32),
            jax.ShapeDtypeStruct((nodes, rows), jnp.bfloat16),
            jax.ShapeDtypeStruct((rows, nodes), jnp.bfloat16),
            jax.ShapeDtypeStruct((8, rows), jnp.float32),
        ),
        grid_spec=pltpu.PrefetchScalarGridSpec(
            num_scalar_prefetch=1,
            grid=(rows // tile,),
            in_specs=[
                whole((nodes, slab)),
                pl.BlockSpec((tile, slab), lambda t, offs: (t, offs[base])),
                turned, by_gene, by_gene, row, row, row,
            ],
            out_specs=(by_gene, by_gene, turned, pl.BlockSpec((8, tile), lambda t, offs: (0, t))),
        ),
        compiler_params=pltpu.CompilerParams(vmem_limit_bytes=VMEM_LIMIT),
        cost_estimate=cost(2, nodes, slab, rows),
    )(offs, x, weights, acc, deriv, states, drive, eps, decay)


def share_kernel(cuts, offs, delta_ref, w_ref, *outs):
    block, tile = pl.program_id(0), w_ref.shape[1]
    nodes = delta_ref.shape[0]
    here = pl.ds(pl.multiple_of(pl.program_id(1) * tile, tile), tile)
    part = jnp.dot(delta_ref[...], w_ref[...], preferred_element_type=jnp.float32)
    for at in range(cuts[-1] // nodes):

        @pl.when(block == at)
        def _():
            for start, end, out_ref in zip(cuts[:-1], cuts[1:], outs):
                low, high = max(start, at * nodes), min(end, (at + 1) * nodes)
                if low < high:
                    rows = part[low - at * nodes : high - at * nodes]
                    out_ref[low - start : high - start, here] = rows.astype(out_ref.dtype)


def shares(offs, at, delta, weights, slab, dtype, cuts):
    nodes, rows = delta.shape
    count = len(at)
    tile = max(slab // 2, 128)
    heights = [end - start for start, end in zip(cuts[:-1], cuts[1:])]

    def place(b, j, offs):
        block = offs[at[-1]]
        for index in range(count - 2, -1, -1):
            block = jnp.where(b == index, offs[at[index]], block)
        return (0, block * (slab // tile) + j)

    return pl.pallas_call(
        functools.partial(share_kernel, cuts),
        out_shape=[jax.ShapeDtypeStruct((height, slab), dtype) for height in heights],
        grid_spec=pltpu.PrefetchScalarGridSpec(
            num_scalar_prefetch=1,
            grid=(count, slab // tile),
            in_specs=[whole((nodes, rows)), pl.BlockSpec((rows, tile), place)],
            out_specs=[whole((height, slab)) for height in heights],
        ),
        compiler_params=pltpu.CompilerParams(vmem_limit_bytes=VMEM_LIMIT),
        cost_estimate=cost(count, nodes, slab, rows),
    )(offs, delta, weights)


def grad_w_kernel(count, *refs):
    delta_ref, xs, (out_ref, mark_ref) = refs[1], refs[2 : 2 + count], refs[-2:]
    block = pl.program_id(0)
    slab = out_ref.shape[1]

    @pl.when(block == 0)
    def _():
        mark_ref[...] = jnp.zeros_like(mark_ref)

    width = min(256, slab)
    for at in range(count):

        @pl.when(block == at)
        def _():
            for col in range(0, slab, width):
                out_ref[:, col : col + width] = jnp.dot(
                    delta_ref[...], xs[at][:, col : col + width],
                    preferred_element_type=jnp.float32,
                ).astype(out_ref.dtype)


def grad_w_piece(offs, base, delta_t, xs, so_far, mark, shape):
    rows, nodes = delta_t.shape
    slab, count = xs[0].shape[1], len(xs)
    first = so_far is None
    return pl.pallas_call(
        functools.partial(grad_w_kernel, count),
        out_shape=(
            jax.ShapeDtypeStruct(shape, jnp.bfloat16),
            jax.ShapeDtypeStruct((8, 128), jnp.float32),
        ),
        grid_spec=pltpu.PrefetchScalarGridSpec(
            num_scalar_prefetch=1,
            grid=(count,),
            in_specs=[whole((rows, nodes))] + [whole((nodes, slab))] * count
            + ([] if first else [pl.BlockSpec(memory_space=pl.ANY)] * 2),
            out_specs=(
                pl.BlockSpec((rows, slab), lambda b, offs: (0, offs[base + b])),
                whole((8, 128)),
            ),
        ),
        input_output_aliases={} if first else {2 + count: 0},
        compiler_params=pltpu.CompilerParams(vmem_limit_bytes=VMEM_LIMIT),
        cost_estimate=cost(count, nodes, slab, rows),
    )(offs, delta_t, *xs, *([] if first else [so_far, mark]))


def ring_body(chips, states, weights, pert_table, eps_gain, decay, perts):
    _, nodes, slab = states.shape
    rows = weights.shape[0]
    order = chip_ring(chips)
    place = np.argsort(order)
    half, cut = chips // 2, nodes // 2

    near = [0]
    for step in range(1, half):
        near += [-step, step]
    near.append(half)
    sides = {}
    listing = [(0, 0)]
    for step in range(half):
        now = [0] if step == 0 else [-step, step]
        then = [half] if step == half - 1 else [-step - 1, step + 1]
        listing += [(at, 1) for at in now] + [(at, 0) for at in then]
    listing.append((half, 1))
    sides = {key: at for at, key in enumerate(listing)}
    table = np.array(
        [
            [
                2 * order[(place[device // 2] + step) % chips] + (device % 2 ^ side)
                for step, side in listing
            ]
            for device in range(2 * chips)
        ],
        dtype=np.int32,
    )
    me = lax.axis_index("row")
    offs = lax.dynamic_slice(jnp.asarray(table), (me, 0), (1, 2 * chips)).reshape(-1)

    def ring(array, way):
        pairs = []
        for at, chip in enumerate(order):
            to = order[(at + way) % chips]
            pairs += [(2 * chip, 2 * to), (2 * chip + 1, 2 * to + 1)]
        return lax.ppermute(array, "row", pairs)

    def swap(array):
        return lax.ppermute(array, "row", [(i, i ^ 1) for i in range(2 * chips)])

    cheb = cheb_matrix(nodes)
    flat = states.reshape(nodes, slab)
    xb = flat.astype(jnp.bfloat16)

    x = {(0, 0): xb}
    acc, base = None, 0
    behind, ahead = xb, xb
    for step in range(1, half + 1):
        if step < half:
            behind, ahead = ring(behind, 1), ring(ahead, -1)
        else:
            behind, ahead = ring(behind[:cut], 1), ring(ahead[cut:], -1)
        for now in [0] if step == 1 else [1 - step, step - 1]:
            x[now, 1] = swap(x[now, 0])
        count = {1: 1, 2: 3}.get(step, 4)
        acc = add_products(
            offs, base, [x[key] for key in listing[base : base + count]], weights, acc
        )
        base += count
        behind, ahead, acc = lax.optimization_barrier((behind, ahead, acc))
        if step < half:
            x[-step, 0], x[step, 0] = behind, ahead
        else:
            x[half, 0] = jnp.concatenate([behind, ahead], axis=0)
    x[half, 1] = swap(x[half, 0])
    count = 3
    acc = add_products(
        offs, base, [x[key] for key in listing[base : base + count]], weights, acc
    )
    base += count

    onehot = (perts[:, None] == jnp.arange(pert_table.shape[0], dtype=jnp.int32)[None, :]).astype(
        jnp.float32
    )
    drive = jnp.dot(onehot, pert_table, precision=lax.Precision.HIGHEST)
    deriv = SCALE * jnp.dot(cheb, flat, precision=lax.Precision.HIGHEST)

    resid, delta, delta_t, sums = middle(
        offs, base, x[half, 1], weights, acc, deriv, flat, drive,
        eps_gain.reshape(1, rows), decay.reshape(1, rows),
    )

    def share(offs, steps):
        count = len(steps)
        pieces = 2 if count == 1 else 3
        cuts = [0] + [count * nodes * at // pieces // 16 * 16 for at in range(1, pieces)]
        cuts.append(count * nodes)
        others = shares(
            offs, [sides[step, 1] for step in steps], delta, weights, slab, jnp.bfloat16, cuts
        )
        offs, *others = lax.optimization_barrier((offs, *others))
        swapped = jnp.concatenate([swap(other) for other in others], axis=0)
        owns = shares(
            offs, [sides[step, 0] for step in steps], delta, weights, slab, jnp.float32,
            [at * nodes for at in range(count + 1)],
        )
        return [
            own + swapped[at * nodes : (at + 1) * nodes].astype(jnp.float32)
            for at, own in enumerate(owns)
        ]

    gate = lax.optimization_barrier
    pieces, cuts = [], [0, 5, 10, len(listing)]
    for base, end in zip(cuts[:-1], cuts[1:]):
        pieces.append((base, listing[base:end]))
    grad_w, mark = None, None

    (far,) = share(offs, [half])
    far = far.astype(jnp.bfloat16)
    far, offs = gate((far, offs))
    ahead, behind = ring(far[:cut], 1), ring(far[cut:], -1)
    for step in range(half - 1, -1, -1):
        if step > 0:
            own_ahead, own_behind = share(offs, [step, -step])
        else:
            (near_share,) = share(offs, [0])
        if step < half - 1:
            base, keys = pieces.pop(0)
            grad_w, mark = grad_w_piece(
                offs, base, delta_t, [x[key] for key in keys], grad_w, mark, weights.shape
            )
            ahead, behind, mark = gate((ahead, behind, mark))
        if step == 0:
            break
        ahead, behind = ahead.astype(jnp.float32), behind.astype(jnp.float32)
        if step == half - 1:
            ahead = jnp.concatenate([own_ahead[:cut] + ahead, own_ahead[cut:]], axis=0)
            behind = jnp.concatenate([own_behind[:cut], own_behind[cut:] + behind], axis=0)
        else:
            ahead, behind = own_ahead + ahead, own_behind + behind
        ahead, behind = ahead.astype(jnp.bfloat16), behind.astype(jnp.bfloat16)
        ahead, behind, offs = gate((ahead, behind, offs))
        ahead, behind = ring(ahead, 1), ring(behind, -1)

    local = (
        SCALE
        * lax.dot_general(
            cheb, resid, (((0,), (0,)), ((), ())), precision=lax.Precision.HIGHEST
        )
        + decay * resid
    )
    local = lax.optimization_barrier(local + near_share)
    grad_x = local + ahead.astype(jnp.float32) + behind.astype(jnp.float32)
    grad_x = grad_x.reshape(states.shape)
    grad_table = onehot.T * sums[0:1]
    return (grad_w, grad_x, grad_table, sums[1], sums[2])


def plain_body(states, weights, pert_table, eps_gain, decay, perts):
    traj, nodes, slab = states.shape
    total = traj * nodes
    cheb = cheb_matrix(nodes)
    xb = states.astype(jnp.bfloat16).reshape(total, slab)
    full = lax.all_gather(xb, "row", axis=1, tiled=True)
    pre = lax.dot_general(
        full, weights, (((1,), (1,)), ((), ())), preferred_element_type=jnp.float32
    )
    onehot = (perts[:, None] == jnp.arange(pert_table.shape[0], dtype=jnp.int32)[None, :]).astype(
        jnp.float32
    )
    drive = jnp.dot(onehot, pert_table, precision=lax.Precision.HIGHEST)
    act = jnp.tanh(pre.reshape(traj, nodes, slab) + drive[:, None, :])
    deriv = SCALE * jnp.einsum("kl,clg->ckg", cheb, states, precision=lax.Precision.HIGHEST)
    resid = deriv - (eps_gain * act - decay * states)
    delta = (-eps_gain * (1.0 - act * act) * resid).astype(jnp.bfloat16)
    dflat = delta.reshape(total, slab)
    grad_w = lax.dot_general(
        dflat, full, (((0,), (0,)), ((), ())), preferred_element_type=jnp.float32
    ).astype(jnp.bfloat16)
    back = jnp.dot(dflat, weights, preferred_element_type=jnp.float32)
    back = lax.psum_scatter(back, "row", scatter_dimension=1, tiled=True)
    grad_x = (
        SCALE * jnp.einsum("lk,clg->ckg", cheb, resid, precision=lax.Precision.HIGHEST)
        + decay * resid
        + back.reshape(traj, nodes, slab)
    )
    node_sums = jnp.sum(delta.astype(jnp.float32), axis=1)
    grad_table = jnp.dot(onehot.T, node_sums, precision=lax.Precision.HIGHEST)
    grad_eps = -jnp.sum(act * resid, axis=(0, 1))
    grad_decay = jnp.sum(states * resid, axis=(0, 1))
    return (grad_w, grad_x, grad_table, grad_eps, grad_decay)


def solution(mesh):
    chips = mesh.shape["row"] // 2
    in_specs = (
        P("rep", None, "row"),
        P(("rep", "row"), None),
        P("rep", "row"),
        P(("rep", "row")),
        P(("rep", "row")),
        P("rep"),
    )
    out_specs = (
        P(("rep", "row"), None),
        P("rep", None, "row"),
        P("rep", "row"),
        P(("rep", "row")),
        P(("rep", "row")),
    )

    def run(states, *others):
        if states.shape[0] == 1 and chips <= LONGEST_RING:
            return ring_body(chips, states, *others)
        return plain_body(states, *others)

    return jax.shard_map(run, mesh=mesh, in_specs=in_specs, out_specs=out_specs, check_vma=False)
```

time: 214 us -> 127 us (0.59)
  waiting for transfers between devices: 137 us -> 4.69 us
  Pallas kernels: 0 us -> 90.2 us
  matrix products: 57.9 us -> 1.41 us
  starting transfers between devices: 0.08 us -> 22.8 us
  between operations: 14.8 us -> 1.83 us
    pallas_call x0 -> x19, Pallas kernels: none -> 90.2 us  [the longest x10 34.4 us: shares(): pl.pallas_call(functools.partial(share_kernel, cuts), out_shape=[jax.Shap...]
    reduce_scatter x1 -> x0, waiting for transfers between devices: 83.8 us -> none  [body(): lax.psum_scatter(contract_cross(weights, dflat), 'row', scatter_dimension...]
    dot_general x6 -> x3, matrix products: 57.9 us -> 1.41 us  [the longest x1 0.69 us: ring_body(): lax.dot_general(cheb, resid, (((0,), (0,)), ((), ())), precision=lax.Prec...]
    all_gather x1 -> x0, waiting for transfers between devices: 53.2 us -> none  [body(): full_state = lax.all_gather(xb, 'row', axis=1, tiled=True)]
    ppermute x0 -> x37, starting transfers between devices: none -> 22.8 us  [the longest x16 17.6 us: ring(): return lax.ppermute(array, 'row', pairs)]
    ppermute x0 -> x37, waiting for transfers between devices: none -> 4.69 us  [the longest x16 4.64 us: ring(): return lax.ppermute(array, 'row', pairs)]
  transfers between devices with their start and end apart: 2 -> 37, of which waited for: 2 -> 3; matrix products, arithmetic and copies ran while one was open for 10% -> 3% of each run, Pallas kernels for 0% -> 61%
where the time goes in v1:
time: 127 us; the launch traced here: 126 us
  Pallas kernels  90.2 us (71%)
  starting transfers between devices  22.8 us (18%)
  waiting for transfers between devices  4.69 us (4%)
  other arithmetic  3.55 us (3%)
  between operations  1.83 us (1%)
  local copies, waits for them, and re-layouts  1.43 us (1%)
  matrix products  1.41 us (1%)
    pallas_call x10, Pallas kernels, shares(): pl.pallas_call(functools.partial(share_kernel, cuts), out_shape=[jax.Shap...  34.4 us
    pallas_call x5, Pallas kernels, add_products(): pl.pallas_call(functools.partial(pre_kernel, count, first), out_shape=jax...  31 us
    pallas_call x3, Pallas kernels, grad_w_piece(): pl.pallas_call(functools.partial(grad_w_kernel, count), out_shape=(jax.Sh...  20.6 us
    ppermute x16, starting transfers between devices, ring(): return lax.ppermute(array, 'row', pairs)  17.6 us
    ppermute x21, starting transfers between devices, swap(): return lax.ppermute(array, 'row', [(i, i ^ 1) for i in range(2 * chips)])  5.18 us
    ppermute x16, waiting for transfers between devices, ring(): return lax.ppermute(array, 'row', pairs)  4.64 us
    pallas_call x1, Pallas kernels, middle(): pl.pallas_call(middle_kernel, out_shape=(jax.ShapeDtypeStruct((nodes, row...  4.16 us
  transfers between devices with their start and end apart: 37, of which 3 were waited for; matrix products, arithmetic and copies ran while one was open for 3% of the time, Pallas kernels for 61%

profile of v1, /device:TPU:0, one launch (start us, length us, event | category | flops | bytes accessed | tf_op | source)
XLA Modules:
  0.0 125.9 jit_solution(15813412980686599266)
XLA Ops:
  0.6 1.1 bitcast_convert_fusion.refs_1_.refs_2_
  1.8 3.0 %collective-permute-start = (bf16[128,1024]{1,0:T(8,128)(2,1)S(1)}, bf16[128,1024]{1,0:T(8,128)(2,1)S(1)}, u32[]{:S(2)}, u32[]{:S(2)}) collective-permute-start(bf16[128,1024]{1,0:T(8,128)(2,1)S(1)} %bitcast_convert_fusion.refs_1_.refs_2_), channel_id=1, source_target_pairs={{0,2},{1,3},{2,6},{3,7},{6,10},{7,11},{10,14},{11,15},{14,12},{15,... | collective-permute-start | bytes 786440 | tf_op jit(solution)/shard_map/ppermute | solution.py:268
  4.8 0.2 collective-permute-start.1
  4.9 0.7 dynamic-slice_bitcast_fusion.refs_0_.offs
  5.6 2.7 %shard_map.119.refs_5_ = f32[1024,128]{1,0:T(8,128)S(1)} custom-call(s32[16]{0:T(128)S(1)} %dynamic-slice_bitcast_fusion.refs_0_.offs, bf16[128,1024]{1,0:T(8,128)(2,1)S(1)} %bitcast_convert_fusion.refs_1_.refs_2_, bf16[1024,16384]{1,0:T(8,128)(2,1)} %w_ref.21), custom_call_target="tpu_custom_call" | custom-call | flops 16777216 | bytes 131072 | tf_op jit(solution)/shard_map/pallas_call | solution.py:74
  8.3 2.9 %collective-permute-done.refs_2_.refs_4_ = bf16[128,1024]{1,0:T(8,128)(2,1)S(1)} collective-permute-done((bf16[128,1024]{1,0:T(8,128)(2,1)S(1)}, bf16[128,1024]{1,0:T(8,128)(2,1)S(1)}, u32[]{:S(2)}, u32[]{:S(2)}) %collective-permute-start) | collective-permute-done | bytes 262176 | tf_op jit(solution)/shard_map/ppermute | solution.py:268
  11.1 1.4 %collective-permute-done.1.refs_3_.refs_5_ = bf16[128,1024]{1,0:T(8,128)(2,1)S(1)} collective-permute-done((bf16[128,1024]{1,0:T(8,128)(2,1)S(1)}, bf16[128,1024]{1,0:T(8,128)(2,1)S(1)}, u32[]{:S(2)}, u32[]{:S(2)}) %collective-permute-start.1) | collective-permute-done | bytes 262176 | tf_op jit(solution)/shard_map/ppermute | solution.py:268
  12.5 1.6 %collective-permute-start.2 = (bf16[128,1024]{1,0:T(8,128)(2,1)S(1)}, bf16[128,1024]{1,0:T(8,128)(2,1)S(1)}, u32[]{:S(2)}, u32[]{:S(2)}) collective-permute-start(bf16[128,1024]{1,0:T(8,128)(2,1)S(1)} %collective-permute-done.refs_2_.refs_4_), channel_id=1, source_target_pairs={{0,2},{1,3},{2,6},{3,7},{6,10},{7,11},{10,14},{11,15},{14,12},{15,... | collective-permute-start | bytes 786440 | tf_op jit(solution)/shard_map/ppermute | solution.py:268
  14.1 0.4 collective-permute-start.3
  14.5 0.5 collective-permute-start.8
  15.1 6.2 %shard_map.120.refs_6_ = f32[1024,128]{1,0:T(8,128)S(1)} custom-call(s32[16]{0:T(128)S(1)} %dynamic-slice_bitcast_fusion.refs_0_.offs, bf16[128,1024]{1,0:T(8,128)(2,1)S(1)} %collective-permute-done.4.refs_1_.refs_3_, bf16[128,1024]{1,0:T(8,128)(2,1)S(1)} %collective-permute-done.refs_2_.refs_4_, ...), custom_call_target="tpu_custom_call" | custom-call | flops 50331648 | bytes 393216 | tf_op jit(solution)/shard_map/pallas_call | solution.py:74
  21.3 1.6 %collective-permute-start.5 = (bf16[128,1024]{1,0:T(8,128)(2,1)S(1)}, bf16[128,1024]{1,0:T(8,128)(2,1)S(1)}, u32[]{:S(2)}, u32[]{:S(2)}) collective-permute-start(bf16[128,1024]{1,0:T(8,128)(2,1)S(1)} %collective-permute-done.2.refs_3_), channel_id=1, source_target_pairs={{0,2},{1,3},{2,6},{3,7},{6,10},{7,11},{10,14},{11,15},{14,12},{15,... | collective-permute-start | bytes 786440 | tf_op jit(solution)/shard_map/ppermute | solution.py:268
  23.0 0.4 collective-permute-start.6
  23.4 0.5 collective-permute-start.12
  23.9 8.0 %shard_map.121.refs_6_ = f32[1024,128]{1,0:T(8,128)S(1)} custom-call(s32[16]{0:T(128)S(1)} %dynamic-slice_bitcast_fusion.refs_0_.offs, bf16[128,1024]{1,0:T(8,128)(2,1)S(1)} %collective-permute-done.7.refs_1_.refs_6_, bf16[128,1024]{1,0:T(8,128)(2,1)S(1)} %collective-permute-done.8.refs_2_, bf16[128,1024]{1,0:T(8,128)(2,1)S(1)} %collective-permute-done.2.refs_3_, ...), custom_call_target="tpu_custom_call" | custom-call | flops 67108864 | bytes 524288 | tf_op jit(solution)/shard_map/pallas_call | solution.py:74
  31.9 1.6 %collective-permute-start.9 = (bf16[64,1024]{1,0:T(8,128)(2,1)S(1)}, bf16[64,1024]{1,0:T(8,128)(2,1)S(1)}, u32[]{:S(2)}, u32[]{:S(2)}) collective-permute-start(bf16[64,1024]{1,0:T(8,128)(2,1)S(1)} %slice.59), channel_id=1, source_target_pairs={{0,2},{1,3},{2,6},{3,7},{6,10},{7,11},{10,14},{11,15},{14,12},{15,... | collective-permute-start | bytes 393224 | tf_op jit(solution)/shard_map/ppermute | solution.py:268
  33.6 0.5 collective-permute-start.10
  34.8 0.5 collective-permute-start.15
  35.3 8.0 %shard_map.122.refs_5_ = f32[1024,128]{1,0:T(8,128)S(1)} custom-call(s32[16]{0:T(128)S(1)} %dynamic-slice_bitcast_fusion.refs_0_.offs, bf16[128,1024]{1,0:T(8,128)(2,1)S(1)} %collective-permute-done.11.refs_1_.refs_5_, bf16[128,1024]{1,0:T(8,128)(2,1)S(1)} %collective-permute-done.12.refs_2_.refs_6_, ...), custom_call_target="tpu_custom_call" | custom-call | flops 67108864 | bytes 524288 | tf_op jit(solution)/shard_map/pallas_call | solution.py:74
  43.4 0.2 collective-permute-start.13
  43.5 0.1 fusion.5.drive_ref
  43.7 0.6 convolution_multiply_fusion.1.deriv_ref
  44.3 6.2 %shard_map.123.acc_ref = f32[1024,128]{1,0:T(8,128)S(1)} custom-call(s32[16]{0:T(128)S(1)} %dynamic-slice_bitcast_fusion.refs_0_.offs, bf16[128,1024]{1,0:T(8,128)(2,1)S(1)} %collective-permute-done.14.refs_1_.refs_4_, bf16[128,1024]{1,0:T(8,128)(2,1)S(1)} %collective-permute-done.15.refs_2_.refs_5_, ...), custom_call_target="tpu_custom_call" | custom-call | flops 50331648 | bytes 393216 | tf_op jit(solution)/shard_map/pallas_call | solution.py:74
  50.6 4.2 %shard_map.124 = (f32[128,1024]{1,0:T(8,128)S(1)}, bf16[128,1024]{1,0:T(8,128)(2,1)S(1)}, bf16[1024,128]{1,0:T(8,128)(2,1)S(1)}, f32[8,1024]{1,0:T(8,128)S(1)}) custom-call(s32[16]{0:T(128)S(1)} %dynamic-slice_bitcast_fusion.refs_0_.offs, bf16[128,1024]{1,0:T(8,128)(2,1)S(1)} %collective-permute-done.13.x_ref.refs_7_, bf16[1024,16384]{1,0:T(8,128)(2,1)} %w_ref.21, ...), custom_call_target="tpu_custom_call" | custom-call | flops 33554432 | bytes 262144 | tf_op jit(solution)/shard_map/pallas_call | solution.py:119
  54.7 2.4 %shard_map.125 = (bf16[64,1024]{1,0:T(8,128)(2,1)S(1)}, bf16[64,1024]{1,0:T(8,128)(2,1)S(1)}) custom-call(s32[16]{0:T(128)S(1)} %dynamic-slice_bitcast_fusion.refs_0_.offs, bf16[128,1024]{1,0:T(8,128)(2,1)S(1)} %get-tuple-element.94.delta_ref, bf16[1024,16384]{1,0:T(8,128)(2,1)} %w_ref.21), custom_call_target="tpu_custom_call" | custom-call | flops 16777216 | bytes 131072 | tf_op jit(solution)/shard_map/pallas_call | solution.py:170
  57.2 0.5 collective-permute-start.17
  57.7 0.1 collective-permute-start.16
  57.8 2.4 %shard_map.126 = f32[128,1024]{1,0:T(8,128)S(1)} custom-call(s32[16]{0:T(128)S(1)} %dynamic-slice_bitcast_fusion.refs_0_.offs, bf16[128,1024]{1,0:T(8,128)(2,1)S(1)} %get-tuple-element.94.delta_ref, bf16[1024,16384]{1,0:T(8,128)(2,1)} %w_ref.21), custom_call_target="tpu_custom_call" | custom-call | flops 16777216 | bytes 131072 | tf_op jit(solution)/shard_map/pallas_call | solution.py:170
  60.3 4.1 %shard_map.127 = (bf16[80,1024]{1,0:T(8,128)(2,1)S(1)}, bf16[80,1024]{1,0:T(8,128)(2,1)S(1)}, bf16[96,1024]{1,0:T(8,128)(2,1)S(1)}) custom-call(s32[16]{0:T(128)S(1)} %dynamic-slice_bitcast_fusion.refs_0_.offs, bf16[128,1024]{1,0:T(8,128)(2,1)S(1)} %get-tuple-element.94.delta_ref, bf16[1024,16384]{1,0:T(8,128)(2,1)} %w_ref.21), custom_call_target="tpu_custom_call" | custom-call | flops 33554432 | bytes 262144 | tf_op jit(solution)/shard_map/pallas_call | solution.py:170
  64.4 0.5 collective-permute-start.21
  64.9 0.1 collective-permute-start.19
  65.0 0.4 collective-permute-start.18
  65.4 1.6 %collective-permute-start.20 = (bf16[64,1024]{1,0:T(8,128)(2,1)S(1)}, bf16[64,1024]{1,0:T(8,128)(2,1)S(1)}, u32[]{:S(2)}, u32[]{:S(2)}) collective-permute-start(bf16[64,1024]{1,0:T(8,128)(2,1)S(1)} %get-tuple-element.160), channel_id=1, source_target_pairs={{0,2},{1,3},{2,6},{3,7},{6,10},{7,11},{10,14},{11,15},{14,12},{15,... | collective-permute-start | bytes 393224 | tf_op jit(solution)/shard_map/ppermute | solution.py:268
  67.1 0.4 collective-permute-start.22
  67.5 4.1 %shard_map.128 = (f32[128,1024]{1,0:T(8,128)S(1)}, f32[128,1024]{1,0:T(8,128)S(1)}) custom-call(s32[16]{0:T(128)S(1)} %dynamic-slice_bitcast_fusion.refs_0_.offs, bf16[128,1024]{1,0:T(8,128)(2,1)S(1)} %get-tuple-element.94.delta_ref, bf16[1024,16384]{1,0:T(8,128)(2,1)} %w_ref.21), custom_call_target="tpu_custom_call" | custom-call | flops 33554432 | bytes 262144 | tf_op jit(solution)/shard_map/pallas_call | solution.py:170
  71.6 0.2 convert_add_fusion
  71.9 0.4 collective-permute-done.22
  72.3 1.6 %collective-permute-start.25 = (bf16[128,1024]{1,0:T(8,128)(2,1)S(1)}, bf16[128,1024]{1,0:T(8,128)(2,1)S(1)}, u32[]{:S(2)}, u32[]{:S(2)}) collective-permute-start(bf16[128,1024]{1,0:T(8,128)(2,1)S(1)} %pad_maximum_fusion.6), channel_id=1, source_target_pairs={{0,2},{1,3},{2,6},{3,7},{6,10},{7,11},{10,14},{11,15},{14,12},{15,... | collective-permute-start | bytes 786440 | tf_op jit(solution)/shard_map/ppermute | solution.py:268
  74.0 0.4 collective-permute-start.26
  74.4 4.1 %shard_map.129 = (bf16[80,1024]{1,0:T(8,128)(2,1)S(1)}, bf16[80,1024]{1,0:T(8,128)(2,1)S(1)}, bf16[96,1024]{1,0:T(8,128)(2,1)S(1)}) custom-call(s32[16]{0:T(128)S(1)} %dynamic-slice_bitcast_fusion.refs_0_.offs, bf16[128,1024]{1,0:T(8,128)(2,1)S(1)} %get-tuple-element.94.delta_ref, bf16[1024,16384]{1,0:T(8,128)(2,1)} %w_ref.21), custom_call_target="tpu_custom_call" | custom-call | flops 33554432 | bytes 262144 | tf_op jit(solution)/shard_map/pallas_call | solution.py:170
  78.6 0.5 collective-permute-start.24
  79.1 0.1 collective-permute-start.23
  79.2 4.1 %shard_map.130 = (f32[128,1024]{1,0:T(8,128)S(1)}, f32[128,1024]{1,0:T(8,128)S(1)}) custom-call(s32[16]{0:T(128)S(1)} %dynamic-slice_bitcast_fusion.refs_0_.offs, bf16[128,1024]{1,0:T(8,128)(2,1)S(1)} %get-tuple-element.94.delta_ref, bf16[1024,16384]{1,0:T(8,128)(2,1)} %w_ref.21), custom_call_target="tpu_custom_call" | custom-call | flops 33554432 | bytes 262144 | tf_op jit(solution)/shard_map/pallas_call | solution.py:170
  83.3 6.6 %shard_map.131 = (bf16[1024,16384]{1,0:T(8,128)(2,1)}, f32[8,128]{1,0:T(8,128)S(1)}) custom-call(s32[16]{0:T(128)S(1)} %dynamic-slice_bitcast_fusion.refs_0_.offs, bf16[1024,128]{1,0:T(8,128)(2,1)S(1)} %get-tuple-element.121.refs_1_, bf16[128,1024]{1,0:T(8,128)(2,1)S(1)} %bitcast_convert_fusion.refs_1_.refs_2_, ...), custom_call_target="tpu_custom_call" | custom-call | flops 83886080 | bytes 655360 | tf_op jit(solution)/shard_map/pallas_call | solution.py:209
  90.0 0.3 add_convert_fusion.2
  90.2 1.6 %collective-permute-start.30 = (bf16[128,1024]{1,0:T(8,128)(2,1)S(1)}, bf16[128,1024]{1,0:T(8,128)(2,1)S(1)}, u32[]{:S(2)}, u32[]{:S(2)}) collective-permute-start(bf16[128,1024]{1,0:T(8,128)(2,1)S(1)} %get-tuple-element.135), channel_id=1, source_target_pairs={{0,2},{1,3},{2,6},{3,7},{6,10},{7,11},{10,14},{11,15},{14,12},{15,... | collective-permute-start | bytes 786440 | tf_op jit(solution)/shard_map/ppermute | solution.py:268
  91.9 0.4 collective-permute-start.31
  92.3 4.1 %shard_map.132 = (bf16[80,1024]{1,0:T(8,128)(2,1)S(1)}, bf16[80,1024]{1,0:T(8,128)(2,1)S(1)}, bf16[96,1024]{1,0:T(8,128)(2,1)S(1)}) custom-call(s32[16]{0:T(128)S(1)} %dynamic-slice_bitcast_fusion.refs_0_.offs, bf16[128,1024]{1,0:T(8,128)(2,1)S(1)} %get-tuple-element.94.delta_ref, bf16[1024,16384]{1,0:T(8,128)(2,1)} %w_ref.21), custom_call_target="tpu_custom_call" | custom-call | flops 33554432 | bytes 262144 | tf_op jit(solution)/shard_map/pallas_call | solution.py:170
  96.5 0.5 collective-permute-start.29
  97.0 0.1 collective-permute-start.28
  97.1 0.6 fusion.12
  97.7 4.1 %shard_map.133 = (f32[128,1024]{1,0:T(8,128)S(1)}, f32[128,1024]{1,0:T(8,128)S(1)}) custom-call(s32[16]{0:T(128)S(1)} %dynamic-slice_bitcast_fusion.refs_0_.offs, bf16[128,1024]{1,0:T(8,128)(2,1)S(1)} %get-tuple-element.94.delta_ref, bf16[1024,16384]{1,0:T(8,128)(2,1)} %w_ref.21), custom_call_target="tpu_custom_call" | custom-call | flops 33554432 | bytes 262144 | tf_op jit(solution)/shard_map/pallas_call | solution.py:170
  101.8 6.6 %shard_map.134 = (bf16[1024,16384]{1,0:T(8,128)(2,1)}, f32[8,128]{1,0:T(8,128)S(1)}) custom-call(s32[16]{0:T(128)S(1)} %dynamic-slice_bitcast_fusion.refs_0_.offs, bf16[1024,128]{1,0:T(8,128)(2,1)S(1)} %get-tuple-element.121.refs_1_, bf16[128,1024]{1,0:T(8,128)(2,1)S(1)} %collective-permute-done.8.refs_2_, ...), custom_call_target="tpu_custom_call", output_to_operand_aliasing={{0}: (7, {})} | custom-call | flops 83886080 | bytes 655360 | tf_op jit(solution)/shard_map/pallas_call | solution.py:209
  108.5 0.3 add_convert_fusion
  108.7 2.4 %shard_map.136 = (bf16[64,1024]{1,0:T(8,128)(2,1)S(1)}, bf16[64,1024]{1,0:T(8,128)(2,1)S(1)}) custom-call(s32[16]{0:T(128)S(1)} %dynamic-slice_bitcast_fusion.refs_0_.offs, bf16[128,1024]{1,0:T(8,128)(2,1)S(1)} %get-tuple-element.94.delta_ref, bf16[1024,16384]{1,0:T(8,128)(2,1)} %w_ref.21), custom_call_target="tpu_custom_call" | custom-call | flops 16777216 | bytes 131072 | tf_op jit(solution)/shard_map/pallas_call | solution.py:170
  111.2 0.5 collective-permute-start.34
  111.7 0.1 collective-permute-start.33
  111.8 0.7 broadcast_multiply_fusion
  112.5 1.6 %collective-permute-start.35 = (bf16[128,1024]{1,0:T(8,128)(2,1)S(1)}, bf16[128,1024]{1,0:T(8,128)(2,1)S(1)}, u32[]{:S(2)}, u32[]{:S(2)}) collective-permute-start(bf16[128,1024]{1,0:T(8,128)(2,1)S(1)} %get-tuple-element.154), channel_id=1, source_target_pairs={{0,2},{1,3},{2,6},{3,7},{6,10},{7,11},{10,14},{11,15},{14,12},{15,... | collective-permute-start | bytes 786440 | tf_op jit(solution)/shard_map/ppermute | solution.py:268
  114.1 0.4 collective-permute-start.36
  114.5 2.4 %shard_map.137 = f32[128,1024]{1,0:T(8,128)S(1)} custom-call(s32[16]{0:T(128)S(1)} %dynamic-slice_bitcast_fusion.refs_0_.offs, bf16[128,1024]{1,0:T(8,128)(2,1)S(1)} %get-tuple-element.94.delta_ref, bf16[1024,16384]{1,0:T(8,128)(2,1)} %w_ref.21), custom_call_target="tpu_custom_call" | custom-call | flops 16777216 | bytes 131072 | tf_op jit(solution)/shard_map/pallas_call | solution.py:170
  116.9 7.4 %shard_map.135 = (bf16[1024,16384]{1,0:T(8,128)(2,1)}, f32[8,128]{1,0:T(8,128)}) custom-call(s32[16]{0:T(128)S(1)} %dynamic-slice_bitcast_fusion.refs_0_.offs, bf16[1024,128]{1,0:T(8,128)(2,1)S(1)} %get-tuple-element.121.refs_1_, bf16[128,1024]{1,0:T(8,128)(2,1)S(1)} %collective-permute-done.5.refs_3_.refs_2_, ...), custom_call_target="tpu_custom_call", output_to_operand_aliasing={{0}: (8, {})} | custom-call | flops 100663296 | bytes 786432 | tf_op jit(solution)/shard_map/pallas_call | solution.py:209
  124.3 0.7 fusion.2
  125.0 0.9 add_bitcast_fusion
  (65 shorter events, 0.6 us)
Async XLA Ops:
  0.6 42.9 %copy-start = (f32[16,1024]{1,0:T(8,128)S(1)}, f32[16,1024]{1,0:T(8,128)}, u32[]{:S(2)}) copy-start(f32[16,1024]{1,0:T(8,128)} %param.10) | copy-start | bytes 196612
  1.8 9.4 %collective-permute-start = (bf16[128,1024]{1,0:T(8,128)(2,1)S(1)}, bf16[128,1024]{1,0:T(8,128)(2,1)S(1)}, u32[]{:S(2)}, u32[]{:S(2)}) collective-permute-start(bf16[128,1024]{1,0:T(8,128)(2,1)S(1)} %bitcast_convert_fusion.refs_1_.refs_2_), channel_id=1, source_target_pairs={{0,2},{1,3},{2,6},{3,7},{6,10},{7,11},{10,14},{11,15},{14,12},{15,... | collective-permute-start | bytes 786440 | tf_op jit(solution)/shard_map/ppermute | solution.py:268
  4.8 7.8 %collective-permute-start.1 = (bf16[128,1024]{1,0:T(8,128)(2,1)S(1)}, bf16[128,1024]{1,0:T(8,128)(2,1)S(1)}, u32[]{:S(2)}, u32[]{:S(2)}) collective-permute-start(bf16[128,1024]{1,0:T(8,128)(2,1)S(1)} %bitcast_convert_fusion.refs_1_.refs_2_), channel_id=1, source_target_pairs={{0,4},{1,5},{2,0},{3,1},{6,2},{7,3},{10,6},{11,7},{14,10},{15,11},... | collective-permute-start | bytes 786440 | tf_op jit(solution)/shard_map/ppermute | solution.py:268
  4.9 10.2 %collective-permute-start.4 = (bf16[128,1024]{1,0:T(8,128)(2,1)S(1)}, bf16[128,1024]{1,0:T(8,128)(2,1)S(1)}, u32[]{:S(2)}, u32[]{:S(2)}) collective-permute-start(bf16[128,1024]{1,0:T(8,128)(2,1)S(1)} %bitcast_convert_fusion.refs_1_.refs_2_), channel_id=1, source_target_pairs={{0,1},{1,0},{2,3},{3,2},{4,5},{5,4},{6,7},{7,6},{8,9},{9,8},{10,11... | collective-permute-start | bytes 786440 | tf_op jit(solution)/shard_map/ppermute | solution.py:271
  12.5 8.8 %collective-permute-start.2 = (bf16[128,1024]{1,0:T(8,128)(2,1)S(1)}, bf16[128,1024]{1,0:T(8,128)(2,1)S(1)}, u32[]{:S(2)}, u32[]{:S(2)}) collective-permute-start(bf16[128,1024]{1,0:T(8,128)(2,1)S(1)} %collective-permute-done.refs_2_.refs_4_), channel_id=1, source_target_pairs={{0,2},{1,3},{2,6},{3,7},{6,10},{7,11},{10,14},{11,15},{14,12},{15,... | collective-permute-start | bytes 786440 | tf_op jit(solution)/shard_map/ppermute | solution.py:268
  14.1 7.2 %collective-permute-start.3 = (bf16[128,1024]{1,0:T(8,128)(2,1)S(1)}, bf16[128,1024]{1,0:T(8,128)(2,1)S(1)}, u32[]{:S(2)}, u32[]{:S(2)}) collective-permute-start(bf16[128,1024]{1,0:T(8,128)(2,1)S(1)} %collective-permute-done.1.refs_3_.refs_5_), channel_id=1, source_target_pairs={{0,4},{1,5},{2,0},{3,1},{6,2},{7,3},{10,6},{11,7},{14,10},{15,11},... | collective-permute-start | bytes 786440 | tf_op jit(solution)/shard_map/ppermute | solution.py:268
  14.5 8.9 %collective-permute-start.7 = (bf16[128,1024]{1,0:T(8,128)(2,1)S(1)}, bf16[128,1024]{1,0:T(8,128)(2,1)S(1)}, u32[]{:S(2)}, u32[]{:S(2)}) collective-permute-start(bf16[128,1024]{1,0:T(8,128)(2,1)S(1)} %collective-permute-done.refs_2_.refs_4_), channel_id=1, source_target_pairs={{0,1},{1,0},{2,3},{3,2},{4,5},{5,4},{6,7},{7,6},{8,9},{9,8},{10,11... | collective-permute-start | bytes 786440 | tf_op jit(solution)/shard_map/ppermute | solution.py:271
  14.5 9.4 %collective-permute-start.8 = (bf16[128,1024]{1,0:T(8,128)(2,1)S(1)}, bf16[128,1024]{1,0:T(8,128)(2,1)S(1)}, u32[]{:S(2)}, u32[]{:S(2)}) collective-permute-start(bf16[128,1024]{1,0:T(8,128)(2,1)S(1)} %collective-permute-done.1.refs_3_.refs_5_), channel_id=1, source_target_pairs={{0,1},{1,0},{2,3},{3,2},{4,5},{5,4},{6,7},{7,6},{8,9},{9,8},{10,11... | collective-permute-start | bytes 786440 | tf_op jit(solution)/shard_map/ppermute | solution.py:271
  21.3 22.4 %copy-start.2 = (f32[1,128,1024]{2,1,0:T(8,128)S(1)}, f32[1,128,1024]{2,1,0:T(8,128)}, u32[]{:S(2)}) copy-start(f32[1,128,1024]{2,1,0:T(8,128)} %param.8) | copy-start | bytes 1572868
  21.3 22.4 %copy-start.5 = (f32[128,128]{1,0:T(8,128)S(1)}, f32[128,128]{1,0:T(8,128)}, u32[]{:S(2)}) copy-start(f32[128,128]{1,0:T(8,128)} %constant.15.clone) | copy-start | bytes 196612
  21.3 10.6 %collective-permute-start.5 = (bf16[128,1024]{1,0:T(8,128)(2,1)S(1)}, bf16[128,1024]{1,0:T(8,128)(2,1)S(1)}, u32[]{:S(2)}, u32[]{:S(2)}) collective-permute-start(bf16[128,1024]{1,0:T(8,128)(2,1)S(1)} %collective-permute-done.2.refs_3_), channel_id=1, source_target_pairs={{0,2},{1,3},{2,6},{3,7},{6,10},{7,11},{10,14},{11,15},{14,12},{15,... | collective-permute-start | bytes 786440 | tf_op jit(solution)/shard_map/ppermute | solution.py:268
  23.0 9.0 %collective-permute-start.6 = (bf16[128,1024]{1,0:T(8,128)(2,1)S(1)}, bf16[128,1024]{1,0:T(8,128)(2,1)S(1)}, u32[]{:S(2)}, u32[]{:S(2)}) collective-permute-start(bf16[128,1024]{1,0:T(8,128)(2,1)S(1)} %collective-permute-done.3.refs_4_), channel_id=1, source_target_pairs={{0,4},{1,5},{2,0},{3,1},{6,2},{7,3},{10,6},{11,7},{14,10},{15,11},... | collective-permute-start | bytes 786440 | tf_op jit(solution)/shard_map/ppermute | solution.py:268
  23.4 11.4 %collective-permute-start.11 = (bf16[128,1024]{1,0:T(8,128)(2,1)S(1)}, bf16[128,1024]{1,0:T(8,128)(2,1)S(1)}, u32[]{:S(2)}, u32[]{:S(2)}) collective-permute-start(bf16[128,1024]{1,0:T(8,128)(2,1)S(1)} %collective-permute-done.2.refs_3_), channel_id=1, source_target_pairs={{0,1},{1,0},{2,3},{3,2},{4,5},{5,4},{6,7},{7,6},{8,9},{9,8},{10,11... | collective-permute-start | bytes 786440 | tf_op jit(solution)/shard_map/ppermute | solution.py:271
  23.4 11.9 %collective-permute-start.12 = (bf16[128,1024]{1,0:T(8,128)(2,1)S(1)}, bf16[128,1024]{1,0:T(8,128)(2,1)S(1)}, u32[]{:S(2)}, u32[]{:S(2)}) collective-permute-start(bf16[128,1024]{1,0:T(8,128)(2,1)S(1)} %collective-permute-done.3.refs_4_), channel_id=1, source_target_pairs={{0,1},{1,0},{2,3},{3,2},{4,5},{5,4},{6,7},{7,6},{8,9},{9,8},{10,11... | collective-permute-start | bytes 786440 | tf_op jit(solution)/shard_map/ppermute | solution.py:271
  31.9 11.4 %collective-permute-start.9 = (bf16[64,1024]{1,0:T(8,128)(2,1)S(1)}, bf16[64,1024]{1,0:T(8,128)(2,1)S(1)}, u32[]{:S(2)}, u32[]{:S(2)}) collective-permute-start(bf16[64,1024]{1,0:T(8,128)(2,1)S(1)} %slice.59), channel_id=1, source_target_pairs={{0,2},{1,3},{2,6},{3,7},{6,10},{7,11},{10,14},{11,15},{14,12},{15,... | collective-permute-start | bytes 393224 | tf_op jit(solution)/shard_map/ppermute | solution.py:268
  33.6 9.8 %collective-permute-start.10 = (bf16[64,1024]{1,0:T(8,128)(2,1)S(1)}, bf16[64,1024]{1,0:T(8,128)(2,1)S(1)}, u32[]{:S(2)}, u32[]{:S(2)}) collective-permute-start(bf16[64,1024]{1,0:T(8,128)(2,1)S(1)} %slice.60), channel_id=1, source_target_pairs={{0,4},{1,5},{2,0},{3,1},{6,2},{7,3},{10,6},{11,7},{14,10},{15,11},... | collective-permute-start | bytes 393224 | tf_op jit(solution)/shard_map/ppermute | solution.py:268
  34.7 15.8 %copy-start.3 = (f32[1024]{0:T(1024)S(1)}, f32[1024]{0:T(1024)}, u32[]{:S(2)}) copy-start(f32[1024]{0:T(1024)} %param.12) | copy-start | bytes 12292
  34.7 15.8 %copy-start.4 = (f32[1024]{0:T(1024)S(1)}, f32[1024]{0:T(1024)}, u32[]{:S(2)}) copy-start(f32[1024]{0:T(1024)} %param.11) | copy-start | bytes 12292
  34.8 9.5 %collective-permute-start.14 = (bf16[128,1024]{1,0:T(8,128)(2,1)S(1)}, bf16[128,1024]{1,0:T(8,128)(2,1)S(1)}, u32[]{:S(2)}, u32[]{:S(2)}) collective-permute-start(bf16[128,1024]{1,0:T(8,128)(2,1)S(1)} %collective-permute-done.5.refs_3_.refs_2_), channel_id=1, source_target_pairs={{0,1},{1,0},{2,3},{3,2},{4,5},{5,4},{6,7},{7,6},{8,9},{9,8},{10,11... | collective-permute-start | bytes 786440 | tf_op jit(solution)/shard_map/ppermute | solution.py:271
  34.8 9.5 %collective-permute-start.15 = (bf16[128,1024]{1,0:T(8,128)(2,1)S(1)}, bf16[128,1024]{1,0:T(8,128)(2,1)S(1)}, u32[]{:S(2)}, u32[]{:S(2)}) collective-permute-start(bf16[128,1024]{1,0:T(8,128)(2,1)S(1)} %collective-permute-done.6.refs_4_.refs_3_), channel_id=1, source_target_pairs={{0,1},{1,0},{2,3},{3,2},{4,5},{5,4},{6,7},{7,6},{8,9},{9,8},{10,11... | collective-permute-start | bytes 786440 | tf_op jit(solution)/shard_map/ppermute | solution.py:271
  43.4 7.2 %collective-permute-start.13 = (bf16[128,1024]{1,0:T(8,128)(2,1)S(1)}, bf16[128,1024]{1,0:T(8,128)(2,1)S(1)}, u32[]{:S(2)}, u32[]{:S(2)}) collective-permute-start(bf16[128,1024]{1,0:T(8,128)(2,1)S(1)} %constant_dynamic-update-slice_fusion.refs_3_.refs_6_), channel_id=1, source_target_pairs={{0,1},{1,0},{2,3},{3,2},{4,5},{5,4},{6,7},{7,6},{8,9},{9,8},{10,11... | collective-permute-start | bytes 786440 | tf_op jit(solution)/shard_map/ppermute | solution.py:271
  57.2 3.0 %collective-permute-start.17 = (bf16[64,1024]{1,0:T(8,128)(2,1)S(1)}, bf16[64,1024]{1,0:T(8,128)(2,1)S(1)}, u32[]{:S(2)}, u32[]{:S(2)}) collective-permute-start(bf16[64,1024]{1,0:T(8,128)(2,1)S(1)} %get-tuple-element.99), channel_id=1, source_target_pairs={{0,1},{1,0},{2,3},{3,2},{4,5},{5,4},{6,7},{7,6},{8,9},{9,8},{10,11... | collective-permute-start | bytes 393224 | tf_op jit(solution)/shard_map/ppermute | solution.py:271
  57.7 2.5 %collective-permute-start.16 = (bf16[64,1024]{1,0:T(8,128)(2,1)S(1)}, bf16[64,1024]{1,0:T(8,128)(2,1)S(1)}, u32[]{:S(2)}, u32[]{:S(2)}) collective-permute-start(bf16[64,1024]{1,0:T(8,128)(2,1)S(1)} %get-tuple-element.98), channel_id=1, source_target_pairs={{0,1},{1,0},{2,3},{3,2},{4,5},{5,4},{6,7},{7,6},{8,9},{9,8},{10,11... | collective-permute-start | bytes 393224 | tf_op jit(solution)/shard_map/ppermute | solution.py:271
  64.4 7.2 %collective-permute-start.21 = (bf16[96,1024]{1,0:T(8,128)(2,1)S(1)}, bf16[96,1024]{1,0:T(8,128)(2,1)S(1)}, u32[]{:S(2)}, u32[]{:S(2)}) collective-permute-start(bf16[96,1024]{1,0:T(8,128)(2,1)S(1)} %get-tuple-element.110), channel_id=1, source_target_pairs={{0,1},{1,0},{2,3},{3,2},{4,5},{5,4},{6,7},{7,6},{8,9},{9,8},{10,11... | collective-permute-start | bytes 589832 | tf_op jit(solution)/shard_map/ppermute | solution.py:271
  64.9 6.7 %collective-permute-start.19 = (bf16[80,1024]{1,0:T(8,128)(2,1)S(1)}, bf16[80,1024]{1,0:T(8,128)(2,1)S(1)}, u32[]{:S(2)}, u32[]{:S(2)}) collective-permute-start(bf16[80,1024]{1,0:T(8,128)(2,1)S(1)} %get-tuple-element.107), channel_id=1, source_target_pairs={{0,1},{1,0},{2,3},{3,2},{4,5},{5,4},{6,7},{7,6},{8,9},{9,8},{10,11... | collective-permute-start | bytes 491528 | tf_op jit(solution)/shard_map/ppermute | solution.py:271
  65.0 6.6 %collective-permute-start.18 = (bf16[80,1024]{1,0:T(8,128)(2,1)S(1)}, bf16[80,1024]{1,0:T(8,128)(2,1)S(1)}, u32[]{:S(2)}, u32[]{:S(2)}) collective-permute-start(bf16[80,1024]{1,0:T(8,128)(2,1)S(1)} %get-tuple-element.106), channel_id=1, source_target_pairs={{0,1},{1,0},{2,3},{3,2},{4,5},{5,4},{6,7},{7,6},{8,9},{9,8},{10,11... | collective-permute-start | bytes 491528 | tf_op jit(solution)/shard_map/ppermute | solution.py:271
  65.4 6.4 %collective-permute-start.20 = (bf16[64,1024]{1,0:T(8,128)(2,1)S(1)}, bf16[64,1024]{1,0:T(8,128)(2,1)S(1)}, u32[]{:S(2)}, u32[]{:S(2)}) collective-permute-start(bf16[64,1024]{1,0:T(8,128)(2,1)S(1)} %get-tuple-element.160), channel_id=1, source_target_pairs={{0,2},{1,3},{2,6},{3,7},{6,10},{7,11},{10,14},{11,15},{14,12},{15,... | collective-permute-start | bytes 393224 | tf_op jit(solution)/shard_map/ppermute | solution.py:268
  67.1 5.2 %collective-permute-start.22 = (bf16[64,1024]{1,0:T(8,128)(2,1)S(1)}, bf16[64,1024]{1,0:T(8,128)(2,1)S(1)}, u32[]{:S(2)}, u32[]{:S(2)}) collective-permute-start(bf16[64,1024]{1,0:T(8,128)(2,1)S(1)} %get-tuple-element.159), channel_id=1, source_target_pairs={{0,4},{1,5},{2,0},{3,1},{6,2},{7,3},{10,6},{11,7},{14,10},{15,11},... | collective-permute-start | bytes 393224 | tf_op jit(solution)/shard_map/ppermute | solution.py:268
  72.3 17.6 %collective-permute-start.25 = (bf16[128,1024]{1,0:T(8,128)(2,1)S(1)}, bf16[128,1024]{1,0:T(8,128)(2,1)S(1)}, u32[]{:S(2)}, u32[]{:S(2)}) collective-permute-start(bf16[128,1024]{1,0:T(8,128)(2,1)S(1)} %pad_maximum_fusion.6), channel_id=1, source_target_pairs={{0,2},{1,3},{2,6},{3,7},{6,10},{7,11},{10,14},{11,15},{14,12},{15,... | collective-permute-start | bytes 786440 | tf_op jit(solution)/shard_map/ppermute | solution.py:268
  74.0 16.0 %collective-permute-start.26 = (bf16[128,1024]{1,0:T(8,128)(2,1)S(1)}, bf16[128,1024]{1,0:T(8,128)(2,1)S(1)}, u32[]{:S(2)}, u32[]{:S(2)}) collective-permute-start(bf16[128,1024]{1,0:T(8,128)(2,1)S(1)} %pad_maximum_fusion.7), channel_id=1, source_target_pairs={{0,4},{1,5},{2,0},{3,1},{6,2},{7,3},{10,6},{11,7},{14,10},{15,11},... | collective-permute-start | bytes 786440 | tf_op jit(solution)/shard_map/ppermute | solution.py:268
  78.5 11.4 %collective-permute-start.27 = (bf16[96,1024]{1,0:T(8,128)(2,1)S(1)}, bf16[96,1024]{1,0:T(8,128)(2,1)S(1)}, u32[]{:S(2)}, u32[]{:S(2)}) collective-permute-start(bf16[96,1024]{1,0:T(8,128)(2,1)S(1)} %get-tuple-element.125), channel_id=1, source_target_pairs={{0,1},{1,0},{2,3},{3,2},{4,5},{5,4},{6,7},{7,6},{8,9},{9,8},{10,11... | collective-permute-start | bytes 589832 | tf_op jit(solution)/shard_map/ppermute | solution.py:271
  78.6 11.3 %collective-permute-start.24 = (bf16[80,1024]{1,0:T(8,128)(2,1)S(1)}, bf16[80,1024]{1,0:T(8,128)(2,1)S(1)}, u32[]{:S(2)}, u32[]{:S(2)}) collective-permute-start(bf16[80,1024]{1,0:T(8,128)(2,1)S(1)} %get-tuple-element.118), channel_id=1, source_target_pairs={{0,1},{1,0},{2,3},{3,2},{4,5},{5,4},{6,7},{7,6},{8,9},{9,8},{10,11... | collective-permute-start | bytes 491528 | tf_op jit(solution)/shard_map/ppermute | solution.py:271
  79.1 10.8 %collective-permute-start.23 = (bf16[80,1024]{1,0:T(8,128)(2,1)S(1)}, bf16[80,1024]{1,0:T(8,128)(2,1)S(1)}, u32[]{:S(2)}, u32[]{:S(2)}) collective-permute-start(bf16[80,1024]{1,0:T(8,128)(2,1)S(1)} %get-tuple-element.117), channel_id=1, source_target_pairs={{0,1},{1,0},{2,3},{3,2},{4,5},{5,4},{6,7},{7,6},{8,9},{9,8},{10,11... | collective-permute-start | bytes 491528 | tf_op jit(solution)/shard_map/ppermute | solution.py:271
  90.2 18.2 %collective-permute-start.30 = (bf16[128,1024]{1,0:T(8,128)(2,1)S(1)}, bf16[128,1024]{1,0:T(8,128)(2,1)S(1)}, u32[]{:S(2)}, u32[]{:S(2)}) collective-permute-start(bf16[128,1024]{1,0:T(8,128)(2,1)S(1)} %get-tuple-element.135), channel_id=1, source_target_pairs={{0,2},{1,3},{2,6},{3,7},{6,10},{7,11},{10,14},{11,15},{14,12},{15,... | collective-permute-start | bytes 786440 | tf_op jit(solution)/shard_map/ppermute | solution.py:268
  91.9 16.6 %collective-permute-start.31 = (bf16[128,1024]{1,0:T(8,128)(2,1)S(1)}, bf16[128,1024]{1,0:T(8,128)(2,1)S(1)}, u32[]{:S(2)}, u32[]{:S(2)}) collective-permute-start(bf16[128,1024]{1,0:T(8,128)(2,1)S(1)} %get-tuple-element.136), channel_id=1, source_target_pairs={{0,4},{1,5},{2,0},{3,1},{6,2},{7,3},{10,6},{11,7},{14,10},{15,11},... | collective-permute-start | bytes 786440 | tf_op jit(solution)/shard_map/ppermute | solution.py:268
  96.4 12.0 %collective-permute-start.32 = (bf16[96,1024]{1,0:T(8,128)(2,1)S(1)}, bf16[96,1024]{1,0:T(8,128)(2,1)S(1)}, u32[]{:S(2)}, u32[]{:S(2)}) collective-permute-start(bf16[96,1024]{1,0:T(8,128)(2,1)S(1)} %get-tuple-element.142), channel_id=1, source_target_pairs={{0,1},{1,0},{2,3},{3,2},{4,5},{5,4},{6,7},{7,6},{8,9},{9,8},{10,11... | collective-permute-start | bytes 589832 | tf_op jit(solution)/shard_map/ppermute | solution.py:271
  96.5 11.9 %collective-permute-start.29 = (bf16[80,1024]{1,0:T(8,128)(2,1)S(1)}, bf16[80,1024]{1,0:T(8,128)(2,1)S(1)}, u32[]{:S(2)}, u32[]{:S(2)}) collective-permute-start(bf16[80,1024]{1,0:T(8,128)(2,1)S(1)} %get-tuple-element.134), channel_id=1, source_target_pairs={{0,1},{1,0},{2,3},{3,2},{4,5},{5,4},{6,7},{7,6},{8,9},{9,8},{10,11... | collective-permute-start | bytes 491528 | tf_op jit(solution)/shard_map/ppermute | solution.py:271
  97.0 11.4 %collective-permute-start.28 = (bf16[80,1024]{1,0:T(8,128)(2,1)S(1)}, bf16[80,1024]{1,0:T(8,128)(2,1)S(1)}, u32[]{:S(2)}, u32[]{:S(2)}) collective-permute-start(bf16[80,1024]{1,0:T(8,128)(2,1)S(1)} %get-tuple-element.133), channel_id=1, source_target_pairs={{0,1},{1,0},{2,3},{3,2},{4,5},{5,4},{6,7},{7,6},{8,9},{9,8},{10,11... | collective-permute-start | bytes 491528 | tf_op jit(solution)/shard_map/ppermute | solution.py:271
  111.2 13.1 %collective-permute-start.34 = (bf16[64,1024]{1,0:T(8,128)(2,1)S(1)}, bf16[64,1024]{1,0:T(8,128)(2,1)S(1)}, u32[]{:S(2)}, u32[]{:S(2)}) collective-permute-start(bf16[64,1024]{1,0:T(8,128)(2,1)S(1)} %get-tuple-element.153), channel_id=1, source_target_pairs={{0,1},{1,0},{2,3},{3,2},{4,5},{5,4},{6,7},{7,6},{8,9},{9,8},{10,11... | collective-permute-start | bytes 393224 | tf_op jit(solution)/shard_map/ppermute | solution.py:271
  111.7 12.6 %collective-permute-start.33 = (bf16[64,1024]{1,0:T(8,128)(2,1)S(1)}, bf16[64,1024]{1,0:T(8,128)(2,1)S(1)}, u32[]{:S(2)}, u32[]{:S(2)}) collective-permute-start(bf16[64,1024]{1,0:T(8,128)(2,1)S(1)} %get-tuple-element.152), channel_id=1, source_target_pairs={{0,1},{1,0},{2,3},{3,2},{4,5},{5,4},{6,7},{7,6},{8,9},{9,8},{10,11... | collective-permute-start | bytes 393224 | tf_op jit(solution)/shard_map/ppermute | solution.py:271
  111.8 14.2 %copy-start.1 = (f32[16,1024]{1,0:T(8,128)S(1)}, f32[16,1024]{1,0:T(8,128)}, u32[]{:S(2)}) copy-start(f32[16,1024]{1,0:T(8,128)} %param.10) | copy-start | bytes 196612
  112.5 12.6 %collective-permute-start.35 = (bf16[128,1024]{1,0:T(8,128)(2,1)S(1)}, bf16[128,1024]{1,0:T(8,128)(2,1)S(1)}, u32[]{:S(2)}, u32[]{:S(2)}) collective-permute-start(bf16[128,1024]{1,0:T(8,128)(2,1)S(1)} %get-tuple-element.154), channel_id=1, source_target_pairs={{0,2},{1,3},{2,6},{3,7},{6,10},{7,11},{10,14},{11,15},{14,12},{15,... | collective-permute-start | bytes 786440 | tf_op jit(solution)/shard_map/ppermute | solution.py:268
  114.1 11.0 %collective-permute-start.36 = (bf16[128,1024]{1,0:T(8,128)(2,1)S(1)}, bf16[128,1024]{1,0:T(8,128)(2,1)S(1)}, u32[]{:S(2)}, u32[]{:S(2)}) collective-permute-start(bf16[128,1024]{1,0:T(8,128)(2,1)S(1)} %get-tuple-element.155), channel_id=1, source_target_pairs={{0,4},{1,5},{2,0},{3,1},{6,2},{7,3},{10,6},{11,7},{14,10},{15,11},... | collective-permute-start | bytes 786440 | tf_op jit(solution)/shard_map/ppermute | solution.py:268

commit v2 on v1

v2 whole, which is shorter than its diff:
```python
import functools

import jax
import jax.numpy as jnp
import numpy as np
from jax import lax
from jax.experimental import pallas as pl
from jax.experimental.pallas import tpu as pltpu
from jax.sharding import PartitionSpec as P

SCALE = 2.0 / 1024.0
VMEM_LIMIT = 16 * 2**20
PARTS = 2
LONGEST_RING = 16


def cheb_matrix(count):
    index = np.arange(count)
    points = np.cos(np.pi * index / (count - 1))
    signs = np.where(index % 2 == 0, 1.0, -1.0)
    weight_c = signs * np.where((index == 0) | (index == count - 1), 2.0, 1.0)
    same = index[:, None] == index[None, :]
    spread = np.where(same, 1.0, points[:, None] - points[None, :])
    off = np.where(same, 0.0, weight_c[:, None] / weight_c[None, :] / spread)
    return jnp.asarray((off - np.diag(np.sum(off, axis=1))).astype(np.float32))


def chip_ring(chips):
    rows = 4
    cols = chips // rows
    cells = [(0, col) for col in range(cols)]
    for row in range(1, rows):
        span = range(1, cols)
        cells += [(row, col) for col in (reversed(span) if row % 2 else span)]
    cells += [(row, 0) for row in range(rows - 1, 0, -1)]
    return [row * cols + col for row, col in cells]


VMEM_REF = pl.BlockSpec(memory_space=pltpu.VMEM)
SMEM_REF = pl.BlockSpec(memory_space=pltpu.SMEM)
ANY_REF = pl.BlockSpec(memory_space=pl.ANY)
HBM_REF = pl.BlockSpec(memory_space=pltpu.HBM)


def cost(products, nodes, slab, rows):
    return pl.CostEstimate(
        flops=2 * products * nodes * slab * rows // 16,
        bytes_accessed=2 * products * slab * rows // 16,
        transcendentals=0,
    )


def call(kernel, out_shape, out_specs, scratch, costs, aliases=None):
    def run(operands, in_specs):
        return pl.pallas_call(
            kernel,
            out_shape=out_shape,
            in_specs=in_specs,
            out_specs=out_specs,
            scratch_shapes=scratch,
            input_output_aliases=aliases or {},
            compiler_params=pltpu.CompilerParams(vmem_limit_bytes=VMEM_LIMIT),
            cost_estimate=costs,
        )(*operands)

    return run


def columns_of(offs_ref, at, slab):
    return pl.ds(pl.multiple_of(offs_ref[at] * slab, slab), slab)


def pre_kernel(base, count, loads, first, *refs):
    offs_ref, w_ref = refs[:2]
    xs = refs[2 : 2 + count]
    rest = refs[2 + count :]
    acc_ref, rest = (None, rest) if first else (rest[0], rest[1:])
    out_ref, blocks, sems = rest[0], rest[1 : 1 + loads], rest[-1]
    rows, slab = blocks[0].shape
    tile = rows // PARTS
    copies = []
    for at in range(loads):
        here = columns_of(offs_ref, base + at, slab)
        for part in range(PARTS):
            band = pl.ds(part * tile, tile)
            copy = pltpu.make_async_copy(
                w_ref.at[band, here], blocks[at].at[band, :], sems.at[at, part]
            )
            copy.start()
            copies.append(copy)
    for at in range(count):
        for part in range(PARTS):
            copies[at * PARTS + part].wait()
            band = pl.ds(part * tile, tile)
            total = lax.dot_general(
                blocks[at][band, :], xs[at][...], (((1,), (1,)), ((), ())),
                preferred_element_type=jnp.float32,
            )
            if at > 0:
                total += out_ref[band, :]
            elif not first:
                total += acc_ref[band, :]
            out_ref[band, :] = total
    for copy in copies[count * PARTS :]:
        copy.wait()


def add_products(offs, base, xs, weights, acc, slab, loads):
    nodes, rows, count = xs[0].shape[0], weights.shape[0], len(xs)
    first = acc is None
    out = call(
        functools.partial(pre_kernel, base, count, loads, first),
        [jax.ShapeDtypeStruct((rows, nodes), jnp.float32)]
        + [pltpu.VMEM((rows, slab), jnp.bfloat16)] * loads,
        [VMEM_REF] * (1 + loads),
        [pltpu.SemaphoreType.DMA((loads, PARTS))],
        cost(count, nodes, slab, rows),
    )(
        [offs, weights, *xs] + ([] if first else [acc]),
        [SMEM_REF, HBM_REF] + [VMEM_REF] * (count + (0 if first else 1)),
    )
    return out[0], out[1:]


def middle_kernel(
    x_ref, w_ref, acc_ref, deriv_ref, states_ref, drive_ref, eps_ref, decay_ref,
    resid_ref, delta_ref, delta_t_ref, sums_ref,
):
    rows = w_ref.shape[0]
    tile = max(rows // 4, 128)
    for start in range(0, rows, tile):
        band = pl.ds(start, tile)
        part = acc_ref[band, :] + lax.dot_general(
            w_ref[band, :], x_ref[...], (((1,), (1,)), ((), ())),
            preferred_element_type=jnp.float32,
        )
        states = states_ref[:, band]
        act = jnp.tanh(part.T + drive_ref[:, band])
        eps = eps_ref[:, band]
        resid = deriv_ref[:, band] - (eps * act - decay_ref[:, band] * states)
        delta = (-eps * (1.0 - act * act) * resid).astype(jnp.bfloat16)
        wide = delta.astype(jnp.float32)
        resid_ref[:, band] = resid
        delta_ref[:, band] = delta
        delta_t_ref[band, :] = wide.T.astype(jnp.bfloat16)
        sums_ref[0:1, band] = jnp.sum(wide, axis=0, keepdims=True)
        sums_ref[1:2, band] = -jnp.sum(act * resid, axis=0, keepdims=True)
        sums_ref[2:3, band] = jnp.sum(states * resid, axis=0, keepdims=True)


def middle(x, block, acc, deriv, states, drive, eps, decay):
    nodes, slab = x.shape
    rows = block.shape[0]
    return call(
        middle_kernel,
        [
            jax.ShapeDtypeStruct((nodes, rows), jnp.float32),
            jax.ShapeDtypeStruct((nodes, rows), jnp.bfloat16),
            jax.ShapeDtypeStruct((rows, nodes), jnp.bfloat16),
            jax.ShapeDtypeStruct((8, rows), jnp.float32),
        ],
        [VMEM_REF] * 4,
        [],
        cost(2, nodes, slab, rows),
    )([x, block, acc, deriv, states, drive, eps, decay], [VMEM_REF] * 8)


def share_kernel(cuts, offs_ref, delta_ref, *refs):
    nodes = delta_ref.shape[0]
    count = cuts[-1] // nodes
    blocks, outs = refs[: 2 * count], refs[2 * count :]
    slab = blocks[0].shape[1]
    tile = max(slab // 2, 128)
    for at, block_ref in enumerate(blocks):
        for col in range(0, slab, tile):
            here = pl.ds(col, tile)
            part = jnp.dot(
                delta_ref[...], block_ref[:, here], preferred_element_type=jnp.float32
            )
            if at >= count:
                outs[len(cuts) - 1 + at - count][:, here] = part
                continue
            for start, end, out_ref in zip(cuts[:-1], cuts[1:], outs):
                low, high = max(start, at * nodes), min(end, (at + 1) * nodes)
                if low < high:
                    rows = part[low - at * nodes : high - at * nodes]
                    out_ref[low - start : high - start, here] = rows.astype(out_ref.dtype)


def shares(offs, delta, blocks, cuts):
    nodes, rows = delta.shape
    slab = blocks[0].shape[1]
    own = len(blocks) // 2
    heights = [end - start for start, end in zip(cuts[:-1], cuts[1:])]
    outs = call(
        functools.partial(share_kernel, cuts),
        [jax.ShapeDtypeStruct((height, slab), jnp.bfloat16) for height in heights]
        + [jax.ShapeDtypeStruct((nodes, slab), jnp.float32)] * own,
        [VMEM_REF] * (len(heights) + own),
        [],
        cost(len(blocks), nodes, slab, rows),
    )([offs, delta, *blocks], [SMEM_REF] + [VMEM_REF] * (1 + len(blocks)))
    return outs[: len(heights)], outs[len(heights) :]


def grad_w_kernel(base, count, *refs):
    offs_ref, delta_ref, xs = refs[0], refs[1], refs[2 : 2 + count]
    out_ref, mark_ref, held, sems = refs[-4:]
    rows, slab = delta_ref.shape[0], xs[0].shape[1]
    slots, tile = held.shape[:2]
    mark_ref[...] = jnp.zeros_like(mark_ref)
    copies = []
    for at in range(count):
        here = columns_of(offs_ref, base + at, slab)
        for start in range(0, rows, tile):
            band = pl.ds(start, tile)
            slot = len(copies) % slots
            if len(copies) >= slots:
                copies[-slots].wait()
            held[slot] = jnp.dot(
                delta_ref[band, :], xs[at][...], preferred_element_type=jnp.float32
            ).astype(held.dtype)
            copy = pltpu.make_async_copy(held.at[slot], out_ref.at[band, here], sems.at[slot])
            copy.start()
            copies.append(copy)
    for copy in copies[-slots:]:
        copy.wait()


def grad_w_piece(offs, base, delta_t, xs, so_far, mark, shape):
    rows, nodes = delta_t.shape
    slab, count = xs[0].shape[1], len(xs)
    tile = max(rows // 4, 128)
    first = so_far is None
    return call(
        functools.partial(grad_w_kernel, base, count),
        [jax.ShapeDtypeStruct(shape, jnp.bfloat16), jax.ShapeDtypeStruct((8, 128), jnp.float32)],
        [ANY_REF, VMEM_REF],
        [pltpu.VMEM((6, tile, slab), jnp.bfloat16), pltpu.SemaphoreType.DMA((6,))],
        cost(count, nodes, slab, rows),
        {} if first else {2 + count: 0},
    )(
        [offs, delta_t, *xs] + ([] if first else [so_far, mark]),
        [SMEM_REF] + [VMEM_REF] * (1 + count) + ([] if first else [ANY_REF] * 2),
    )


def ring_body(chips, states, weights, pert_table, eps_gain, decay, perts):
    _, nodes, slab = states.shape
    rows = weights.shape[0]
    order = chip_ring(chips)
    place = np.argsort(order)
    half, cut = chips // 2, nodes // 2

    near = [0]
    for step in range(1, half):
        near += [-step, step]
    near.append(half)
    listing = [(0, 0)]
    for step in range(half):
        now = [0] if step == 0 else [-step, step]
        then = [half] if step == half - 1 else [-step - 1, step + 1]
        listing += [(at, 1) for at in now] + [(at, 0) for at in then]
    listing.append((half, 1))
    table = np.array(
        [
            [
                2 * order[(place[device // 2] + step) % chips] + (device % 2 ^ side)
                for step, side in listing
            ]
            for device in range(2 * chips)
        ],
        dtype=np.int32,
    )
    me = lax.axis_index("row")
    offs = lax.dynamic_slice(jnp.asarray(table), (me, 0), (1, 2 * chips)).reshape(-1)

    def ring(array, way):
        pairs = []
        for at, chip in enumerate(order):
            to = order[(at + way) % chips]
            pairs += [(2 * chip, 2 * to), (2 * chip + 1, 2 * to + 1)]
        return lax.ppermute(array, "row", pairs)

    def swap(array):
        return lax.ppermute(array, "row", [(i, i ^ 1) for i in range(2 * chips)])

    weights = pltpu.with_memory_space_constraint(weights, pltpu.HBM)
    cheb = cheb_matrix(nodes)
    flat = states.reshape(nodes, slab)
    xb = flat.astype(jnp.bfloat16)

    x = {(0, 0): xb}
    acc, base, block = None, 0, {}

    def next_products(acc, base, count, loads):
        keys = listing[base : base + loads]
        acc, loaded = add_products(
            offs, base, [x[key] for key in keys[:count]], weights, acc, slab, loads
        )
        block.update(zip(keys, loaded))
        return acc, base + count

    behind, ahead = xb, xb
    for step in range(1, half + 1):
        if step < half:
            behind, ahead = ring(behind, 1), ring(ahead, -1)
        else:
            behind, ahead = ring(behind[:cut], 1), ring(ahead[cut:], -1)
        for now in [0] if step == 1 else [1 - step, step - 1]:
            x[now, 1] = swap(x[now, 0])
        count = {1: 1, 2: 3}.get(step, 4)
        acc, base = next_products(acc, base, count, count)
        behind, ahead, acc = lax.optimization_barrier((behind, ahead, acc))
        if step < half:
            x[-step, 0], x[step, 0] = behind, ahead
        else:
            x[half, 0] = jnp.concatenate([behind, ahead], axis=0)
    x[half, 1] = swap(x[half, 0])
    acc, base = next_products(acc, base, 3, 4)

    onehot = (perts[:, None] == jnp.arange(pert_table.shape[0], dtype=jnp.int32)[None, :]).astype(
        jnp.float32
    )
    drive = jnp.dot(onehot, pert_table, precision=lax.Precision.HIGHEST)
    deriv = SCALE * jnp.dot(cheb, flat, precision=lax.Precision.HIGHEST)

    resid, delta, delta_t, sums = middle(
        x[half, 1], block[half, 1], acc, deriv, flat, drive,
        eps_gain.reshape(1, rows), decay.reshape(1, rows),
    )

    def share(steps):
        count = len(steps)
        parts = 2 if count == 1 else 3
        cuts = [0] + [count * nodes * at // parts // 16 * 16 for at in range(1, parts)]
        cuts.append(count * nodes)
        blocks = [block[step, side] for side in (1, 0) for step in steps]
        others, owns = shares(offs, delta, blocks, cuts)
        swapped = jnp.concatenate([swap(other) for other in others], axis=0)
        return [
            own + swapped[at * nodes : (at + 1) * nodes].astype(jnp.float32)
            for at, own in enumerate(owns)
        ]

    gate = lax.optimization_barrier
    first = len(listing) // 8
    each = (len(listing) - first) // (half - 1)
    cuts = [0] + [first + each * at for at in range(half - 1)] + [len(listing)]
    pieces = [(base, listing[base:end]) for base, end in zip(cuts[:-1], cuts[1:])]
    grad_w, mark = None, None

    def next_piece(grad_w, mark):
        base, keys = pieces.pop(0)
        return grad_w_piece(
            offs, base, delta_t, [x[key] for key in keys], grad_w, mark, weights.shape
        )

    (far,) = share([half])
    far = far.astype(jnp.bfloat16)
    grad_w, mark = next_piece(grad_w, mark)
    far, offs, mark = gate((far, offs, mark))
    ahead, behind = ring(far[:cut], 1), ring(far[cut:], -1)
    for step in range(half - 1, -1, -1):
        if step > 0:
            own_ahead, own_behind = share([step, -step])
        else:
            (near_share,) = share([0])
        if step < half - 1:
            grad_w, mark = next_piece(grad_w, mark)
            ahead, behind, mark = gate((ahead, behind, mark))
        if step == 0:
            break
        ahead, behind = ahead.astype(jnp.float32), behind.astype(jnp.float32)
        if step == half - 1:
            ahead = jnp.concatenate([own_ahead[:cut] + ahead, own_ahead[cut:]], axis=0)
            behind = jnp.concatenate([own_behind[:cut], own_behind[cut:] + behind], axis=0)
        else:
            ahead, behind = own_ahead + ahead, own_behind + behind
        ahead, behind = ahead.astype(jnp.bfloat16), behind.astype(jnp.bfloat16)
        ahead, behind, offs = gate((ahead, behind, offs))
        ahead, behind = ring(ahead, 1), ring(behind, -1)

    local = (
        SCALE
        * lax.dot_general(
            cheb, resid, (((0,), (0,)), ((), ())), precision=lax.Precision.HIGHEST
        )
        + decay * resid
    )
    local = gate(local)
    grad_x = local + near_share + ahead.astype(jnp.float32) + behind.astype(jnp.float32)
    grad_x = grad_x.reshape(states.shape)
    grad_table = onehot.T * sums[0:1]
    return (grad_w, grad_x, grad_table, sums[1], sums[2])


def plain_body(states, weights, pert_table, eps_gain, decay, perts):
    traj, nodes, slab = states.shape
    total = traj * nodes
    cheb = cheb_matrix(nodes)
    xb = states.astype(jnp.bfloat16).reshape(total, slab)
    full = lax.all_gather(xb, "row", axis=1, tiled=True)
    pre = lax.dot_general(
        full, weights, (((1,), (1,)), ((), ())), preferred_element_type=jnp.float32
    )
    onehot = (perts[:, None] == jnp.arange(pert_table.shape[0], dtype=jnp.int32)[None, :]).astype(
        jnp.float32
    )
    drive = jnp.dot(onehot, pert_table, precision=lax.Precision.HIGHEST)
    act = jnp.tanh(pre.reshape(traj, nodes, slab) + drive[:, None, :])
    deriv = SCALE * jnp.einsum("kl,clg->ckg", cheb, states, precision=lax.Precision.HIGHEST)
    resid = deriv - (eps_gain * act - decay * states)
    delta = (-eps_gain * (1.0 - act * act) * resid).astype(jnp.bfloat16)
    dflat = delta.reshape(total, slab)
    grad_w = lax.dot_general(
        dflat, full, (((0,), (0,)), ((), ())), preferred_element_type=jnp.float32
    ).astype(jnp.bfloat16)
    back = jnp.dot(dflat, weights, preferred_element_type=jnp.float32)
    back = lax.psum_scatter(back, "row", scatter_dimension=1, tiled=True)
    grad_x = (
        SCALE * jnp.einsum("lk,clg->ckg", cheb, resid, precision=lax.Precision.HIGHEST)
        + decay * resid
        + back.reshape(traj, nodes, slab)
    )
    node_sums = jnp.sum(delta.astype(jnp.float32), axis=1)
    grad_table = jnp.dot(onehot.T, node_sums, precision=lax.Precision.HIGHEST)
    grad_eps = -jnp.sum(act * resid, axis=(0, 1))
    grad_decay = jnp.sum(states * resid, axis=(0, 1))
    return (grad_w, grad_x, grad_table, grad_eps, grad_decay)


def solution(mesh):
    chips = mesh.shape["row"] // 2
    in_specs = (
        P("rep", None, "row"),
        P(("rep", "row"), None),
        P("rep", "row"),
        P(("rep", "row")),
        P(("rep", "row")),
        P("rep"),
    )
    out_specs = (
        P(("rep", "row"), None),
        P("rep", None, "row"),
        P("rep", "row"),
        P(("rep", "row")),
        P(("rep", "row")),
    )

    def run(states, *others):
        if states.shape[0] == 1 and chips <= LONGEST_RING:
            return ring_body(chips, states, *others)
        return plain_body(states, *others)

    return jax.shard_map(run, mesh=mesh, in_specs=in_specs, out_specs=out_specs, check_vma=False)
```

time: 127 us -> 97.3 us (0.77)
  Pallas kernels: 90.2 us -> 58.4 us
  waiting for transfers between devices: 4.69 us -> 7.49 us
    pallas_call x19 -> x15, Pallas kernels: 90.2 us -> 58.4 us  [run(): pl.pallas_call(kernel, out_shape=out_shape, in_specs=in_specs, out_specs=...]
    ppermute x16, waiting for transfers between devices: 4.64 us -> 7.43 us  [ring(): return lax.ppermute(array, 'row', pairs)]
  transfers between devices with their start and end apart: 37 -> 37, of which waited for: 3 -> 6; matrix products, arithmetic and copies ran while one was open for 3% -> 4% of each run, Pallas kernels for 61% -> 56%
where the time goes in v2:
time: 97.3 us; the launch traced here: 97.1 us
  Pallas kernels  58.4 us (60%)
  starting transfers between devices  23 us (24%)
  waiting for transfers between devices  7.49 us (8%)
  other arithmetic  3.6 us (4%)
  between operations  1.83 us (2%)
  local copies, waits for them, and re-layouts  1.43 us (1%)
  matrix products  1.37 us (1%)
    pallas_call x15, Pallas kernels, run(): pl.pallas_call(kernel, out_shape=out_shape, in_specs=in_specs, out_specs=...  58.4 us
    ppermute x16, starting transfers between devices, ring(): return lax.ppermute(array, 'row', pairs)  17.8 us
    ppermute x16, waiting for transfers between devices, ring(): return lax.ppermute(array, 'row', pairs)  7.43 us
    ppermute x21, starting transfers between devices, swap(): return lax.ppermute(array, 'row', [(i, i ^ 1) for i in range(2 * chips)])  5.18 us
  transfers between devices with their start and end apart: 37, of which 6 were waited for; matrix products, arithmetic and copies ran while one was open for 4% of the time, Pallas kernels for 56%

profile of v2, /device:TPU:0, one launch (start us, length us, event | category | flops | bytes accessed | tf_op | source)
XLA Modules:
  0.0 97.1 jit_solution(3146885172311031521)
XLA Ops:
  0.6 1.1 %bitcast_convert_fusion.refs_2_ = bf16[128,1024]{1,0:T(8,128)(2,1)S(1)} fusion(f32[1,128,1024]{2,1,0:T(8,128)} %param.8), kind=kLoop, calls=%fused_computation.37 | loop fusion | flops 131072 | bytes 786432 | tf_op jit(solution)/shard_map/convert_element_type | solution.py:291
  1.8 3.0 %collective-permute-start = (bf16[128,1024]{1,0:T(8,128)(2,1)S(1)}, bf16[128,1024]{1,0:T(8,128)(2,1)S(1)}, u32[]{:S(2)}, u32[]{:S(2)}) collective-permute-start(bf16[128,1024]{1,0:T(8,128)(2,1)S(1)} %bitcast_convert_fusion.refs_2_), channel_id=1, source_target_pairs={{0,2},{1,3},{2,6},{3,7},{6,10},{7,11},{10,14},{11,15},{14,12},{15,... | collective-permute-start | bytes 786440 | tf_op jit(solution)/shard_map/ppermute | solution.py:283
  4.8 0.2 collective-permute-start.1
  4.9 0.7 dynamic-slice_bitcast_fusion.refs_0_.offs_ref
  5.6 3.2 %shard_map.119 = (f32[1024,128]{1,0:T(8,128)S(1)}, bf16[1024,1024]{1,0:T(8,128)(2,1)S(1)}) custom-call(s32[16]{0:T(128)S(1)} %dynamic-slice_bitcast_fusion.refs_0_.offs_ref, bf16[1024,16384]{1,0:T(8,128)(2,1)} %refs_1_.9, bf16[128,1024]{1,0:T(8,128)(2,1)S(1)} %bitcast_convert_fusion.refs_2_), custom_call_target="tpu_custom_call" | custom-call | flops 16777216 | bytes 131072 | tf_op jit(solution)/shard_map/pallas_call | solution.py:55
  8.8 2.4 %collective-permute-done.refs_3_.refs_2_ = bf16[128,1024]{1,0:T(8,128)(2,1)S(1)} collective-permute-done((bf16[128,1024]{1,0:T(8,128)(2,1)S(1)}, bf16[128,1024]{1,0:T(8,128)(2,1)S(1)}, u32[]{:S(2)}, u32[]{:S(2)}) %collective-permute-start) | collective-permute-done | bytes 262176 | tf_op jit(solution)/shard_map/ppermute | solution.py:283
  11.1 1.4 %collective-permute-done.1.refs_4_.refs_3_ = bf16[128,1024]{1,0:T(8,128)(2,1)S(1)} collective-permute-done((bf16[128,1024]{1,0:T(8,128)(2,1)S(1)}, bf16[128,1024]{1,0:T(8,128)(2,1)S(1)}, u32[]{:S(2)}, u32[]{:S(2)}) %collective-permute-start.1) | collective-permute-done | bytes 262176 | tf_op jit(solution)/shard_map/ppermute | solution.py:283
  12.5 1.6 %collective-permute-start.2 = (bf16[128,1024]{1,0:T(8,128)(2,1)S(1)}, bf16[128,1024]{1,0:T(8,128)(2,1)S(1)}, u32[]{:S(2)}, u32[]{:S(2)}) collective-permute-start(bf16[128,1024]{1,0:T(8,128)(2,1)S(1)} %collective-permute-done.refs_3_.refs_2_), channel_id=1, source_target_pairs={{0,2},{1,3},{2,6},{3,7},{6,10},{7,11},{10,14},{11,15},{14,12},{15,... | collective-permute-start | bytes 786440 | tf_op jit(solution)/shard_map/ppermute | solution.py:283
  14.1 0.4 collective-permute-start.3
  14.5 0.5 collective-permute-start.8
  15.1 5.5 %shard_map.120 = (f32[1024,128]{1,0:T(8,128)S(1)}, bf16[1024,1024]{1,0:T(8,128)(2,1)S(1)}, bf16[1024,1024]{1,0:T(8,128)(2,1)S(1)}, bf16[1024,1024]{1,0:T(8,128)(2,1)S(1)}) custom-call(s32[16]{0:T(128)S(1)} %dynamic-slice_bitcast_fusion.refs_0_.offs_ref, bf16[1024,16384]{1,0:T(8,128)(2,1)} %refs_1_.9, ...), custom_call_target="tpu_custom_call" | custom-call | flops 50331648 | bytes 393216 | tf_op jit(solution)/shard_map/pallas_call | solution.py:55
  20.7 1.6 %collective-permute-start.5 = (bf16[128,1024]{1,0:T(8,128)(2,1)S(1)}, bf16[128,1024]{1,0:T(8,128)(2,1)S(1)}, u32[]{:S(2)}, u32[]{:S(2)}) collective-permute-start(bf16[128,1024]{1,0:T(8,128)(2,1)S(1)} %collective-permute-done.2.refs_4_.refs_2_), channel_id=1, source_target_pairs={{0,2},{1,3},{2,6},{3,7},{6,10},{7,11},{10,14},{11,15},{14,12},{15,... | collective-permute-start | bytes 786440 | tf_op jit(solution)/shard_map/ppermute | solution.py:283
  22.2 0.4 collective-permute-start.6
  22.7 0.5 collective-permute-start.12
  23.2 6.7 %shard_map.121 = (f32[1024,128]{1,0:T(8,128)S(1)}, bf16[1024,1024]{1,0:T(8,128)(2,1)S(1)}, bf16[1024,1024]{1,0:T(8,128)(2,1)S(1)}, bf16[1024,1024]{1,0:T(8,128)(2,1)S(1)}, bf16[1024,1024]{1,0:T(8,128)(2,1)S(1)}) custom-call(s32[16]{0:T(128)S(1)} %dynamic-slice_bitcast_fusion.refs_0_.offs_ref, bf16[1024,16384]{1,0:T(8,128)(2,1)} %refs_1_.9, ...), custom_call_target="tpu_custom_call" | custom-call | flops 67108864 | bytes 524288 | tf_op jit(solution)/shard_map/pallas_call | solution.py:55
  29.9 0.3 collective-permute-done.6.refs_5_.refs_3_
  30.2 0.5 collective-permute-start.10
  30.7 1.8 %collective-permute-start.9 = (bf16[64,1024]{1,0:T(8,128)(2,1)S(1)}, bf16[64,1024]{1,0:T(8,128)(2,1)S(1)}, u32[]{:S(2)}, u32[]{:S(2)}) collective-permute-start(bf16[64,1024]{1,0:T(8,128)(2,1)S(1)} %slice.59), channel_id=1, source_target_pairs={{0,2},{1,3},{2,6},{3,7},{6,10},{7,11},{10,14},{11,15},{14,12},{15,... | collective-permute-start | bytes 393224 | tf_op jit(solution)/shard_map/ppermute | solution.py:283
  33.2 0.1 collective-permute-start.14
  33.3 0.5 collective-permute-start.15
  33.8 6.7 %shard_map.122 = (f32[1024,128]{1,0:T(8,128)S(1)}, bf16[1024,1024]{1,0:T(8,128)(2,1)S(1)}, bf16[1024,1024]{1,0:T(8,128)(2,1)S(1)}, bf16[1024,1024]{1,0:T(8,128)(2,1)S(1)}, bf16[1024,1024]{1,0:T(8,128)(2,1)S(1)}) custom-call(s32[16]{0:T(128)S(1)} %dynamic-slice_bitcast_fusion.refs_0_.offs_ref, bf16[1024,16384]{1,0:T(8,128)(2,1)} %refs_1_.9, ...), custom_call_target="tpu_custom_call" | custom-call | flops 67108864 | bytes 524288 | tf_op jit(solution)/shard_map/pallas_call | solution.py:55
  40.5 0.2 collective-permute-start.13
  40.7 0.1 fusion.4.drive_ref
  40.8 0.6 convolution_multiply_fusion.1.deriv_ref
  41.5 5.5 %shard_map.123 = (f32[1024,128]{1,0:T(8,128)S(1)}, bf16[1024,1024]{1,0:T(8,128)(2,1)S(1)}, bf16[1024,1024]{1,0:T(8,128)(2,1)S(1)}, bf16[1024,1024]{1,0:T(8,128)(2,1)S(1)}, bf16[1024,1024]{1,0:T(8,128)(2,1)S(1)}) custom-call(s32[16]{0:T(128)S(1)} %dynamic-slice_bitcast_fusion.refs_0_.offs_ref, bf16[1024,16384]{1,0:T(8,128)(2,1)} %refs_1_.9, ...), custom_call_target="tpu_custom_call" | custom-call | flops 50331648 | bytes 393216 | tf_op jit(solution)/shard_map/pallas_call | solution.py:55
  47.1 0.9 shard_map.124
  48.0 1.3 %shard_map.125 = (bf16[64,1024]{1,0:T(8,128)(2,1)S(1)}, bf16[64,1024]{1,0:T(8,128)(2,1)S(1)}, f32[128,1024]{1,0:T(8,128)S(1)}) custom-call(s32[16]{0:T(128)S(1)} %dynamic-slice_bitcast_fusion.refs_0_.offs_ref, bf16[128,1024]{1,0:T(8,128)(2,1)S(1)} %get-tuple-element.108.delta_ref, bf16[1024,1024]{1,0:T(8,128)(2,1)S(1)} %get-tuple-element.106.w_ref.refs_0_, ...), custom_call_target="tpu_custom_call" | custom-call | flops 33554432 | bytes 262144 | tf_op jit(solution)/shard_map/pallas_call | solution.py:55
  49.3 0.5 collective-permute-start.16
  49.8 0.1 collective-permute-start.17
  49.9 3.0 %shard_map.126 = (bf16[1024,16384]{1,0:T(8,128)(2,1)}, f32[8,128]{1,0:T(8,128)S(1)}) custom-call(s32[16]{0:T(128)S(1)} %dynamic-slice_bitcast_fusion.refs_0_.offs_ref, bf16[1024,128]{1,0:T(8,128)(2,1)S(1)} %get-tuple-element.113.refs_1_, bf16[128,1024]{1,0:T(8,128)(2,1)S(1)} %bitcast_convert_fusion.refs_2_, ...), custom_call_target="tpu_custom_call" | custom-call | flops 33554432 | bytes 262144 | tf_op jit(solution)/shard_map/pallas_call | solution.py:55
  53.0 1.8 %shard_map.127 = (bf16[80,1024]{1,0:T(8,128)(2,1)S(1)}, bf16[80,1024]{1,0:T(8,128)(2,1)S(1)}, bf16[96,1024]{1,0:T(8,128)(2,1)S(1)}, f32[128,1024]{1,0:T(8,128)S(1)}, f32[128,1024]{1,0:T(8,128)S(1)}) custom-call(s32[16]{0:T(128)S(1)} %dynamic-slice_bitcast_fusion.refs_0_.offs_ref, bf16[128,1024]{1,0:T(8,128)(2,1)S(1)} %get-tuple-element.108.delta_ref, ...), custom_call_target="tpu_custom_call" | custom-call | flops 67108864 | bytes 524288 | tf_op jit(solution)/shard_map/pallas_call | solution.py:55
  54.8 0.5 collective-permute-start.21
  55.3 0.1 collective-permute-start.18
  55.4 0.4 collective-permute-start.19
  55.8 0.5 collective-permute-start.22
  56.3 1.6 %collective-permute-start.20 = (bf16[64,1024]{1,0:T(8,128)(2,1)S(1)}, bf16[64,1024]{1,0:T(8,128)(2,1)S(1)}, u32[]{:S(2)}, u32[]{:S(2)}) collective-permute-start(bf16[64,1024]{1,0:T(8,128)(2,1)S(1)} %get-tuple-element.176), channel_id=1, source_target_pairs={{0,2},{1,3},{2,6},{3,7},{6,10},{7,11},{10,14},{11,15},{14,12},{15,... | collective-permute-start | bytes 393224 | tf_op jit(solution)/shard_map/ppermute | solution.py:283
  57.9 0.2 convert_add_fusion
  58.1 3.3 %collective-permute-done.22 = bf16[64,1024]{1,0:T(8,128)(2,1)S(1)} collective-permute-done((bf16[64,1024]{1,0:T(8,128)(2,1)S(1)}, bf16[64,1024]{1,0:T(8,128)(2,1)S(1)}, u32[]{:S(2)}, u32[]{:S(2)}) %collective-permute-start.22) | collective-permute-done | bytes 131104 | tf_op jit(solution)/shard_map/ppermute | solution.py:283
  61.6 1.6 %collective-permute-start.25 = (bf16[128,1024]{1,0:T(8,128)(2,1)S(1)}, bf16[128,1024]{1,0:T(8,128)(2,1)S(1)}, u32[]{:S(2)}, u32[]{:S(2)}) collective-permute-start(bf16[128,1024]{1,0:T(8,128)(2,1)S(1)} %pad_maximum_fusion.6), channel_id=1, source_target_pairs={{0,2},{1,3},{2,6},{3,7},{6,10},{7,11},{10,14},{11,15},{14,12},{15,... | collective-permute-start | bytes 786440 | tf_op jit(solution)/shard_map/ppermute | solution.py:283
  63.2 0.5 collective-permute-start.26
  63.7 1.8 %shard_map.128 = (bf16[80,1024]{1,0:T(8,128)(2,1)S(1)}, bf16[80,1024]{1,0:T(8,128)(2,1)S(1)}, bf16[96,1024]{1,0:T(8,128)(2,1)S(1)}, f32[128,1024]{1,0:T(8,128)S(1)}, f32[128,1024]{1,0:T(8,128)S(1)}) custom-call(s32[16]{0:T(128)S(1)} %dynamic-slice_bitcast_fusion.refs_0_.offs_ref, bf16[128,1024]{1,0:T(8,128)(2,1)S(1)} %get-tuple-element.108.delta_ref, ...), custom_call_target="tpu_custom_call" | custom-call | flops 67108864 | bytes 524288 | tf_op jit(solution)/shard_map/pallas_call | solution.py:55
  65.5 0.1 collective-permute-start.27
  65.6 0.5 collective-permute-start.23
  66.1 0.1 collective-permute-start.24
  66.1 5.3 %shard_map.129 = (bf16[1024,16384]{1,0:T(8,128)(2,1)}, f32[8,128]{1,0:T(8,128)S(1)}) custom-call(s32[16]{0:T(128)S(1)} %dynamic-slice_bitcast_fusion.refs_0_.offs_ref, bf16[1024,128]{1,0:T(8,128)(2,1)S(1)} %get-tuple-element.113.refs_1_, bf16[128,1024]{1,0:T(8,128)(2,1)S(1)} %collective-permute-done.refs_3_.refs_2_, ...), custom_call_target="tpu_custom_call", output_to_operand_aliasing={{0}: (6, {})} | custom-call | flops 67108864 | bytes 524288 | tf_op jit(solution)/shard_map/pallas_call | solution.py:55
  71.5 0.3 add_convert_fusion.2
  71.8 1.6 %collective-permute-start.30 = (bf16[128,1024]{1,0:T(8,128)(2,1)S(1)}, bf16[128,1024]{1,0:T(8,128)(2,1)S(1)}, u32[]{:S(2)}, u32[]{:S(2)}) collective-permute-start(bf16[128,1024]{1,0:T(8,128)(2,1)S(1)} %get-tuple-element.151), channel_id=1, source_target_pairs={{0,2},{1,3},{2,6},{3,7},{6,10},{7,11},{10,14},{11,15},{14,12},{15,... | collective-permute-start | bytes 786440 | tf_op jit(solution)/shard_map/ppermute | solution.py:283
  73.4 0.5 collective-permute-start.31
  73.9 1.8 %shard_map.130 = (bf16[80,1024]{1,0:T(8,128)(2,1)S(1)}, bf16[80,1024]{1,0:T(8,128)(2,1)S(1)}, bf16[96,1024]{1,0:T(8,128)(2,1)S(1)}, f32[128,1024]{1,0:T(8,128)S(1)}, f32[128,1024]{1,0:T(8,128)S(1)}) custom-call(s32[16]{0:T(128)S(1)} %dynamic-slice_bitcast_fusion.refs_0_.offs_ref, bf16[128,1024]{1,0:T(8,128)(2,1)S(1)} %get-tuple-element.108.delta_ref, ...), custom_call_target="tpu_custom_call" | custom-call | flops 67108864 | bytes 524288 | tf_op jit(solution)/shard_map/pallas_call | solution.py:55
  75.7 0.1 collective-permute-start.32
  75.8 0.5 collective-permute-start.28
  76.3 0.1 collective-permute-start.29
  76.3 0.6 fusion.1
  77.0 5.3 %shard_map.131 = (bf16[1024,16384]{1,0:T(8,128)(2,1)}, f32[8,128]{1,0:T(8,128)S(1)}) custom-call(s32[16]{0:T(128)S(1)} %dynamic-slice_bitcast_fusion.refs_0_.offs_ref, bf16[1024,128]{1,0:T(8,128)(2,1)S(1)} %get-tuple-element.113.refs_1_, bf16[128,1024]{1,0:T(8,128)(2,1)S(1)} %collective-permute-done.2.refs_4_.refs_2_, ...), custom_call_target="tpu_custom_call", output_to_operand_aliasing={{0}: (6, {})} | custom-call | flops 67108864 | bytes 524288 | tf_op jit(solution)/shard_map/pallas_call | solution.py:55
  82.4 0.3 add_convert_fusion
  82.6 1.6 %collective-permute-start.35 = (bf16[128,1024]{1,0:T(8,128)(2,1)S(1)}, bf16[128,1024]{1,0:T(8,128)(2,1)S(1)}, u32[]{:S(2)}, u32[]{:S(2)}) collective-permute-start(bf16[128,1024]{1,0:T(8,128)(2,1)S(1)} %get-tuple-element.170), channel_id=1, source_target_pairs={{0,2},{1,3},{2,6},{3,7},{6,10},{7,11},{10,14},{11,15},{14,12},{15,... | collective-permute-start | bytes 786440 | tf_op jit(solution)/shard_map/ppermute | solution.py:283
  84.3 0.5 collective-permute-start.36
  84.7 0.6 fusion.11
  85.3 1.3 %shard_map.133 = (bf16[64,1024]{1,0:T(8,128)(2,1)S(1)}, bf16[64,1024]{1,0:T(8,128)(2,1)S(1)}, f32[128,1024]{1,0:T(8,128)S(1)}) custom-call(s32[16]{0:T(128)S(1)} %dynamic-slice_bitcast_fusion.refs_0_.offs_ref, bf16[128,1024]{1,0:T(8,128)(2,1)S(1)} %get-tuple-element.108.delta_ref, bf16[1024,1024]{1,0:T(8,128)(2,1)S(1)} %get-tuple-element.165.refs_0_, ...), custom_call_target="tpu_custom_call" | custom-call | flops 33554432 | bytes 262144 | tf_op jit(solution)/shard_map/pallas_call | solution.py:55
  86.6 0.1 collective-permute-start.33
  86.7 0.5 collective-permute-start.34
  87.2 0.7 broadcast_multiply_fusion
  87.9 8.2 %shard_map.132 = (bf16[1024,16384]{1,0:T(8,128)(2,1)}, f32[8,128]{1,0:T(8,128)}) custom-call(s32[16]{0:T(128)S(1)} %dynamic-slice_bitcast_fusion.refs_0_.offs_ref, bf16[1024,128]{1,0:T(8,128)(2,1)S(1)} %get-tuple-element.113.refs_1_, bf16[128,1024]{1,0:T(8,128)(2,1)S(1)} %collective-permute-done.5.refs_4_.refs_2_, ...), custom_call_target="tpu_custom_call", output_to_operand_aliasing={{0}: (8, {})} | custom-call | flops 100663296 | bytes 786432 | tf_op jit(solution)/shard_map/pallas_call | solution.py:55
  96.1 1.0 add_bitcast_fusion
  (61 shorter events, 0.5 us)
Async XLA Ops:
  0.6 40.1 %copy-start = (f32[16,1024]{1,0:T(8,128)S(1)}, f32[16,1024]{1,0:T(8,128)}, u32[]{:S(2)}) copy-start(f32[16,1024]{1,0:T(8,128)} %param.10) | copy-start | bytes 196612
  1.8 9.4 %collective-permute-start = (bf16[128,1024]{1,0:T(8,128)(2,1)S(1)}, bf16[128,1024]{1,0:T(8,128)(2,1)S(1)}, u32[]{:S(2)}, u32[]{:S(2)}) collective-permute-start(bf16[128,1024]{1,0:T(8,128)(2,1)S(1)} %bitcast_convert_fusion.refs_2_), channel_id=1, source_target_pairs={{0,2},{1,3},{2,6},{3,7},{6,10},{7,11},{10,14},{11,15},{14,12},{15,... | collective-permute-start | bytes 786440 | tf_op jit(solution)/shard_map/ppermute | solution.py:283
  4.8 7.8 %collective-permute-start.1 = (bf16[128,1024]{1,0:T(8,128)(2,1)S(1)}, bf16[128,1024]{1,0:T(8,128)(2,1)S(1)}, u32[]{:S(2)}, u32[]{:S(2)}) collective-permute-start(bf16[128,1024]{1,0:T(8,128)(2,1)S(1)} %bitcast_convert_fusion.refs_2_), channel_id=1, source_target_pairs={{0,4},{1,5},{2,0},{3,1},{6,2},{7,3},{10,6},{11,7},{14,10},{15,11},... | collective-permute-start | bytes 786440 | tf_op jit(solution)/shard_map/ppermute | solution.py:283
  4.9 10.2 %collective-permute-start.4 = (bf16[128,1024]{1,0:T(8,128)(2,1)S(1)}, bf16[128,1024]{1,0:T(8,128)(2,1)S(1)}, u32[]{:S(2)}, u32[]{:S(2)}) collective-permute-start(bf16[128,1024]{1,0:T(8,128)(2,1)S(1)} %bitcast_convert_fusion.refs_2_), channel_id=1, source_target_pairs={{0,1},{1,0},{2,3},{3,2},{4,5},{5,4},{6,7},{7,6},{8,9},{9,8},{10,11... | collective-permute-start | bytes 786440 | tf_op jit(solution)/shard_map/ppermute | solution.py:286
  12.5 8.1 %collective-permute-start.2 = (bf16[128,1024]{1,0:T(8,128)(2,1)S(1)}, bf16[128,1024]{1,0:T(8,128)(2,1)S(1)}, u32[]{:S(2)}, u32[]{:S(2)}) collective-permute-start(bf16[128,1024]{1,0:T(8,128)(2,1)S(1)} %collective-permute-done.refs_3_.refs_2_), channel_id=1, source_target_pairs={{0,2},{1,3},{2,6},{3,7},{6,10},{7,11},{10,14},{11,15},{14,12},{15,... | collective-permute-start | bytes 786440 | tf_op jit(solution)/shard_map/ppermute | solution.py:283
  14.1 6.6 %collective-permute-start.3 = (bf16[128,1024]{1,0:T(8,128)(2,1)S(1)}, bf16[128,1024]{1,0:T(8,128)(2,1)S(1)}, u32[]{:S(2)}, u32[]{:S(2)}) collective-permute-start(bf16[128,1024]{1,0:T(8,128)(2,1)S(1)} %collective-permute-done.1.refs_4_.refs_3_), channel_id=1, source_target_pairs={{0,4},{1,5},{2,0},{3,1},{6,2},{7,3},{10,6},{11,7},{14,10},{15,11},... | collective-permute-start | bytes 786440 | tf_op jit(solution)/shard_map/ppermute | solution.py:283
  14.5 8.2 %collective-permute-start.7 = (bf16[128,1024]{1,0:T(8,128)(2,1)S(1)}, bf16[128,1024]{1,0:T(8,128)(2,1)S(1)}, u32[]{:S(2)}, u32[]{:S(2)}) collective-permute-start(bf16[128,1024]{1,0:T(8,128)(2,1)S(1)} %collective-permute-done.refs_3_.refs_2_), channel_id=1, source_target_pairs={{0,1},{1,0},{2,3},{3,2},{4,5},{5,4},{6,7},{7,6},{8,9},{9,8},{10,11... | collective-permute-start | bytes 786440 | tf_op jit(solution)/shard_map/ppermute | solution.py:286
  14.5 8.7 %collective-permute-start.8 = (bf16[128,1024]{1,0:T(8,128)(2,1)S(1)}, bf16[128,1024]{1,0:T(8,128)(2,1)S(1)}, u32[]{:S(2)}, u32[]{:S(2)}) collective-permute-start(bf16[128,1024]{1,0:T(8,128)(2,1)S(1)} %collective-permute-done.1.refs_4_.refs_3_), channel_id=1, source_target_pairs={{0,1},{1,0},{2,3},{3,2},{4,5},{5,4},{6,7},{7,6},{8,9},{9,8},{10,11... | collective-permute-start | bytes 786440 | tf_op jit(solution)/shard_map/ppermute | solution.py:286
  20.7 9.2 %collective-permute-start.5 = (bf16[128,1024]{1,0:T(8,128)(2,1)S(1)}, bf16[128,1024]{1,0:T(8,128)(2,1)S(1)}, u32[]{:S(2)}, u32[]{:S(2)}) collective-permute-start(bf16[128,1024]{1,0:T(8,128)(2,1)S(1)} %collective-permute-done.2.refs_4_.refs_2_), channel_id=1, source_target_pairs={{0,2},{1,3},{2,6},{3,7},{6,10},{7,11},{10,14},{11,15},{14,12},{15,... | collective-permute-start | bytes 786440 | tf_op jit(solution)/shard_map/ppermute | solution.py:283
  22.2 7.9 %collective-permute-start.6 = (bf16[128,1024]{1,0:T(8,128)(2,1)S(1)}, bf16[128,1024]{1,0:T(8,128)(2,1)S(1)}, u32[]{:S(2)}, u32[]{:S(2)}) collective-permute-start(bf16[128,1024]{1,0:T(8,128)(2,1)S(1)} %collective-permute-done.3.refs_5_.refs_3_), channel_id=1, source_target_pairs={{0,4},{1,5},{2,0},{3,1},{6,2},{7,3},{10,6},{11,7},{14,10},{15,11},... | collective-permute-start | bytes 786440 | tf_op jit(solution)/shard_map/ppermute | solution.py:283
  22.7 10.6 %collective-permute-start.11 = (bf16[128,1024]{1,0:T(8,128)(2,1)S(1)}, bf16[128,1024]{1,0:T(8,128)(2,1)S(1)}, u32[]{:S(2)}, u32[]{:S(2)}) collective-permute-start(bf16[128,1024]{1,0:T(8,128)(2,1)S(1)} %collective-permute-done.2.refs_4_.refs_2_), channel_id=1, source_target_pairs={{0,1},{1,0},{2,3},{3,2},{4,5},{5,4},{6,7},{7,6},{8,9},{9,8},{10,11... | collective-permute-start | bytes 786440 | tf_op jit(solution)/shard_map/ppermute | solution.py:286
  22.7 11.1 %collective-permute-start.12 = (bf16[128,1024]{1,0:T(8,128)(2,1)S(1)}, bf16[128,1024]{1,0:T(8,128)(2,1)S(1)}, u32[]{:S(2)}, u32[]{:S(2)}) collective-permute-start(bf16[128,1024]{1,0:T(8,128)(2,1)S(1)} %collective-permute-done.3.refs_5_.refs_3_), channel_id=1, source_target_pairs={{0,1},{1,0},{2,3},{3,2},{4,5},{5,4},{6,7},{7,6},{8,9},{9,8},{10,11... | collective-permute-start | bytes 786440 | tf_op jit(solution)/shard_map/ppermute | solution.py:286
  30.2 10.3 %collective-permute-start.10 = (bf16[64,1024]{1,0:T(8,128)(2,1)S(1)}, bf16[64,1024]{1,0:T(8,128)(2,1)S(1)}, u32[]{:S(2)}, u32[]{:S(2)}) collective-permute-start(bf16[64,1024]{1,0:T(8,128)(2,1)S(1)} %slice.60), channel_id=1, source_target_pairs={{0,4},{1,5},{2,0},{3,1},{6,2},{7,3},{10,6},{11,7},{14,10},{15,11},... | collective-permute-start | bytes 393224 | tf_op jit(solution)/shard_map/ppermute | solution.py:283
  30.7 9.8 %collective-permute-start.9 = (bf16[64,1024]{1,0:T(8,128)(2,1)S(1)}, bf16[64,1024]{1,0:T(8,128)(2,1)S(1)}, u32[]{:S(2)}, u32[]{:S(2)}) collective-permute-start(bf16[64,1024]{1,0:T(8,128)(2,1)S(1)} %slice.59), channel_id=1, source_target_pairs={{0,2},{1,3},{2,6},{3,7},{6,10},{7,11},{10,14},{11,15},{14,12},{15,... | collective-permute-start | bytes 393224 | tf_op jit(solution)/shard_map/ppermute | solution.py:283
  33.2 7.7 %copy-start.2 = (f32[1,128,1024]{2,1,0:T(8,128)S(1)}, f32[1,128,1024]{2,1,0:T(8,128)}, u32[]{:S(2)}) copy-start(f32[1,128,1024]{2,1,0:T(8,128)} %param.8) | copy-start | bytes 1572868
  33.2 7.7 %copy-start.5 = (f32[128,128]{1,0:T(8,128)S(1)}, f32[128,128]{1,0:T(8,128)}, u32[]{:S(2)}) copy-start(f32[128,128]{1,0:T(8,128)} %constant.15.clone) | copy-start | bytes 196612
  33.2 8.3 %collective-permute-start.14 = (bf16[128,1024]{1,0:T(8,128)(2,1)S(1)}, bf16[128,1024]{1,0:T(8,128)(2,1)S(1)}, u32[]{:S(2)}, u32[]{:S(2)}) collective-permute-start(bf16[128,1024]{1,0:T(8,128)(2,1)S(1)} %collective-permute-done.5.refs_4_.refs_2_), channel_id=1, source_target_pairs={{0,1},{1,0},{2,3},{3,2},{4,5},{5,4},{6,7},{7,6},{8,9},{9,8},{10,11... | collective-permute-start | bytes 786440 | tf_op jit(solution)/shard_map/ppermute | solution.py:286
  33.3 8.2 %collective-permute-start.15 = (bf16[128,1024]{1,0:T(8,128)(2,1)S(1)}, bf16[128,1024]{1,0:T(8,128)(2,1)S(1)}, u32[]{:S(2)}, u32[]{:S(2)}) collective-permute-start(bf16[128,1024]{1,0:T(8,128)(2,1)S(1)} %collective-permute-done.6.refs_5_.refs_3_), channel_id=1, source_target_pairs={{0,1},{1,0},{2,3},{3,2},{4,5},{5,4},{6,7},{7,6},{8,9},{9,8},{10,11... | collective-permute-start | bytes 786440 | tf_op jit(solution)/shard_map/ppermute | solution.py:286
  40.5 6.5 %collective-permute-start.13 = (bf16[128,1024]{1,0:T(8,128)(2,1)S(1)}, bf16[128,1024]{1,0:T(8,128)(2,1)S(1)}, u32[]{:S(2)}, u32[]{:S(2)}) collective-permute-start(bf16[128,1024]{1,0:T(8,128)(2,1)S(1)} %constant_dynamic-update-slice_fusion.refs_4_.refs_6_), channel_id=1, source_target_pairs={{0,1},{1,0},{2,3},{3,2},{4,5},{5,4},{6,7},{7,6},{8,9},{9,8},{10,11... | collective-permute-start | bytes 786440 | tf_op jit(solution)/shard_map/ppermute | solution.py:286
  41.4 5.6 %copy-start.3 = (f32[1024]{0:T(1024)S(1)}, f32[1024]{0:T(1024)}, u32[]{:S(2)}) copy-start(f32[1024]{0:T(1024)} %param.12) | copy-start | bytes 12292
  41.5 5.6 %copy-start.4 = (f32[1024]{0:T(1024)S(1)}, f32[1024]{0:T(1024)}, u32[]{:S(2)}) copy-start(f32[1024]{0:T(1024)} %param.11) | copy-start | bytes 12292
  49.3 3.6 %collective-permute-start.16 = (bf16[64,1024]{1,0:T(8,128)(2,1)S(1)}, bf16[64,1024]{1,0:T(8,128)(2,1)S(1)}, u32[]{:S(2)}, u32[]{:S(2)}) collective-permute-start(bf16[64,1024]{1,0:T(8,128)(2,1)S(1)} %get-tuple-element.111), channel_id=1, source_target_pairs={{0,1},{1,0},{2,3},{3,2},{4,5},{5,4},{6,7},{7,6},{8,9},{9,8},{10,11... | collective-permute-start | bytes 393224 | tf_op jit(solution)/shard_map/ppermute | solution.py:286
  49.8 3.1 %collective-permute-start.17 = (bf16[64,1024]{1,0:T(8,128)(2,1)S(1)}, bf16[64,1024]{1,0:T(8,128)(2,1)S(1)}, u32[]{:S(2)}, u32[]{:S(2)}) collective-permute-start(bf16[64,1024]{1,0:T(8,128)(2,1)S(1)} %get-tuple-element.112), channel_id=1, source_target_pairs={{0,1},{1,0},{2,3},{3,2},{4,5},{5,4},{6,7},{7,6},{8,9},{9,8},{10,11... | collective-permute-start | bytes 393224 | tf_op jit(solution)/shard_map/ppermute | solution.py:286
  54.8 3.1 %collective-permute-start.21 = (bf16[96,1024]{1,0:T(8,128)(2,1)S(1)}, bf16[96,1024]{1,0:T(8,128)(2,1)S(1)}, u32[]{:S(2)}, u32[]{:S(2)}) collective-permute-start(bf16[96,1024]{1,0:T(8,128)(2,1)S(1)} %get-tuple-element.125), channel_id=1, source_target_pairs={{0,1},{1,0},{2,3},{3,2},{4,5},{5,4},{6,7},{7,6},{8,9},{9,8},{10,11... | collective-permute-start | bytes 589832 | tf_op jit(solution)/shard_map/ppermute | solution.py:286
  55.3 2.6 %collective-permute-start.18 = (bf16[80,1024]{1,0:T(8,128)(2,1)S(1)}, bf16[80,1024]{1,0:T(8,128)(2,1)S(1)}, u32[]{:S(2)}, u32[]{:S(2)}) collective-permute-start(bf16[80,1024]{1,0:T(8,128)(2,1)S(1)} %get-tuple-element.121), channel_id=1, source_target_pairs={{0,1},{1,0},{2,3},{3,2},{4,5},{5,4},{6,7},{7,6},{8,9},{9,8},{10,11... | collective-permute-start | bytes 491528 | tf_op jit(solution)/shard_map/ppermute | solution.py:286
  55.4 2.5 %collective-permute-start.19 = (bf16[80,1024]{1,0:T(8,128)(2,1)S(1)}, bf16[80,1024]{1,0:T(8,128)(2,1)S(1)}, u32[]{:S(2)}, u32[]{:S(2)}) collective-permute-start(bf16[80,1024]{1,0:T(8,128)(2,1)S(1)} %get-tuple-element.122), channel_id=1, source_target_pairs={{0,1},{1,0},{2,3},{3,2},{4,5},{5,4},{6,7},{7,6},{8,9},{9,8},{10,11... | collective-permute-start | bytes 491528 | tf_op jit(solution)/shard_map/ppermute | solution.py:286
  55.8 5.5 %collective-permute-start.22 = (bf16[64,1024]{1,0:T(8,128)(2,1)S(1)}, bf16[64,1024]{1,0:T(8,128)(2,1)S(1)}, u32[]{:S(2)}, u32[]{:S(2)}) collective-permute-start(bf16[64,1024]{1,0:T(8,128)(2,1)S(1)} %get-tuple-element.175), channel_id=1, source_target_pairs={{0,4},{1,5},{2,0},{3,1},{6,2},{7,3},{10,6},{11,7},{14,10},{15,11},... | collective-permute-start | bytes 393224 | tf_op jit(solution)/shard_map/ppermute | solution.py:283
  56.3 5.2 %collective-permute-start.20 = (bf16[64,1024]{1,0:T(8,128)(2,1)S(1)}, bf16[64,1024]{1,0:T(8,128)(2,1)S(1)}, u32[]{:S(2)}, u32[]{:S(2)}) collective-permute-start(bf16[64,1024]{1,0:T(8,128)(2,1)S(1)} %get-tuple-element.176), channel_id=1, source_target_pairs={{0,2},{1,3},{2,6},{3,7},{6,10},{7,11},{10,14},{11,15},{14,12},{15,... | collective-permute-start | bytes 393224 | tf_op jit(solution)/shard_map/ppermute | solution.py:283
  61.6 9.9 %collective-permute-start.25 = (bf16[128,1024]{1,0:T(8,128)(2,1)S(1)}, bf16[128,1024]{1,0:T(8,128)(2,1)S(1)}, u32[]{:S(2)}, u32[]{:S(2)}) collective-permute-start(bf16[128,1024]{1,0:T(8,128)(2,1)S(1)} %pad_maximum_fusion.6), channel_id=1, source_target_pairs={{0,2},{1,3},{2,6},{3,7},{6,10},{7,11},{10,14},{11,15},{14,12},{15,... | collective-permute-start | bytes 786440 | tf_op jit(solution)/shard_map/ppermute | solution.py:283
  63.2 8.3 %collective-permute-start.26 = (bf16[128,1024]{1,0:T(8,128)(2,1)S(1)}, bf16[128,1024]{1,0:T(8,128)(2,1)S(1)}, u32[]{:S(2)}, u32[]{:S(2)}) collective-permute-start(bf16[128,1024]{1,0:T(8,128)(2,1)S(1)} %pad_maximum_fusion.7), channel_id=1, source_target_pairs={{0,4},{1,5},{2,0},{3,1},{6,2},{7,3},{10,6},{11,7},{14,10},{15,11},... | collective-permute-start | bytes 786440 | tf_op jit(solution)/shard_map/ppermute | solution.py:283
  65.5 6.0 %collective-permute-start.27 = (bf16[96,1024]{1,0:T(8,128)(2,1)S(1)}, bf16[96,1024]{1,0:T(8,128)(2,1)S(1)}, u32[]{:S(2)}, u32[]{:S(2)}) collective-permute-start(bf16[96,1024]{1,0:T(8,128)(2,1)S(1)} %get-tuple-element.141), channel_id=1, source_target_pairs={{0,1},{1,0},{2,3},{3,2},{4,5},{5,4},{6,7},{7,6},{8,9},{9,8},{10,11... | collective-permute-start | bytes 589832 | tf_op jit(solution)/shard_map/ppermute | solution.py:286
  65.6 5.9 %collective-permute-start.23 = (bf16[80,1024]{1,0:T(8,128)(2,1)S(1)}, bf16[80,1024]{1,0:T(8,128)(2,1)S(1)}, u32[]{:S(2)}, u32[]{:S(2)}) collective-permute-start(bf16[80,1024]{1,0:T(8,128)(2,1)S(1)} %get-tuple-element.132), channel_id=1, source_target_pairs={{0,1},{1,0},{2,3},{3,2},{4,5},{5,4},{6,7},{7,6},{8,9},{9,8},{10,11... | collective-permute-start | bytes 491528 | tf_op jit(solution)/shard_map/ppermute | solution.py:286
  66.1 5.4 %collective-permute-start.24 = (bf16[80,1024]{1,0:T(8,128)(2,1)S(1)}, bf16[80,1024]{1,0:T(8,128)(2,1)S(1)}, u32[]{:S(2)}, u32[]{:S(2)}) collective-permute-start(bf16[80,1024]{1,0:T(8,128)(2,1)S(1)} %get-tuple-element.133), channel_id=1, source_target_pairs={{0,1},{1,0},{2,3},{3,2},{4,5},{5,4},{6,7},{7,6},{8,9},{9,8},{10,11... | collective-permute-start | bytes 491528 | tf_op jit(solution)/shard_map/ppermute | solution.py:286
  71.8 10.5 %collective-permute-start.30 = (bf16[128,1024]{1,0:T(8,128)(2,1)S(1)}, bf16[128,1024]{1,0:T(8,128)(2,1)S(1)}, u32[]{:S(2)}, u32[]{:S(2)}) collective-permute-start(bf16[128,1024]{1,0:T(8,128)(2,1)S(1)} %get-tuple-element.151), channel_id=1, source_target_pairs={{0,2},{1,3},{2,6},{3,7},{6,10},{7,11},{10,14},{11,15},{14,12},{15,... | collective-permute-start | bytes 786440 | tf_op jit(solution)/shard_map/ppermute | solution.py:283
  73.4 8.9 %collective-permute-start.31 = (bf16[128,1024]{1,0:T(8,128)(2,1)S(1)}, bf16[128,1024]{1,0:T(8,128)(2,1)S(1)}, u32[]{:S(2)}, u32[]{:S(2)}) collective-permute-start(bf16[128,1024]{1,0:T(8,128)(2,1)S(1)} %get-tuple-element.152), channel_id=1, source_target_pairs={{0,4},{1,5},{2,0},{3,1},{6,2},{7,3},{10,6},{11,7},{14,10},{15,11},... | collective-permute-start | bytes 786440 | tf_op jit(solution)/shard_map/ppermute | solution.py:283
  75.7 6.7 %collective-permute-start.32 = (bf16[96,1024]{1,0:T(8,128)(2,1)S(1)}, bf16[96,1024]{1,0:T(8,128)(2,1)S(1)}, u32[]{:S(2)}, u32[]{:S(2)}) collective-permute-start(bf16[96,1024]{1,0:T(8,128)(2,1)S(1)} %get-tuple-element.158), channel_id=1, source_target_pairs={{0,1},{1,0},{2,3},{3,2},{4,5},{5,4},{6,7},{7,6},{8,9},{9,8},{10,11... | collective-permute-start | bytes 589832 | tf_op jit(solution)/shard_map/ppermute | solution.py:286
  75.8 6.6 %collective-permute-start.28 = (bf16[80,1024]{1,0:T(8,128)(2,1)S(1)}, bf16[80,1024]{1,0:T(8,128)(2,1)S(1)}, u32[]{:S(2)}, u32[]{:S(2)}) collective-permute-start(bf16[80,1024]{1,0:T(8,128)(2,1)S(1)} %get-tuple-element.149), channel_id=1, source_target_pairs={{0,1},{1,0},{2,3},{3,2},{4,5},{5,4},{6,7},{7,6},{8,9},{9,8},{10,11... | collective-permute-start | bytes 491528 | tf_op jit(solution)/shard_map/ppermute | solution.py:286
  76.3 6.1 %collective-permute-start.29 = (bf16[80,1024]{1,0:T(8,128)(2,1)S(1)}, bf16[80,1024]{1,0:T(8,128)(2,1)S(1)}, u32[]{:S(2)}, u32[]{:S(2)}) collective-permute-start(bf16[80,1024]{1,0:T(8,128)(2,1)S(1)} %get-tuple-element.150), channel_id=1, source_target_pairs={{0,1},{1,0},{2,3},{3,2},{4,5},{5,4},{6,7},{7,6},{8,9},{9,8},{10,11... | collective-permute-start | bytes 491528 | tf_op jit(solution)/shard_map/ppermute | solution.py:286
  82.6 13.4 %collective-permute-start.35 = (bf16[128,1024]{1,0:T(8,128)(2,1)S(1)}, bf16[128,1024]{1,0:T(8,128)(2,1)S(1)}, u32[]{:S(2)}, u32[]{:S(2)}) collective-permute-start(bf16[128,1024]{1,0:T(8,128)(2,1)S(1)} %get-tuple-element.170), channel_id=1, source_target_pairs={{0,2},{1,3},{2,6},{3,7},{6,10},{7,11},{10,14},{11,15},{14,12},{15,... | collective-permute-start | bytes 786440 | tf_op jit(solution)/shard_map/ppermute | solution.py:283
  84.3 11.8 %collective-permute-start.36 = (bf16[128,1024]{1,0:T(8,128)(2,1)S(1)}, bf16[128,1024]{1,0:T(8,128)(2,1)S(1)}, u32[]{:S(2)}, u32[]{:S(2)}) collective-permute-start(bf16[128,1024]{1,0:T(8,128)(2,1)S(1)} %get-tuple-element.171), channel_id=1, source_target_pairs={{0,4},{1,5},{2,0},{3,1},{6,2},{7,3},{10,6},{11,7},{14,10},{15,11},... | collective-permute-start | bytes 786440 | tf_op jit(solution)/shard_map/ppermute | solution.py:283
  86.6 9.5 %collective-permute-start.33 = (bf16[64,1024]{1,0:T(8,128)(2,1)S(1)}, bf16[64,1024]{1,0:T(8,128)(2,1)S(1)}, u32[]{:S(2)}, u32[]{:S(2)}) collective-permute-start(bf16[64,1024]{1,0:T(8,128)(2,1)S(1)} %get-tuple-element.168), channel_id=1, source_target_pairs={{0,1},{1,0},{2,3},{3,2},{4,5},{5,4},{6,7},{7,6},{8,9},{9,8},{10,11... | collective-permute-start | bytes 393224 | tf_op jit(solution)/shard_map/ppermute | solution.py:286
  86.7 9.4 %collective-permute-start.34 = (bf16[64,1024]{1,0:T(8,128)(2,1)S(1)}, bf16[64,1024]{1,0:T(8,128)(2,1)S(1)}, u32[]{:S(2)}, u32[]{:S(2)}) collective-permute-start(bf16[64,1024]{1,0:T(8,128)(2,1)S(1)} %get-tuple-element.169), channel_id=1, source_target_pairs={{0,1},{1,0},{2,3},{3,2},{4,5},{5,4},{6,7},{7,6},{8,9},{9,8},{10,11... | collective-permute-start | bytes 393224 | tf_op jit(solution)/shard_map/ppermute | solution.py:286
  87.9 9.2 %copy-start.1 = (f32[16,1024]{1,0:T(8,128)S(1)}, f32[16,1024]{1,0:T(8,128)}, u32[]{:S(2)}) copy-start(f32[16,1024]{1,0:T(8,128)} %param.10) | copy-start | bytes 196612

commit v3 on v2

--- a/solution.py
+++ b/solution.py
@@ -9,8 +9,8 @@
 from jax.sharding import PartitionSpec as P
 
 SCALE = 2.0 / 1024.0
-VMEM_LIMIT = 16 * 2**20
-PARTS = 2
+VMEM_LIMIT = 4 * 2**20
+BANDS = 8
 LONGEST_RING = 16
 
 
@@ -50,7 +50,7 @@
     )
 
 
-def call(kernel, out_shape, out_specs, scratch, costs, aliases=None):
+def call(kernel, out_shape, out_specs, scratch, costs, aliases=None, more=0):
     def run(operands, in_specs):
         return pl.pallas_call(
             kernel,
@@ -59,7 +59,7 @@
             out_specs=out_specs,
             scratch_shapes=scratch,
             input_output_aliases=aliases or {},
-            compiler_params=pltpu.CompilerParams(vmem_limit_bytes=VMEM_LIMIT),
+            compiler_params=pltpu.CompilerParams(vmem_limit_bytes=VMEM_LIMIT + more),
             cost_estimate=costs,
         )(*operands)
 
@@ -70,70 +70,124 @@
     return pl.ds(pl.multiple_of(offs_ref[at] * slab, slab), slab)
 
 
-def pre_kernel(base, count, loads, first, *refs):
-    offs_ref, w_ref = refs[:2]
-    xs = refs[2 : 2 + count]
-    rest = refs[2 + count :]
-    acc_ref, rest = (None, rest) if first else (rest[0], rest[1:])
-    out_ref, blocks, sems = rest[0], rest[1 : 1 + loads], rest[-1]
-    rows, slab = blocks[0].shape
-    tile = rows // PARTS
+def load_rows(w_ref, held_ref, sems, start):
+    tile = held_ref.shape[0] // sems.shape[0]
     copies = []
-    for at in range(loads):
-        here = columns_of(offs_ref, base + at, slab)
-        for part in range(PARTS):
-            band = pl.ds(part * tile, tile)
-            copy = pltpu.make_async_copy(
-                w_ref.at[band, here], blocks[at].at[band, :], sems.at[at, part]
-            )
-            copy.start()
-            copies.append(copy)
+    for at in range(sems.shape[0]):
+        band = pl.ds(at * tile, tile)
+        copy = pltpu.make_async_copy(
+            w_ref.at[pl.ds(start + at * tile, tile), :], held_ref.at[band, :], sems.at[at]
+        )
+        copy.start()
+        copies.append(copy)
+    return copies
+
+
+def product(held_ref, band, here, x_ref):
+    return lax.dot_general(
+        held_ref[band, here], x_ref[...], (((1,), (1,)), ((), ())),
+        preferred_element_type=jnp.float32,
+    )
+
+
+def first_kernel(base, offs_ref, w_ref, x_ref, out_ref, head_ref, sems):
+    slab = x_ref.shape[1]
+    tile = head_ref.shape[0] // sems.shape[0]
+    here = columns_of(offs_ref, base, slab)
+    for at, copy in enumerate(load_rows(w_ref, head_ref, sems, 0)):
+        copy.wait()
+        band = pl.ds(at * tile, tile)
+        out_ref[band, :] = product(head_ref, band, here, x_ref)
+
+
+def second_kernel(base, count, *refs):
+    offs_ref, w_ref, acc_ref, head_ref = refs[:4]
+    xs, (out_ref, rest_ref, sems) = refs[4 : 4 + count], refs[4 + count :]
+    slab = xs[0].shape[1]
+    start = head_ref.shape[0]
+    copies = load_rows(w_ref, rest_ref, sems, start)
+    tile = rest_ref.shape[0]
+    for low in range(0, start, tile):
+        band = pl.ds(low, tile)
+        total = acc_ref[band, :]
+        for at in range(1, count):
+            total += product(head_ref, band, columns_of(offs_ref, base + at, slab), xs[at])
+        out_ref[band, :] = total
+    for copy in copies:
+        copy.wait()
+    total = None
     for at in range(count):
-        for part in range(PARTS):
-            copies[at * PARTS + part].wait()
-            band = pl.ds(part * tile, tile)
-            total = lax.dot_general(
-                blocks[at][band, :], xs[at][...], (((1,), (1,)), ((), ())),
-                preferred_element_type=jnp.float32,
-            )
-            if at > 0:
-                total += out_ref[band, :]
-            elif not first:
-                total += acc_ref[band, :]
-            out_ref[band, :] = total
-    for copy in copies[count * PARTS :]:
-        copy.wait()
-
-
-def add_products(offs, base, xs, weights, acc, slab, loads):
-    nodes, rows, count = xs[0].shape[0], weights.shape[0], len(xs)
-    first = acc is None
-    out = call(
-        functools.partial(pre_kernel, base, count, loads, first),
-        [jax.ShapeDtypeStruct((rows, nodes), jnp.float32)]
-        + [pltpu.VMEM((rows, slab), jnp.bfloat16)] * loads,
-        [VMEM_REF] * (1 + loads),
-        [pltpu.SemaphoreType.DMA((loads, PARTS))],
+        part = product(rest_ref, slice(None), columns_of(offs_ref, base + at, slab), xs[at])
+        total = part if total is None else total + part
+    out_ref[pl.ds(start, tile), :] = total
+
+
+def pre_kernel(base, count, offs_ref, acc_ref, head_ref, rest_ref, *refs):
+    xs, out_ref = refs[:count], refs[count]
+    slab = xs[0].shape[1]
+    tile = rest_ref.shape[0]
+    rows = out_ref.shape[0]
+    for low in range(0, rows, tile):
+        held_ref, start = (head_ref, low) if low < rows - tile else (rest_ref, 0)
+        total = acc_ref[pl.ds(low, tile), :]
+        for at in range(count):
+            here = columns_of(offs_ref, base + at, slab)
+            total += product(held_ref, pl.ds(start, tile), here, xs[at])
+        out_ref[pl.ds(low, tile), :] = total
+
+
+def first_products(offs, base, x, weights):
+    (nodes, slab), (rows, genes) = x.shape, weights.shape
+    head = rows * 3 // 4
+    return call(
+        functools.partial(first_kernel, base),
+        [
+            jax.ShapeDtypeStruct((rows, nodes), jnp.float32),
+            pltpu.VMEM((head, genes), jnp.bfloat16),
+        ],
+        [VMEM_REF] * 2,
+        [pltpu.SemaphoreType.DMA((6,))],
+        cost(1, nodes, slab, rows),
+    )([offs, weights, x], [SMEM_REF, HBM_REF, VMEM_REF])
+
+
+def second_products(offs, base, xs, weights, acc, head):
+    (nodes, slab), (rows, genes) = xs[0].shape, weights.shape
+    count = len(xs)
+    return call(
+        functools.partial(second_kernel, base, count),
+        [
+            jax.ShapeDtypeStruct((rows, nodes), jnp.float32),
+            pltpu.VMEM((rows - head.shape[0], genes), jnp.bfloat16),
+        ],
+        [VMEM_REF] * 2,
+        [pltpu.SemaphoreType.DMA((2,))],
         cost(count, nodes, slab, rows),
-    )(
-        [offs, weights, *xs] + ([] if first else [acc]),
-        [SMEM_REF, HBM_REF] + [VMEM_REF] * (count + (0 if first else 1)),
-    )
-    return out[0], out[1:]
+    )([offs, weights, acc, head, *xs], [SMEM_REF, HBM_REF] + [VMEM_REF] * (2 + count))
+
+
+def add_products(offs, base, xs, acc, head, rest):
+    nodes, slab = xs[0].shape
+    rows, count = acc.shape[0], len(xs)
+    return call(
+        functools.partial(pre_kernel, base, count),
+        jax.ShapeDtypeStruct((rows, nodes), jnp.float32),
+        VMEM_REF,
+        [],
+        cost(count, nodes, slab, rows),
+    )([offs, acc, head, rest, *xs], [SMEM_REF] + [VMEM_REF] * (3 + count))
 
 
 def middle_kernel(
-    x_ref, w_ref, acc_ref, deriv_ref, states_ref, drive_ref, eps_ref, decay_ref,
-    resid_ref, delta_ref, delta_t_ref, sums_ref,
+    base, offs_ref, x_ref, head_ref, rest_ref, acc_ref, deriv_ref, states_ref, drive_ref,
+    eps_ref, decay_ref, resid_ref, delta_ref, delta_t_ref, sums_ref,
 ):
-    rows = w_ref.shape[0]
-    tile = max(rows // 4, 128)
+    rows, tile = acc_ref.shape[0], rest_ref.shape[0]
+    here = columns_of(offs_ref, base, x_ref.shape[1])
     for start in range(0, rows, tile):
+        held_ref, low = (head_ref, start) if start < rows - tile else (rest_ref, 0)
         band = pl.ds(start, tile)
-        part = acc_ref[band, :] + lax.dot_general(
-            w_ref[band, :], x_ref[...], (((1,), (1,)), ((), ())),
-            preferred_element_type=jnp.float32,
-        )
+        part = acc_ref[band, :] + product(held_ref, pl.ds(low, tile), here, x_ref)
         states = states_ref[:, band]
         act = jnp.tanh(part.T + drive_ref[:, band])
         eps = eps_ref[:, band]
@@ -148,11 +202,11 @@
         sums_ref[2:3, band] = jnp.sum(states * resid, axis=0, keepdims=True)
 
 
-def middle(x, block, acc, deriv, states, drive, eps, decay):
+def middle(offs, base, x, head, rest, acc, deriv, states, drive, eps, decay):
     nodes, slab = x.shape
-    rows = block.shape[0]
+    rows = acc.shape[0]
     return call(
-        middle_kernel,
+        functools.partial(middle_kernel, base),
         [
             jax.ShapeDtypeStruct((nodes, rows), jnp.float32),
             jax.ShapeDtypeStruct((nodes, rows), jnp.bfloat16),
@@ -162,20 +216,26 @@
         [VMEM_REF] * 4,
         [],
         cost(2, nodes, slab, rows),
-    )([x, block, acc, deriv, states, drive, eps, decay], [VMEM_REF] * 8)
-
-
-def share_kernel(cuts, offs_ref, delta_ref, *refs):
+    )(
+        [offs, x, head, rest, acc, deriv, states, drive, eps, decay],
+        [SMEM_REF] + [VMEM_REF] * 9,
+    )
+
+
+def share_kernel(at_places, cuts, offs_ref, delta_ref, head_ref, rest_ref, *outs):
     nodes = delta_ref.shape[0]
     count = cuts[-1] // nodes
-    blocks, outs = refs[: 2 * count], refs[2 * count :]
-    slab = blocks[0].shape[1]
+    slab = outs[0].shape[1]
+    split = head_ref.shape[0]
     tile = max(slab // 2, 128)
-    for at, block_ref in enumerate(blocks):
+    for at, place in enumerate(at_places):
         for col in range(0, slab, tile):
             here = pl.ds(col, tile)
+            there = pl.ds(pl.multiple_of(offs_ref[place] * slab + col, tile), tile)
             part = jnp.dot(
-                delta_ref[...], block_ref[:, here], preferred_element_type=jnp.float32
+                delta_ref[:, :split], head_ref[:, there], preferred_element_type=jnp.float32
+            ) + jnp.dot(
+                delta_ref[:, split:], rest_ref[:, there], preferred_element_type=jnp.float32
             )
             if at >= count:
                 outs[len(cuts) - 1 + at - count][:, here] = part
@@ -187,61 +247,59 @@
                     out_ref[low - start : high - start, here] = rows.astype(out_ref.dtype)
 
 
-def shares(offs, delta, blocks, cuts):
+def shares(offs, at_places, delta, head, rest, slab, cuts):
     nodes, rows = delta.shape
-    slab = blocks[0].shape[1]
-    own = len(blocks) // 2
+    own = len(at_places) // 2
     heights = [end - start for start, end in zip(cuts[:-1], cuts[1:])]
     outs = call(
-        functools.partial(share_kernel, cuts),
+        functools.partial(share_kernel, at_places, cuts),
         [jax.ShapeDtypeStruct((height, slab), jnp.bfloat16) for height in heights]
         + [jax.ShapeDtypeStruct((nodes, slab), jnp.float32)] * own,
         [VMEM_REF] * (len(heights) + own),
         [],
-        cost(len(blocks), nodes, slab, rows),
-    )([offs, delta, *blocks], [SMEM_REF] + [VMEM_REF] * (1 + len(blocks)))
+        cost(len(at_places), nodes, slab, rows),
+    )([offs, delta, head, rest], [SMEM_REF] + [VMEM_REF] * 3)
     return outs[: len(heights)], outs[len(heights) :]
 
 
-def grad_w_kernel(base, count, *refs):
+def grad_w_kernel(first, last, count, *refs):
     offs_ref, delta_ref, xs = refs[0], refs[1], refs[2 : 2 + count]
     out_ref, mark_ref, held, sems = refs[-4:]
-    rows, slab = delta_ref.shape[0], xs[0].shape[1]
+    slab = xs[0].shape[1]
     slots, tile = held.shape[:2]
     mark_ref[...] = jnp.zeros_like(mark_ref)
     copies = []
-    for at in range(count):
-        here = columns_of(offs_ref, base + at, slab)
-        for start in range(0, rows, tile):
-            band = pl.ds(start, tile)
-            slot = len(copies) % slots
-            if len(copies) >= slots:
-                copies[-slots].wait()
-            held[slot] = jnp.dot(
+    for row in range(first, last):
+        band = pl.ds(row * tile, tile)
+        slot = len(copies) % slots
+        if len(copies) >= slots:
+            copies[-slots].wait()
+        for at in range(count):
+            held[slot, :, columns_of(offs_ref, at, slab)] = jnp.dot(
                 delta_ref[band, :], xs[at][...], preferred_element_type=jnp.float32
             ).astype(held.dtype)
-            copy = pltpu.make_async_copy(held.at[slot], out_ref.at[band, here], sems.at[slot])
-            copy.start()
-            copies.append(copy)
+        copy = pltpu.make_async_copy(held.at[slot], out_ref.at[band, :], sems.at[slot])
+        copy.start()
+        copies.append(copy)
     for copy in copies[-slots:]:
         copy.wait()
 
 
-def grad_w_piece(offs, base, delta_t, xs, so_far, mark, shape):
+def grad_w_piece(offs, first, last, bands, delta_t, xs, so_far, mark, shape):
     rows, nodes = delta_t.shape
     slab, count = xs[0].shape[1], len(xs)
-    tile = max(rows // 4, 128)
-    first = so_far is None
+    start = so_far is None
     return call(
-        functools.partial(grad_w_kernel, base, count),
+        functools.partial(grad_w_kernel, first, last, count),
         [jax.ShapeDtypeStruct(shape, jnp.bfloat16), jax.ShapeDtypeStruct((8, 128), jnp.float32)],
         [ANY_REF, VMEM_REF],
-        [pltpu.VMEM((6, tile, slab), jnp.bfloat16), pltpu.SemaphoreType.DMA((6,))],
-        cost(count, nodes, slab, rows),
-        {} if first else {2 + count: 0},
+        [pltpu.VMEM((2, rows // bands, shape[1]), jnp.bfloat16), pltpu.SemaphoreType.DMA((2,))],
+        cost((last - first) * count // bands, nodes, slab, rows),
+        {} if start else {2 + count: 0},
+        2 * 2 * (rows // bands) * shape[1],
     )(
-        [offs, delta_t, *xs] + ([] if first else [so_far, mark]),
-        [SMEM_REF] + [VMEM_REF] * (1 + count) + ([] if first else [ANY_REF] * 2),
+        [offs, delta_t, *xs] + ([] if start else [so_far, mark]),
+        [SMEM_REF] + [VMEM_REF] * (1 + count) + ([] if start else [ANY_REF] * 2),
     )
 
 
@@ -262,6 +320,7 @@
         then = [half] if step == half - 1 else [-step - 1, step + 1]
         listing += [(at, 1) for at in now] + [(at, 0) for at in then]
     listing.append((half, 1))
+    sides = {key: at for at, key in enumerate(listing)}
     table = np.array(
         [
             [
@@ -291,17 +350,7 @@
     xb = flat.astype(jnp.bfloat16)
 
     x = {(0, 0): xb}
-    acc, base, block = None, 0, {}
-
-    def next_products(acc, base, count, loads):
-        keys = listing[base : base + loads]
-        acc, loaded = add_products(
-            offs, base, [x[key] for key in keys[:count]], weights, acc, slab, loads
-        )
-        block.update(zip(keys, loaded))
-        return acc, base + count
-
-    behind, ahead = xb, xb
+    behind, ahead, base = xb, xb, 0
     for step in range(1, half + 1):
         if step < half:
             behind, ahead = ring(behind, 1), ring(ahead, -1)
@@ -310,14 +359,23 @@
         for now in [0] if step == 1 else [1 - step, step - 1]:
             x[now, 1] = swap(x[now, 0])
         count = {1: 1, 2: 3}.get(step, 4)
-        acc, base = next_products(acc, base, count, count)
+        xs = [x[key] for key in listing[base : base + count]]
+        if step == 1:
+            acc, head = first_products(offs, 0, xs[0], weights)
+        elif step == 2:
+            acc, rest = second_products(offs, 0, [x[0, 0], *xs], weights, acc, head)
+        else:
+            acc = add_products(offs, base, xs, acc, head, rest)
+        base += count
         behind, ahead, acc = lax.optimization_barrier((behind, ahead, acc))
         if step < half:
             x[-step, 0], x[step, 0] = behind, ahead
         else:
             x[half, 0] = jnp.concatenate([behind, ahead], axis=0)
     x[half, 1] = swap(x[half, 0])
-    acc, base = next_products(acc, base, 3, 4)
+    xs = [x[key] for key in listing[base : base + 3]]
+    acc = add_products(offs, base, xs, acc, head, rest)
+    base += 3
 
     onehot = (perts[:, None] == jnp.arange(pert_table.shape[0], dtype=jnp.int32)[None, :]).astype(
         jnp.float32
@@ -326,7 +384,7 @@
     deriv = SCALE * jnp.dot(cheb, flat, precision=lax.Precision.HIGHEST)
 
     resid, delta, delta_t, sums = middle(
-        x[half, 1], block[half, 1], acc, deriv, flat, drive,
+        offs, base, x[half, 1], head, rest, acc, deriv, flat, drive,
         eps_gain.reshape(1, rows), decay.reshape(1, rows),
     )
 
@@ -335,8 +393,8 @@
         parts = 2 if count == 1 else 3
         cuts = [0] + [count * nodes * at // parts // 16 * 16 for at in range(1, parts)]
         cuts.append(count * nodes)
-        blocks = [block[step, side] for side in (1, 0) for step in steps]
-        others, owns = shares(offs, delta, blocks, cuts)
+        places = [sides[step, side] for side in (1, 0) for step in steps]
+        others, owns = shares(offs, places, delta, head, rest, slab, cuts)
         swapped = jnp.concatenate([swap(other) for other in others], axis=0)
         return [
             own + swapped[at * nodes : (at + 1) * nodes].astype(jnp.float32)
@@ -344,16 +402,15 @@
         ]
 
     gate = lax.optimization_barrier
-    first = len(listing) // 8
-    each = (len(listing) - first) // (half - 1)
-    cuts = [0] + [first + each * at for at in range(half - 1)] + [len(listing)]
-    pieces = [(base, listing[base:end]) for base, end in zip(cuts[:-1], cuts[1:])]
+    cuts = [0, 1] + [1 + (BANDS - 1) * at // (half - 1) for at in range(1, half)]
+    pieces = list(zip(cuts[:-1], cuts[1:]))
     grad_w, mark = None, None
 
     def next_piece(grad_w, mark):
-        base, keys = pieces.pop(0)
+        first, last = pieces.pop(0)
         return grad_w_piece(
-            offs, base, delta_t, [x[key] for key in keys], grad_w, mark, weights.shape
+            offs, first, last, BANDS, delta_t, [x[key] for key in listing], grad_w, mark,
+            weights.shape,
         )
 
     (far,) = share([half])

time: 97.3 us -> 145 us (1.49)
  local copies, waits for them, and re-layouts: 1.43 us -> 54.9 us
  Pallas kernels: 58.4 us -> 54.7 us
  waiting for transfers between devices: 7.49 us -> 4.87 us
    unnamed x13 -> x119, local copies, waits for them, and re-layouts: 0.05 us -> 53.5 us
    pallas_call x15, Pallas kernels: 58.4 us -> 54.7 us  [run(): pl.pallas_call(kernel, out_shape=out_shape, in_specs=in_specs, out_specs=...]
    ppermute x16, waiting for transfers between devices: 7.43 us -> 4.81 us  [ring(): return lax.ppermute(array, 'row', pairs)]
  transfers between devices with their start and end apart: 37 -> 37, of which waited for: 6 -> 2; matrix products, arithmetic and copies ran while one was open for 4% -> 3% of each run, Pallas kernels for 56% -> 35%
where the time goes in v3:
time: 145 us
  local copies, waits for them, and re-layouts  54.9 us (38%)
  Pallas kernels  54.7 us (38%)
  starting transfers between devices  23.1 us (16%)
  waiting for transfers between devices  4.87 us (3%)
  other arithmetic  3.63 us (3%)
  between operations  2.35 us (2%)
    pallas_call x15, Pallas kernels, run(): pl.pallas_call(kernel, out_shape=out_shape, in_specs=in_specs, out_specs=...  54.7 us
    unnamed x119, local copies, waits for them, and re-layouts  53.5 us
    ppermute x16, starting transfers between devices, ring(): return lax.ppermute(array, 'row', pairs)  17.9 us
    ppermute x21, starting transfers between devices, swap(): return lax.ppermute(array, 'row', [(i, i ^ 1) for i in range(2 * chips)])  5.15 us
    ppermute x16, waiting for transfers between devices, ring(): return lax.ppermute(array, 'row', pairs)  4.81 us
  transfers between devices with their start and end apart: 37, of which 2 were waited for; matrix products, arithmetic and copies ran while one was open for 3% of the time, Pallas kernels for 35%

profile of v3, /device:TPU:0, one launch (start us, length us, event | category | flops | bytes accessed | tf_op | source)
XLA Modules:
  0.0 144.9 jit_solution(8432757646540359312)
XLA Ops:
  0.6 1.1 bitcast_convert_fusion.x_ref.refs_4_.refs_2_
  1.8 3.0 %collective-permute-start = (bf16[128,1024]{1,0:T(8,128)(2,1)S(1)}, bf16[128,1024]{1,0:T(8,128)(2,1)S(1)}, u32[]{:S(2)}, u32[]{:S(2)}) collective-permute-start(bf16[128,1024]{1,0:T(8,128)(2,1)S(1)} %bitcast_convert_fusion.x_ref.refs_4_.refs_2_), channel_id=1, source_target_pairs={{0,2},{1,3},{2,6},{3,7},{6,10},{7,11},{10,14},{11,15},{14,12},{15,... | collective-permute-start | bytes 786440 | tf_op jit(solution)/shard_map/ppermute | solution.py:342
  4.9 0.7 dynamic-slice_bitcast_fusion.offs_ref.refs_0_
  5.6 9.1 %shard_map.119 = (f32[1024,128]{1,0:T(8,128)S(1)}, bf16[768,16384]{1,0:T(8,128)(2,1)S(1)}) custom-call(s32[16]{0:T(128)S(1)} %dynamic-slice_bitcast_fusion.offs_ref.refs_0_, bf16[1024,16384]{1,0:T(8,128)(2,1)} %refs_1_.1, bf16[128,1024]{1,0:T(8,128)(2,1)S(1)} %bitcast_convert_fusion.x_ref.refs_4_.refs_2_), custom_call_target="tpu_custom_call" | custom-call | flops 16777216 | bytes 131072 | tf_op jit(solution)/shard_map/pallas_call | solution.py:55
  14.7 1.9 %collective-permute-start.2 = (bf16[128,1024]{1,0:T(8,128)(2,1)S(1)}, bf16[128,1024]{1,0:T(8,128)(2,1)S(1)}, u32[]{:S(2)}, u32[]{:S(2)}) collective-permute-start(bf16[128,1024]{1,0:T(8,128)(2,1)S(1)} %collective-permute-done.refs_6_.refs_4_), channel_id=1, source_target_pairs={{0,2},{1,3},{2,6},{3,7},{6,10},{7,11},{10,14},{11,15},{14,12},{15,... | collective-permute-start | bytes 786440 | tf_op jit(solution)/shard_map/ppermute | solution.py:342
  16.8 0.2 collective-permute-start.7
  17.0 0.3 collective-permute-start.8
  17.3 6.0 %shard_map.120 = (f32[1024,128]{1,0:T(8,128)S(1)}, bf16[256,16384]{1,0:T(8,128)(2,1)S(1)}) custom-call(s32[16]{0:T(128)S(1)} %dynamic-slice_bitcast_fusion.offs_ref.refs_0_, bf16[1024,16384]{1,0:T(8,128)(2,1)} %refs_1_.1, f32[1024,128]{1,0:T(8,128)S(1)} %get-tuple-element.76.refs_2_, bf16[768,16384]{1,0:T(8,128)(2,1)S(1)} %get-tuple-element.77.refs_3_.head_ref, ...), custom_call_target="tpu_custom_call" | custom-call | flops 67108864 | bytes 524288 | tf_op jit(solution)/shard_map/pallas_call | solution.py:55
  23.4 8.3 %copy-done.2 = bf16[768,16384]{1,0:T(8,128)(2,1)} copy-done((bf16[768,16384]{1,0:T(8,128)(2,1)}, bf16[768,16384]{1,0:T(8,128)(2,1)S(1)}, u32[]{:S(2)}) %copy-start.2) | copy-done | bytes 25165848
  31.7 1.9 %collective-permute-start.5 = (bf16[128,1024]{1,0:T(8,128)(2,1)S(1)}, bf16[128,1024]{1,0:T(8,128)(2,1)S(1)}, u32[]{:S(2)}, u32[]{:S(2)}) collective-permute-start(bf16[128,1024]{1,0:T(8,128)(2,1)S(1)} %collective-permute-done.2.refs_2_.refs_8_), channel_id=1, source_target_pairs={{0,2},{1,3},{2,6},{3,7},{6,10},{7,11},{10,14},{11,15},{14,12},{15,... | collective-permute-start | bytes 786440 | tf_op jit(solution)/shard_map/ppermute | solution.py:342
  33.8 0.5 collective-permute-start.12
  34.3 8.7 %copy-done.3 = bf16[768,16384]{1,0:T(8,128)(2,1)S(1)} copy-done((bf16[768,16384]{1,0:T(8,128)(2,1)S(1)}, bf16[768,16384]{1,0:T(8,128)(2,1)}, u32[]{:S(2)}) %copy-start.3) | copy-done | bytes 25165848
  43.0 2.9 %shard_map.121.acc_ref = f32[1024,128]{1,0:T(8,128)S(1)} custom-call(s32[16]{0:T(128)S(1)} %dynamic-slice_bitcast_fusion.offs_ref.refs_0_, f32[1024,128]{1,0:T(8,128)S(1)} %get-tuple-element.81.acc_ref, bf16[768,16384]{1,0:T(8,128)(2,1)S(1)} %copy-done.3, bf16[256,16384]{1,0:T(8,128)(2,1)S(1)} %get-tuple-element.82.rest_ref, ...), custom_call_target="tpu_custom_call" | custom-call | flops 67108864 | bytes 524288 | tf_op jit(solution)/shard_map/pallas_call | solution.py:55
  45.9 1.9 %collective-permute-start.9 = (bf16[64,1024]{1,0:T(8,128)(2,1)S(1)}, bf16[64,1024]{1,0:T(8,128)(2,1)S(1)}, u32[]{:S(2)}, u32[]{:S(2)}) collective-permute-start(bf16[64,1024]{1,0:T(8,128)(2,1)S(1)} %slice.59), channel_id=1, source_target_pairs={{0,2},{1,3},{2,6},{3,7},{6,10},{7,11},{10,14},{11,15},{14,12},{15,... | collective-permute-start | bytes 393224 | tf_op jit(solution)/shard_map/ppermute | solution.py:342
  47.8 0.4 collective-permute-start.10
  49.0 0.5 collective-permute-start.15
  49.5 8.2 %copy-done.4 = bf16[768,16384]{1,0:T(8,128)(2,1)S(1)} copy-done((bf16[768,16384]{1,0:T(8,128)(2,1)S(1)}, bf16[768,16384]{1,0:T(8,128)(2,1)}, u32[]{:S(2)}) %copy-start.4) | copy-done | bytes 25165848
  57.6 2.9 %shard_map.122.acc_ref = f32[1024,128]{1,0:T(8,128)S(1)} custom-call(s32[16]{0:T(128)S(1)} %dynamic-slice_bitcast_fusion.offs_ref.refs_0_, f32[1024,128]{1,0:T(8,128)S(1)} %shard_map.121.acc_ref, bf16[768,16384]{1,0:T(8,128)(2,1)S(1)} %copy-done.4, bf16[256,16384]{1,0:T(8,128)(2,1)S(1)} %get-tuple-element.82.rest_ref, ...), custom_call_target="tpu_custom_call" | custom-call | flops 67108864 | bytes 524288 | tf_op jit(solution)/shard_map/pallas_call | solution.py:55
  60.6 0.2 collective-permute-start.13
  60.9 0.6 convolution_multiply_fusion.1.deriv_ref
  61.6 8.2 %copy-done.5 = bf16[768,16384]{1,0:T(8,128)(2,1)S(1)} copy-done((bf16[768,16384]{1,0:T(8,128)(2,1)S(1)}, bf16[768,16384]{1,0:T(8,128)(2,1)}, u32[]{:S(2)}) %copy-start.5) | copy-done | bytes 25165848
  69.8 2.3 %shard_map.123.acc_ref = f32[1024,128]{1,0:T(8,128)S(1)} custom-call(s32[16]{0:T(128)S(1)} %dynamic-slice_bitcast_fusion.offs_ref.refs_0_, f32[1024,128]{1,0:T(8,128)S(1)} %shard_map.122.acc_ref, bf16[768,16384]{1,0:T(8,128)(2,1)S(1)} %copy-done.5, bf16[256,16384]{1,0:T(8,128)(2,1)S(1)} %get-tuple-element.82.rest_ref, ...), custom_call_target="tpu_custom_call" | custom-call | flops 50331648 | bytes 393216 | tf_op jit(solution)/shard_map/pallas_call | solution.py:55
  72.3 1.5 %shard_map.124 = (f32[128,1024]{1,0:T(8,128)S(1)}, bf16[128,1024]{1,0:T(8,128)(2,1)S(1)}, bf16[1024,128]{1,0:T(8,128)(2,1)S(1)}, f32[8,1024]{1,0:T(8,128)S(1)}) custom-call(s32[16]{0:T(128)S(1)} %dynamic-slice_bitcast_fusion.offs_ref.refs_0_, bf16[128,1024]{1,0:T(8,128)(2,1)S(1)} %collective-permute-done.13.x_ref.refs_17_, bf16[768,16384]{1,0:T(8,128)(2,1)S(1)} %copy-done.5, ...), custom_call_target="tpu_custom_call" | custom-call | flops 33554432 | bytes 262144 | tf_op jit(solution)/shard_map/pallas_call | solution.py:55
  73.8 0.8 copy-done.48
  74.6 4.2 %copy-done.8 = bf16[256,16384]{1,0:T(8,128)(2,1)S(1)} copy-done((bf16[256,16384]{1,0:T(8,128)(2,1)S(1)}, bf16[256,16384]{1,0:T(8,128)(2,1)}, u32[]{:S(2)}) %copy-start.8) | copy-done | bytes 8388632
  78.8 1.3 shard_map.125
  80.1 0.5 collective-permute-start.17
  80.7 1.7 %copy-done.10 = bf16[128,1024]{1,0:T(8,128)(2,1)S(1)} copy-done((bf16[128,1024]{1,0:T(8,128)(2,1)S(1)}, bf16[128,1024]{1,0:T(8,128)(2,1)}, u32[]{:S(2)}) %copy-start.10) | copy-done | bytes 262168
  82.4 1.2 copy-done.13
  83.7 0.9 copy-done.17
  84.6 0.9 copy-done.21
  85.6 0.9 copy-done.25
  86.5 0.9 copy-done.29
  87.5 3.8 %shard_map.126 = (bf16[1024,16384]{1,0:T(8,128)(2,1)}, f32[8,128]{1,0:T(8,128)S(1)}) custom-call(s32[16]{0:T(128)S(1)} %dynamic-slice_bitcast_fusion.offs_ref.refs_0_, bf16[1024,128]{1,0:T(8,128)(2,1)S(1)} %get-tuple-element.93.refs_1_, bf16[128,1024]{1,0:T(8,128)(2,1)S(1)} %bitcast_convert_fusion.x_ref.refs_4_.refs_2_, ...), custom_call_target="tpu_custom_call" | custom-call | flops 33554432 | bytes 262144 | tf_op jit(solution)/shard_map/pallas_call | solution.py:55
  91.5 1.9 %shard_map.127 = (bf16[80,1024]{1,0:T(8,128)(2,1)S(1)}, bf16[80,1024]{1,0:T(8,128)(2,1)S(1)}, bf16[96,1024]{1,0:T(8,128)(2,1)S(1)}, f32[128,1024]{1,0:T(8,128)S(1)}, f32[128,1024]{1,0:T(8,128)S(1)}) custom-call(s32[16]{0:T(128)S(1)} %dynamic-slice_bitcast_fusion.offs_ref.refs_0_, bf16[128,1024]{1,0:T(8,128)(2,1)S(1)} %get-tuple-element.89.delta_ref, ...), custom_call_target="tpu_custom_call" | custom-call | flops 67108864 | bytes 524288 | tf_op jit(solution)/shard_map/pallas_call | solution.py:55
  93.4 0.5 collective-permute-start.21
  94.0 0.4 collective-permute-start.18
  94.4 1.9 %collective-permute-start.20 = (bf16[64,1024]{1,0:T(8,128)(2,1)S(1)}, bf16[64,1024]{1,0:T(8,128)(2,1)S(1)}, u32[]{:S(2)}, u32[]{:S(2)}) collective-permute-start(bf16[64,1024]{1,0:T(8,128)(2,1)S(1)} %get-tuple-element.142), channel_id=1, source_target_pairs={{0,2},{1,3},{2,6},{3,7},{6,10},{7,11},{10,14},{11,15},{14,12},{15,... | collective-permute-start | bytes 393224 | tf_op jit(solution)/shard_map/ppermute | solution.py:342
  96.3 0.2 collective-permute-start.22
  96.5 0.2 convert_add_fusion
  96.7 3.5 %collective-permute-done.20 = bf16[64,1024]{1,0:T(8,128)(2,1)S(1)} collective-permute-done((bf16[64,1024]{1,0:T(8,128)(2,1)S(1)}, bf16[64,1024]{1,0:T(8,128)(2,1)S(1)}, u32[]{:S(2)}, u32[]{:S(2)}) %collective-permute-start.20) | collective-permute-done | bytes 131104 | tf_op jit(solution)/shard_map/ppermute | solution.py:342
  100.3 1.3 collective-permute-done.22
  101.6 1.6 %collective-permute-start.25 = (bf16[128,1024]{1,0:T(8,128)(2,1)S(1)}, bf16[128,1024]{1,0:T(8,128)(2,1)S(1)}, u32[]{:S(2)}, u32[]{:S(2)}) collective-permute-start(bf16[128,1024]{1,0:T(8,128)(2,1)S(1)} %pad_maximum_fusion.6), channel_id=1, source_target_pairs={{0,2},{1,3},{2,6},{3,7},{6,10},{7,11},{10,14},{11,15},{14,12},{15,... | collective-permute-start | bytes 786440 | tf_op jit(solution)/shard_map/ppermute | solution.py:342
  103.2 0.4 collective-permute-start.26
  103.7 1.8 %shard_map.128 = (bf16[80,1024]{1,0:T(8,128)(2,1)S(1)}, bf16[80,1024]{1,0:T(8,128)(2,1)S(1)}, bf16[96,1024]{1,0:T(8,128)(2,1)S(1)}, f32[128,1024]{1,0:T(8,128)S(1)}, f32[128,1024]{1,0:T(8,128)S(1)}) custom-call(s32[16]{0:T(128)S(1)} %dynamic-slice_bitcast_fusion.offs_ref.refs_0_, bf16[128,1024]{1,0:T(8,128)(2,1)S(1)} %get-tuple-element.89.delta_ref, ...), custom_call_target="tpu_custom_call" | custom-call | flops 67108864 | bytes 524288 | tf_op jit(solution)/shard_map/pallas_call | solution.py:55
  105.6 0.5 collective-permute-start.24
  106.3 5.2 %shard_map.129 = (bf16[1024,16384]{1,0:T(8,128)(2,1)}, f32[8,128]{1,0:T(8,128)S(1)}) custom-call(s32[16]{0:T(128)S(1)} %dynamic-slice_bitcast_fusion.offs_ref.refs_0_, bf16[1024,128]{1,0:T(8,128)(2,1)S(1)} %copy-done.46, bf16[128,1024]{1,0:T(8,128)(2,1)S(1)} %bitcast_convert_fusion.x_ref.refs_4_.refs_2_, ...), custom_call_target="tpu_custom_call", output_to_operand_aliasing={{0}: (18, {})} | custom-call | flops 67108864 | bytes 524288 | tf_op jit(solution)/shard_map/pallas_call | solution.py:55
  111.6 0.3 add_convert_fusion.2
  111.8 1.6 %collective-permute-start.30 = (bf16[128,1024]{1,0:T(8,128)(2,1)S(1)}, bf16[128,1024]{1,0:T(8,128)(2,1)S(1)}, u32[]{:S(2)}, u32[]{:S(2)}) collective-permute-start(bf16[128,1024]{1,0:T(8,128)(2,1)S(1)} %get-tuple-element.119), channel_id=1, source_target_pairs={{0,2},{1,3},{2,6},{3,7},{6,10},{7,11},{10,14},{11,15},{14,12},{15,... | collective-permute-start | bytes 786440 | tf_op jit(solution)/shard_map/ppermute | solution.py:342
  113.5 0.4 collective-permute-start.31
  113.9 1.8 %shard_map.130 = (bf16[80,1024]{1,0:T(8,128)(2,1)S(1)}, bf16[80,1024]{1,0:T(8,128)(2,1)S(1)}, bf16[96,1024]{1,0:T(8,128)(2,1)S(1)}, f32[128,1024]{1,0:T(8,128)S(1)}, f32[128,1024]{1,0:T(8,128)S(1)}) custom-call(s32[16]{0:T(128)S(1)} %dynamic-slice_bitcast_fusion.offs_ref.refs_0_, bf16[128,1024]{1,0:T(8,128)(2,1)S(1)} %get-tuple-element.89.delta_ref, ...), custom_call_target="tpu_custom_call" | custom-call | flops 67108864 | bytes 524288 | tf_op jit(solution)/shard_map/pallas_call | solution.py:55
  115.8 0.5 collective-permute-start.29
  116.4 0.6 fusion.1
  117.2 5.2 %shard_map.131 = (bf16[1024,16384]{1,0:T(8,128)(2,1)}, f32[8,128]{1,0:T(8,128)S(1)}) custom-call(s32[16]{0:T(128)S(1)} %dynamic-slice_bitcast_fusion.offs_ref.refs_0_, bf16[1024,128]{1,0:T(8,128)(2,1)S(1)} %copy-done.46, bf16[128,1024]{1,0:T(8,128)(2,1)S(1)} %bitcast_convert_fusion.x_ref.refs_4_.refs_2_, ...), custom_call_target="tpu_custom_call", output_to_operand_aliasing={{0}: (18, {})} | custom-call | flops 67108864 | bytes 524288 | tf_op jit(solution)/shard_map/pallas_call | solution.py:55
  122.4 0.3 add_convert_fusion
  122.7 1.6 %collective-permute-start.35 = (bf16[128,1024]{1,0:T(8,128)(2,1)S(1)}, bf16[128,1024]{1,0:T(8,128)(2,1)S(1)}, u32[]{:S(2)}, u32[]{:S(2)}) collective-permute-start(bf16[128,1024]{1,0:T(8,128)(2,1)S(1)} %get-tuple-element.136), channel_id=1, source_target_pairs={{0,2},{1,3},{2,6},{3,7},{6,10},{7,11},{10,14},{11,15},{14,12},{15,... | collective-permute-start | bytes 786440 | tf_op jit(solution)/shard_map/ppermute | solution.py:342
  124.4 0.4 collective-permute-start.36
  124.8 0.6 fusion.11
  125.4 8.2 %copy-done.6 = bf16[768,16384]{1,0:T(8,128)(2,1)S(1)} copy-done((bf16[768,16384]{1,0:T(8,128)(2,1)S(1)}, bf16[768,16384]{1,0:T(8,128)(2,1)}, u32[]{:S(2)}) %copy-start.6) | copy-done | bytes 25165848
  133.6 1.3 shard_map.133
  134.9 0.5 collective-permute-start.33
  135.4 0.7 broadcast_multiply_fusion
  136.2 7.7 %shard_map.132 = (bf16[1024,16384]{1,0:T(8,128)(2,1)}, f32[8,128]{1,0:T(8,128)}) custom-call(s32[16]{0:T(128)S(1)} %dynamic-slice_bitcast_fusion.offs_ref.refs_0_, bf16[1024,128]{1,0:T(8,128)(2,1)S(1)} %copy-done.47, bf16[128,1024]{1,0:T(8,128)(2,1)S(1)} %bitcast_convert_fusion.x_ref.refs_4_.refs_2_, ...), custom_call_target="tpu_custom_call", output_to_operand_aliasing={{0}: (18, {})} | custom-call | flops 100663296 | bytes 786432 | tf_op jit(solution)/shard_map/pallas_call | solution.py:55
  143.9 1.0 add_bitcast_fusion
  (168 shorter events, 1.8 us)
Async XLA Ops:
  0.6 60.1 %copy-start = (f32[16,1024]{1,0:T(8,128)S(1)}, f32[16,1024]{1,0:T(8,128)}, u32[]{:S(2)}) copy-start(f32[16,1024]{1,0:T(8,128)} %param.10) | copy-start | bytes 196612
  1.8 13.0 %collective-permute-start = (bf16[128,1024]{1,0:T(8,128)(2,1)S(1)}, bf16[128,1024]{1,0:T(8,128)(2,1)S(1)}, u32[]{:S(2)}, u32[]{:S(2)}) collective-permute-start(bf16[128,1024]{1,0:T(8,128)(2,1)S(1)} %bitcast_convert_fusion.x_ref.refs_4_.refs_2_), channel_id=1, source_target_pairs={{0,2},{1,3},{2,6},{3,7},{6,10},{7,11},{10,14},{11,15},{14,12},{15,... | collective-permute-start | bytes 786440 | tf_op jit(solution)/shard_map/ppermute | solution.py:342
  4.7 10.0 %collective-permute-start.1 = (bf16[128,1024]{1,0:T(8,128)(2,1)S(1)}, bf16[128,1024]{1,0:T(8,128)(2,1)S(1)}, u32[]{:S(2)}, u32[]{:S(2)}) collective-permute-start(bf16[128,1024]{1,0:T(8,128)(2,1)S(1)} %bitcast_convert_fusion.x_ref.refs_4_.refs_2_), channel_id=1, source_target_pairs={{0,4},{1,5},{2,0},{3,1},{6,2},{7,3},{10,6},{11,7},{14,10},{15,11},... | collective-permute-start | bytes 786440 | tf_op jit(solution)/shard_map/ppermute | solution.py:342
  4.9 12.4 %collective-permute-start.4 = (bf16[128,1024]{1,0:T(8,128)(2,1)S(1)}, bf16[128,1024]{1,0:T(8,128)(2,1)S(1)}, u32[]{:S(2)}, u32[]{:S(2)}) collective-permute-start(bf16[128,1024]{1,0:T(8,128)(2,1)S(1)} %bitcast_convert_fusion.x_ref.refs_4_.refs_2_), channel_id=1, source_target_pairs={{0,1},{1,0},{2,3},{3,2},{4,5},{5,4},{6,7},{7,6},{8,9},{9,8},{10,11... | collective-permute-start | bytes 786440 | tf_op jit(solution)/shard_map/ppermute | solution.py:345
  14.7 17.0 %collective-permute-start.2 = (bf16[128,1024]{1,0:T(8,128)(2,1)S(1)}, bf16[128,1024]{1,0:T(8,128)(2,1)S(1)}, u32[]{:S(2)}, u32[]{:S(2)}) collective-permute-start(bf16[128,1024]{1,0:T(8,128)(2,1)S(1)} %collective-permute-done.refs_6_.refs_4_), channel_id=1, source_target_pairs={{0,2},{1,3},{2,6},{3,7},{6,10},{7,11},{10,14},{11,15},{14,12},{15,... | collective-permute-start | bytes 786440 | tf_op jit(solution)/shard_map/ppermute | solution.py:342
  16.7 15.0 %collective-permute-start.3 = (bf16[128,1024]{1,0:T(8,128)(2,1)S(1)}, bf16[128,1024]{1,0:T(8,128)(2,1)S(1)}, u32[]{:S(2)}, u32[]{:S(2)}) collective-permute-start(bf16[128,1024]{1,0:T(8,128)(2,1)S(1)} %collective-permute-done.1.refs_7_.refs_5_), channel_id=1, source_target_pairs={{0,4},{1,5},{2,0},{3,1},{6,2},{7,3},{10,6},{11,7},{14,10},{15,11},... | collective-permute-start | bytes 786440 | tf_op jit(solution)/shard_map/ppermute | solution.py:342
  16.8 17.0 %collective-permute-start.7 = (bf16[128,1024]{1,0:T(8,128)(2,1)S(1)}, bf16[128,1024]{1,0:T(8,128)(2,1)S(1)}, u32[]{:S(2)}, u32[]{:S(2)}) collective-permute-start(bf16[128,1024]{1,0:T(8,128)(2,1)S(1)} %collective-permute-done.refs_6_.refs_4_), channel_id=1, source_target_pairs={{0,1},{1,0},{2,3},{3,2},{4,5},{5,4},{6,7},{7,6},{8,9},{9,8},{10,11... | collective-permute-start | bytes 786440 | tf_op jit(solution)/shard_map/ppermute | solution.py:345
  17.0 17.3 %collective-permute-start.8 = (bf16[128,1024]{1,0:T(8,128)(2,1)S(1)}, bf16[128,1024]{1,0:T(8,128)(2,1)S(1)}, u32[]{:S(2)}, u32[]{:S(2)}) collective-permute-start(bf16[128,1024]{1,0:T(8,128)(2,1)S(1)} %collective-permute-done.1.refs_7_.refs_5_), channel_id=1, source_target_pairs={{0,1},{1,0},{2,3},{3,2},{4,5},{5,4},{6,7},{7,6},{8,9},{9,8},{10,11... | collective-permute-start | bytes 786440 | tf_op jit(solution)/shard_map/ppermute | solution.py:345
  31.7 40.5 %copy-start.7 = (bf16[256,16384]{1,0:T(8,128)(2,1)}, bf16[256,16384]{1,0:T(8,128)(2,1)S(1)}, u32[]{:S(2)}) copy-start(bf16[256,16384]{1,0:T(8,128)(2,1)S(1)} %get-tuple-element.82.rest_ref) | copy-start | bytes 25165828
  31.7 28.8 %copy-start.9 = (bf16[128,1024]{1,0:T(8,128)(2,1)}, bf16[128,1024]{1,0:T(8,128)(2,1)S(1)}, u32[]{:S(2)}) copy-start(bf16[128,1024]{1,0:T(8,128)(2,1)S(1)} %collective-permute-done.2.refs_2_.refs_8_) | copy-start | bytes 786436
  31.7 28.8 %copy-start.12 = (bf16[128,1024]{1,0:T(8,128)(2,1)}, bf16[128,1024]{1,0:T(8,128)(2,1)S(1)}, u32[]{:S(2)}) copy-start(bf16[128,1024]{1,0:T(8,128)(2,1)S(1)} %collective-permute-done.3.refs_3_.refs_9_) | copy-start | bytes 786436
  31.7 14.1 %collective-permute-start.5 = (bf16[128,1024]{1,0:T(8,128)(2,1)S(1)}, bf16[128,1024]{1,0:T(8,128)(2,1)S(1)}, u32[]{:S(2)}, u32[]{:S(2)}) collective-permute-start(bf16[128,1024]{1,0:T(8,128)(2,1)S(1)} %collective-permute-done.2.refs_2_.refs_8_), channel_id=1, source_target_pairs={{0,2},{1,3},{2,6},{3,7},{6,10},{7,11},{10,14},{11,15},{14,12},{15,... | collective-permute-start | bytes 786440 | tf_op jit(solution)/shard_map/ppermute | solution.py:342
  33.6 12.2 %collective-permute-start.6 = (bf16[128,1024]{1,0:T(8,128)(2,1)S(1)}, bf16[128,1024]{1,0:T(8,128)(2,1)S(1)}, u32[]{:S(2)}, u32[]{:S(2)}) collective-permute-start(bf16[128,1024]{1,0:T(8,128)(2,1)S(1)} %collective-permute-done.3.refs_3_.refs_9_), channel_id=1, source_target_pairs={{0,4},{1,5},{2,0},{3,1},{6,2},{7,3},{10,6},{11,7},{14,10},{15,11},... | collective-permute-start | bytes 786440 | tf_op jit(solution)/shard_map/ppermute | solution.py:342
  33.8 15.2 %collective-permute-start.11 = (bf16[128,1024]{1,0:T(8,128)(2,1)S(1)}, bf16[128,1024]{1,0:T(8,128)(2,1)S(1)}, u32[]{:S(2)}, u32[]{:S(2)}) collective-permute-start(bf16[128,1024]{1,0:T(8,128)(2,1)S(1)} %collective-permute-done.2.refs_2_.refs_8_), channel_id=1, source_target_pairs={{0,1},{1,0},{2,3},{3,2},{4,5},{5,4},{6,7},{7,6},{8,9},{9,8},{10,11... | collective-permute-start | bytes 786440 | tf_op jit(solution)/shard_map/ppermute | solution.py:345
  33.8 26.7 %copy-start.16 = (bf16[128,1024]{1,0:T(8,128)(2,1)}, bf16[128,1024]{1,0:T(8,128)(2,1)S(1)}, u32[]{:S(2)}) copy-start(bf16[128,1024]{1,0:T(8,128)(2,1)S(1)} %collective-permute-done.7.refs_0_.refs_6_) | copy-start | bytes 786436
  33.8 15.7 %collective-permute-start.12 = (bf16[128,1024]{1,0:T(8,128)(2,1)S(1)}, bf16[128,1024]{1,0:T(8,128)(2,1)S(1)}, u32[]{:S(2)}, u32[]{:S(2)}) collective-permute-start(bf16[128,1024]{1,0:T(8,128)(2,1)S(1)} %collective-permute-done.3.refs_3_.refs_9_), channel_id=1, source_target_pairs={{0,1},{1,0},{2,3},{3,2},{4,5},{5,4},{6,7},{7,6},{8,9},{9,8},{10,11... | collective-permute-start | bytes 786440 | tf_op jit(solution)/shard_map/ppermute | solution.py:345
  34.3 26.2 %copy-start.20 = (bf16[128,1024]{1,0:T(8,128)(2,1)}, bf16[128,1024]{1,0:T(8,128)(2,1)S(1)}, u32[]{:S(2)}) copy-start(bf16[128,1024]{1,0:T(8,128)(2,1)S(1)} %collective-permute-done.8.refs_1_.refs_7_) | copy-start | bytes 786436
  43.0 17.9 %copy-start.44 = (f32[1,128,1024]{2,1,0:T(8,128)S(1)}, f32[1,128,1024]{2,1,0:T(8,128)}, u32[]{:S(2)}) copy-start(f32[1,128,1024]{2,1,0:T(8,128)} %param.8) | copy-start | bytes 1572868
  43.0 17.9 %copy-start.52 = (f32[128,128]{1,0:T(8,128)S(1)}, f32[128,128]{1,0:T(8,128)}, u32[]{:S(2)}) copy-start(f32[128,128]{1,0:T(8,128)} %constant.15.clone) | copy-start | bytes 196612
  45.9 14.6 %collective-permute-start.9 = (bf16[64,1024]{1,0:T(8,128)(2,1)S(1)}, bf16[64,1024]{1,0:T(8,128)(2,1)S(1)}, u32[]{:S(2)}, u32[]{:S(2)}) collective-permute-start(bf16[64,1024]{1,0:T(8,128)(2,1)S(1)} %slice.59), channel_id=1, source_target_pairs={{0,2},{1,3},{2,6},{3,7},{6,10},{7,11},{10,14},{11,15},{14,12},{15,... | collective-permute-start | bytes 393224 | tf_op jit(solution)/shard_map/ppermute | solution.py:342
  47.8 24.4 %copy-start.50 = (f32[1024]{0:T(1024)S(1)}, f32[1024]{0:T(1024)}, u32[]{:S(2)}) copy-start(f32[1024]{0:T(1024)} %param.12) | copy-start | bytes 12292
  47.8 24.4 %copy-start.51 = (f32[1024]{0:T(1024)S(1)}, f32[1024]{0:T(1024)}, u32[]{:S(2)}) copy-start(f32[1024]{0:T(1024)} %param.11) | copy-start | bytes 12292
  47.8 12.7 %collective-permute-start.10 = (bf16[64,1024]{1,0:T(8,128)(2,1)S(1)}, bf16[64,1024]{1,0:T(8,128)(2,1)S(1)}, u32[]{:S(2)}, u32[]{:S(2)}) collective-permute-start(bf16[64,1024]{1,0:T(8,128)(2,1)S(1)} %slice.60), channel_id=1, source_target_pairs={{0,4},{1,5},{2,0},{3,1},{6,2},{7,3},{10,6},{11,7},{14,10},{15,11},... | collective-permute-start | bytes 393224 | tf_op jit(solution)/shard_map/ppermute | solution.py:342
  48.9 12.6 %collective-permute-start.14 = (bf16[128,1024]{1,0:T(8,128)(2,1)S(1)}, bf16[128,1024]{1,0:T(8,128)(2,1)S(1)}, u32[]{:S(2)}, u32[]{:S(2)}) collective-permute-start(bf16[128,1024]{1,0:T(8,128)(2,1)S(1)} %collective-permute-done.5.refs_2_.refs_12_), channel_id=1, source_target_pairs={{0,1},{1,0},{2,3},{3,2},{4,5},{5,4},{6,7},{7,6},{8,9},{9,8},{10,11... | collective-permute-start | bytes 786440 | tf_op jit(solution)/shard_map/ppermute | solution.py:345
  49.0 23.2 %copy-start.24 = (bf16[128,1024]{1,0:T(8,128)(2,1)}, bf16[128,1024]{1,0:T(8,128)(2,1)S(1)}, u32[]{:S(2)}) copy-start(bf16[128,1024]{1,0:T(8,128)(2,1)S(1)} %collective-permute-done.11.refs_0_.refs_10_) | copy-start | bytes 786436
  49.0 12.6 %collective-permute-start.15 = (bf16[128,1024]{1,0:T(8,128)(2,1)S(1)}, bf16[128,1024]{1,0:T(8,128)(2,1)S(1)}, u32[]{:S(2)}, u32[]{:S(2)}) collective-permute-start(bf16[128,1024]{1,0:T(8,128)(2,1)S(1)} %collective-permute-done.6.refs_3_.refs_13_), channel_id=1, source_target_pairs={{0,1},{1,0},{2,3},{3,2},{4,5},{5,4},{6,7},{7,6},{8,9},{9,8},{10,11... | collective-permute-start | bytes 786440 | tf_op jit(solution)/shard_map/ppermute | solution.py:345
  60.6 11.6 %collective-permute-start.13 = (bf16[128,1024]{1,0:T(8,128)(2,1)S(1)}, bf16[128,1024]{1,0:T(8,128)(2,1)S(1)}, u32[]{:S(2)}, u32[]{:S(2)}) collective-permute-start(bf16[128,1024]{1,0:T(8,128)(2,1)S(1)} %constant_dynamic-update-slice_fusion.refs_2_.refs_16_), channel_id=1, source_target_pairs={{0,1},{1,0},{2,3},{3,2},{4,5},{5,4},{6,7},{7,6},{8,9},{9,8},{10,11... | collective-permute-start | bytes 786440 | tf_op jit(solution)/shard_map/ppermute | solution.py:345
  72.2 19.1 %slice-start = ((s8[25165824]{0:T(1024)(128)(4,1)}), s8[4194304]{0:T(1024)(128)(4,1)S(1)}, s32[]{:S(2)}) async-start(s8[25165824]{0:T(1024)(128)(4,1)} %bitcast.28), calls=%async_computation | async-start | bytes 8388608
  72.2 19.1 %slice-start.1 = ((s8[25165824]{0:T(1024)(128)(4,1)}), s8[4194304]{0:T(1024)(128)(4,1)S(1)}, s32[]{:S(2)}) async-start(s8[25165824]{0:T(1024)(128)(4,1)} %bitcast.28), calls=%async_computation.1 | async-start | bytes 8388608
  72.3 19.1 %slice-start.2 = ((s8[25165824]{0:T(1024)(128)(4,1)}), s8[4194304]{0:T(1024)(128)(4,1)S(1)}, s32[]{:S(2)}) async-start(s8[25165824]{0:T(1024)(128)(4,1)} %bitcast.28), calls=%async_computation.2 | async-start | bytes 8388608
  74.6 16.8 %copy-start.45 = (bf16[1024,128]{1,0:T(8,128)(2,1)}, bf16[1024,128]{1,0:T(8,128)(2,1)S(1)}, u32[]{:S(2)}) copy-start(bf16[1024,128]{1,0:T(8,128)(2,1)S(1)} %get-tuple-element.93.refs_1_) | copy-start | bytes 786436
  80.1 11.1 %collective-permute-start.17 = (bf16[64,1024]{1,0:T(8,128)(2,1)S(1)}, bf16[64,1024]{1,0:T(8,128)(2,1)S(1)}, u32[]{:S(2)}, u32[]{:S(2)}) collective-permute-start(bf16[64,1024]{1,0:T(8,128)(2,1)S(1)} %get-tuple-element.92), channel_id=1, source_target_pairs={{0,1},{1,0},{2,3},{3,2},{4,5},{5,4},{6,7},{7,6},{8,9},{9,8},{10,11... | collective-permute-start | bytes 393224 | tf_op jit(solution)/shard_map/ppermute | solution.py:345
  80.6 10.7 %collective-permute-start.16 = (bf16[64,1024]{1,0:T(8,128)(2,1)S(1)}, bf16[64,1024]{1,0:T(8,128)(2,1)S(1)}, u32[]{:S(2)}, u32[]{:S(2)}) collective-permute-start(bf16[64,1024]{1,0:T(8,128)(2,1)S(1)} %get-tuple-element.91), channel_id=1, source_target_pairs={{0,1},{1,0},{2,3},{3,2},{4,5},{5,4},{6,7},{7,6},{8,9},{9,8},{10,11... | collective-permute-start | bytes 393224 | tf_op jit(solution)/shard_map/ppermute | solution.py:345
  91.4 14.8 %copy-start.11 = (bf16[128,1024]{1,0:T(8,128)(2,1)S(1)}, bf16[128,1024]{1,0:T(8,128)(2,1)}, u32[]{:S(2)}) copy-start(bf16[128,1024]{1,0:T(8,128)(2,1)} %copy-done.9) | copy-start | bytes 786436
  91.4 14.7 %copy-start.14 = (bf16[128,1024]{1,0:T(8,128)(2,1)S(1)}, bf16[128,1024]{1,0:T(8,128)(2,1)}, u32[]{:S(2)}) copy-start(bf16[128,1024]{1,0:T(8,128)(2,1)} %copy-done.12) | copy-start | bytes 786436
  93.4 3.1 %collective-permute-start.21 = (bf16[96,1024]{1,0:T(8,128)(2,1)S(1)}, bf16[96,1024]{1,0:T(8,128)(2,1)S(1)}, u32[]{:S(2)}, u32[]{:S(2)}) collective-permute-start(bf16[96,1024]{1,0:T(8,128)(2,1)S(1)} %get-tuple-element.101), channel_id=1, source_target_pairs={{0,1},{1,0},{2,3},{3,2},{4,5},{5,4},{6,7},{7,6},{8,9},{9,8},{10,11... | collective-permute-start | bytes 589832 | tf_op jit(solution)/shard_map/ppermute | solution.py:345
  93.9 2.6 %collective-permute-start.19 = (bf16[80,1024]{1,0:T(8,128)(2,1)S(1)}, bf16[80,1024]{1,0:T(8,128)(2,1)S(1)}, u32[]{:S(2)}, u32[]{:S(2)}) collective-permute-start(bf16[80,1024]{1,0:T(8,128)(2,1)S(1)} %get-tuple-element.98), channel_id=1, source_target_pairs={{0,1},{1,0},{2,3},{3,2},{4,5},{5,4},{6,7},{7,6},{8,9},{9,8},{10,11... | collective-permute-start | bytes 491528 | tf_op jit(solution)/shard_map/ppermute | solution.py:345
  94.0 2.5 %collective-permute-start.18 = (bf16[80,1024]{1,0:T(8,128)(2,1)S(1)}, bf16[80,1024]{1,0:T(8,128)(2,1)S(1)}, u32[]{:S(2)}, u32[]{:S(2)}) collective-permute-start(bf16[80,1024]{1,0:T(8,128)(2,1)S(1)} %get-tuple-element.97), channel_id=1, source_target_pairs={{0,1},{1,0},{2,3},{3,2},{4,5},{5,4},{6,7},{7,6},{8,9},{9,8},{10,11... | collective-permute-start | bytes 491528 | tf_op jit(solution)/shard_map/ppermute | solution.py:345
  94.4 5.8 %collective-permute-start.20 = (bf16[64,1024]{1,0:T(8,128)(2,1)S(1)}, bf16[64,1024]{1,0:T(8,128)(2,1)S(1)}, u32[]{:S(2)}, u32[]{:S(2)}) collective-permute-start(bf16[64,1024]{1,0:T(8,128)(2,1)S(1)} %get-tuple-element.142), channel_id=1, source_target_pairs={{0,2},{1,3},{2,6},{3,7},{6,10},{7,11},{10,14},{11,15},{14,12},{15,... | collective-permute-start | bytes 393224 | tf_op jit(solution)/shard_map/ppermute | solution.py:342
  96.3 5.2 %collective-permute-start.22 = (bf16[64,1024]{1,0:T(8,128)(2,1)S(1)}, bf16[64,1024]{1,0:T(8,128)(2,1)S(1)}, u32[]{:S(2)}, u32[]{:S(2)}) collective-permute-start(bf16[64,1024]{1,0:T(8,128)(2,1)S(1)} %get-tuple-element.141), channel_id=1, source_target_pairs={{0,4},{1,5},{2,0},{3,1},{6,2},{7,3},{10,6},{11,7},{14,10},{15,11},... | collective-permute-start | bytes 393224 | tf_op jit(solution)/shard_map/ppermute | solution.py:342
  101.6 9.9 %collective-permute-start.25 = (bf16[128,1024]{1,0:T(8,128)(2,1)S(1)}, bf16[128,1024]{1,0:T(8,128)(2,1)S(1)}, u32[]{:S(2)}, u32[]{:S(2)}) collective-permute-start(bf16[128,1024]{1,0:T(8,128)(2,1)S(1)} %pad_maximum_fusion.6), channel_id=1, source_target_pairs={{0,2},{1,3},{2,6},{3,7},{6,10},{7,11},{10,14},{11,15},{14,12},{15,... | collective-permute-start | bytes 786440 | tf_op jit(solution)/shard_map/ppermute | solution.py:342
  103.2 8.3 %collective-permute-start.26 = (bf16[128,1024]{1,0:T(8,128)(2,1)S(1)}, bf16[128,1024]{1,0:T(8,128)(2,1)S(1)}, u32[]{:S(2)}, u32[]{:S(2)}) collective-permute-start(bf16[128,1024]{1,0:T(8,128)(2,1)S(1)} %pad_maximum_fusion.7), channel_id=1, source_target_pairs={{0,4},{1,5},{2,0},{3,1},{6,2},{7,3},{10,6},{11,7},{14,10},{15,11},... | collective-permute-start | bytes 786440 | tf_op jit(solution)/shard_map/ppermute | solution.py:342
  105.5 6.0 %collective-permute-start.27 = (bf16[96,1024]{1,0:T(8,128)(2,1)S(1)}, bf16[96,1024]{1,0:T(8,128)(2,1)S(1)}, u32[]{:S(2)}, u32[]{:S(2)}) collective-permute-start(bf16[96,1024]{1,0:T(8,128)(2,1)S(1)} %get-tuple-element.113), channel_id=1, source_target_pairs={{0,1},{1,0},{2,3},{3,2},{4,5},{5,4},{6,7},{7,6},{8,9},{9,8},{10,11... | collective-permute-start | bytes 589832 | tf_op jit(solution)/shard_map/ppermute | solution.py:345
  105.6 5.9 %collective-permute-start.24 = (bf16[80,1024]{1,0:T(8,128)(2,1)S(1)}, bf16[80,1024]{1,0:T(8,128)(2,1)S(1)}, u32[]{:S(2)}, u32[]{:S(2)}) collective-permute-start(bf16[80,1024]{1,0:T(8,128)(2,1)S(1)} %get-tuple-element.105), channel_id=1, source_target_pairs={{0,1},{1,0},{2,3},{3,2},{4,5},{5,4},{6,7},{7,6},{8,9},{9,8},{10,11... | collective-permute-start | bytes 491528 | tf_op jit(solution)/shard_map/ppermute | solution.py:345
  106.1 5.4 %collective-permute-start.23 = (bf16[80,1024]{1,0:T(8,128)(2,1)S(1)}, bf16[80,1024]{1,0:T(8,128)(2,1)S(1)}, u32[]{:S(2)}, u32[]{:S(2)}) collective-permute-start(bf16[80,1024]{1,0:T(8,128)(2,1)S(1)} %get-tuple-element.104), channel_id=1, source_target_pairs={{0,1},{1,0},{2,3},{3,2},{4,5},{5,4},{6,7},{7,6},{8,9},{9,8},{10,11... | collective-permute-start | bytes 491528 | tf_op jit(solution)/shard_map/ppermute | solution.py:345
  111.8 10.6 %collective-permute-start.30 = (bf16[128,1024]{1,0:T(8,128)(2,1)S(1)}, bf16[128,1024]{1,0:T(8,128)(2,1)S(1)}, u32[]{:S(2)}, u32[]{:S(2)}) collective-permute-start(bf16[128,1024]{1,0:T(8,128)(2,1)S(1)} %get-tuple-element.119), channel_id=1, source_target_pairs={{0,2},{1,3},{2,6},{3,7},{6,10},{7,11},{10,14},{11,15},{14,12},{15,... | collective-permute-start | bytes 786440 | tf_op jit(solution)/shard_map/ppermute | solution.py:342
  113.5 8.9 %collective-permute-start.31 = (bf16[128,1024]{1,0:T(8,128)(2,1)S(1)}, bf16[128,1024]{1,0:T(8,128)(2,1)S(1)}, u32[]{:S(2)}, u32[]{:S(2)}) collective-permute-start(bf16[128,1024]{1,0:T(8,128)(2,1)S(1)} %get-tuple-element.120), channel_id=1, source_target_pairs={{0,4},{1,5},{2,0},{3,1},{6,2},{7,3},{10,6},{11,7},{14,10},{15,11},... | collective-permute-start | bytes 786440 | tf_op jit(solution)/shard_map/ppermute | solution.py:342
  115.8 6.7 %collective-permute-start.32 = (bf16[96,1024]{1,0:T(8,128)(2,1)S(1)}, bf16[96,1024]{1,0:T(8,128)(2,1)S(1)}, u32[]{:S(2)}, u32[]{:S(2)}) collective-permute-start(bf16[96,1024]{1,0:T(8,128)(2,1)S(1)} %get-tuple-element.126), channel_id=1, source_target_pairs={{0,1},{1,0},{2,3},{3,2},{4,5},{5,4},{6,7},{7,6},{8,9},{9,8},{10,11... | collective-permute-start | bytes 589832 | tf_op jit(solution)/shard_map/ppermute | solution.py:345
  115.8 6.6 %collective-permute-start.29 = (bf16[80,1024]{1,0:T(8,128)(2,1)S(1)}, bf16[80,1024]{1,0:T(8,128)(2,1)S(1)}, u32[]{:S(2)}, u32[]{:S(2)}) collective-permute-start(bf16[80,1024]{1,0:T(8,128)(2,1)S(1)} %get-tuple-element.118), channel_id=1, source_target_pairs={{0,1},{1,0},{2,3},{3,2},{4,5},{5,4},{6,7},{7,6},{8,9},{9,8},{10,11... | collective-permute-start | bytes 491528 | tf_op jit(solution)/shard_map/ppermute | solution.py:345
  116.3 6.1 %collective-permute-start.28 = (bf16[80,1024]{1,0:T(8,128)(2,1)S(1)}, bf16[80,1024]{1,0:T(8,128)(2,1)S(1)}, u32[]{:S(2)}, u32[]{:S(2)}) collective-permute-start(bf16[80,1024]{1,0:T(8,128)(2,1)S(1)} %get-tuple-element.117), channel_id=1, source_target_pairs={{0,1},{1,0},{2,3},{3,2},{4,5},{5,4},{6,7},{7,6},{8,9},{9,8},{10,11... | collective-permute-start | bytes 491528 | tf_op jit(solution)/shard_map/ppermute | solution.py:345
  117.1 19.0 %copy-start.15 = (bf16[128,1024]{1,0:T(8,128)(2,1)S(1)}, bf16[128,1024]{1,0:T(8,128)(2,1)}, u32[]{:S(2)}) copy-start(bf16[128,1024]{1,0:T(8,128)(2,1)} %copy-done.12) | copy-start | bytes 786436
  117.1 19.0 %copy-start.19 = (bf16[128,1024]{1,0:T(8,128)(2,1)S(1)}, bf16[128,1024]{1,0:T(8,128)(2,1)}, u32[]{:S(2)}) copy-start(bf16[128,1024]{1,0:T(8,128)(2,1)} %copy-done.16) | copy-start | bytes 786436
  117.1 19.0 %copy-start.23 = (bf16[128,1024]{1,0:T(8,128)(2,1)S(1)}, bf16[128,1024]{1,0:T(8,128)(2,1)}, u32[]{:S(2)}) copy-start(bf16[128,1024]{1,0:T(8,128)(2,1)} %copy-done.20) | copy-start | bytes 786436
  117.1 19.0 %copy-start.27 = (bf16[128,1024]{1,0:T(8,128)(2,1)S(1)}, bf16[128,1024]{1,0:T(8,128)(2,1)}, u32[]{:S(2)}) copy-start(bf16[128,1024]{1,0:T(8,128)(2,1)} %copy-done.24) | copy-start | bytes 786436
  117.1 19.0 %copy-start.31 = (bf16[128,1024]{1,0:T(8,128)(2,1)S(1)}, bf16[128,1024]{1,0:T(8,128)(2,1)}, u32[]{:S(2)}) copy-start(bf16[128,1024]{1,0:T(8,128)(2,1)} %copy-done.28) | copy-start | bytes 786436
  117.1 19.0 %copy-start.35 = (bf16[128,1024]{1,0:T(8,128)(2,1)S(1)}, bf16[128,1024]{1,0:T(8,128)(2,1)}, u32[]{:S(2)}) copy-start(bf16[128,1024]{1,0:T(8,128)(2,1)} %copy-done.32) | copy-start | bytes 786436
  117.1 19.0 %copy-start.39 = (bf16[128,1024]{1,0:T(8,128)(2,1)S(1)}, bf16[128,1024]{1,0:T(8,128)(2,1)}, u32[]{:S(2)}) copy-start(bf16[128,1024]{1,0:T(8,128)(2,1)} %copy-done.36) | copy-start | bytes 786436
  117.2 19.0 %copy-start.43 = (bf16[128,1024]{1,0:T(8,128)(2,1)S(1)}, bf16[128,1024]{1,0:T(8,128)(2,1)}, u32[]{:S(2)}) copy-start(bf16[128,1024]{1,0:T(8,128)(2,1)} %copy-done.40) | copy-start | bytes 786436
  117.2 19.0 %copy-start.47 = (bf16[1024,128]{1,0:T(8,128)(2,1)S(1)}, bf16[1024,128]{1,0:T(8,128)(2,1)}, u32[]{:S(2)}) copy-start(bf16[1024,128]{1,0:T(8,128)(2,1)} %copy-done.45) | copy-start | bytes 786436
  122.7 21.2 %collective-permute-start.35 = (bf16[128,1024]{1,0:T(8,128)(2,1)S(1)}, bf16[128,1024]{1,0:T(8,128)(2,1)S(1)}, u32[]{:S(2)}, u32[]{:S(2)}) collective-permute-start(bf16[128,1024]{1,0:T(8,128)(2,1)S(1)} %get-tuple-element.136), channel_id=1, source_target_pairs={{0,2},{1,3},{2,6},{3,7},{6,10},{7,11},{10,14},{11,15},{14,12},{15,... | collective-permute-start | bytes 786440 | tf_op jit(solution)/shard_map/ppermute | solution.py:342
  124.4 19.5 %collective-permute-start.36 = (bf16[128,1024]{1,0:T(8,128)(2,1)S(1)}, bf16[128,1024]{1,0:T(8,128)(2,1)S(1)}, u32[]{:S(2)}, u32[]{:S(2)}) collective-permute-start(bf16[128,1024]{1,0:T(8,128)(2,1)S(1)} %get-tuple-element.137), channel_id=1, source_target_pairs={{0,4},{1,5},{2,0},{3,1},{6,2},{7,3},{10,6},{11,7},{14,10},{15,11},... | collective-permute-start | bytes 786440 | tf_op jit(solution)/shard_map/ppermute | solution.py:342
  124.8 20.1 %copy-start.1 = (f32[16,1024]{1,0:T(8,128)S(1)}, f32[16,1024]{1,0:T(8,128)}, u32[]{:S(2)}) copy-start(f32[16,1024]{1,0:T(8,128)} %param.10) | copy-start | bytes 196612
  134.8 9.1 %collective-permute-start.34 = (bf16[64,1024]{1,0:T(8,128)(2,1)S(1)}, bf16[64,1024]{1,0:T(8,128)(2,1)S(1)}, u32[]{:S(2)}, u32[]{:S(2)}) collective-permute-start(bf16[64,1024]{1,0:T(8,128)(2,1)S(1)} %get-tuple-element.135), channel_id=1, source_target_pairs={{0,1},{1,0},{2,3},{3,2},{4,5},{5,4},{6,7},{7,6},{8,9},{9,8},{10,11... | collective-permute-start | bytes 393224 | tf_op jit(solution)/shard_map/ppermute | solution.py:345
  134.9 9.0 %collective-permute-start.33 = (bf16[64,1024]{1,0:T(8,128)(2,1)S(1)}, bf16[64,1024]{1,0:T(8,128)(2,1)S(1)}, u32[]{:S(2)}, u32[]{:S(2)}) collective-permute-start(bf16[64,1024]{1,0:T(8,128)(2,1)S(1)} %get-tuple-element.134), channel_id=1, source_target_pairs={{0,1},{1,0},{2,3},{3,2},{4,5},{5,4},{6,7},{7,6},{8,9},{9,8},{10,11... | collective-permute-start | bytes 393224 | tf_op jit(solution)/shard_map/ppermute | solution.py:345
  (32 other events, 243.5 us)

commit v4 on v2

--- a/solution.py
+++ b/solution.py
@@ -9,8 +9,9 @@
 from jax.sharding import PartitionSpec as P
 
 SCALE = 2.0 / 1024.0
-VMEM_LIMIT = 16 * 2**20
-PARTS = 2
+VMEM_LIMIT = 4 * 2**20
+BANDS = 8
+FIRST_BANDS = 5
 LONGEST_RING = 16
 
 
@@ -50,7 +51,7 @@
     )
 
 
-def call(kernel, out_shape, out_specs, scratch, costs, aliases=None):
+def call(kernel, out_shape, out_specs, scratch, costs, aliases=None, more=0):
     def run(operands, in_specs):
         return pl.pallas_call(
             kernel,
@@ -59,7 +60,7 @@
             out_specs=out_specs,
             scratch_shapes=scratch,
             input_output_aliases=aliases or {},
-            compiler_params=pltpu.CompilerParams(vmem_limit_bytes=VMEM_LIMIT),
+            compiler_params=pltpu.CompilerParams(vmem_limit_bytes=VMEM_LIMIT + more),
             cost_estimate=costs,
         )(*operands)
 
@@ -70,72 +71,141 @@
     return pl.ds(pl.multiple_of(offs_ref[at] * slab, slab), slab)
 
 
-def pre_kernel(base, count, loads, first, *refs):
-    offs_ref, w_ref = refs[:2]
-    xs = refs[2 : 2 + count]
-    rest = refs[2 + count :]
-    acc_ref, rest = (None, rest) if first else (rest[0], rest[1:])
-    out_ref, blocks, sems = rest[0], rest[1 : 1 + loads], rest[-1]
-    rows, slab = blocks[0].shape
-    tile = rows // PARTS
+def load_bands(w_ref, bands, sems, first):
     copies = []
-    for at in range(loads):
-        here = columns_of(offs_ref, base + at, slab)
-        for part in range(PARTS):
-            band = pl.ds(part * tile, tile)
-            copy = pltpu.make_async_copy(
-                w_ref.at[band, here], blocks[at].at[band, :], sems.at[at, part]
-            )
-            copy.start()
-            copies.append(copy)
-    for at in range(count):
-        for part in range(PARTS):
-            copies[at * PARTS + part].wait()
-            band = pl.ds(part * tile, tile)
-            total = lax.dot_general(
-                blocks[at][band, :], xs[at][...], (((1,), (1,)), ((), ())),
-                preferred_element_type=jnp.float32,
-            )
-            if at > 0:
-                total += out_ref[band, :]
-            elif not first:
-                total += acc_ref[band, :]
-            out_ref[band, :] = total
-    for copy in copies[count * PARTS :]:
+    for at, band_ref in enumerate(bands):
+        tile = band_ref.shape[0]
+        rows = pl.ds((first + at) * tile, tile)
+        copies.append(pltpu.make_async_copy(w_ref.at[rows, :], band_ref, sems.at[at]))
+        copies[-1].start()
+    return copies
+
+
+def product(bands, here, x_ref):
+    rows = [band_ref[:, here] for band_ref in bands]
+    return lax.dot_general(
+        rows[0] if len(rows) == 1 else jnp.concatenate(rows, axis=0),
+        x_ref[...], (((1,), (1,)), ((), ())), preferred_element_type=jnp.float32,
+    )
+
+
+def first_kernel(base, offs_ref, w_ref, x_ref, out_ref, *refs):
+    bands, sems = refs[:-1], refs[-1]
+    here = columns_of(offs_ref, base, x_ref.shape[1])
+    tile = bands[0].shape[0]
+    for at, copy in enumerate(load_bands(w_ref, bands, sems, 0)):
         copy.wait()
-
-
-def add_products(offs, base, xs, weights, acc, slab, loads):
-    nodes, rows, count = xs[0].shape[0], weights.shape[0], len(xs)
-    first = acc is None
-    out = call(
-        functools.partial(pre_kernel, base, count, loads, first),
-        [jax.ShapeDtypeStruct((rows, nodes), jnp.float32)]
-        + [pltpu.VMEM((rows, slab), jnp.bfloat16)] * loads,
-        [VMEM_REF] * (1 + loads),
-        [pltpu.SemaphoreType.DMA((loads, PARTS))],
+        out_ref[pl.ds(at * tile, tile), :] = product(bands[at : at + 1], here, x_ref)
+
+
+def second_kernel(base, count, early, *refs):
+    offs_ref, w_ref, acc_ref = refs[:3]
+    bands, refs = refs[3 : 3 + early], refs[3 + early :]
+    xs, out_ref, late, sems = refs[:count], refs[count], refs[count + 1 : -1], refs[-1]
+    slab, tile = xs[0].shape[1], bands[0].shape[0]
+    copies = load_bands(w_ref, late, sems, early)
+    places = [columns_of(offs_ref, base + at, slab) for at in range(count)]
+    for low in range(0, early, 2):
+        pair = bands[low : low + 2]
+        rows = pl.ds(low * tile, len(pair) * tile)
+        total = acc_ref[rows, :]
+        for at in range(1, count):
+            total += product(pair, places[at], xs[at])
+        out_ref[rows, :] = total
+    for at, copy in enumerate(copies):
+        copy.wait()
+        rows = pl.ds((early + at) * tile, tile)
+        total = product(late[at : at + 1], places[0], xs[0])
+        for index in range(1, count):
+            total += product(late[at : at + 1], places[index], xs[index])
+        out_ref[rows, :] = total
+
+
+def pre_kernel(base, count, many, offs_ref, acc_ref, *refs):
+    bands, xs, out_ref = refs[:many], refs[many:-1], refs[-1]
+    slab, tile = xs[0].shape[1], bands[0].shape[0]
+    for low in range(0, many, 2):
+        rows = pl.ds(low * tile, 2 * tile)
+        total = acc_ref[rows, :]
+        for at in range(count):
+            total += product(bands[low : low + 2], columns_of(offs_ref, base + at, slab), xs[at])
+        out_ref[rows, :] = total
+
+
+def band_shapes(count, weights):
+    return [pltpu.VMEM((weights.shape[0] // BANDS, weights.shape[1]), weights.dtype)] * count
+
+
+def first_products(offs, base, x, weights):
+    (nodes, slab), rows = x.shape, weights.shape[0]
+    acc, *bands = call(
+        functools.partial(first_kernel, base),
+        [jax.ShapeDtypeStruct((rows, nodes), jnp.float32)] + band_shapes(FIRST_BANDS, weights),
+        [VMEM_REF] * (1 + FIRST_BANDS),
+        [pltpu.SemaphoreType.DMA((FIRST_BANDS,))],
+        cost(1, nodes, slab, rows),
+    )([offs, weights, x], [SMEM_REF, HBM_REF, VMEM_REF])
+    return acc, bands
+
+
+def second_products(offs, base, xs, weights, acc, bands):
+    (nodes, slab), rows = xs[0].shape, weights.shape[0]
+    late = BANDS - len(bands)
+    acc, *others = call(
+        functools.partial(second_kernel, base, len(xs), len(bands)),
+        [jax.ShapeDtypeStruct((rows, nodes), jnp.float32)] + band_shapes(late, weights),
+        [VMEM_REF] * (1 + late),
+        [pltpu.SemaphoreType.DMA((late,))],
+        cost(len(xs), nodes, slab, rows),
+    )(
+        [offs, weights, acc, *bands, *xs],
+        [SMEM_REF, HBM_REF] + [VMEM_REF] * (1 + len(bands) + len(xs)),
+    )
+    return acc, bands + others
+
+
+def add_products(offs, base, xs, acc, bands):
+    nodes, slab = xs[0].shape
+    rows, count = acc.shape[0], len(xs)
+    return call(
+        functools.partial(pre_kernel, base, count, len(bands)),
+        jax.ShapeDtypeStruct((rows, nodes), jnp.float32),
+        VMEM_REF,
+        [],
         cost(count, nodes, slab, rows),
-    )(
-        [offs, weights, *xs] + ([] if first else [acc]),
-        [SMEM_REF, HBM_REF] + [VMEM_REF] * (count + (0 if first else 1)),
-    )
-    return out[0], out[1:]
-
-
-def middle_kernel(
-    x_ref, w_ref, acc_ref, deriv_ref, states_ref, drive_ref, eps_ref, decay_ref,
-    resid_ref, delta_ref, delta_t_ref, sums_ref,
-):
-    rows = w_ref.shape[0]
-    tile = max(rows // 4, 128)
-    for start in range(0, rows, tile):
-        band = pl.ds(start, tile)
-        part = acc_ref[band, :] + lax.dot_general(
-            w_ref[band, :], x_ref[...], (((1,), (1,)), ((), ())),
-            preferred_element_type=jnp.float32,
-        )
+    )([offs, acc, *bands, *xs], [SMEM_REF] + [VMEM_REF] * (1 + len(bands) + count))
+
+
+def cheb_kernel(turned, cheb_ref, array_ref, out_ref):
+    out_ref[...] = SCALE * lax.dot_general(
+        cheb_ref[...], array_ref[...], (((0 if turned else 1,), (0,)), ((), ())),
+        precision=lax.Precision.HIGHEST, preferred_element_type=jnp.float32,
+    )
+
+
+def cheb_product(turned, cheb, array):
+    return call(
+        functools.partial(cheb_kernel, turned),
+        jax.ShapeDtypeStruct(array.shape, jnp.float32),
+        VMEM_REF,
+        [],
+        cost(1, *array.shape, array.shape[0]),
+    )([cheb, array], [VMEM_REF] * 2)
+
+
+def middle_kernel(base, many, offs_ref, perts_ref, x_ref, *refs):
+    bands = refs[:many]
+    acc_ref, deriv_ref, states_ref, pert_ref, eps_ref, decay_ref = refs[many:-6]
+    resid_ref, delta_ref, delta_t_ref, table_ref, sum_eps_ref, sum_decay_ref = refs[-6:]
+    tile = 2 * bands[0].shape[0]
+    here = columns_of(offs_ref, base, x_ref.shape[1])
+    pert = perts_ref[0]
+    chosen = lax.broadcasted_iota(jnp.int32, (pert_ref.shape[0], tile), 0) == pert
+    for at in range(many // 2):
+        band = pl.ds(at * tile, tile)
+        part = acc_ref[band, :] + product(bands[2 * at : 2 * at + 2], here, x_ref)
         states = states_ref[:, band]
-        act = jnp.tanh(part.T + drive_ref[:, band])
+        act = jnp.tanh(part.T + pert_ref[pl.ds(pert, 1), band])
         eps = eps_ref[:, band]
         resid = deriv_ref[:, band] - (eps * act - decay_ref[:, band] * states)
         delta = (-eps * (1.0 - act * act) * resid).astype(jnp.bfloat16)
@@ -143,40 +213,52 @@
         resid_ref[:, band] = resid
         delta_ref[:, band] = delta
         delta_t_ref[band, :] = wide.T.astype(jnp.bfloat16)
-        sums_ref[0:1, band] = jnp.sum(wide, axis=0, keepdims=True)
-        sums_ref[1:2, band] = -jnp.sum(act * resid, axis=0, keepdims=True)
-        sums_ref[2:3, band] = jnp.sum(states * resid, axis=0, keepdims=True)
-
-
-def middle(x, block, acc, deriv, states, drive, eps, decay):
+        table_ref[:, band] = jnp.where(chosen, jnp.sum(wide, axis=0, keepdims=True), 0.0)
+        sum_eps_ref[:, band] = -jnp.sum(act * resid, axis=0, keepdims=True)
+        sum_decay_ref[:, band] = jnp.sum(states * resid, axis=0, keepdims=True)
+
+
+def middle(offs, perts, base, x, bands, acc, deriv, states, pert_table, eps, decay):
     nodes, slab = x.shape
-    rows = block.shape[0]
+    rows = acc.shape[0]
+    wide = functools.partial(jax.ShapeDtypeStruct, dtype=jnp.float32)
     return call(
-        middle_kernel,
+        functools.partial(middle_kernel, base, len(bands)),
         [
-            jax.ShapeDtypeStruct((nodes, rows), jnp.float32),
+            wide((nodes, rows)),
             jax.ShapeDtypeStruct((nodes, rows), jnp.bfloat16),
             jax.ShapeDtypeStruct((rows, nodes), jnp.bfloat16),
-            jax.ShapeDtypeStruct((8, rows), jnp.float32),
+            wide(pert_table.shape),
+            wide((1, rows)),
+            wide((1, rows)),
         ],
-        [VMEM_REF] * 4,
+        [VMEM_REF] * 6,
         [],
         cost(2, nodes, slab, rows),
-    )([x, block, acc, deriv, states, drive, eps, decay], [VMEM_REF] * 8)
-
-
-def share_kernel(cuts, offs_ref, delta_ref, *refs):
+    )(
+        [offs, perts, x, *bands, acc, deriv, states, pert_table, eps, decay],
+        [SMEM_REF] * 2 + [VMEM_REF] * (7 + len(bands)),
+    )
+
+
+def share_kernel(at_places, cuts, many, offs_ref, delta_ref, *refs):
+    bands, outs = refs[:many], refs[many:]
     nodes = delta_ref.shape[0]
     count = cuts[-1] // nodes
-    blocks, outs = refs[: 2 * count], refs[2 * count :]
-    slab = blocks[0].shape[1]
+    slab, depth = outs[0].shape[1], 2 * bands[0].shape[0]
     tile = max(slab // 2, 128)
-    for at, block_ref in enumerate(blocks):
+    for at, place in enumerate(at_places):
         for col in range(0, slab, tile):
             here = pl.ds(col, tile)
-            part = jnp.dot(
-                delta_ref[...], block_ref[:, here], preferred_element_type=jnp.float32
-            )
+            there = pl.ds(pl.multiple_of(offs_ref[place] * slab + col, tile), tile)
+            part = None
+            for low in range(0, many, 2):
+                pair = jnp.concatenate([ref[:, there] for ref in bands[low : low + 2]], axis=0)
+                more = jnp.dot(
+                    delta_ref[:, low // 2 * depth : (low // 2 + 1) * depth], pair,
+                    preferred_element_type=jnp.float32,
+                )
+                part = more if part is None else part + more
             if at >= count:
                 outs[len(cuts) - 1 + at - count][:, here] = part
                 continue
@@ -187,40 +269,41 @@
                     out_ref[low - start : high - start, here] = rows.astype(out_ref.dtype)
 
 
-def shares(offs, delta, blocks, cuts):
+def shares(offs, at_places, delta, bands, slab, cuts):
     nodes, rows = delta.shape
-    slab = blocks[0].shape[1]
-    own = len(blocks) // 2
+    own = len(at_places) // 2
     heights = [end - start for start, end in zip(cuts[:-1], cuts[1:])]
     outs = call(
-        functools.partial(share_kernel, cuts),
+        functools.partial(share_kernel, at_places, cuts, len(bands)),
         [jax.ShapeDtypeStruct((height, slab), jnp.bfloat16) for height in heights]
         + [jax.ShapeDtypeStruct((nodes, slab), jnp.float32)] * own,
         [VMEM_REF] * (len(heights) + own),
         [],
-        cost(len(blocks), nodes, slab, rows),
-    )([offs, delta, *blocks], [SMEM_REF] + [VMEM_REF] * (1 + len(blocks)))
+        cost(len(at_places), nodes, slab, rows),
+    )([offs, delta, *bands], [SMEM_REF] + [VMEM_REF] * (1 + len(bands)))
     return outs[: len(heights)], outs[len(heights) :]
 
 
 def grad_w_kernel(base, count, *refs):
     offs_ref, delta_ref, xs = refs[0], refs[1], refs[2 : 2 + count]
     out_ref, mark_ref, held, sems = refs[-4:]
-    rows, slab = delta_ref.shape[0], xs[0].shape[1]
-    slots, tile = held.shape[:2]
+    slab = xs[0].shape[1]
+    slots, _, width = held.shape
+    step = min(256, width)
     mark_ref[...] = jnp.zeros_like(mark_ref)
     copies = []
     for at in range(count):
-        here = columns_of(offs_ref, base + at, slab)
-        for start in range(0, rows, tile):
-            band = pl.ds(start, tile)
+        for start in range(0, slab, width):
             slot = len(copies) % slots
             if len(copies) >= slots:
                 copies[-slots].wait()
-            held[slot] = jnp.dot(
-                delta_ref[band, :], xs[at][...], preferred_element_type=jnp.float32
-            ).astype(held.dtype)
-            copy = pltpu.make_async_copy(held.at[slot], out_ref.at[band, here], sems.at[slot])
+            for col in range(0, width, step):
+                held[slot, :, col : col + step] = jnp.dot(
+                    delta_ref[...], xs[at][:, start + col : start + col + step],
+                    preferred_element_type=jnp.float32,
+                ).astype(held.dtype)
+            there = pl.ds(pl.multiple_of(offs_ref[base + at] * slab + start, width), width)
+            copy = pltpu.make_async_copy(held.at[slot], out_ref.at[:, there], sems.at[slot])
             copy.start()
             copies.append(copy)
     for copy in copies[-slots:]:
@@ -230,15 +313,16 @@
 def grad_w_piece(offs, base, delta_t, xs, so_far, mark, shape):
     rows, nodes = delta_t.shape
     slab, count = xs[0].shape[1], len(xs)
-    tile = max(rows // 4, 128)
+    width = max(slab // 2, 128)
     first = so_far is None
     return call(
         functools.partial(grad_w_kernel, base, count),
         [jax.ShapeDtypeStruct(shape, jnp.bfloat16), jax.ShapeDtypeStruct((8, 128), jnp.float32)],
         [ANY_REF, VMEM_REF],
-        [pltpu.VMEM((6, tile, slab), jnp.bfloat16), pltpu.SemaphoreType.DMA((6,))],
+        [pltpu.VMEM((4, rows, width), jnp.bfloat16), pltpu.SemaphoreType.DMA((4,))],
         cost(count, nodes, slab, rows),
         {} if first else {2 + count: 0},
+        4 * 2 * rows * width,
     )(
         [offs, delta_t, *xs] + ([] if first else [so_far, mark]),
         [SMEM_REF] + [VMEM_REF] * (1 + count) + ([] if first else [ANY_REF] * 2),
@@ -262,6 +346,7 @@
         then = [half] if step == half - 1 else [-step - 1, step + 1]
         listing += [(at, 1) for at in now] + [(at, 0) for at in then]
     listing.append((half, 1))
+    sides = {key: at for at, key in enumerate(listing)}
     table = np.array(
         [
             [
@@ -291,17 +376,7 @@
     xb = flat.astype(jnp.bfloat16)
 
     x = {(0, 0): xb}
-    acc, base, block = None, 0, {}
-
-    def next_products(acc, base, count, loads):
-        keys = listing[base : base + loads]
-        acc, loaded = add_products(
-            offs, base, [x[key] for key in keys[:count]], weights, acc, slab, loads
-        )
-        block.update(zip(keys, loaded))
-        return acc, base + count
-
-    behind, ahead = xb, xb
+    behind, ahead, base = xb, xb, 0
     for step in range(1, half + 1):
         if step < half:
             behind, ahead = ring(behind, 1), ring(ahead, -1)
@@ -310,24 +385,27 @@
         for now in [0] if step == 1 else [1 - step, step - 1]:
             x[now, 1] = swap(x[now, 0])
         count = {1: 1, 2: 3}.get(step, 4)
-        acc, base = next_products(acc, base, count, count)
+        xs = [x[key] for key in listing[base : base + count]]
+        if step == 1:
+            acc, bands = first_products(offs, 0, xs[0], weights)
+        elif step == 2:
+            acc, bands = second_products(offs, 0, [x[0, 0], *xs], weights, acc, bands)
+        else:
+            acc = add_products(offs, base, xs, acc, bands)
+        base += count
         behind, ahead, acc = lax.optimization_barrier((behind, ahead, acc))
         if step < half:
             x[-step, 0], x[step, 0] = behind, ahead
         else:
             x[half, 0] = jnp.concatenate([behind, ahead], axis=0)
     x[half, 1] = swap(x[half, 0])
-    acc, base = next_products(acc, base, 3, 4)
-
-    onehot = (perts[:, None] == jnp.arange(pert_table.shape[0], dtype=jnp.int32)[None, :]).astype(
-        jnp.float32
-    )
-    drive = jnp.dot(onehot, pert_table, precision=lax.Precision.HIGHEST)
-    deriv = SCALE * jnp.dot(cheb, flat, precision=lax.Precision.HIGHEST)
-
-    resid, delta, delta_t, sums = middle(
-        x[half, 1], block[half, 1], acc, deriv, flat, drive,
-        eps_gain.reshape(1, rows), decay.reshape(1, rows),
+    xs = [x[key] for key in listing[base : base + 3]]
+    acc = add_products(offs, base, xs, acc, bands)
+    base += 3
+
+    resid, delta, delta_t, grad_table, grad_eps, grad_decay = middle(
+        offs, perts, base, x[half, 1], bands, acc, cheb_product(False, cheb, flat), flat,
+        pert_table, eps_gain.reshape(1, rows), decay.reshape(1, rows),
     )
 
     def share(steps):
@@ -335,8 +413,8 @@
         parts = 2 if count == 1 else 3
         cuts = [0] + [count * nodes * at // parts // 16 * 16 for at in range(1, parts)]
         cuts.append(count * nodes)
-        blocks = [block[step, side] for side in (1, 0) for step in steps]
-        others, owns = shares(offs, delta, blocks, cuts)
+        places = [sides[step, side] for side in (1, 0) for step in steps]
+        others, owns = shares(offs, places, delta, bands, slab, cuts)
         swapped = jnp.concatenate([swap(other) for other in others], axis=0)
         return [
             own + swapped[at * nodes : (at + 1) * nodes].astype(jnp.float32)
@@ -381,18 +459,10 @@
         ahead, behind, offs = gate((ahead, behind, offs))
         ahead, behind = ring(ahead, 1), ring(behind, -1)
 
-    local = (
-        SCALE
-        * lax.dot_general(
-            cheb, resid, (((0,), (0,)), ((), ())), precision=lax.Precision.HIGHEST
-        )
-        + decay * resid
-    )
-    local = gate(local)
+    local = gate(cheb_product(True, cheb, resid) + decay * resid)
     grad_x = local + near_share + ahead.astype(jnp.float32) + behind.astype(jnp.float32)
     grad_x = grad_x.reshape(states.shape)
-    grad_table = onehot.T * sums[0:1]
-    return (grad_w, grad_x, grad_table, sums[1], sums[2])
+    return (grad_w, grad_x, grad_table, grad_eps.reshape(rows), grad_decay.reshape(rows))
 
 
 def plain_body(states, weights, pert_table, eps_gain, decay, perts):

time: 97.3 us -> 91.2 us (0.937)
  Pallas kernels: 58.4 us -> 53.6 us
  waiting for transfers between devices: 7.49 us -> 9.08 us
  matrix products: 1.37 us -> 0 us
    pallas_call x15 -> x17, Pallas kernels: 58.4 us -> 53.6 us  [run(): pl.pallas_call(kernel, out_shape=out_shape, in_specs=in_specs, out_specs=...]
    ppermute x16, waiting for transfers between devices: 7.43 us -> 9.02 us  [ring(): return lax.ppermute(array, 'row', pairs)]
    dot_general x3 -> x0, matrix products: 1.37 us -> none  [the longest x1 0.64 us: ring_body(): lax.dot_general(cheb, resid, (((0,), (0,)), ((), ())), precision=lax.Prec...]
  transfers between devices with their start and end apart: 37 -> 37, of which waited for: 6 -> 5; matrix products, arithmetic and copies ran while one was open for 4% -> 1% of each run, Pallas kernels for 56% -> 52%
where the time goes in v4:
time: 91.2 us; the launch traced here: 91 us
  Pallas kernels  53.6 us (59%)
  starting transfers between devices  22.7 us (25%)
  waiting for transfers between devices  9.08 us (10%)
  other arithmetic  2.97 us (3%)
  between operations  1.83 us (2%)
    pallas_call x17, Pallas kernels, run(): pl.pallas_call(kernel, out_shape=out_shape, in_specs=in_specs, out_specs=...  53.6 us
    ppermute x16, starting transfers between devices, ring(): return lax.ppermute(array, 'row', pairs)  17.6 us
    ppermute x16, waiting for transfers between devices, ring(): return lax.ppermute(array, 'row', pairs)  9.02 us
    ppermute x21, starting transfers between devices, swap(): return lax.ppermute(array, 'row', [(i, i ^ 1) for i in range(2 * chips)])  5.13 us
  transfers between devices with their start and end apart: 37, of which 5 were waited for; matrix products, arithmetic and copies ran while one was open for 1% of the time, Pallas kernels for 52%

profile of v4, /device:TPU:0, one launch (start us, length us, event | category | flops | bytes accessed | tf_op | source)
XLA Modules:
  0.0 91.0 jit_solution(16734406494777053486)
XLA Ops:
  0.6 1.1 %bitcast_convert_fusion.x_ref.refs_8_.refs_2_ = bf16[128,1024]{1,0:T(8,128)(2,1)S(1)} fusion(f32[1,128,1024]{2,1,0:T(8,128)} %param.8), kind=kLoop, calls=%fused_computation.26 | loop fusion | flops 131072 | bytes 786432 | tf_op jit(solution)/shard_map/convert_element_type | solution.py:376
  1.7 3.1 %collective-permute-start.1 = (bf16[128,1024]{1,0:T(8,128)(2,1)S(1)}, bf16[128,1024]{1,0:T(8,128)(2,1)S(1)}, u32[]{:S(2)}, u32[]{:S(2)}) collective-permute-start(bf16[128,1024]{1,0:T(8,128)(2,1)S(1)} %bitcast_convert_fusion.x_ref.refs_8_.refs_2_), channel_id=1, source_target_pairs={{0,4},{1,5},{2,0},{3,1},{6,2},{7,3},{10,6},{11,7},{14,10},{15,11},... | collective-permute-start | bytes 786440 | tf_op jit(solution)/shard_map/ppermute | solution.py:368
  4.8 0.7 dynamic-slice_bitcast_fusion.offs_ref.refs_0_
  5.5 7.9 %shard_map.119 = (f32[1024,128]{1,0:T(8,128)S(1)}, bf16[128,16384]{1,0:T(8,128)(2,1)S(1)}, bf16[128,16384]{1,0:T(8,128)(2,1)S(1)}, bf16[128,16384]{1,0:T(8,128)(...) custom-call(s32[16]{0:T(128)S(1)} %dynamic-slice_bitcast_fusion.offs_ref.refs_0_, ...), custom_call_target="tpu_custom_call" | custom-call | flops 16777216 | bytes 131072 | tf_op jit(solution)/shard_map/pallas_call | solution.py:56
  13.4 2.0 %collective-permute-start.2 = (bf16[128,1024]{1,0:T(8,128)(2,1)S(1)}, bf16[128,1024]{1,0:T(8,128)(2,1)S(1)}, u32[]{:S(2)}, u32[]{:S(2)}) collective-permute-start(bf16[128,1024]{1,0:T(8,128)(2,1)S(1)} %collective-permute-done.refs_10_.refs_2_), channel_id=1, source_target_pairs={{0,2},{1,3},{2,6},{3,7},{6,10},{7,11},{10,14},{11,15},{14,12},{15,... | collective-permute-start | bytes 786440 | tf_op jit(solution)/shard_map/ppermute | solution.py:368
  15.4 0.1 collective-permute-start.3
  15.6 0.2 collective-permute-start.7
  15.8 0.3 collective-permute-start.8
  16.1 7.0 %shard_map.120 = (f32[1024,128]{1,0:T(8,128)S(1)}, bf16[128,16384]{1,0:T(8,128)(2,1)S(1)}, bf16[128,16384]{1,0:T(8,128)(2,1)S(1)}, bf16[128,16384]{1,0:T(8,128)(2,1)S(1)}) custom-call(s32[16]{0:T(128)S(1)} %dynamic-slice_bitcast_fusion.offs_ref.refs_0_, bf16[1024,16384]{1,0:T(8,128)(2,1)} %refs_1_.1, f32[1024,128]{1,0:T(8,128)S(1)} %get-tuple-element.84.refs_2_, ...), custom_call_target="tpu_custom_call" | custom-call | flops 67108864 | bytes 524288 | tf_op jit(solution)/shard_map/pallas_call | solution.py:56
  23.1 0.7 collective-permute-done.3.refs_11_.refs_3_
  23.9 1.6 %collective-permute-start.5 = (bf16[128,1024]{1,0:T(8,128)(2,1)S(1)}, bf16[128,1024]{1,0:T(8,128)(2,1)S(1)}, u32[]{:S(2)}, u32[]{:S(2)}) collective-permute-start(bf16[128,1024]{1,0:T(8,128)(2,1)S(1)} %collective-permute-done.2.refs_10_.refs_2_), channel_id=1, source_target_pairs={{0,2},{1,3},{2,6},{3,7},{6,10},{7,11},{10,14},{11,15},{14,12},{15,... | collective-permute-start | bytes 786440 | tf_op jit(solution)/shard_map/ppermute | solution.py:368
  25.4 0.4 collective-permute-start.6
  25.9 0.5 collective-permute-start.12
  26.4 2.9 %shard_map.121.acc_ref = f32[1024,128]{1,0:T(8,128)S(1)} custom-call(s32[16]{0:T(128)S(1)} %dynamic-slice_bitcast_fusion.offs_ref.refs_0_, f32[1024,128]{1,0:T(8,128)S(1)} %get-tuple-element.93.acc_ref, bf16[128,16384]{1,0:T(8,128)(2,1)S(1)} %get-tuple-element.85.refs_3_.refs_0_, bf16[128,16384]{1,0:T(8,128)(2,1)S(1)} %get-tuple-element.86.refs_4_.refs_1_, ...), custom_call_target="tpu_custom_call" | custom-call | flops 67108864 | bytes 524288 | tf_op jit(solution)/shard_map/pallas_call | solution.py:56
  29.3 2.3 %collective-permute-done.5.refs_10_.refs_2_ = bf16[128,1024]{1,0:T(8,128)(2,1)S(1)} collective-permute-done((bf16[128,1024]{1,0:T(8,128)(2,1)S(1)}, bf16[128,1024]{1,0:T(8,128)(2,1)S(1)}, u32[]{:S(2)}, u32[]{:S(2)}) %collective-permute-start.5) | collective-permute-done | bytes 262176 | tf_op jit(solution)/shard_map/ppermute | solution.py:368
  31.6 1.4 %collective-permute-done.6.refs_11_.refs_3_ = bf16[128,1024]{1,0:T(8,128)(2,1)S(1)} collective-permute-done((bf16[128,1024]{1,0:T(8,128)(2,1)S(1)}, bf16[128,1024]{1,0:T(8,128)(2,1)S(1)}, u32[]{:S(2)}, u32[]{:S(2)}) %collective-permute-start.6) | collective-permute-done | bytes 262176 | tf_op jit(solution)/shard_map/ppermute | solution.py:368
  33.0 0.0 copy-start.1
  33.0 0.5 collective-permute-start.10
  33.5 1.6 %collective-permute-start.9 = (bf16[64,1024]{1,0:T(8,128)(2,1)S(1)}, bf16[64,1024]{1,0:T(8,128)(2,1)S(1)}, u32[]{:S(2)}, u32[]{:S(2)}) collective-permute-start(bf16[64,1024]{1,0:T(8,128)(2,1)S(1)} %slice.50), channel_id=1, source_target_pairs={{0,2},{1,3},{2,6},{3,7},{6,10},{7,11},{10,14},{11,15},{14,12},{15,... | collective-permute-start | bytes 393224 | tf_op jit(solution)/shard_map/ppermute | solution.py:368
  35.1 0.5 collective-permute-start.15
  35.6 2.9 %shard_map.122.acc_ref = f32[1024,128]{1,0:T(8,128)S(1)} custom-call(s32[16]{0:T(128)S(1)} %dynamic-slice_bitcast_fusion.offs_ref.refs_0_, f32[1024,128]{1,0:T(8,128)S(1)} %shard_map.121.acc_ref, bf16[128,16384]{1,0:T(8,128)(2,1)S(1)} %get-tuple-element.85.refs_3_.refs_0_, bf16[128,16384]{1,0:T(8,128)(2,1)S(1)} %get-tuple-element.86.refs_4_.refs_1_, ...), custom_call_target="tpu_custom_call" | custom-call | flops 67108864 | bytes 524288 | tf_op jit(solution)/shard_map/pallas_call | solution.py:56
  38.6 0.1 collective-permute-start.13
  39.3 0.6 shard_map.124.refs_9_
  40.0 2.3 %shard_map.123.refs_8_ = f32[1024,128]{1,0:T(8,128)S(1)} custom-call(s32[16]{0:T(128)S(1)} %dynamic-slice_bitcast_fusion.offs_ref.refs_0_, f32[1024,128]{1,0:T(8,128)S(1)} %shard_map.122.acc_ref, bf16[128,16384]{1,0:T(8,128)(2,1)S(1)} %get-tuple-element.85.refs_3_.refs_0_, bf16[128,16384]{1,0:T(8,128)(2,1)S(1)} %get-tuple-element.86.refs_4_.refs_1_, ...), custom_call_target="tpu_custom_call" | custom-call | flops 50331648 | bytes 393216 | tf_op jit(solution)/shard_map/pallas_call | solution.py:56
  42.3 2.1 %shard_map.125 = (f32[128,1024]{1,0:T(8,128)S(1)}, bf16[128,1024]{1,0:T(8,128)(2,1)S(1)}, bf16[1024,128]{1,0:T(8,128)(2,1)S(1)}, f32[16,1024]{1,0:T(8,128)}, f32[1,1024]{1,0:T(1,128)}, /*index=5*/f32[1,1024]{1,0:T(1,128)}) custom-call(s32[16]{0:T(128)S(1)} %dynamic-slice_bitcast_fusion.offs_ref.refs_0_, s32[1]{0:T(128)S(6)} %copy.20.perts_ref, ...), custom_call_target="tpu_custom_call" | custom-call | flops 33554432 | bytes 262144 | tf_op jit(solution)/shard_map/pallas_call | solution.py:56
  44.4 1.3 %shard_map.126 = (bf16[64,1024]{1,0:T(8,128)(2,1)S(1)}, bf16[64,1024]{1,0:T(8,128)(2,1)S(1)}, f32[128,1024]{1,0:T(8,128)S(1)}) custom-call(s32[16]{0:T(128)S(1)} %dynamic-slice_bitcast_fusion.offs_ref.refs_0_, bf16[128,1024]{1,0:T(8,128)(2,1)S(1)} %get-tuple-element.103.delta_ref, bf16[128,16384]{1,0:T(8,128)(2,1)S(1)} %get-tuple-element.85.refs_3_.refs_0_, ...), custom_call_target="tpu_custom_call" | custom-call | flops 33554432 | bytes 262144 | tf_op jit(solution)/shard_map/pallas_call | solution.py:56
  45.7 0.6 collective-permute-start.16
  46.3 0.1 collective-permute-start.17
  46.4 3.0 %shard_map.127 = (bf16[1024,16384]{1,0:T(8,128)(2,1)}, f32[8,128]{1,0:T(8,128)S(1)}) custom-call(s32[16]{0:T(128)S(1)} %dynamic-slice_bitcast_fusion.offs_ref.refs_0_, bf16[1024,128]{1,0:T(8,128)(2,1)S(1)} %get-tuple-element.107.refs_1_, bf16[128,1024]{1,0:T(8,128)(2,1)S(1)} %bitcast_convert_fusion.x_ref.refs_8_.refs_2_, ...), custom_call_target="tpu_custom_call" | custom-call | flops 33554432 | bytes 262144 | tf_op jit(solution)/shard_map/pallas_call | solution.py:56
  49.4 0.1 add_convert_fusion.4
  49.5 1.8 %shard_map.128 = (bf16[80,1024]{1,0:T(8,128)(2,1)S(1)}, bf16[80,1024]{1,0:T(8,128)(2,1)S(1)}, bf16[96,1024]{1,0:T(8,128)(2,1)S(1)}, f32[128,1024]{1,0:T(8,128)S(1)}, f32[128,1024]{1,0:T(8,128)S(1)}) custom-call(s32[16]{0:T(128)S(1)} %dynamic-slice_bitcast_fusion.offs_ref.refs_0_, bf16[128,1024]{1,0:T(8,128)(2,1)S(1)} %get-tuple-element.103.delta_ref, ...), custom_call_target="tpu_custom_call" | custom-call | flops 67108864 | bytes 524288 | tf_op jit(solution)/shard_map/pallas_call | solution.py:56
  51.3 0.5 collective-permute-start.18
  51.8 0.1 collective-permute-start.19
  51.9 0.4 collective-permute-start.21
  52.3 1.7 %collective-permute-start.22 = (bf16[64,1024]{1,0:T(8,128)(2,1)S(1)}, bf16[64,1024]{1,0:T(8,128)(2,1)S(1)}, u32[]{:S(2)}, u32[]{:S(2)}) collective-permute-start(bf16[64,1024]{1,0:T(8,128)(2,1)S(1)} %get-tuple-element.157), channel_id=1, source_target_pairs={{0,4},{1,5},{2,0},{3,1},{6,2},{7,3},{10,6},{11,7},{14,10},{15,11},... | collective-permute-start | bytes 393224 | tf_op jit(solution)/shard_map/ppermute | solution.py:368
  54.0 0.4 collective-permute-start.20
  54.4 0.2 convert_add_fusion
  54.6 3.3 %collective-permute-done.22 = bf16[64,1024]{1,0:T(8,128)(2,1)S(1)} collective-permute-done((bf16[64,1024]{1,0:T(8,128)(2,1)S(1)}, bf16[64,1024]{1,0:T(8,128)(2,1)S(1)}, u32[]{:S(2)}, u32[]{:S(2)}) %collective-permute-start.22) | collective-permute-done | bytes 131104 | tf_op jit(solution)/shard_map/ppermute | solution.py:368
  58.0 1.3 %collective-permute-done.20 = bf16[64,1024]{1,0:T(8,128)(2,1)S(1)} collective-permute-done((bf16[64,1024]{1,0:T(8,128)(2,1)S(1)}, bf16[64,1024]{1,0:T(8,128)(2,1)S(1)}, u32[]{:S(2)}, u32[]{:S(2)}) %collective-permute-start.20) | collective-permute-done | bytes 131104 | tf_op jit(solution)/shard_map/ppermute | solution.py:368
  59.3 0.4 collective-permute-start.25
  59.7 1.6 %collective-permute-start.26 = (bf16[128,1024]{1,0:T(8,128)(2,1)S(1)}, bf16[128,1024]{1,0:T(8,128)(2,1)S(1)}, u32[]{:S(2)}, u32[]{:S(2)}) collective-permute-start(bf16[128,1024]{1,0:T(8,128)(2,1)S(1)} %pad_maximum_fusion.7), channel_id=1, source_target_pairs={{0,4},{1,5},{2,0},{3,1},{6,2},{7,3},{10,6},{11,7},{14,10},{15,11},... | collective-permute-start | bytes 786440 | tf_op jit(solution)/shard_map/ppermute | solution.py:368
  61.4 1.8 %shard_map.129 = (bf16[80,1024]{1,0:T(8,128)(2,1)S(1)}, bf16[80,1024]{1,0:T(8,128)(2,1)S(1)}, bf16[96,1024]{1,0:T(8,128)(2,1)S(1)}, f32[128,1024]{1,0:T(8,128)S(1)}, f32[128,1024]{1,0:T(8,128)S(1)}) custom-call(s32[16]{0:T(128)S(1)} %dynamic-slice_bitcast_fusion.offs_ref.refs_0_, bf16[128,1024]{1,0:T(8,128)(2,1)S(1)} %get-tuple-element.103.delta_ref, ...), custom_call_target="tpu_custom_call" | custom-call | flops 67108864 | bytes 524288 | tf_op jit(solution)/shard_map/pallas_call | solution.py:56
  63.2 0.1 collective-permute-start.27
  63.3 0.5 collective-permute-start.23
  63.8 0.1 collective-permute-start.24
  63.9 4.6 %shard_map.130 = (bf16[1024,16384]{1,0:T(8,128)(2,1)}, f32[8,128]{1,0:T(8,128)S(1)}) custom-call(s32[16]{0:T(128)S(1)} %dynamic-slice_bitcast_fusion.offs_ref.refs_0_, bf16[1024,128]{1,0:T(8,128)(2,1)S(1)} %get-tuple-element.107.refs_1_, bf16[128,1024]{1,0:T(8,128)(2,1)S(1)} %collective-permute-done.refs_10_.refs_2_, ...), custom_call_target="tpu_custom_call", output_to_operand_aliasing={{0}: (6, {})} | custom-call | flops 67108864 | bytes 524288 | tf_op jit(solution)/shard_map/pallas_call | solution.py:56
  68.6 0.3 add_convert_fusion.2
  68.8 0.4 collective-permute-start.30
  69.3 1.6 %collective-permute-start.31 = (bf16[128,1024]{1,0:T(8,128)(2,1)S(1)}, bf16[128,1024]{1,0:T(8,128)(2,1)S(1)}, u32[]{:S(2)}, u32[]{:S(2)}) collective-permute-start(bf16[128,1024]{1,0:T(8,128)(2,1)S(1)} %get-tuple-element.134), channel_id=1, source_target_pairs={{0,4},{1,5},{2,0},{3,1},{6,2},{7,3},{10,6},{11,7},{14,10},{15,11},... | collective-permute-start | bytes 786440 | tf_op jit(solution)/shard_map/ppermute | solution.py:368
  70.9 1.8 %shard_map.131 = (bf16[80,1024]{1,0:T(8,128)(2,1)S(1)}, bf16[80,1024]{1,0:T(8,128)(2,1)S(1)}, bf16[96,1024]{1,0:T(8,128)(2,1)S(1)}, f32[128,1024]{1,0:T(8,128)S(1)}, f32[128,1024]{1,0:T(8,128)S(1)}) custom-call(s32[16]{0:T(128)S(1)} %dynamic-slice_bitcast_fusion.offs_ref.refs_0_, bf16[128,1024]{1,0:T(8,128)(2,1)S(1)} %get-tuple-element.103.delta_ref, ...), custom_call_target="tpu_custom_call" | custom-call | flops 67108864 | bytes 524288 | tf_op jit(solution)/shard_map/pallas_call | solution.py:56
  72.8 0.1 collective-permute-start.32
  72.9 0.5 collective-permute-start.28
  73.4 0.1 collective-permute-start.29
  73.4 0.6 shard_map.134
  74.1 4.6 %shard_map.132 = (bf16[1024,16384]{1,0:T(8,128)(2,1)}, f32[8,128]{1,0:T(8,128)S(1)}) custom-call(s32[16]{0:T(128)S(1)} %dynamic-slice_bitcast_fusion.offs_ref.refs_0_, bf16[1024,128]{1,0:T(8,128)(2,1)S(1)} %get-tuple-element.107.refs_1_, bf16[128,1024]{1,0:T(8,128)(2,1)S(1)} %collective-permute-done.2.refs_10_.refs_2_, ...), custom_call_target="tpu_custom_call", output_to_operand_aliasing={{0}: (6, {})} | custom-call | flops 67108864 | bytes 524288 | tf_op jit(solution)/shard_map/pallas_call | solution.py:56
  78.8 0.3 add_convert_fusion
  79.0 1.3 %shard_map.135 = (bf16[64,1024]{1,0:T(8,128)(2,1)S(1)}, bf16[64,1024]{1,0:T(8,128)(2,1)S(1)}, f32[128,1024]{1,0:T(8,128)S(1)}) custom-call(s32[16]{0:T(128)S(1)} %dynamic-slice_bitcast_fusion.offs_ref.refs_0_, bf16[128,1024]{1,0:T(8,128)(2,1)S(1)} %get-tuple-element.103.delta_ref, bf16[128,16384]{1,0:T(8,128)(2,1)S(1)} %get-tuple-element.85.refs_3_.refs_0_, ...), custom_call_target="tpu_custom_call" | custom-call | flops 33554432 | bytes 262144 | tf_op jit(solution)/shard_map/pallas_call | solution.py:56
  80.3 0.5 collective-permute-start.33
  80.8 0.1 collective-permute-start.34
  80.9 0.5 collective-permute-start.35
  81.4 1.5 %collective-permute-start.36 = (bf16[128,1024]{1,0:T(8,128)(2,1)S(1)}, bf16[128,1024]{1,0:T(8,128)(2,1)S(1)}, u32[]{:S(2)}, u32[]{:S(2)}) collective-permute-start(bf16[128,1024]{1,0:T(8,128)(2,1)S(1)} %get-tuple-element.151), channel_id=1, source_target_pairs={{0,4},{1,5},{2,0},{3,1},{6,2},{7,3},{10,6},{11,7},{14,10},{15,11},... | collective-permute-start | bytes 786440 | tf_op jit(solution)/shard_map/ppermute | solution.py:368
  82.9 0.1 multiply_add_fusion
  83.0 6.9 %shard_map.133 = (bf16[1024,16384]{1,0:T(8,128)(2,1)}, f32[8,128]{1,0:T(8,128)}) custom-call(s32[16]{0:T(128)S(1)} %dynamic-slice_bitcast_fusion.offs_ref.refs_0_, bf16[1024,128]{1,0:T(8,128)(2,1)S(1)} %get-tuple-element.107.refs_1_, bf16[128,1024]{1,0:T(8,128)(2,1)S(1)} %collective-permute-done.5.refs_10_.refs_2_, ...), custom_call_target="tpu_custom_call", output_to_operand_aliasing={{0}: (8, {})} | custom-call | flops 100663296 | bytes 786432 | tf_op jit(solution)/shard_map/pallas_call | solution.py:56
  90.0 1.0 %add_bitcast_fusion = f32[1,128,1024]{2,1,0:T(8,128)} fusion(bf16[128,1024]{1,0:T(8,128)(2,1)S(1)} %collective-permute-done.36, bf16[128,1024]{1,0:T(8,128)(2,1)S(1)} %collective-permute-done.35, f32[128,1024]{1,0:T(8,128)S(1)} %multiply_add_fusion, f32[128,1024]{1,0:T(8,128)S(1)} %get-tuple-element.147, bf16[64,1024]{1,0:T(8,128)(2,1)S(1)} %collective-permute-done.34, ...), kind=kLoop, calls=%fused_computation | loop fusion | flops 1310720 | bytes 2359296 | tf_op jit(solution)/shard_map/reshape | solution.py:464
  (56 shorter events, 0.3 us)
Async XLA Ops:
  1.7 11.7 %collective-permute-start.1 = (bf16[128,1024]{1,0:T(8,128)(2,1)S(1)}, bf16[128,1024]{1,0:T(8,128)(2,1)S(1)}, u32[]{:S(2)}, u32[]{:S(2)}) collective-permute-start(bf16[128,1024]{1,0:T(8,128)(2,1)S(1)} %bitcast_convert_fusion.x_ref.refs_8_.refs_2_), channel_id=1, source_target_pairs={{0,4},{1,5},{2,0},{3,1},{6,2},{7,3},{10,6},{11,7},{14,10},{15,11},... | collective-permute-start | bytes 786440 | tf_op jit(solution)/shard_map/ppermute | solution.py:368
  4.8 8.6 %collective-permute-start = (bf16[128,1024]{1,0:T(8,128)(2,1)S(1)}, bf16[128,1024]{1,0:T(8,128)(2,1)S(1)}, u32[]{:S(2)}, u32[]{:S(2)}) collective-permute-start(bf16[128,1024]{1,0:T(8,128)(2,1)S(1)} %bitcast_convert_fusion.x_ref.refs_8_.refs_2_), channel_id=1, source_target_pairs={{0,2},{1,3},{2,6},{3,7},{6,10},{7,11},{10,14},{11,15},{14,12},{15,... | collective-permute-start | bytes 786440 | tf_op jit(solution)/shard_map/ppermute | solution.py:368
  4.8 11.3 %collective-permute-start.4 = (bf16[128,1024]{1,0:T(8,128)(2,1)S(1)}, bf16[128,1024]{1,0:T(8,128)(2,1)S(1)}, u32[]{:S(2)}, u32[]{:S(2)}) collective-permute-start(bf16[128,1024]{1,0:T(8,128)(2,1)S(1)} %bitcast_convert_fusion.x_ref.refs_8_.refs_2_), channel_id=1, source_target_pairs={{0,1},{1,0},{2,3},{3,2},{4,5},{5,4},{6,7},{7,6},{8,9},{9,8},{10,11... | collective-permute-start | bytes 786440 | tf_op jit(solution)/shard_map/ppermute | solution.py:371
  13.4 9.7 %collective-permute-start.2 = (bf16[128,1024]{1,0:T(8,128)(2,1)S(1)}, bf16[128,1024]{1,0:T(8,128)(2,1)S(1)}, u32[]{:S(2)}, u32[]{:S(2)}) collective-permute-start(bf16[128,1024]{1,0:T(8,128)(2,1)S(1)} %collective-permute-done.refs_10_.refs_2_), channel_id=1, source_target_pairs={{0,2},{1,3},{2,6},{3,7},{6,10},{7,11},{10,14},{11,15},{14,12},{15,... | collective-permute-start | bytes 786440 | tf_op jit(solution)/shard_map/ppermute | solution.py:368
  15.4 8.4 %collective-permute-start.3 = (bf16[128,1024]{1,0:T(8,128)(2,1)S(1)}, bf16[128,1024]{1,0:T(8,128)(2,1)S(1)}, u32[]{:S(2)}, u32[]{:S(2)}) collective-permute-start(bf16[128,1024]{1,0:T(8,128)(2,1)S(1)} %collective-permute-done.1.refs_11_.refs_3_), channel_id=1, source_target_pairs={{0,4},{1,5},{2,0},{3,1},{6,2},{7,3},{10,6},{11,7},{14,10},{15,11},... | collective-permute-start | bytes 786440 | tf_op jit(solution)/shard_map/ppermute | solution.py:368
  15.6 10.3 %collective-permute-start.7 = (bf16[128,1024]{1,0:T(8,128)(2,1)S(1)}, bf16[128,1024]{1,0:T(8,128)(2,1)S(1)}, u32[]{:S(2)}, u32[]{:S(2)}) collective-permute-start(bf16[128,1024]{1,0:T(8,128)(2,1)S(1)} %collective-permute-done.refs_10_.refs_2_), channel_id=1, source_target_pairs={{0,1},{1,0},{2,3},{3,2},{4,5},{5,4},{6,7},{7,6},{8,9},{9,8},{10,11... | collective-permute-start | bytes 786440 | tf_op jit(solution)/shard_map/ppermute | solution.py:371
  15.8 10.6 %collective-permute-start.8 = (bf16[128,1024]{1,0:T(8,128)(2,1)S(1)}, bf16[128,1024]{1,0:T(8,128)(2,1)S(1)}, u32[]{:S(2)}, u32[]{:S(2)}) collective-permute-start(bf16[128,1024]{1,0:T(8,128)(2,1)S(1)} %collective-permute-done.1.refs_11_.refs_3_), channel_id=1, source_target_pairs={{0,1},{1,0},{2,3},{3,2},{4,5},{5,4},{6,7},{7,6},{8,9},{9,8},{10,11... | collective-permute-start | bytes 786440 | tf_op jit(solution)/shard_map/ppermute | solution.py:371
  23.9 7.8 %collective-permute-start.5 = (bf16[128,1024]{1,0:T(8,128)(2,1)S(1)}, bf16[128,1024]{1,0:T(8,128)(2,1)S(1)}, u32[]{:S(2)}, u32[]{:S(2)}) collective-permute-start(bf16[128,1024]{1,0:T(8,128)(2,1)S(1)} %collective-permute-done.2.refs_10_.refs_2_), channel_id=1, source_target_pairs={{0,2},{1,3},{2,6},{3,7},{6,10},{7,11},{10,14},{11,15},{14,12},{15,... | collective-permute-start | bytes 786440 | tf_op jit(solution)/shard_map/ppermute | solution.py:368
  25.4 7.6 %collective-permute-start.6 = (bf16[128,1024]{1,0:T(8,128)(2,1)S(1)}, bf16[128,1024]{1,0:T(8,128)(2,1)S(1)}, u32[]{:S(2)}, u32[]{:S(2)}) collective-permute-start(bf16[128,1024]{1,0:T(8,128)(2,1)S(1)} %collective-permute-done.3.refs_11_.refs_3_), channel_id=1, source_target_pairs={{0,4},{1,5},{2,0},{3,1},{6,2},{7,3},{10,6},{11,7},{14,10},{15,11},... | collective-permute-start | bytes 786440 | tf_op jit(solution)/shard_map/ppermute | solution.py:368
  25.9 9.2 %collective-permute-start.11 = (bf16[128,1024]{1,0:T(8,128)(2,1)S(1)}, bf16[128,1024]{1,0:T(8,128)(2,1)S(1)}, u32[]{:S(2)}, u32[]{:S(2)}) collective-permute-start(bf16[128,1024]{1,0:T(8,128)(2,1)S(1)} %collective-permute-done.2.refs_10_.refs_2_), channel_id=1, source_target_pairs={{0,1},{1,0},{2,3},{3,2},{4,5},{5,4},{6,7},{7,6},{8,9},{9,8},{10,11... | collective-permute-start | bytes 786440 | tf_op jit(solution)/shard_map/ppermute | solution.py:371
  25.9 9.8 %collective-permute-start.12 = (bf16[128,1024]{1,0:T(8,128)(2,1)S(1)}, bf16[128,1024]{1,0:T(8,128)(2,1)S(1)}, u32[]{:S(2)}, u32[]{:S(2)}) collective-permute-start(bf16[128,1024]{1,0:T(8,128)(2,1)S(1)} %collective-permute-done.3.refs_11_.refs_3_), channel_id=1, source_target_pairs={{0,1},{1,0},{2,3},{3,2},{4,5},{5,4},{6,7},{7,6},{8,9},{9,8},{10,11... | collective-permute-start | bytes 786440 | tf_op jit(solution)/shard_map/ppermute | solution.py:371
  33.0 6.3 %copy-start = (f32[1,128,1024]{2,1,0:T(8,128)S(1)}, f32[1,128,1024]{2,1,0:T(8,128)}, u32[]{:S(2)}) copy-start(f32[1,128,1024]{2,1,0:T(8,128)} %param.8) | copy-start | bytes 1572868
  33.0 6.3 %copy-start.1 = (f32[128,128]{1,0:T(8,128)S(1)}, f32[128,128]{1,0:T(8,128)}, u32[]{:S(2)}) copy-start(f32[128,128]{1,0:T(8,128)} %constant.13.clone.cheb_ref) | copy-start | bytes 196612
  33.0 5.5 %collective-permute-start.10 = (bf16[64,1024]{1,0:T(8,128)(2,1)S(1)}, bf16[64,1024]{1,0:T(8,128)(2,1)S(1)}, u32[]{:S(2)}, u32[]{:S(2)}) collective-permute-start(bf16[64,1024]{1,0:T(8,128)(2,1)S(1)} %slice.51), channel_id=1, source_target_pairs={{0,4},{1,5},{2,0},{3,1},{6,2},{7,3},{10,6},{11,7},{14,10},{15,11},... | collective-permute-start | bytes 393224 | tf_op jit(solution)/shard_map/ppermute | solution.py:368
  33.5 5.0 %collective-permute-start.9 = (bf16[64,1024]{1,0:T(8,128)(2,1)S(1)}, bf16[64,1024]{1,0:T(8,128)(2,1)S(1)}, u32[]{:S(2)}, u32[]{:S(2)}) collective-permute-start(bf16[64,1024]{1,0:T(8,128)(2,1)S(1)} %slice.50), channel_id=1, source_target_pairs={{0,2},{1,3},{2,6},{3,7},{6,10},{7,11},{10,14},{11,15},{14,12},{15,... | collective-permute-start | bytes 393224 | tf_op jit(solution)/shard_map/ppermute | solution.py:368
  35.1 4.8 %collective-permute-start.14 = (bf16[128,1024]{1,0:T(8,128)(2,1)S(1)}, bf16[128,1024]{1,0:T(8,128)(2,1)S(1)}, u32[]{:S(2)}, u32[]{:S(2)}) collective-permute-start(bf16[128,1024]{1,0:T(8,128)(2,1)S(1)} %collective-permute-done.5.refs_10_.refs_2_), channel_id=1, source_target_pairs={{0,1},{1,0},{2,3},{3,2},{4,5},{5,4},{6,7},{7,6},{8,9},{9,8},{10,11... | collective-permute-start | bytes 786440 | tf_op jit(solution)/shard_map/ppermute | solution.py:371
  35.1 4.8 %collective-permute-start.15 = (bf16[128,1024]{1,0:T(8,128)(2,1)S(1)}, bf16[128,1024]{1,0:T(8,128)(2,1)S(1)}, u32[]{:S(2)}, u32[]{:S(2)}) collective-permute-start(bf16[128,1024]{1,0:T(8,128)(2,1)S(1)} %collective-permute-done.6.refs_11_.refs_3_), channel_id=1, source_target_pairs={{0,1},{1,0},{2,3},{3,2},{4,5},{5,4},{6,7},{7,6},{8,9},{9,8},{10,11... | collective-permute-start | bytes 786440 | tf_op jit(solution)/shard_map/ppermute | solution.py:371
  38.6 3.7 %collective-permute-start.13 = (bf16[128,1024]{1,0:T(8,128)(2,1)S(1)}, bf16[128,1024]{1,0:T(8,128)(2,1)S(1)}, u32[]{:S(2)}, u32[]{:S(2)}) collective-permute-start(bf16[128,1024]{1,0:T(8,128)(2,1)S(1)} %constant_dynamic-update-slice_fusion.refs_10_.refs_6_), channel_id=1, source_target_pairs={{0,1},{1,0},{2,3},{3,2},{4,5},{5,4},{6,7},{7,6},{8,9},{9,8},{10,11... | collective-permute-start | bytes 786440 | tf_op jit(solution)/shard_map/ppermute | solution.py:371
  39.9 2.4 %copy-start.2 = (f32[16,1024]{1,0:T(8,128)S(1)}, f32[16,1024]{1,0:T(8,128)}, u32[]{:S(2)}) copy-start(f32[16,1024]{1,0:T(8,128)} %refs_11_.1) | copy-start | bytes 196612
  39.9 2.4 %copy-start.3 = (f32[1024]{0:T(1024)S(1)}, f32[1024]{0:T(1024)}, u32[]{:S(2)}) copy-start(f32[1024]{0:T(1024)} %param.12) | copy-start | bytes 12292
  39.9 2.4 %copy-start.4 = (f32[1024]{0:T(1024)S(1)}, f32[1024]{0:T(1024)}, u32[]{:S(2)}) copy-start(f32[1024]{0:T(1024)} %param.11) | copy-start | bytes 12292
  45.7 3.7 %collective-permute-start.16 = (bf16[64,1024]{1,0:T(8,128)(2,1)S(1)}, bf16[64,1024]{1,0:T(8,128)(2,1)S(1)}, u32[]{:S(2)}, u32[]{:S(2)}) collective-permute-start(bf16[64,1024]{1,0:T(8,128)(2,1)S(1)} %get-tuple-element.105), channel_id=1, source_target_pairs={{0,1},{1,0},{2,3},{3,2},{4,5},{5,4},{6,7},{7,6},{8,9},{9,8},{10,11... | collective-permute-start | bytes 393224 | tf_op jit(solution)/shard_map/ppermute | solution.py:371
  46.3 3.1 %collective-permute-start.17 = (bf16[64,1024]{1,0:T(8,128)(2,1)S(1)}, bf16[64,1024]{1,0:T(8,128)(2,1)S(1)}, u32[]{:S(2)}, u32[]{:S(2)}) collective-permute-start(bf16[64,1024]{1,0:T(8,128)(2,1)S(1)} %get-tuple-element.106), channel_id=1, source_target_pairs={{0,1},{1,0},{2,3},{3,2},{4,5},{5,4},{6,7},{7,6},{8,9},{9,8},{10,11... | collective-permute-start | bytes 393224 | tf_op jit(solution)/shard_map/ppermute | solution.py:371
  51.3 3.1 %collective-permute-start.18 = (bf16[80,1024]{1,0:T(8,128)(2,1)S(1)}, bf16[80,1024]{1,0:T(8,128)(2,1)S(1)}, u32[]{:S(2)}, u32[]{:S(2)}) collective-permute-start(bf16[80,1024]{1,0:T(8,128)(2,1)S(1)} %get-tuple-element.111), channel_id=1, source_target_pairs={{0,1},{1,0},{2,3},{3,2},{4,5},{5,4},{6,7},{7,6},{8,9},{9,8},{10,11... | collective-permute-start | bytes 491528 | tf_op jit(solution)/shard_map/ppermute | solution.py:371
  51.8 2.6 %collective-permute-start.19 = (bf16[80,1024]{1,0:T(8,128)(2,1)S(1)}, bf16[80,1024]{1,0:T(8,128)(2,1)S(1)}, u32[]{:S(2)}, u32[]{:S(2)}) collective-permute-start(bf16[80,1024]{1,0:T(8,128)(2,1)S(1)} %get-tuple-element.112), channel_id=1, source_target_pairs={{0,1},{1,0},{2,3},{3,2},{4,5},{5,4},{6,7},{7,6},{8,9},{9,8},{10,11... | collective-permute-start | bytes 491528 | tf_op jit(solution)/shard_map/ppermute | solution.py:371
  51.9 2.5 %collective-permute-start.21 = (bf16[96,1024]{1,0:T(8,128)(2,1)S(1)}, bf16[96,1024]{1,0:T(8,128)(2,1)S(1)}, u32[]{:S(2)}, u32[]{:S(2)}) collective-permute-start(bf16[96,1024]{1,0:T(8,128)(2,1)S(1)} %get-tuple-element.115), channel_id=1, source_target_pairs={{0,1},{1,0},{2,3},{3,2},{4,5},{5,4},{6,7},{7,6},{8,9},{9,8},{10,11... | collective-permute-start | bytes 589832 | tf_op jit(solution)/shard_map/ppermute | solution.py:371
  52.3 5.5 %collective-permute-start.22 = (bf16[64,1024]{1,0:T(8,128)(2,1)S(1)}, bf16[64,1024]{1,0:T(8,128)(2,1)S(1)}, u32[]{:S(2)}, u32[]{:S(2)}) collective-permute-start(bf16[64,1024]{1,0:T(8,128)(2,1)S(1)} %get-tuple-element.157), channel_id=1, source_target_pairs={{0,4},{1,5},{2,0},{3,1},{6,2},{7,3},{10,6},{11,7},{14,10},{15,11},... | collective-permute-start | bytes 393224 | tf_op jit(solution)/shard_map/ppermute | solution.py:368
  54.0 5.2 %collective-permute-start.20 = (bf16[64,1024]{1,0:T(8,128)(2,1)S(1)}, bf16[64,1024]{1,0:T(8,128)(2,1)S(1)}, u32[]{:S(2)}, u32[]{:S(2)}) collective-permute-start(bf16[64,1024]{1,0:T(8,128)(2,1)S(1)} %get-tuple-element.158), channel_id=1, source_target_pairs={{0,2},{1,3},{2,6},{3,7},{6,10},{7,11},{10,14},{11,15},{14,12},{15,... | collective-permute-start | bytes 393224 | tf_op jit(solution)/shard_map/ppermute | solution.py:368
  59.3 9.2 %collective-permute-start.25 = (bf16[128,1024]{1,0:T(8,128)(2,1)S(1)}, bf16[128,1024]{1,0:T(8,128)(2,1)S(1)}, u32[]{:S(2)}, u32[]{:S(2)}) collective-permute-start(bf16[128,1024]{1,0:T(8,128)(2,1)S(1)} %pad_maximum_fusion.6), channel_id=1, source_target_pairs={{0,2},{1,3},{2,6},{3,7},{6,10},{7,11},{10,14},{11,15},{14,12},{15,... | collective-permute-start | bytes 786440 | tf_op jit(solution)/shard_map/ppermute | solution.py:368
  59.7 8.8 %collective-permute-start.26 = (bf16[128,1024]{1,0:T(8,128)(2,1)S(1)}, bf16[128,1024]{1,0:T(8,128)(2,1)S(1)}, u32[]{:S(2)}, u32[]{:S(2)}) collective-permute-start(bf16[128,1024]{1,0:T(8,128)(2,1)S(1)} %pad_maximum_fusion.7), channel_id=1, source_target_pairs={{0,4},{1,5},{2,0},{3,1},{6,2},{7,3},{10,6},{11,7},{14,10},{15,11},... | collective-permute-start | bytes 786440 | tf_op jit(solution)/shard_map/ppermute | solution.py:368
  63.2 5.3 %collective-permute-start.27 = (bf16[96,1024]{1,0:T(8,128)(2,1)S(1)}, bf16[96,1024]{1,0:T(8,128)(2,1)S(1)}, u32[]{:S(2)}, u32[]{:S(2)}) collective-permute-start(bf16[96,1024]{1,0:T(8,128)(2,1)S(1)} %get-tuple-element.127), channel_id=1, source_target_pairs={{0,1},{1,0},{2,3},{3,2},{4,5},{5,4},{6,7},{7,6},{8,9},{9,8},{10,11... | collective-permute-start | bytes 589832 | tf_op jit(solution)/shard_map/ppermute | solution.py:371
  63.3 5.2 %collective-permute-start.23 = (bf16[80,1024]{1,0:T(8,128)(2,1)S(1)}, bf16[80,1024]{1,0:T(8,128)(2,1)S(1)}, u32[]{:S(2)}, u32[]{:S(2)}) collective-permute-start(bf16[80,1024]{1,0:T(8,128)(2,1)S(1)} %get-tuple-element.118), channel_id=1, source_target_pairs={{0,1},{1,0},{2,3},{3,2},{4,5},{5,4},{6,7},{7,6},{8,9},{9,8},{10,11... | collective-permute-start | bytes 491528 | tf_op jit(solution)/shard_map/ppermute | solution.py:371
  63.8 4.8 %collective-permute-start.24 = (bf16[80,1024]{1,0:T(8,128)(2,1)S(1)}, bf16[80,1024]{1,0:T(8,128)(2,1)S(1)}, u32[]{:S(2)}, u32[]{:S(2)}) collective-permute-start(bf16[80,1024]{1,0:T(8,128)(2,1)S(1)} %get-tuple-element.119), channel_id=1, source_target_pairs={{0,1},{1,0},{2,3},{3,2},{4,5},{5,4},{6,7},{7,6},{8,9},{9,8},{10,11... | collective-permute-start | bytes 491528 | tf_op jit(solution)/shard_map/ppermute | solution.py:371
  68.8 9.9 %collective-permute-start.30 = (bf16[128,1024]{1,0:T(8,128)(2,1)S(1)}, bf16[128,1024]{1,0:T(8,128)(2,1)S(1)}, u32[]{:S(2)}, u32[]{:S(2)}) collective-permute-start(bf16[128,1024]{1,0:T(8,128)(2,1)S(1)} %get-tuple-element.133), channel_id=1, source_target_pairs={{0,2},{1,3},{2,6},{3,7},{6,10},{7,11},{10,14},{11,15},{14,12},{15,... | collective-permute-start | bytes 786440 | tf_op jit(solution)/shard_map/ppermute | solution.py:368
  69.3 9.4 %collective-permute-start.31 = (bf16[128,1024]{1,0:T(8,128)(2,1)S(1)}, bf16[128,1024]{1,0:T(8,128)(2,1)S(1)}, u32[]{:S(2)}, u32[]{:S(2)}) collective-permute-start(bf16[128,1024]{1,0:T(8,128)(2,1)S(1)} %get-tuple-element.134), channel_id=1, source_target_pairs={{0,4},{1,5},{2,0},{3,1},{6,2},{7,3},{10,6},{11,7},{14,10},{15,11},... | collective-permute-start | bytes 786440 | tf_op jit(solution)/shard_map/ppermute | solution.py:368
  72.8 6.0 %collective-permute-start.32 = (bf16[96,1024]{1,0:T(8,128)(2,1)S(1)}, bf16[96,1024]{1,0:T(8,128)(2,1)S(1)}, u32[]{:S(2)}, u32[]{:S(2)}) collective-permute-start(bf16[96,1024]{1,0:T(8,128)(2,1)S(1)} %get-tuple-element.140), channel_id=1, source_target_pairs={{0,1},{1,0},{2,3},{3,2},{4,5},{5,4},{6,7},{7,6},{8,9},{9,8},{10,11... | collective-permute-start | bytes 589832 | tf_op jit(solution)/shard_map/ppermute | solution.py:371
  72.9 5.9 %collective-permute-start.28 = (bf16[80,1024]{1,0:T(8,128)(2,1)S(1)}, bf16[80,1024]{1,0:T(8,128)(2,1)S(1)}, u32[]{:S(2)}, u32[]{:S(2)}) collective-permute-start(bf16[80,1024]{1,0:T(8,128)(2,1)S(1)} %get-tuple-element.131), channel_id=1, source_target_pairs={{0,1},{1,0},{2,3},{3,2},{4,5},{5,4},{6,7},{7,6},{8,9},{9,8},{10,11... | collective-permute-start | bytes 491528 | tf_op jit(solution)/shard_map/ppermute | solution.py:371
  73.4 5.4 %collective-permute-start.29 = (bf16[80,1024]{1,0:T(8,128)(2,1)S(1)}, bf16[80,1024]{1,0:T(8,128)(2,1)S(1)}, u32[]{:S(2)}, u32[]{:S(2)}) collective-permute-start(bf16[80,1024]{1,0:T(8,128)(2,1)S(1)} %get-tuple-element.132), channel_id=1, source_target_pairs={{0,1},{1,0},{2,3},{3,2},{4,5},{5,4},{6,7},{7,6},{8,9},{9,8},{10,11... | collective-permute-start | bytes 491528 | tf_op jit(solution)/shard_map/ppermute | solution.py:371
  80.3 9.7 %collective-permute-start.33 = (bf16[64,1024]{1,0:T(8,128)(2,1)S(1)}, bf16[64,1024]{1,0:T(8,128)(2,1)S(1)}, u32[]{:S(2)}, u32[]{:S(2)}) collective-permute-start(bf16[64,1024]{1,0:T(8,128)(2,1)S(1)} %get-tuple-element.148), channel_id=1, source_target_pairs={{0,1},{1,0},{2,3},{3,2},{4,5},{5,4},{6,7},{7,6},{8,9},{9,8},{10,11... | collective-permute-start | bytes 393224 | tf_op jit(solution)/shard_map/ppermute | solution.py:371
  80.8 9.2 %collective-permute-start.34 = (bf16[64,1024]{1,0:T(8,128)(2,1)S(1)}, bf16[64,1024]{1,0:T(8,128)(2,1)S(1)}, u32[]{:S(2)}, u32[]{:S(2)}) collective-permute-start(bf16[64,1024]{1,0:T(8,128)(2,1)S(1)} %get-tuple-element.149), channel_id=1, source_target_pairs={{0,1},{1,0},{2,3},{3,2},{4,5},{5,4},{6,7},{7,6},{8,9},{9,8},{10,11... | collective-permute-start | bytes 393224 | tf_op jit(solution)/shard_map/ppermute | solution.py:371
  80.9 9.1 %collective-permute-start.35 = (bf16[128,1024]{1,0:T(8,128)(2,1)S(1)}, bf16[128,1024]{1,0:T(8,128)(2,1)S(1)}, u32[]{:S(2)}, u32[]{:S(2)}) collective-permute-start(bf16[128,1024]{1,0:T(8,128)(2,1)S(1)} %get-tuple-element.150), channel_id=1, source_target_pairs={{0,2},{1,3},{2,6},{3,7},{6,10},{7,11},{10,14},{11,15},{14,12},{15,... | collective-permute-start | bytes 786440 | tf_op jit(solution)/shard_map/ppermute | solution.py:368
  81.4 8.6 %collective-permute-start.36 = (bf16[128,1024]{1,0:T(8,128)(2,1)S(1)}, bf16[128,1024]{1,0:T(8,128)(2,1)S(1)}, u32[]{:S(2)}, u32[]{:S(2)}) collective-permute-start(bf16[128,1024]{1,0:T(8,128)(2,1)S(1)} %get-tuple-element.151), channel_id=1, source_target_pairs={{0,4},{1,5},{2,0},{3,1},{6,2},{7,3},{10,6},{11,7},{14,10},{15,11},... | collective-permute-start | bytes 786440 | tf_op jit(solution)/shard_map/ppermute | solution.py:368

commit v5 on v4

--- a/solution.py
+++ b/solution.py
@@ -176,36 +176,60 @@
     )([offs, acc, *bands, *xs], [SMEM_REF] + [VMEM_REF] * (1 + len(bands) + count))
 
 
-def cheb_kernel(turned, cheb_ref, array_ref, out_ref):
-    out_ref[...] = SCALE * lax.dot_general(
+def cheb_dot(turned, cheb_ref, array_ref):
+    return SCALE * lax.dot_general(
         cheb_ref[...], array_ref[...], (((0 if turned else 1,), (0,)), ((), ())),
         precision=lax.Precision.HIGHEST, preferred_element_type=jnp.float32,
     )
 
 
-def cheb_product(turned, cheb, array):
+def deriv_kernel(perts_ref, cheb_ref, states_ref, pert_ref, deriv_ref, drive_ref, chosen_ref):
+    pert = perts_ref[0]
+    deriv_ref[...] = cheb_dot(False, cheb_ref, states_ref)
+    drive_ref[...] = pert_ref[pl.ds(pert, 1), :]
+    rows = lax.broadcasted_iota(jnp.int32, chosen_ref.shape, 0)
+    chosen_ref[...] = (rows == pert).astype(jnp.float32)
+
+
+def derivatives(perts, cheb, states, pert_table):
     return call(
-        functools.partial(cheb_kernel, turned),
-        jax.ShapeDtypeStruct(array.shape, jnp.float32),
+        deriv_kernel,
+        [
+            jax.ShapeDtypeStruct(states.shape, jnp.float32),
+            jax.ShapeDtypeStruct((1, states.shape[1]), jnp.float32),
+            jax.ShapeDtypeStruct(pert_table.shape, jnp.float32),
+        ],
+        [VMEM_REF] * 3,
+        [],
+        cost(1, *states.shape, states.shape[0]),
+    )([perts, cheb, states, pert_table], [SMEM_REF] + [VMEM_REF] * 3)
+
+
+def local_kernel(cheb_ref, resid_ref, decay_ref, out_ref):
+    out_ref[...] = cheb_dot(True, cheb_ref, resid_ref) + decay_ref[...] * resid_ref[...]
+
+
+def local_terms(cheb, resid, decay):
+    return call(
+        local_kernel,
+        jax.ShapeDtypeStruct(resid.shape, jnp.float32),
         VMEM_REF,
         [],
-        cost(1, *array.shape, array.shape[0]),
-    )([cheb, array], [VMEM_REF] * 2)
-
-
-def middle_kernel(base, many, offs_ref, perts_ref, x_ref, *refs):
+        cost(1, *resid.shape, resid.shape[0]),
+    )([cheb, resid, decay], [VMEM_REF] * 3)
+
+
+def middle_kernel(base, many, offs_ref, x_ref, *refs):
     bands = refs[:many]
-    acc_ref, deriv_ref, states_ref, pert_ref, eps_ref, decay_ref = refs[many:-6]
+    acc_ref, deriv_ref, drive_ref, chosen_ref, states_ref, eps_ref, decay_ref = refs[many:-6]
     resid_ref, delta_ref, delta_t_ref, table_ref, sum_eps_ref, sum_decay_ref = refs[-6:]
     tile = 2 * bands[0].shape[0]
     here = columns_of(offs_ref, base, x_ref.shape[1])
-    pert = perts_ref[0]
-    chosen = lax.broadcasted_iota(jnp.int32, (pert_ref.shape[0], tile), 0) == pert
     for at in range(many // 2):
         band = pl.ds(at * tile, tile)
         part = acc_ref[band, :] + product(bands[2 * at : 2 * at + 2], here, x_ref)
         states = states_ref[:, band]
-        act = jnp.tanh(part.T + pert_ref[pl.ds(pert, 1), band])
+        act = jnp.tanh(part.T + drive_ref[:, band])
         eps = eps_ref[:, band]
         resid = deriv_ref[:, band] - (eps * act - decay_ref[:, band] * states)
         delta = (-eps * (1.0 - act * act) * resid).astype(jnp.bfloat16)
@@ -213,12 +237,12 @@
         resid_ref[:, band] = resid
         delta_ref[:, band] = delta
         delta_t_ref[band, :] = wide.T.astype(jnp.bfloat16)
-        table_ref[:, band] = jnp.where(chosen, jnp.sum(wide, axis=0, keepdims=True), 0.0)
+        table_ref[:, band] = chosen_ref[:, band] * jnp.sum(wide, axis=0, keepdims=True)
         sum_eps_ref[:, band] = -jnp.sum(act * resid, axis=0, keepdims=True)
         sum_decay_ref[:, band] = jnp.sum(states * resid, axis=0, keepdims=True)
 
 
-def middle(offs, perts, base, x, bands, acc, deriv, states, pert_table, eps, decay):
+def middle(offs, base, x, bands, acc, derivs, states, eps, decay):
     nodes, slab = x.shape
     rows = acc.shape[0]
     wide = functools.partial(jax.ShapeDtypeStruct, dtype=jnp.float32)
@@ -228,7 +252,7 @@
             wide((nodes, rows)),
             jax.ShapeDtypeStruct((nodes, rows), jnp.bfloat16),
             jax.ShapeDtypeStruct((rows, nodes), jnp.bfloat16),
-            wide(pert_table.shape),
+            wide(derivs[2].shape),
             wide((1, rows)),
             wide((1, rows)),
         ],
@@ -236,97 +260,95 @@
         [],
         cost(2, nodes, slab, rows),
     )(
-        [offs, perts, x, *bands, acc, deriv, states, pert_table, eps, decay],
-        [SMEM_REF] * 2 + [VMEM_REF] * (7 + len(bands)),
-    )
-
-
-def share_kernel(at_places, cuts, many, offs_ref, delta_ref, *refs):
-    bands, outs = refs[:many], refs[many:]
-    nodes = delta_ref.shape[0]
-    count = cuts[-1] // nodes
-    slab, depth = outs[0].shape[1], 2 * bands[0].shape[0]
-    tile = max(slab // 2, 128)
-    for at, place in enumerate(at_places):
+        [offs, x, *bands, acc, *derivs, states, eps, decay],
+        [SMEM_REF] + [VMEM_REF] * (8 + len(bands)),
+    )
+
+
+def grad_w_part(base, offs_ref, delta_t_ref, xs, out_ref, held, sems):
+    slab = xs[0].shape[1]
+    slots, _, width = held.shape
+    step = min(256, width)
+    copies = []
+    for at, x_ref in enumerate(xs):
+        for start in range(0, slab, width):
+            slot = len(copies) % slots
+            if len(copies) >= slots:
+                copies[-slots].wait()
+            for col in range(0, width, step):
+                held[slot, :, col : col + step] = jnp.dot(
+                    delta_t_ref[...], x_ref[:, start + col : start + col + step],
+                    preferred_element_type=jnp.float32,
+                ).astype(held.dtype)
+            there = pl.ds(pl.multiple_of(offs_ref[base + at] * slab + start, width), width)
+            copy = pltpu.make_async_copy(held.at[slot], out_ref.at[:, there], sems.at[slot])
+            copy.start()
+            copies.append(copy)
+    return copies[-slots:]
+
+
+def share_part(places, offs_ref, delta_ref, bands, outs):
+    depth = 2 * bands[0].shape[0]
+    for place, out_ref in zip(places, outs):
+        slab = out_ref.shape[1]
+        tile = max(slab // 2, 128)
         for col in range(0, slab, tile):
-            here = pl.ds(col, tile)
             there = pl.ds(pl.multiple_of(offs_ref[place] * slab + col, tile), tile)
             part = None
-            for low in range(0, many, 2):
+            for low in range(0, len(bands), 2):
                 pair = jnp.concatenate([ref[:, there] for ref in bands[low : low + 2]], axis=0)
                 more = jnp.dot(
                     delta_ref[:, low // 2 * depth : (low // 2 + 1) * depth], pair,
                     preferred_element_type=jnp.float32,
                 )
                 part = more if part is None else part + more
-            if at >= count:
-                outs[len(cuts) - 1 + at - count][:, here] = part
-                continue
-            for start, end, out_ref in zip(cuts[:-1], cuts[1:], outs):
-                low, high = max(start, at * nodes), min(end, (at + 1) * nodes)
-                if low < high:
-                    rows = part[low - at * nodes : high - at * nodes]
-                    out_ref[low - start : high - start, here] = rows.astype(out_ref.dtype)
-
-
-def shares(offs, at_places, delta, bands, slab, cuts):
+            out_ref[:, pl.ds(col, tile)] = part.astype(out_ref.dtype)
+
+
+def sums_kernel(base, count, places, many, first, *refs):
+    offs_ref, delta_ref, delta_t_ref = refs[:3]
+    xs, bands = refs[3 : 3 + count], refs[3 + count : 3 + count + many]
+    refs = refs[3 + count + many + (0 if first else 1) :]
+    outs, copies = refs[: len(places)], []
+    if count:
+        out_ref, mark_ref, held, sems = refs[len(places) :]
+        mark_ref[...] = jnp.zeros_like(mark_ref)
+        copies = grad_w_part(base, offs_ref, delta_t_ref, xs, out_ref, held, sems)
+    share_part(places, offs_ref, delta_ref, bands, outs)
+    for copy in copies:
+        copy.wait()
+
+
+def sums(offs, base, xs, places, delta, delta_t, bands, slab, so_far, shape):
     nodes, rows = delta.shape
-    own = len(at_places) // 2
-    heights = [end - start for start, end in zip(cuts[:-1], cuts[1:])]
-    outs = call(
-        functools.partial(share_kernel, at_places, cuts, len(bands)),
-        [jax.ShapeDtypeStruct((height, slab), jnp.bfloat16) for height in heights]
-        + [jax.ShapeDtypeStruct((nodes, slab), jnp.float32)] * own,
-        [VMEM_REF] * (len(heights) + own),
-        [],
-        cost(len(at_places), nodes, slab, rows),
-    )([offs, delta, *bands], [SMEM_REF] + [VMEM_REF] * (1 + len(bands)))
-    return outs[: len(heights)], outs[len(heights) :]
-
-
-def grad_w_kernel(base, count, *refs):
-    offs_ref, delta_ref, xs = refs[0], refs[1], refs[2 : 2 + count]
-    out_ref, mark_ref, held, sems = refs[-4:]
-    slab = xs[0].shape[1]
-    slots, _, width = held.shape
-    step = min(256, width)
-    mark_ref[...] = jnp.zeros_like(mark_ref)
-    copies = []
-    for at in range(count):
-        for start in range(0, slab, width):
-            slot = len(copies) % slots
-            if len(copies) >= slots:
-                copies[-slots].wait()
-            for col in range(0, width, step):
-                held[slot, :, col : col + step] = jnp.dot(
-                    delta_ref[...], xs[at][:, start + col : start + col + step],
-                    preferred_element_type=jnp.float32,
-                ).astype(held.dtype)
-            there = pl.ds(pl.multiple_of(offs_ref[base + at] * slab + start, width), width)
-            copy = pltpu.make_async_copy(held.at[slot], out_ref.at[:, there], sems.at[slot])
-            copy.start()
-            copies.append(copy)
-    for copy in copies[-slots:]:
-        copy.wait()
-
-
-def grad_w_piece(offs, base, delta_t, xs, so_far, mark, shape):
-    rows, nodes = delta_t.shape
-    slab, count = xs[0].shape[1], len(xs)
+    count, own = len(xs), len(places) // 2
     width = max(slab // 2, 128)
     first = so_far is None
-    return call(
-        functools.partial(grad_w_kernel, base, count),
-        [jax.ShapeDtypeStruct(shape, jnp.bfloat16), jax.ShapeDtypeStruct((8, 128), jnp.float32)],
-        [ANY_REF, VMEM_REF],
-        [pltpu.VMEM((4, rows, width), jnp.bfloat16), pltpu.SemaphoreType.DMA((4,))],
-        cost(count, nodes, slab, rows),
-        {} if first else {2 + count: 0},
-        4 * 2 * rows * width,
+    shapes = [jax.ShapeDtypeStruct((nodes, slab), jnp.bfloat16)] * own
+    shapes += [jax.ShapeDtypeStruct((nodes, slab), jnp.float32)] * own
+    specs, scratch, more = [VMEM_REF] * (2 * own), [], 0
+    if count:
+        shapes += [
+            jax.ShapeDtypeStruct(shape, jnp.bfloat16),
+            jax.ShapeDtypeStruct((8, 128), jnp.float32),
+        ]
+        specs += [ANY_REF, VMEM_REF]
+        scratch = [pltpu.VMEM((4, rows, width), jnp.bfloat16), pltpu.SemaphoreType.DMA((4,))]
+        more = 4 * 2 * rows * width
+    operands = [offs, delta, delta_t, *xs, *bands] + ([] if first else [so_far])
+    outs = call(
+        functools.partial(sums_kernel, base, count, places, len(bands), first),
+        shapes,
+        specs,
+        scratch,
+        cost(count + 2 * own, nodes, slab, rows),
+        {} if first else {len(operands) - 1: 2 * own},
+        more,
     )(
-        [offs, delta_t, *xs] + ([] if first else [so_far, mark]),
-        [SMEM_REF] + [VMEM_REF] * (1 + count) + ([] if first else [ANY_REF] * 2),
-    )
+        operands,
+        [SMEM_REF] + [VMEM_REF] * (2 + count + len(bands)) + ([] if first else [ANY_REF]),
+    )
+    return outs[:own], outs[own : 2 * own], outs[2 * own :]
 
 
 def ring_body(chips, states, weights, pert_table, eps_gain, decay, perts):
@@ -375,6 +397,8 @@
     flat = states.reshape(nodes, slab)
     xb = flat.astype(jnp.bfloat16)
 
+    gate = lax.optimization_barrier
+
     x = {(0, 0): xb}
     behind, ahead, base = xb, xb, 0
     for step in range(1, half + 1):
@@ -393,7 +417,10 @@
         else:
             acc = add_products(offs, base, xs, acc, bands)
         base += count
-        behind, ahead, acc = lax.optimization_barrier((behind, ahead, acc))
+        if step == half - 1:
+            derivs = derivatives(perts, cheb, flat, pert_table)
+            acc, *derivs = gate((acc, *derivs))
+        behind, ahead, acc = gate((behind, ahead, acc))
         if step < half:
             x[-step, 0], x[step, 0] = behind, ahead
         else:
@@ -403,52 +430,39 @@
     acc = add_products(offs, base, xs, acc, bands)
     base += 3
 
+    decay = decay.reshape(1, rows)
     resid, delta, delta_t, grad_table, grad_eps, grad_decay = middle(
-        offs, perts, base, x[half, 1], bands, acc, cheb_product(False, cheb, flat), flat,
-        pert_table, eps_gain.reshape(1, rows), decay.reshape(1, rows),
-    )
-
-    def share(steps):
-        count = len(steps)
-        parts = 2 if count == 1 else 3
-        cuts = [0] + [count * nodes * at // parts // 16 * 16 for at in range(1, parts)]
-        cuts.append(count * nodes)
+        offs, base, x[half, 1], bands, acc, derivs, flat, eps_gain.reshape(1, rows), decay
+    )
+
+    grad_w, base = None, 0
+
+    def work(offs, count, steps, grad_w, base):
         places = [sides[step, side] for side in (1, 0) for step in steps]
-        others, owns = shares(offs, places, delta, bands, slab, cuts)
-        swapped = jnp.concatenate([swap(other) for other in others], axis=0)
-        return [
-            own + swapped[at * nodes : (at + 1) * nodes].astype(jnp.float32)
-            for at, own in enumerate(owns)
-        ]
-
-    gate = lax.optimization_barrier
-    first = len(listing) // 8
-    each = (len(listing) - first) // (half - 1)
-    cuts = [0] + [first + each * at for at in range(half - 1)] + [len(listing)]
-    pieces = [(base, listing[base:end]) for base, end in zip(cuts[:-1], cuts[1:])]
-    grad_w, mark = None, None
-
-    def next_piece(grad_w, mark):
-        base, keys = pieces.pop(0)
-        return grad_w_piece(
-            offs, base, delta_t, [x[key] for key in keys], grad_w, mark, weights.shape
+        xs = [x[key] for key in listing[base : base + count]]
+        others, owns, rest = sums(
+            offs, base, xs, places, delta, delta_t, bands, slab, grad_w, weights.shape
         )
-
-    (far,) = share([half])
-    far = far.astype(jnp.bfloat16)
-    grad_w, mark = next_piece(grad_w, mark)
-    far, offs, mark = gate((far, offs, mark))
+        grad_w, mark = rest if count else (grad_w, None)
+        return others, owns, grad_w, base + count, mark
+
+    def joined(others, owns):
+        return [own + swap(other).astype(jnp.float32) for other, own in zip(others, owns)]
+
+    counts = [2, 5, 5]
+    counts.append(len(listing) - sum(counts))
+    others, owns, _, _, _ = work(offs, 0, [half], None, 0)
+    (far,) = joined(others, owns)
+    others, owns, _, _, _ = work(offs, 0, [half - 1, 1 - half], None, 0)
+    far, offs, *owns = gate((far.astype(jnp.bfloat16), offs, *owns))
+    own_ahead, own_behind = joined(others, owns)
     ahead, behind = ring(far[:cut], 1), ring(far[cut:], -1)
     for step in range(half - 1, -1, -1):
-        if step > 0:
-            own_ahead, own_behind = share([step, -step])
-        else:
-            (near_share,) = share([0])
-        if step < half - 1:
-            grad_w, mark = next_piece(grad_w, mark)
-            ahead, behind, mark = gate((ahead, behind, mark))
+        steps = [] if step == 0 else [0] if step == 1 else [step - 1, 1 - step]
+        others, owns, grad_w, base, mark = work(offs, counts.pop(0), steps, grad_w, base)
         if step == 0:
             break
+        ahead, behind, *owns = gate((ahead, behind, *owns))
         ahead, behind = ahead.astype(jnp.float32), behind.astype(jnp.float32)
         if step == half - 1:
             ahead = jnp.concatenate([own_ahead[:cut] + ahead, own_ahead[cut:]], axis=0)
@@ -456,10 +470,15 @@
         else:
             ahead, behind = own_ahead + ahead, own_behind + behind
         ahead, behind = ahead.astype(jnp.bfloat16), behind.astype(jnp.bfloat16)
+        if step > 1:
+            own_ahead, own_behind = joined(others, owns)
+        else:
+            (near_share,) = joined(others, owns)
         ahead, behind, offs = gate((ahead, behind, offs))
         ahead, behind = ring(ahead, 1), ring(behind, -1)
 
-    local = gate(cheb_product(True, cheb, resid) + decay * resid)
+    local = local_terms(cheb, resid, decay)
+    ahead, behind, local = gate((ahead, behind, local))
     grad_x = local + near_share + ahead.astype(jnp.float32) + behind.astype(jnp.float32)
     grad_x = grad_x.reshape(states.shape)
     return (grad_w, grad_x, grad_table, grad_eps.reshape(rows), grad_decay.reshape(rows))

time: 91.2 us -> 86.6 us (0.950)
  waiting for transfers between devices: 9.08 us -> 4.82 us
  local copies, waits for them, and re-layouts: 0.82 us -> 2.48 us
  starting transfers between devices: 22.7 us -> 21.4 us
    ppermute x16, waiting for transfers between devices: 9.02 us -> 4.78 us  [ring(): return lax.ppermute(array, 'row', pairs)]
    unnamed x11 -> x21, local copies, waits for them, and re-layouts: 0.04 us -> 1.71 us
    ppermute x21 -> x16, starting transfers between devices: 5.13 us -> 3.75 us  [swap(): return lax.ppermute(array, 'row', [(i, i ^ 1) for i in range(2 * chips)])]
    pallas_call x17 -> x14, Pallas kernels: 53.6 us -> 53 us  [run(): pl.pallas_call(kernel, out_shape=out_shape, in_specs=in_specs, out_specs=...]
  transfers between devices with their start and end apart: 37 -> 32, of which waited for: 5 -> 5; matrix products, arithmetic and copies ran while one was open for 1% -> 1% of each run, Pallas kernels for 52% -> 58%
where the time goes in v5:
time: 86.6 us; the launch traced here: 86.3 us
  Pallas kernels  53 us (61%)
  starting transfers between devices  21.4 us (25%)
  waiting for transfers between devices  4.82 us (6%)
  other arithmetic  2.76 us (3%)
  local copies, waits for them, and re-layouts  2.48 us (3%)
  between operations  1.77 us (2%)
    pallas_call x14, Pallas kernels, run(): pl.pallas_call(kernel, out_shape=out_shape, in_specs=in_specs, out_specs=...  53 us
    ppermute x16, starting transfers between devices, ring(): return lax.ppermute(array, 'row', pairs)  17.7 us
    ppermute x16, waiting for transfers between devices, ring(): return lax.ppermute(array, 'row', pairs)  4.78 us
    ppermute x16, starting transfers between devices, swap(): return lax.ppermute(array, 'row', [(i, i ^ 1) for i in range(2 * chips)])  3.75 us
  transfers between devices with their start and end apart: 32, of which 5 were waited for; matrix products, arithmetic and copies ran while one was open for 1% of the time, Pallas kernels for 58%

profile of v5, /device:TPU:0, one launch (start us, length us, event | category | flops | bytes accessed | tf_op | source)
XLA Modules:
  0.0 86.3 jit_solution(7645187909446126727)
XLA Ops:
  0.6 1.1 %bitcast_convert_fusion.x_ref.refs_8_.refs_3_ = bf16[128,1024]{1,0:T(8,128)(2,1)S(1)} fusion(f32[1,128,1024]{2,1,0:T(8,128)} %param.8), kind=kLoop, calls=%fused_computation.19 | loop fusion | flops 131072 | bytes 786432 | tf_op jit(solution)/shard_map/convert_element_type | solution.py:398
  1.7 3.1 %collective-permute-start.1 = (bf16[128,1024]{1,0:T(8,128)(2,1)S(1)}, bf16[128,1024]{1,0:T(8,128)(2,1)S(1)}, u32[]{:S(2)}, u32[]{:S(2)}) collective-permute-start(bf16[128,1024]{1,0:T(8,128)(2,1)S(1)} %bitcast_convert_fusion.x_ref.refs_8_.refs_3_), channel_id=1, source_target_pairs={{0,4},{1,5},{2,0},{3,1},{6,2},{7,3},{10,6},{11,7},{14,10},{15,11},... | collective-permute-start | bytes 786440 | tf_op jit(solution)/shard_map/ppermute | solution.py:390
  4.8 0.0 collective-permute-start
  4.8 0.0 collective-permute-start.4
  4.8 0.7 dynamic-slice_bitcast_fusion.offs_ref.refs_0_
  5.5 7.9 %shard_map.119 = (f32[1024,128]{1,0:T(8,128)S(1)}, bf16[128,16384]{1,0:T(8,128)(2,1)S(1)}, bf16[128,16384]{1,0:T(8,128)(2,1)S(1)}, bf16[128,16384]{1,0:T(8,128)(...) custom-call(s32[16]{0:T(128)S(1)} %dynamic-slice_bitcast_fusion.offs_ref.refs_0_, ...), custom_call_target="tpu_custom_call" | custom-call | flops 16777216 | bytes 131072 | tf_op jit(solution)/shard_map/pallas_call | solution.py:56
  13.4 0.0 collective-permute-done.refs_10_.refs_3_
  13.4 2.0 %collective-permute-start.2 = (bf16[128,1024]{1,0:T(8,128)(2,1)}, bf16[128,1024]{1,0:T(8,128)(2,1)S(1)}, u32[]{:S(2)}, u32[]{:S(2)}) collective-permute-start(bf16[128,1024]{1,0:T(8,128)(2,1)} %collective-permute-done.refs_10_.refs_3_), channel_id=1, source_target_pairs={{0,2},{1,3},{2,6},{3,7},{6,10},{7,11},{10,14},{11,15},{14,12},{15,... | collective-permute-start | bytes 786440 | tf_op jit(solution)/shard_map/ppermute | solution.py:390
  15.4 0.1 collective-permute-start.3
  15.6 0.2 collective-permute-start.7
  15.8 0.3 collective-permute-start.8
  16.1 0.0 collective-permute-done.4.refs_9_.refs_4_
  16.1 0.7 copy-done.3
  16.8 0.9 %copy-done.4 = bf16[128,1024]{1,0:T(8,128)(2,1)S(1)} copy-done((bf16[128,1024]{1,0:T(8,128)(2,1)S(1)}, bf16[128,1024]{1,0:T(8,128)(2,1)}, u32[]{:S(2)}) %copy-start.4) | copy-done | bytes 262168
  17.7 7.4 %shard_map.120 = (f32[1024,128]{1,0:T(8,128)S(1)}, bf16[128,16384]{1,0:T(8,128)(2,1)S(1)}, bf16[128,16384]{1,0:T(8,128)(2,1)S(1)}, bf16[128,16384]{1,0:T(8,128)(2,1)S(1)}) custom-call(s32[16]{0:T(128)S(1)} %dynamic-slice_bitcast_fusion.offs_ref.refs_0_, bf16[1024,16384]{1,0:T(8,128)(2,1)} %refs_1_.1, f32[1024,128]{1,0:T(8,128)S(1)} %get-tuple-element.90.refs_2_, ...), custom_call_target="tpu_custom_call" | custom-call | flops 67108864 | bytes 524288 | tf_op jit(solution)/shard_map/pallas_call | solution.py:56
  25.1 0.0 copy-start
  25.2 1.9 %collective-permute-start.5 = (bf16[128,1024]{1,0:T(8,128)(2,1)S(1)}, bf16[128,1024]{1,0:T(8,128)(2,1)S(1)}, u32[]{:S(2)}, u32[]{:S(2)}) collective-permute-start(bf16[128,1024]{1,0:T(8,128)(2,1)S(1)} %collective-permute-done.2.refs_10_.refs_7_), channel_id=1, source_target_pairs={{0,2},{1,3},{2,6},{3,7},{6,10},{7,11},{10,14},{11,15},{14,12},{15,... | collective-permute-start | bytes 786440 | tf_op jit(solution)/shard_map/ppermute | solution.py:390
  27.1 0.1 collective-permute-start.6
  27.2 0.5 collective-permute-start.12
  28.4 0.6 shard_map.122
  29.0 2.9 %shard_map.121.acc_ref = f32[1024,128]{1,0:T(8,128)S(1)} custom-call(s32[16]{0:T(128)S(1)} %dynamic-slice_bitcast_fusion.offs_ref.refs_0_, f32[1024,128]{1,0:T(8,128)S(1)} %get-tuple-element.99.acc_ref, bf16[128,16384]{1,0:T(8,128)(2,1)S(1)} %get-tuple-element.91.refs_3_.refs_0_.refs_5_.refs_8_.refs_7_, ...), custom_call_target="tpu_custom_call" | custom-call | flops 67108864 | bytes 524288 | tf_op jit(solution)/shard_map/pallas_call | solution.py:56
  31.9 1.8 %collective-permute-done.5.refs_10_.refs_6_ = bf16[128,1024]{1,0:T(8,128)(2,1)S(1)} collective-permute-done((bf16[128,1024]{1,0:T(8,128)(2,1)S(1)}, bf16[128,1024]{1,0:T(8,128)(2,1)S(1)}, u32[]{:S(2)}, u32[]{:S(2)}) %collective-permute-start.5) | collective-permute-done | bytes 262176 | tf_op jit(solution)/shard_map/ppermute | solution.py:390
  33.7 1.4 %collective-permute-done.6.refs_11_.refs_7_ = bf16[128,1024]{1,0:T(8,128)(2,1)S(1)} collective-permute-done((bf16[128,1024]{1,0:T(8,128)(2,1)S(1)}, bf16[128,1024]{1,0:T(8,128)(2,1)S(1)}, u32[]{:S(2)}, u32[]{:S(2)}) %collective-permute-start.6) | collective-permute-done | bytes 262176 | tf_op jit(solution)/shard_map/ppermute | solution.py:390
  35.1 0.5 collective-permute-start.10
  35.5 1.6 %collective-permute-start.9 = (bf16[64,1024]{1,0:T(8,128)(2,1)S(1)}, bf16[64,1024]{1,0:T(8,128)(2,1)S(1)}, u32[]{:S(2)}, u32[]{:S(2)}) collective-permute-start(bf16[64,1024]{1,0:T(8,128)(2,1)S(1)} %slice.26), channel_id=1, source_target_pairs={{0,2},{1,3},{2,6},{3,7},{6,10},{7,11},{10,14},{11,15},{14,12},{15,... | collective-permute-start | bytes 393224 | tf_op jit(solution)/shard_map/ppermute | solution.py:390
  37.1 0.5 collective-permute-start.15
  37.6 2.9 %shard_map.123.acc_ref = f32[1024,128]{1,0:T(8,128)S(1)} custom-call(s32[16]{0:T(128)S(1)} %dynamic-slice_bitcast_fusion.offs_ref.refs_0_, f32[1024,128]{1,0:T(8,128)S(1)} %shard_map.121.acc_ref, bf16[128,16384]{1,0:T(8,128)(2,1)S(1)} %get-tuple-element.91.refs_3_.refs_0_.refs_5_.refs_8_.refs_7_, ...), custom_call_target="tpu_custom_call" | custom-call | flops 67108864 | bytes 524288 | tf_op jit(solution)/shard_map/pallas_call | solution.py:56
  40.6 0.0 copy-start.8
  40.6 0.0 copy-start.9
  40.6 0.1 collective-permute-start.13
  40.7 2.3 %shard_map.124.refs_8_ = f32[1024,128]{1,0:T(8,128)S(1)} custom-call(s32[16]{0:T(128)S(1)} %dynamic-slice_bitcast_fusion.offs_ref.refs_0_, f32[1024,128]{1,0:T(8,128)S(1)} %shard_map.123.acc_ref, bf16[128,16384]{1,0:T(8,128)(2,1)S(1)} %get-tuple-element.91.refs_3_.refs_0_.refs_5_.refs_8_.refs_7_, ...), custom_call_target="tpu_custom_call" | custom-call | flops 50331648 | bytes 393216 | tf_op jit(solution)/shard_map/pallas_call | solution.py:56
  43.1 2.1 %shard_map.125 = (f32[128,1024]{1,0:T(8,128)S(1)}, bf16[128,1024]{1,0:T(8,128)(2,1)S(1)}, bf16[1024,128]{1,0:T(8,128)(2,1)S(1)}, f32[16,1024]{1,0:T(8,128)}, f32[1,1024]{1,0:T(1,128)}, /*index=5*/f32[1,1024]{1,0:T(1,128)}) custom-call(s32[16]{0:T(128)S(1)} %dynamic-slice_bitcast_fusion.offs_ref.refs_0_, ...), custom_call_target="tpu_custom_call" | custom-call | flops 33554432 | bytes 262144 | tf_op jit(solution)/shard_map/pallas_call | solution.py:56
  45.1 1.3 %shard_map.126 = (bf16[128,1024]{1,0:T(8,128)(2,1)S(1)}, f32[128,1024]{1,0:T(8,128)S(1)}) custom-call(s32[16]{0:T(128)S(1)} %dynamic-slice_bitcast_fusion.offs_ref.refs_0_, bf16[128,1024]{1,0:T(8,128)(2,1)S(1)} %get-tuple-element.116.refs_1_, bf16[1024,128]{1,0:T(8,128)(2,1)S(1)} %get-tuple-element.117.refs_2_, ...), custom_call_target="tpu_custom_call" | custom-call | flops 33554432 | bytes 262144 | tf_op jit(solution)/shard_map/pallas_call | solution.py:56
  46.4 0.5 collective-permute-start.16
  47.0 1.8 %shard_map.127 = (bf16[128,1024]{1,0:T(8,128)(2,1)S(1)}, bf16[128,1024]{1,0:T(8,128)(2,1)S(1)}, f32[128,1024]{1,0:T(8,128)S(1)}, f32[128,1024]{1,0:T(8,128)S(1)}) custom-call(s32[16]{0:T(128)S(1)} %dynamic-slice_bitcast_fusion.offs_ref.refs_0_, bf16[128,1024]{1,0:T(8,128)(2,1)S(1)} %get-tuple-element.116.refs_1_, ...), custom_call_target="tpu_custom_call" | custom-call | flops 67108864 | bytes 524288 | tf_op jit(solution)/shard_map/pallas_call | solution.py:56
  48.8 0.0 copy-start.1
  48.8 0.0 copy-start.5
  48.8 0.1 collective-permute-start.17
  48.9 0.5 collective-permute-start.20
  49.4 0.1 add_convert_fusion.4
  49.5 1.7 %collective-permute-start.19 = (bf16[64,1024]{1,0:T(8,128)(2,1)S(1)}, bf16[64,1024]{1,0:T(8,128)(2,1)S(1)}, u32[]{:S(2)}, u32[]{:S(2)}) collective-permute-start(bf16[64,1024]{1,0:T(8,128)(2,1)S(1)} %get-tuple-element.169), channel_id=1, source_target_pairs={{0,4},{1,5},{2,0},{3,1},{6,2},{7,3},{10,6},{11,7},{14,10},{15,11},... | collective-permute-start | bytes 393224 | tf_op jit(solution)/shard_map/ppermute | solution.py:390
  51.2 0.4 collective-permute-start.18
  51.6 0.1 convert_add_fusion
  51.8 4.3 %shard_map.128 = (bf16[128,1024]{1,0:T(8,128)(2,1)S(1)}, bf16[128,1024]{1,0:T(8,128)(2,1)S(1)}, f32[128,1024]{1,0:T(8,128)S(1)}, f32[128,1024]{1,0:T(8,128)S(1)}...) custom-call(s32[16]{0:T(128)S(1)} %dynamic-slice_bitcast_fusion.offs_ref.refs_0_, ...), custom_call_target="tpu_custom_call" | custom-call | flops 100663296 | bytes 786432 | tf_op jit(solution)/shard_map/pallas_call | solution.py:56
  56.2 0.2 collective-permute-done.18
  56.5 1.4 %collective-permute-start.21 = (bf16[128,1024]{1,0:T(8,128)(2,1)S(1)}, bf16[128,1024]{1,0:T(8,128)(2,1)S(1)}, u32[]{:S(2)}, u32[]{:S(2)}) collective-permute-start(bf16[128,1024]{1,0:T(8,128)(2,1)S(1)} %pad_maximum_fusion), channel_id=1, source_target_pairs={{0,2},{1,3},{2,6},{3,7},{6,10},{7,11},{10,14},{11,15},{14,12},{15,... | collective-permute-start | bytes 786440 | tf_op jit(solution)/shard_map/ppermute | solution.py:390
  57.9 0.7 collective-permute-start.22
  58.6 0.5 collective-permute-start.25
  59.1 7.4 %shard_map.129 = (bf16[128,1024]{1,0:T(8,128)(2,1)S(1)}, bf16[128,1024]{1,0:T(8,128)(2,1)S(1)}, f32[128,1024]{1,0:T(8,128)S(1)}, f32[128,1024]{1,0:T(8,128)S(1)}...) custom-call(s32[16]{0:T(128)S(1)} %dynamic-slice_bitcast_fusion.offs_ref.refs_0_, ...), custom_call_target="tpu_custom_call", output_to_operand_aliasing={{4}: (16, {})} | custom-call | flops 150994944 | bytes 1179648 | tf_op jit(solution)/shard_map/pallas_call | solution.py:56
  66.5 0.1 add_convert_fusion.3
  66.6 0.1 add_convert_fusion.2
  66.7 1.4 %collective-permute-start.26 = (bf16[128,1024]{1,0:T(8,128)(2,1)S(1)}, bf16[128,1024]{1,0:T(8,128)(2,1)S(1)}, u32[]{:S(2)}, u32[]{:S(2)}) collective-permute-start(bf16[128,1024]{1,0:T(8,128)(2,1)S(1)} %add_convert_fusion.3), channel_id=1, source_target_pairs={{0,2},{1,3},{2,6},{3,7},{6,10},{7,11},{10,14},{11,15},{14,12},{15,... | collective-permute-start | bytes 786440 | tf_op jit(solution)/shard_map/ppermute | solution.py:390
  68.2 0.7 collective-permute-start.27
  68.8 0.5 collective-permute-start.23
  69.3 6.3 %shard_map.130 = (bf16[128,1024]{1,0:T(8,128)(2,1)S(1)}, f32[128,1024]{1,0:T(8,128)S(1)}, bf16[1024,16384]{1,0:T(8,128)(2,1)}, f32[8,128]{1,0:T(8,128)}) custom-call(s32[16]{0:T(128)S(1)} %dynamic-slice_bitcast_fusion.offs_ref.refs_0_, bf16[128,1024]{1,0:T(8,128)(2,1)S(1)} %get-tuple-element.116.refs_1_, ...), custom_call_target="tpu_custom_call", output_to_operand_aliasing={{2}: (16, {})} | custom-call | flops 117440512 | bytes 917504 | tf_op jit(solution)/shard_map/pallas_call | solution.py:56
  75.7 0.4 collective-permute-done.27
  76.1 0.1 add_convert_fusion
  76.2 0.1 add_convert_fusion.1
  76.3 1.6 %collective-permute-start.29 = (bf16[128,1024]{1,0:T(8,128)(2,1)S(1)}, bf16[128,1024]{1,0:T(8,128)(2,1)S(1)}, u32[]{:S(2)}, u32[]{:S(2)}) collective-permute-start(bf16[128,1024]{1,0:T(8,128)(2,1)S(1)} %add_convert_fusion.1), channel_id=1, source_target_pairs={{0,2},{1,3},{2,6},{3,7},{6,10},{7,11},{10,14},{11,15},{14,12},{15,... | collective-permute-start | bytes 786440 | tf_op jit(solution)/shard_map/ppermute | solution.py:390
  77.9 0.5 collective-permute-start.30
  78.4 0.6 shard_map.132
  79.0 5.2 %shard_map.131 = (bf16[1024,16384]{1,0:T(8,128)(2,1)}, f32[8,128]{1,0:T(8,128)}) custom-call(s32[16]{0:T(128)S(1)} %dynamic-slice_bitcast_fusion.offs_ref.refs_0_, bf16[128,1024]{1,0:T(8,128)(2,1)S(1)} %get-tuple-element.116.refs_1_, bf16[1024,128]{1,0:T(8,128)(2,1)S(1)} %get-tuple-element.117.refs_2_, ...), custom_call_target="tpu_custom_call", output_to_operand_aliasing={{0}: (15, {})} | custom-call | flops 67108864 | bytes 524288 | tf_op jit(solution)/shard_map/pallas_call | solution.py:56
  84.3 1.0 %collective-permute-done.30 = bf16[128,1024]{1,0:T(8,128)(2,1)S(1)} collective-permute-done((bf16[128,1024]{1,0:T(8,128)(2,1)S(1)}, bf16[128,1024]{1,0:T(8,128)(2,1)S(1)}, u32[]{:S(2)}, u32[]{:S(2)}) %collective-permute-start.30) | collective-permute-done | bytes 262176 | tf_op jit(solution)/shard_map/ppermute | solution.py:390
  85.3 1.0 %add_bitcast_fusion = f32[1,128,1024]{2,1,0:T(8,128)} fusion(bf16[128,1024]{1,0:T(8,128)(2,1)S(1)} %collective-permute-done.30, bf16[128,1024]{1,0:T(8,128)(2,1)S(1)} %collective-permute-done.29, f32[128,1024]{1,0:T(8,128)S(1)} %shard_map.132, f32[128,1024]{1,0:T(8,128)S(1)} %get-tuple-element.162, bf16[128,1024]{1,0:T(8,128)(2,1)S(1)} %collective-permute-done.31), kind=kLoop, calls=%fused_computation | loop fusion | flops 917504 | bytes 2359296 | tf_op jit(solution)/shard_map/reshape | solution.py:483
  (54 shorter events, 0.3 us)
Async XLA Ops:
  1.7 11.7 %collective-permute-start.1 = (bf16[128,1024]{1,0:T(8,128)(2,1)S(1)}, bf16[128,1024]{1,0:T(8,128)(2,1)S(1)}, u32[]{:S(2)}, u32[]{:S(2)}) collective-permute-start(bf16[128,1024]{1,0:T(8,128)(2,1)S(1)} %bitcast_convert_fusion.x_ref.refs_8_.refs_3_), channel_id=1, source_target_pairs={{0,4},{1,5},{2,0},{3,1},{6,2},{7,3},{10,6},{11,7},{14,10},{15,11},... | collective-permute-start | bytes 786440 | tf_op jit(solution)/shard_map/ppermute | solution.py:390
  4.8 8.6 %collective-permute-start = (bf16[128,1024]{1,0:T(8,128)(2,1)S(1)}, bf16[128,1024]{1,0:T(8,128)(2,1)}, u32[]{:S(2)}, u32[]{:S(2)}) collective-permute-start(bf16[128,1024]{1,0:T(8,128)(2,1)S(1)} %bitcast_convert_fusion.x_ref.refs_8_.refs_3_), channel_id=1, source_target_pairs={{0,2},{1,3},{2,6},{3,7},{6,10},{7,11},{10,14},{11,15},{14,12},{15,... | collective-permute-start | bytes 786440 | tf_op jit(solution)/shard_map/ppermute | solution.py:390
  4.8 11.3 %collective-permute-start.4 = (bf16[128,1024]{1,0:T(8,128)(2,1)S(1)}, bf16[128,1024]{1,0:T(8,128)(2,1)S(1)}, u32[]{:S(2)}, u32[]{:S(2)}) collective-permute-start(bf16[128,1024]{1,0:T(8,128)(2,1)S(1)} %bitcast_convert_fusion.x_ref.refs_8_.refs_3_), channel_id=1, source_target_pairs={{0,1},{1,0},{2,3},{3,2},{4,5},{5,4},{6,7},{7,6},{8,9},{9,8},{10,11... | collective-permute-start | bytes 786440 | tf_op jit(solution)/shard_map/ppermute | solution.py:393
  13.4 11.7 %collective-permute-start.2 = (bf16[128,1024]{1,0:T(8,128)(2,1)}, bf16[128,1024]{1,0:T(8,128)(2,1)S(1)}, u32[]{:S(2)}, u32[]{:S(2)}) collective-permute-start(bf16[128,1024]{1,0:T(8,128)(2,1)} %collective-permute-done.refs_10_.refs_3_), channel_id=1, source_target_pairs={{0,2},{1,3},{2,6},{3,7},{6,10},{7,11},{10,14},{11,15},{14,12},{15,... | collective-permute-start | bytes 786440 | tf_op jit(solution)/shard_map/ppermute | solution.py:390
  15.4 9.7 %collective-permute-start.3 = (bf16[128,1024]{1,0:T(8,128)(2,1)S(1)}, bf16[128,1024]{1,0:T(8,128)(2,1)S(1)}, u32[]{:S(2)}, u32[]{:S(2)}) collective-permute-start(bf16[128,1024]{1,0:T(8,128)(2,1)S(1)} %collective-permute-done.1.refs_11_.refs_4_), channel_id=1, source_target_pairs={{0,4},{1,5},{2,0},{3,1},{6,2},{7,3},{10,6},{11,7},{14,10},{15,11},... | collective-permute-start | bytes 786440 | tf_op jit(solution)/shard_map/ppermute | solution.py:390
  15.6 11.7 %collective-permute-start.7 = (bf16[128,1024]{1,0:T(8,128)(2,1)}, bf16[128,1024]{1,0:T(8,128)(2,1)S(1)}, u32[]{:S(2)}, u32[]{:S(2)}) collective-permute-start(bf16[128,1024]{1,0:T(8,128)(2,1)} %collective-permute-done.refs_10_.refs_3_), channel_id=1, source_target_pairs={{0,1},{1,0},{2,3},{3,2},{4,5},{5,4},{6,7},{7,6},{8,9},{9,8},{10,11... | collective-permute-start | bytes 786440 | tf_op jit(solution)/shard_map/ppermute | solution.py:393
  15.8 13.2 %collective-permute-start.8 = (bf16[128,1024]{1,0:T(8,128)(2,1)S(1)}, bf16[128,1024]{1,0:T(8,128)(2,1)S(1)}, u32[]{:S(2)}, u32[]{:S(2)}) collective-permute-start(bf16[128,1024]{1,0:T(8,128)(2,1)S(1)} %collective-permute-done.1.refs_11_.refs_4_), channel_id=1, source_target_pairs={{0,1},{1,0},{2,3},{3,2},{4,5},{5,4},{6,7},{7,6},{8,9},{9,8},{10,11... | collective-permute-start | bytes 786440 | tf_op jit(solution)/shard_map/ppermute | solution.py:393
  16.1 0.7 copy-start.3
  16.8 0.9 %copy-start.4 = (bf16[128,1024]{1,0:T(8,128)(2,1)S(1)}, bf16[128,1024]{1,0:T(8,128)(2,1)}, u32[]{:S(2)}) copy-start(bf16[128,1024]{1,0:T(8,128)(2,1)} %copy-done.3) | copy-start | bytes 786436
  17.7 10.7 %copy-start.2 = (f32[1,128,1024]{2,1,0:T(8,128)S(1)}, f32[1,128,1024]{2,1,0:T(8,128)}, u32[]{:S(2)}) copy-start(f32[1,128,1024]{2,1,0:T(8,128)} %param.8) | copy-start | bytes 1572868
  17.7 10.7 %copy-start.6 = (f32[128,128]{1,0:T(8,128)S(1)}, f32[128,128]{1,0:T(8,128)}, u32[]{:S(2)}) copy-start(f32[128,128]{1,0:T(8,128)} %constant.13.clone.cheb_ref) | copy-start | bytes 196612
  17.7 10.7 %copy-start.7 = (f32[16,1024]{1,0:T(8,128)S(1)}, f32[16,1024]{1,0:T(8,128)}, u32[]{:S(2)}) copy-start(f32[16,1024]{1,0:T(8,128)} %pert_ref.1) | copy-start | bytes 196612
  25.1 21.8 %copy-start = (bf16[128,16384]{1,0:T(8,128)(2,1)}, bf16[128,16384]{1,0:T(8,128)(2,1)S(1)}, u32[]{:S(2)}) copy-start(bf16[128,16384]{1,0:T(8,128)(2,1)S(1)} %get-tuple-element.102.refs_7_.refs_10_.refs_12_.refs_15_.refs_14_) | copy-start | bytes 12582916
  25.2 8.5 %collective-permute-start.5 = (bf16[128,1024]{1,0:T(8,128)(2,1)S(1)}, bf16[128,1024]{1,0:T(8,128)(2,1)S(1)}, u32[]{:S(2)}, u32[]{:S(2)}) collective-permute-start(bf16[128,1024]{1,0:T(8,128)(2,1)S(1)} %collective-permute-done.2.refs_10_.refs_7_), channel_id=1, source_target_pairs={{0,2},{1,3},{2,6},{3,7},{6,10},{7,11},{10,14},{11,15},{14,12},{15,... | collective-permute-start | bytes 786440 | tf_op jit(solution)/shard_map/ppermute | solution.py:390
  27.1 7.9 %collective-permute-start.6 = (bf16[128,1024]{1,0:T(8,128)(2,1)S(1)}, bf16[128,1024]{1,0:T(8,128)(2,1)S(1)}, u32[]{:S(2)}, u32[]{:S(2)}) collective-permute-start(bf16[128,1024]{1,0:T(8,128)(2,1)S(1)} %collective-permute-done.3.refs_11_.refs_3_), channel_id=1, source_target_pairs={{0,4},{1,5},{2,0},{3,1},{6,2},{7,3},{10,6},{11,7},{14,10},{15,11},... | collective-permute-start | bytes 786440 | tf_op jit(solution)/shard_map/ppermute | solution.py:390
  27.2 9.9 %collective-permute-start.11 = (bf16[128,1024]{1,0:T(8,128)(2,1)S(1)}, bf16[128,1024]{1,0:T(8,128)(2,1)S(1)}, u32[]{:S(2)}, u32[]{:S(2)}) collective-permute-start(bf16[128,1024]{1,0:T(8,128)(2,1)S(1)} %collective-permute-done.2.refs_10_.refs_7_), channel_id=1, source_target_pairs={{0,1},{1,0},{2,3},{3,2},{4,5},{5,4},{6,7},{7,6},{8,9},{9,8},{10,11... | collective-permute-start | bytes 786440 | tf_op jit(solution)/shard_map/ppermute | solution.py:393
  27.2 10.4 %collective-permute-start.12 = (bf16[128,1024]{1,0:T(8,128)(2,1)S(1)}, bf16[128,1024]{1,0:T(8,128)(2,1)S(1)}, u32[]{:S(2)}, u32[]{:S(2)}) collective-permute-start(bf16[128,1024]{1,0:T(8,128)(2,1)S(1)} %collective-permute-done.3.refs_11_.refs_3_), channel_id=1, source_target_pairs={{0,1},{1,0},{2,3},{3,2},{4,5},{5,4},{6,7},{7,6},{8,9},{9,8},{10,11... | collective-permute-start | bytes 786440 | tf_op jit(solution)/shard_map/ppermute | solution.py:393
  35.1 5.5 %collective-permute-start.10 = (bf16[64,1024]{1,0:T(8,128)(2,1)S(1)}, bf16[64,1024]{1,0:T(8,128)(2,1)S(1)}, u32[]{:S(2)}, u32[]{:S(2)}) collective-permute-start(bf16[64,1024]{1,0:T(8,128)(2,1)S(1)} %slice.27), channel_id=1, source_target_pairs={{0,4},{1,5},{2,0},{3,1},{6,2},{7,3},{10,6},{11,7},{14,10},{15,11},... | collective-permute-start | bytes 393224 | tf_op jit(solution)/shard_map/ppermute | solution.py:390
  35.5 5.0 %collective-permute-start.9 = (bf16[64,1024]{1,0:T(8,128)(2,1)S(1)}, bf16[64,1024]{1,0:T(8,128)(2,1)S(1)}, u32[]{:S(2)}, u32[]{:S(2)}) collective-permute-start(bf16[64,1024]{1,0:T(8,128)(2,1)S(1)} %slice.26), channel_id=1, source_target_pairs={{0,2},{1,3},{2,6},{3,7},{6,10},{7,11},{10,14},{11,15},{14,12},{15,... | collective-permute-start | bytes 393224 | tf_op jit(solution)/shard_map/ppermute | solution.py:390
  37.1 3.6 %collective-permute-start.14 = (bf16[128,1024]{1,0:T(8,128)(2,1)S(1)}, bf16[128,1024]{1,0:T(8,128)(2,1)S(1)}, u32[]{:S(2)}, u32[]{:S(2)}) collective-permute-start(bf16[128,1024]{1,0:T(8,128)(2,1)S(1)} %collective-permute-done.5.refs_10_.refs_6_), channel_id=1, source_target_pairs={{0,1},{1,0},{2,3},{3,2},{4,5},{5,4},{6,7},{7,6},{8,9},{9,8},{10,11... | collective-permute-start | bytes 786440 | tf_op jit(solution)/shard_map/ppermute | solution.py:393
  37.1 3.6 %collective-permute-start.15 = (bf16[128,1024]{1,0:T(8,128)(2,1)S(1)}, bf16[128,1024]{1,0:T(8,128)(2,1)S(1)}, u32[]{:S(2)}, u32[]{:S(2)}) collective-permute-start(bf16[128,1024]{1,0:T(8,128)(2,1)S(1)} %collective-permute-done.6.refs_11_.refs_7_), channel_id=1, source_target_pairs={{0,1},{1,0},{2,3},{3,2},{4,5},{5,4},{6,7},{7,6},{8,9},{9,8},{10,11... | collective-permute-start | bytes 786440 | tf_op jit(solution)/shard_map/ppermute | solution.py:393
  40.6 2.5 %copy-start.8 = (f32[1024]{0:T(1024)S(1)}, f32[1024]{0:T(1024)}, u32[]{:S(2)}) copy-start(f32[1024]{0:T(1024)} %param.12) | copy-start | bytes 12292
  40.6 2.5 %copy-start.9 = (f32[1024]{0:T(1024)S(1)}, f32[1024]{0:T(1024)}, u32[]{:S(2)}) copy-start(f32[1024]{0:T(1024)} %param.11) | copy-start | bytes 12292
  40.6 2.4 %collective-permute-start.13 = (bf16[128,1024]{1,0:T(8,128)(2,1)S(1)}, bf16[128,1024]{1,0:T(8,128)(2,1)S(1)}, u32[]{:S(2)}, u32[]{:S(2)}) collective-permute-start(bf16[128,1024]{1,0:T(8,128)(2,1)S(1)} %constant_dynamic-update-slice_fusion.refs_10_.refs_5_), channel_id=1, source_target_pairs={{0,1},{1,0},{2,3},{3,2},{4,5},{5,4},{6,7},{7,6},{8,9},{9,8},{10,11... | collective-permute-start | bytes 786440 | tf_op jit(solution)/shard_map/ppermute | solution.py:393
  46.4 3.0 %collective-permute-start.16 = (bf16[128,1024]{1,0:T(8,128)(2,1)S(1)}, bf16[128,1024]{1,0:T(8,128)(2,1)S(1)}, u32[]{:S(2)}, u32[]{:S(2)}) collective-permute-start(bf16[128,1024]{1,0:T(8,128)(2,1)S(1)} %get-tuple-element.119), channel_id=1, source_target_pairs={{0,1},{1,0},{2,3},{3,2},{4,5},{5,4},{6,7},{7,6},{8,9},{9,8},{10,11... | collective-permute-start | bytes 786440 | tf_op jit(solution)/shard_map/ppermute | solution.py:393
  48.8 3.0 %copy-start.1 = (bf16[128,16384]{1,0:T(8,128)(2,1)S(1)}, bf16[128,16384]{1,0:T(8,128)(2,1)}, u32[]{:S(2)}) copy-start(bf16[128,16384]{1,0:T(8,128)(2,1)} %copy-done) | copy-start | bytes 12582916
  48.8 3.0 %copy-start.5 = (bf16[128,1024]{1,0:T(8,128)(2,1)S(1)}, bf16[128,1024]{1,0:T(8,128)(2,1)}, u32[]{:S(2)}) copy-start(bf16[128,1024]{1,0:T(8,128)(2,1)} %copy-done.3) | copy-start | bytes 786436
  48.8 2.8 %collective-permute-start.17 = (bf16[128,1024]{1,0:T(8,128)(2,1)S(1)}, bf16[128,1024]{1,0:T(8,128)(2,1)S(1)}, u32[]{:S(2)}, u32[]{:S(2)}) collective-permute-start(bf16[128,1024]{1,0:T(8,128)(2,1)S(1)} %get-tuple-element.123), channel_id=1, source_target_pairs={{0,1},{1,0},{2,3},{3,2},{4,5},{5,4},{6,7},{7,6},{8,9},{9,8},{10,11... | collective-permute-start | bytes 786440 | tf_op jit(solution)/shard_map/ppermute | solution.py:393
  48.9 2.7 %collective-permute-start.20 = (bf16[128,1024]{1,0:T(8,128)(2,1)S(1)}, bf16[128,1024]{1,0:T(8,128)(2,1)S(1)}, u32[]{:S(2)}, u32[]{:S(2)}) collective-permute-start(bf16[128,1024]{1,0:T(8,128)(2,1)S(1)} %get-tuple-element.130), channel_id=1, source_target_pairs={{0,1},{1,0},{2,3},{3,2},{4,5},{5,4},{6,7},{7,6},{8,9},{9,8},{10,11... | collective-permute-start | bytes 786440 | tf_op jit(solution)/shard_map/ppermute | solution.py:393
  49.5 6.7 %collective-permute-start.19 = (bf16[64,1024]{1,0:T(8,128)(2,1)S(1)}, bf16[64,1024]{1,0:T(8,128)(2,1)S(1)}, u32[]{:S(2)}, u32[]{:S(2)}) collective-permute-start(bf16[64,1024]{1,0:T(8,128)(2,1)S(1)} %get-tuple-element.169), channel_id=1, source_target_pairs={{0,4},{1,5},{2,0},{3,1},{6,2},{7,3},{10,6},{11,7},{14,10},{15,11},... | collective-permute-start | bytes 393224 | tf_op jit(solution)/shard_map/ppermute | solution.py:390
  51.2 5.2 %collective-permute-start.18 = (bf16[64,1024]{1,0:T(8,128)(2,1)S(1)}, bf16[64,1024]{1,0:T(8,128)(2,1)S(1)}, u32[]{:S(2)}, u32[]{:S(2)}) collective-permute-start(bf16[64,1024]{1,0:T(8,128)(2,1)S(1)} %get-tuple-element.170), channel_id=1, source_target_pairs={{0,2},{1,3},{2,6},{3,7},{6,10},{7,11},{10,14},{11,15},{14,12},{15,... | collective-permute-start | bytes 393224 | tf_op jit(solution)/shard_map/ppermute | solution.py:390
  56.5 10.0 %collective-permute-start.21 = (bf16[128,1024]{1,0:T(8,128)(2,1)S(1)}, bf16[128,1024]{1,0:T(8,128)(2,1)S(1)}, u32[]{:S(2)}, u32[]{:S(2)}) collective-permute-start(bf16[128,1024]{1,0:T(8,128)(2,1)S(1)} %pad_maximum_fusion), channel_id=1, source_target_pairs={{0,2},{1,3},{2,6},{3,7},{6,10},{7,11},{10,14},{11,15},{14,12},{15,... | collective-permute-start | bytes 786440 | tf_op jit(solution)/shard_map/ppermute | solution.py:390
  57.9 8.6 %collective-permute-start.22 = (bf16[128,1024]{1,0:T(8,128)(2,1)S(1)}, bf16[128,1024]{1,0:T(8,128)(2,1)S(1)}, u32[]{:S(2)}, u32[]{:S(2)}) collective-permute-start(bf16[128,1024]{1,0:T(8,128)(2,1)S(1)} %pad_maximum_fusion.1), channel_id=1, source_target_pairs={{0,4},{1,5},{2,0},{3,1},{6,2},{7,3},{10,6},{11,7},{14,10},{15,11},... | collective-permute-start | bytes 786440 | tf_op jit(solution)/shard_map/ppermute | solution.py:390
  58.6 7.9 %collective-permute-start.24 = (bf16[128,1024]{1,0:T(8,128)(2,1)S(1)}, bf16[128,1024]{1,0:T(8,128)(2,1)S(1)}, u32[]{:S(2)}, u32[]{:S(2)}) collective-permute-start(bf16[128,1024]{1,0:T(8,128)(2,1)S(1)} %get-tuple-element.141), channel_id=1, source_target_pairs={{0,1},{1,0},{2,3},{3,2},{4,5},{5,4},{6,7},{7,6},{8,9},{9,8},{10,11... | collective-permute-start | bytes 786440 | tf_op jit(solution)/shard_map/ppermute | solution.py:393
  58.6 8.0 %collective-permute-start.25 = (bf16[128,1024]{1,0:T(8,128)(2,1)S(1)}, bf16[128,1024]{1,0:T(8,128)(2,1)S(1)}, u32[]{:S(2)}, u32[]{:S(2)}) collective-permute-start(bf16[128,1024]{1,0:T(8,128)(2,1)S(1)} %get-tuple-element.144), channel_id=1, source_target_pairs={{0,1},{1,0},{2,3},{3,2},{4,5},{5,4},{6,7},{7,6},{8,9},{9,8},{10,11... | collective-permute-start | bytes 786440 | tf_op jit(solution)/shard_map/ppermute | solution.py:393
  66.7 8.9 %collective-permute-start.26 = (bf16[128,1024]{1,0:T(8,128)(2,1)S(1)}, bf16[128,1024]{1,0:T(8,128)(2,1)S(1)}, u32[]{:S(2)}, u32[]{:S(2)}) collective-permute-start(bf16[128,1024]{1,0:T(8,128)(2,1)S(1)} %add_convert_fusion.3), channel_id=1, source_target_pairs={{0,2},{1,3},{2,6},{3,7},{6,10},{7,11},{10,14},{11,15},{14,12},{15,... | collective-permute-start | bytes 786440 | tf_op jit(solution)/shard_map/ppermute | solution.py:390
  68.2 7.9 %collective-permute-start.27 = (bf16[128,1024]{1,0:T(8,128)(2,1)S(1)}, bf16[128,1024]{1,0:T(8,128)(2,1)S(1)}, u32[]{:S(2)}, u32[]{:S(2)}) collective-permute-start(bf16[128,1024]{1,0:T(8,128)(2,1)S(1)} %add_convert_fusion.2), channel_id=1, source_target_pairs={{0,4},{1,5},{2,0},{3,1},{6,2},{7,3},{10,6},{11,7},{14,10},{15,11},... | collective-permute-start | bytes 786440 | tf_op jit(solution)/shard_map/ppermute | solution.py:390
  68.8 7.3 %collective-permute-start.28 = (bf16[128,1024]{1,0:T(8,128)(2,1)S(1)}, bf16[128,1024]{1,0:T(8,128)(2,1)S(1)}, u32[]{:S(2)}, u32[]{:S(2)}) collective-permute-start(bf16[128,1024]{1,0:T(8,128)(2,1)S(1)} %get-tuple-element.153), channel_id=1, source_target_pairs={{0,1},{1,0},{2,3},{3,2},{4,5},{5,4},{6,7},{7,6},{8,9},{9,8},{10,11... | collective-permute-start | bytes 786440 | tf_op jit(solution)/shard_map/ppermute | solution.py:393
  68.8 7.4 %collective-permute-start.23 = (bf16[128,1024]{1,0:T(8,128)(2,1)S(1)}, bf16[128,1024]{1,0:T(8,128)(2,1)S(1)}, u32[]{:S(2)}, u32[]{:S(2)}) collective-permute-start(bf16[128,1024]{1,0:T(8,128)(2,1)S(1)} %get-tuple-element.139), channel_id=1, source_target_pairs={{0,1},{1,0},{2,3},{3,2},{4,5},{5,4},{6,7},{7,6},{8,9},{9,8},{10,11... | collective-permute-start | bytes 786440 | tf_op jit(solution)/shard_map/ppermute | solution.py:393
  76.3 8.0 %collective-permute-start.29 = (bf16[128,1024]{1,0:T(8,128)(2,1)S(1)}, bf16[128,1024]{1,0:T(8,128)(2,1)S(1)}, u32[]{:S(2)}, u32[]{:S(2)}) collective-permute-start(bf16[128,1024]{1,0:T(8,128)(2,1)S(1)} %add_convert_fusion.1), channel_id=1, source_target_pairs={{0,2},{1,3},{2,6},{3,7},{6,10},{7,11},{10,14},{11,15},{14,12},{15,... | collective-permute-start | bytes 786440 | tf_op jit(solution)/shard_map/ppermute | solution.py:390
  77.9 7.4 %collective-permute-start.30 = (bf16[128,1024]{1,0:T(8,128)(2,1)S(1)}, bf16[128,1024]{1,0:T(8,128)(2,1)S(1)}, u32[]{:S(2)}, u32[]{:S(2)}) collective-permute-start(bf16[128,1024]{1,0:T(8,128)(2,1)S(1)} %add_convert_fusion), channel_id=1, source_target_pairs={{0,4},{1,5},{2,0},{3,1},{6,2},{7,3},{10,6},{11,7},{14,10},{15,11},... | collective-permute-start | bytes 786440 | tf_op jit(solution)/shard_map/ppermute | solution.py:390
  78.4 6.9 %collective-permute-start.31 = (bf16[128,1024]{1,0:T(8,128)(2,1)S(1)}, bf16[128,1024]{1,0:T(8,128)(2,1)S(1)}, u32[]{:S(2)}, u32[]{:S(2)}) collective-permute-start(bf16[128,1024]{1,0:T(8,128)(2,1)S(1)} %get-tuple-element.163), channel_id=1, source_target_pairs={{0,1},{1,0},{2,3},{3,2},{4,5},{5,4},{6,7},{7,6},{8,9},{9,8},{10,11... | collective-permute-start | bytes 786440 | tf_op jit(solution)/shard_map/ppermute | solution.py:393

commit v6 on v5

--- a/solution.py
+++ b/solution.py
@@ -11,7 +11,7 @@
 SCALE = 2.0 / 1024.0
 VMEM_LIMIT = 4 * 2**20
 BANDS = 8
-FIRST_BANDS = 5
+FIRST_BANDS = 4
 LONGEST_RING = 16
 
 
@@ -89,7 +89,7 @@
     )
 
 
-def first_kernel(base, offs_ref, w_ref, x_ref, out_ref, *refs):
+def first_kernel(base, offs_ref, perts_ref, w_ref, x_ref, out_ref, *refs):
     bands, sems = refs[:-1], refs[-1]
     here = columns_of(offs_ref, base, x_ref.shape[1])
     tile = bands[0].shape[0]
@@ -105,30 +105,27 @@
     slab, tile = xs[0].shape[1], bands[0].shape[0]
     copies = load_bands(w_ref, late, sems, early)
     places = [columns_of(offs_ref, base + at, slab) for at in range(count)]
-    for low in range(0, early, 2):
-        pair = bands[low : low + 2]
-        rows = pl.ds(low * tile, len(pair) * tile)
-        total = acc_ref[rows, :]
-        for at in range(1, count):
-            total += product(pair, places[at], xs[at])
-        out_ref[rows, :] = total
-    for at, copy in enumerate(copies):
+    rows = pl.ds(0, early * tile)
+    total = acc_ref[rows, :]
+    for at in range(1, count):
+        total += product(bands, places[at], xs[at])
+    out_ref[rows, :] = total
+    for copy in copies:
         copy.wait()
-        rows = pl.ds((early + at) * tile, tile)
-        total = product(late[at : at + 1], places[0], xs[0])
-        for index in range(1, count):
-            total += product(late[at : at + 1], places[index], xs[index])
-        out_ref[rows, :] = total
+    total = product(late, places[0], xs[0])
+    for at in range(1, count):
+        total += product(late, places[at], xs[at])
+    out_ref[pl.ds(early * tile, len(late) * tile), :] = total
 
 
 def pre_kernel(base, count, many, offs_ref, acc_ref, *refs):
     bands, xs, out_ref = refs[:many], refs[many:-1], refs[-1]
     slab, tile = xs[0].shape[1], bands[0].shape[0]
-    for low in range(0, many, 2):
-        rows = pl.ds(low * tile, 2 * tile)
+    for low in range(0, many, 4):
+        rows = pl.ds(low * tile, 4 * tile)
         total = acc_ref[rows, :]
         for at in range(count):
-            total += product(bands[low : low + 2], columns_of(offs_ref, base + at, slab), xs[at])
+            total += product(bands[low : low + 4], columns_of(offs_ref, base + at, slab), xs[at])
         out_ref[rows, :] = total
 
 
@@ -136,7 +133,7 @@
     return [pltpu.VMEM((weights.shape[0] // BANDS, weights.shape[1]), weights.dtype)] * count
 
 
-def first_products(offs, base, x, weights):
+def first_products(offs, perts, base, x, weights):
     (nodes, slab), rows = x.shape, weights.shape[0]
     acc, *bands = call(
         functools.partial(first_kernel, base),
@@ -144,7 +141,7 @@
         [VMEM_REF] * (1 + FIRST_BANDS),
         [pltpu.SemaphoreType.DMA((FIRST_BANDS,))],
         cost(1, nodes, slab, rows),
-    )([offs, weights, x], [SMEM_REF, HBM_REF, VMEM_REF])
+    )([offs, perts, weights, x], [SMEM_REF, SMEM_REF, HBM_REF, VMEM_REF])
     return acc, bands
 
 
@@ -266,22 +263,22 @@
 
 
 def grad_w_part(base, offs_ref, delta_t_ref, xs, out_ref, held, sems):
-    slab = xs[0].shape[1]
-    slots, _, width = held.shape
-    step = min(256, width)
+    rows, slab = delta_t_ref.shape[0], xs[0].shape[1]
+    slots, tile = held.shape[:2]
+    step = min(256, slab)
     copies = []
     for at, x_ref in enumerate(xs):
-        for start in range(0, slab, width):
-            slot = len(copies) % slots
+        for start in range(0, rows, tile):
+            slot, band = len(copies) % slots, pl.ds(start, tile)
             if len(copies) >= slots:
                 copies[-slots].wait()
-            for col in range(0, width, step):
+            for col in range(0, slab, step):
                 held[slot, :, col : col + step] = jnp.dot(
-                    delta_t_ref[...], x_ref[:, start + col : start + col + step],
+                    delta_t_ref[band, :], x_ref[:, col : col + step],
                     preferred_element_type=jnp.float32,
                 ).astype(held.dtype)
-            there = pl.ds(pl.multiple_of(offs_ref[base + at] * slab + start, width), width)
-            copy = pltpu.make_async_copy(held.at[slot], out_ref.at[:, there], sems.at[slot])
+            there = columns_of(offs_ref, base + at, slab)
+            copy = pltpu.make_async_copy(held.at[slot], out_ref.at[band, there], sems.at[slot])
             copy.start()
             copies.append(copy)
     return copies[-slots:]
@@ -322,7 +319,7 @@
 def sums(offs, base, xs, places, delta, delta_t, bands, slab, so_far, shape):
     nodes, rows = delta.shape
     count, own = len(xs), len(places) // 2
-    width = max(slab // 2, 128)
+    tile = rows // 2
     first = so_far is None
     shapes = [jax.ShapeDtypeStruct((nodes, slab), jnp.bfloat16)] * own
     shapes += [jax.ShapeDtypeStruct((nodes, slab), jnp.float32)] * own
@@ -333,8 +330,8 @@
             jax.ShapeDtypeStruct((8, 128), jnp.float32),
         ]
         specs += [ANY_REF, VMEM_REF]
-        scratch = [pltpu.VMEM((4, rows, width), jnp.bfloat16), pltpu.SemaphoreType.DMA((4,))]
-        more = 4 * 2 * rows * width
+        scratch = [pltpu.VMEM((4, tile, slab), jnp.bfloat16), pltpu.SemaphoreType.DMA((4,))]
+        more = 4 * 2 * tile * slab
     operands = [offs, delta, delta_t, *xs, *bands] + ([] if first else [so_far])
     outs = call(
         functools.partial(sums_kernel, base, count, places, len(bands), first),
@@ -411,7 +408,7 @@
         count = {1: 1, 2: 3}.get(step, 4)
         xs = [x[key] for key in listing[base : base + count]]
         if step == 1:
-            acc, bands = first_products(offs, 0, xs[0], weights)
+            acc, bands = first_products(offs, perts, 0, xs[0], weights)
         elif step == 2:
             acc, bands = second_products(offs, 0, [x[0, 0], *xs], weights, acc, bands)
         else:

time: 86.6 us -> 89.2 us (1.030)
  Pallas kernels: 53 us -> 55 us
    pallas_call x14, Pallas kernels: 53 us -> 55 us  [run(): pl.pallas_call(kernel, out_shape=out_shape, in_specs=in_specs, out_specs=...]
  transfers between devices with their start and end apart: 32 -> 32, of which waited for: 5 -> 6; matrix products, arithmetic and copies ran while one was open for 1% -> 1% of each run, Pallas kernels for 58% -> 58%
where the time goes in v6:
time: 89.2 us; the launch traced here: 88.9 us
  Pallas kernels  55 us (62%)
  starting transfers between devices  21.4 us (24%)
  waiting for transfers between devices  5.49 us (6%)
  other arithmetic  2.76 us (3%)
  local copies, waits for them, and re-layouts  2.48 us (3%)
  between operations  1.74 us (2%)
    pallas_call x14, Pallas kernels, run(): pl.pallas_call(kernel, out_shape=out_shape, in_specs=in_specs, out_specs=...  55 us
    ppermute x16, starting transfers between devices, ring(): return lax.ppermute(array, 'row', pairs)  17.7 us
    ppermute x16, waiting for transfers between devices, ring(): return lax.ppermute(array, 'row', pairs)  5.45 us
    ppermute x16, starting transfers between devices, swap(): return lax.ppermute(array, 'row', [(i, i ^ 1) for i in range(2 * chips)])  3.74 us
  transfers between devices with their start and end apart: 32, of which 6 were waited for; matrix products, arithmetic and copies ran while one was open for 1% of the time, Pallas kernels for 58%

profile of v6, /device:TPU:0, one launch (start us, length us, event | category | flops | bytes accessed | tf_op | source)
XLA Modules:
  0.0 88.9 jit_solution(7368741185198243833)
XLA Ops:
  0.6 1.1 %bitcast_convert_fusion.x_ref.refs_7_.refs_3_ = bf16[128,1024]{1,0:T(8,128)(2,1)S(1)} fusion(f32[1,128,1024]{2,1,0:T(8,128)} %param.8), kind=kLoop, calls=%fused_computation.19 | loop fusion | flops 131072 | bytes 786432 | tf_op jit(solution)/shard_map/convert_element_type | solution.py:395
  1.7 3.1 %collective-permute-start.1 = (bf16[128,1024]{1,0:T(8,128)(2,1)S(1)}, bf16[128,1024]{1,0:T(8,128)(2,1)S(1)}, u32[]{:S(2)}, u32[]{:S(2)}) collective-permute-start(bf16[128,1024]{1,0:T(8,128)(2,1)S(1)} %bitcast_convert_fusion.x_ref.refs_7_.refs_3_), channel_id=1, source_target_pairs={{0,4},{1,5},{2,0},{3,1},{6,2},{7,3},{10,6},{11,7},{14,10},{15,11},... | collective-permute-start | bytes 786440 | tf_op jit(solution)/shard_map/ppermute | solution.py:387
  4.8 0.0 collective-permute-start
  4.8 0.0 collective-permute-start.4
  4.8 0.7 dynamic-slice_bitcast_fusion.offs_ref.refs_0_
  6.1 6.7 %shard_map.119 = (f32[1024,128]{1,0:T(8,128)S(1)}, bf16[128,16384]{1,0:T(8,128)(2,1)S(1)}, bf16[128,16384]{1,0:T(8,128)(2,1)S(1)}, bf16[128,16384]{1,0:T(8,128)(2,1)S(1)}, bf16[128,16384]{1,0:T(8,128)(2,1)S(1)}) custom-call(s32[16]{0:T(128)S(1)} %dynamic-slice_bitcast_fusion.offs_ref.refs_0_, s32[1]{0:T(128)S(6)} %copy.20.perts_ref, ...), custom_call_target="tpu_custom_call" | custom-call | flops 16777216 | bytes 131072 | tf_op jit(solution)/shard_map/pallas_call | solution.py:56
  12.9 0.0 collective-permute-done.1.refs_10_.refs_4_
  12.9 2.0 %collective-permute-start.2 = (bf16[128,1024]{1,0:T(8,128)(2,1)}, bf16[128,1024]{1,0:T(8,128)(2,1)S(1)}, u32[]{:S(2)}, u32[]{:S(2)}) collective-permute-start(bf16[128,1024]{1,0:T(8,128)(2,1)} %collective-permute-done.refs_9_.refs_3_), channel_id=1, source_target_pairs={{0,2},{1,3},{2,6},{3,7},{6,10},{7,11},{10,14},{11,15},{14,12},{15,... | collective-permute-start | bytes 786440 | tf_op jit(solution)/shard_map/ppermute | solution.py:387
  14.9 0.1 collective-permute-start.3
  15.0 0.2 collective-permute-start.7
  15.2 0.3 collective-permute-start.8
  15.5 0.7 copy-done.3
  16.2 0.9 %copy-done.4 = bf16[128,1024]{1,0:T(8,128)(2,1)S(1)} copy-done((bf16[128,1024]{1,0:T(8,128)(2,1)S(1)}, bf16[128,1024]{1,0:T(8,128)(2,1)}, u32[]{:S(2)}) %copy-start.4) | copy-done | bytes 262168
  17.2 10.4 %shard_map.120 = (f32[1024,128]{1,0:T(8,128)S(1)}, bf16[128,16384]{1,0:T(8,128)(2,1)S(1)}, bf16[128,16384]{1,0:T(8,128)(2,1)S(1)}, bf16[128,16384]{1,0:T(8,128)(2,1)S(1)}, bf16[128,16384]{1,0:T(8,128)(2,1)S(1)}) custom-call(s32[16]{0:T(128)S(1)} %dynamic-slice_bitcast_fusion.offs_ref.refs_0_, bf16[1024,16384]{1,0:T(8,128)(2,1)} %refs_1_.1, ...), custom_call_target="tpu_custom_call" | custom-call | flops 67108864 | bytes 524288 | tf_op jit(solution)/shard_map/pallas_call | solution.py:56
  27.6 0.0 copy-start
  27.7 1.9 %collective-permute-start.5 = (bf16[128,1024]{1,0:T(8,128)(2,1)S(1)}, bf16[128,1024]{1,0:T(8,128)(2,1)S(1)}, u32[]{:S(2)}, u32[]{:S(2)}) collective-permute-start(bf16[128,1024]{1,0:T(8,128)(2,1)S(1)} %collective-permute-done.2.refs_10_.refs_7_), channel_id=1, source_target_pairs={{0,2},{1,3},{2,6},{3,7},{6,10},{7,11},{10,14},{11,15},{14,12},{15,... | collective-permute-start | bytes 786440 | tf_op jit(solution)/shard_map/ppermute | solution.py:387
  29.6 0.1 collective-permute-start.6
  29.8 0.5 collective-permute-start.12
  30.3 0.6 shard_map.122
  30.9 2.9 %shard_map.121.acc_ref = f32[1024,128]{1,0:T(8,128)S(1)} custom-call(s32[16]{0:T(128)S(1)} %dynamic-slice_bitcast_fusion.offs_ref.refs_0_, f32[1024,128]{1,0:T(8,128)S(1)} %get-tuple-element.98.acc_ref, bf16[128,16384]{1,0:T(8,128)(2,1)S(1)} %get-tuple-element.91.refs_3_.refs_0_.refs_5_.refs_8_.refs_7_, ...), custom_call_target="tpu_custom_call" | custom-call | flops 67108864 | bytes 524288 | tf_op jit(solution)/shard_map/pallas_call | solution.py:56
  33.7 2.4 %collective-permute-done.5.refs_10_.refs_6_ = bf16[128,1024]{1,0:T(8,128)(2,1)S(1)} collective-permute-done((bf16[128,1024]{1,0:T(8,128)(2,1)S(1)}, bf16[128,1024]{1,0:T(8,128)(2,1)S(1)}, u32[]{:S(2)}, u32[]{:S(2)}) %collective-permute-start.5) | collective-permute-done | bytes 262176 | tf_op jit(solution)/shard_map/ppermute | solution.py:387
  36.2 1.4 %collective-permute-done.6.refs_11_.refs_7_ = bf16[128,1024]{1,0:T(8,128)(2,1)S(1)} collective-permute-done((bf16[128,1024]{1,0:T(8,128)(2,1)S(1)}, bf16[128,1024]{1,0:T(8,128)(2,1)S(1)}, u32[]{:S(2)}, u32[]{:S(2)}) %collective-permute-start.6) | collective-permute-done | bytes 262176 | tf_op jit(solution)/shard_map/ppermute | solution.py:387
  37.6 0.5 collective-permute-start.10
  38.0 1.6 %collective-permute-start.9 = (bf16[64,1024]{1,0:T(8,128)(2,1)S(1)}, bf16[64,1024]{1,0:T(8,128)(2,1)S(1)}, u32[]{:S(2)}, u32[]{:S(2)}) collective-permute-start(bf16[64,1024]{1,0:T(8,128)(2,1)S(1)} %slice.26), channel_id=1, source_target_pairs={{0,2},{1,3},{2,6},{3,7},{6,10},{7,11},{10,14},{11,15},{14,12},{15,... | collective-permute-start | bytes 393224 | tf_op jit(solution)/shard_map/ppermute | solution.py:387
  39.6 0.5 collective-permute-start.15
  40.2 2.9 %shard_map.123.acc_ref = f32[1024,128]{1,0:T(8,128)S(1)} custom-call(s32[16]{0:T(128)S(1)} %dynamic-slice_bitcast_fusion.offs_ref.refs_0_, f32[1024,128]{1,0:T(8,128)S(1)} %shard_map.121.acc_ref, bf16[128,16384]{1,0:T(8,128)(2,1)S(1)} %get-tuple-element.91.refs_3_.refs_0_.refs_5_.refs_8_.refs_7_, ...), custom_call_target="tpu_custom_call" | custom-call | flops 67108864 | bytes 524288 | tf_op jit(solution)/shard_map/pallas_call | solution.py:56
  43.1 0.0 copy-start.8
  43.1 0.0 copy-start.9
  43.1 0.1 collective-permute-start.13
  43.2 2.3 %shard_map.124.refs_8_ = f32[1024,128]{1,0:T(8,128)S(1)} custom-call(s32[16]{0:T(128)S(1)} %dynamic-slice_bitcast_fusion.offs_ref.refs_0_, f32[1024,128]{1,0:T(8,128)S(1)} %shard_map.123.acc_ref, bf16[128,16384]{1,0:T(8,128)(2,1)S(1)} %get-tuple-element.91.refs_3_.refs_0_.refs_5_.refs_8_.refs_7_, ...), custom_call_target="tpu_custom_call" | custom-call | flops 50331648 | bytes 393216 | tf_op jit(solution)/shard_map/pallas_call | solution.py:56
  45.6 2.1 %shard_map.125 = (f32[128,1024]{1,0:T(8,128)S(1)}, bf16[128,1024]{1,0:T(8,128)(2,1)S(1)}, bf16[1024,128]{1,0:T(8,128)(2,1)S(1)}, f32[16,1024]{1,0:T(8,128)}, f32[1,1024]{1,0:T(1,128)}, /*index=5*/f32[1,1024]{1,0:T(1,128)}) custom-call(s32[16]{0:T(128)S(1)} %dynamic-slice_bitcast_fusion.offs_ref.refs_0_, ...), custom_call_target="tpu_custom_call" | custom-call | flops 33554432 | bytes 262144 | tf_op jit(solution)/shard_map/pallas_call | solution.py:56
  47.6 1.3 %shard_map.126 = (bf16[128,1024]{1,0:T(8,128)(2,1)S(1)}, f32[128,1024]{1,0:T(8,128)S(1)}) custom-call(s32[16]{0:T(128)S(1)} %dynamic-slice_bitcast_fusion.offs_ref.refs_0_, bf16[128,1024]{1,0:T(8,128)(2,1)S(1)} %get-tuple-element.116.refs_1_, bf16[1024,128]{1,0:T(8,128)(2,1)S(1)} %get-tuple-element.117.refs_2_, ...), custom_call_target="tpu_custom_call" | custom-call | flops 33554432 | bytes 262144 | tf_op jit(solution)/shard_map/pallas_call | solution.py:56
  48.9 0.5 collective-permute-start.16
  49.5 1.8 %shard_map.127 = (bf16[128,1024]{1,0:T(8,128)(2,1)S(1)}, bf16[128,1024]{1,0:T(8,128)(2,1)S(1)}, f32[128,1024]{1,0:T(8,128)S(1)}, f32[128,1024]{1,0:T(8,128)S(1)}) custom-call(s32[16]{0:T(128)S(1)} %dynamic-slice_bitcast_fusion.offs_ref.refs_0_, bf16[128,1024]{1,0:T(8,128)(2,1)S(1)} %get-tuple-element.116.refs_1_, ...), custom_call_target="tpu_custom_call" | custom-call | flops 67108864 | bytes 524288 | tf_op jit(solution)/shard_map/pallas_call | solution.py:56
  51.3 0.0 copy-start.1
  51.3 0.0 copy-start.5
  51.3 0.1 collective-permute-start.17
  51.4 0.5 collective-permute-start.20
  51.9 0.1 add_convert_fusion.4
  52.0 1.7 %collective-permute-start.19 = (bf16[64,1024]{1,0:T(8,128)(2,1)S(1)}, bf16[64,1024]{1,0:T(8,128)(2,1)S(1)}, u32[]{:S(2)}, u32[]{:S(2)}) collective-permute-start(bf16[64,1024]{1,0:T(8,128)(2,1)S(1)} %get-tuple-element.169), channel_id=1, source_target_pairs={{0,4},{1,5},{2,0},{3,1},{6,2},{7,3},{10,6},{11,7},{14,10},{15,11},... | collective-permute-start | bytes 393224 | tf_op jit(solution)/shard_map/ppermute | solution.py:387
  53.7 0.4 collective-permute-start.18
  54.1 0.1 convert_add_fusion
  54.3 4.3 %shard_map.128 = (bf16[128,1024]{1,0:T(8,128)(2,1)S(1)}, bf16[128,1024]{1,0:T(8,128)(2,1)S(1)}, f32[128,1024]{1,0:T(8,128)S(1)}, f32[128,1024]{1,0:T(8,128)S(1)}...) custom-call(s32[16]{0:T(128)S(1)} %dynamic-slice_bitcast_fusion.offs_ref.refs_0_, ...), custom_call_target="tpu_custom_call" | custom-call | flops 100663296 | bytes 786432 | tf_op jit(solution)/shard_map/pallas_call | solution.py:56
  58.6 0.2 collective-permute-done.18
  59.0 1.4 %collective-permute-start.21 = (bf16[128,1024]{1,0:T(8,128)(2,1)S(1)}, bf16[128,1024]{1,0:T(8,128)(2,1)S(1)}, u32[]{:S(2)}, u32[]{:S(2)}) collective-permute-start(bf16[128,1024]{1,0:T(8,128)(2,1)S(1)} %pad_maximum_fusion), channel_id=1, source_target_pairs={{0,2},{1,3},{2,6},{3,7},{6,10},{7,11},{10,14},{11,15},{14,12},{15,... | collective-permute-start | bytes 786440 | tf_op jit(solution)/shard_map/ppermute | solution.py:387
  60.4 0.7 collective-permute-start.22
  61.1 0.5 collective-permute-start.25
  61.6 7.4 %shard_map.129 = (bf16[128,1024]{1,0:T(8,128)(2,1)S(1)}, bf16[128,1024]{1,0:T(8,128)(2,1)S(1)}, f32[128,1024]{1,0:T(8,128)S(1)}, f32[128,1024]{1,0:T(8,128)S(1)}...) custom-call(s32[16]{0:T(128)S(1)} %dynamic-slice_bitcast_fusion.offs_ref.refs_0_, ...), custom_call_target="tpu_custom_call", output_to_operand_aliasing={{4}: (16, {})} | custom-call | flops 150994944 | bytes 1179648 | tf_op jit(solution)/shard_map/pallas_call | solution.py:56
  69.0 0.1 add_convert_fusion.3
  69.2 0.1 add_convert_fusion.2
  69.3 1.4 %collective-permute-start.26 = (bf16[128,1024]{1,0:T(8,128)(2,1)S(1)}, bf16[128,1024]{1,0:T(8,128)(2,1)S(1)}, u32[]{:S(2)}, u32[]{:S(2)}) collective-permute-start(bf16[128,1024]{1,0:T(8,128)(2,1)S(1)} %add_convert_fusion.3), channel_id=1, source_target_pairs={{0,2},{1,3},{2,6},{3,7},{6,10},{7,11},{10,14},{11,15},{14,12},{15,... | collective-permute-start | bytes 786440 | tf_op jit(solution)/shard_map/ppermute | solution.py:387
  70.7 0.7 collective-permute-start.27
  71.3 0.5 collective-permute-start.23
  71.8 6.5 %shard_map.130 = (bf16[128,1024]{1,0:T(8,128)(2,1)S(1)}, f32[128,1024]{1,0:T(8,128)S(1)}, bf16[1024,16384]{1,0:T(8,128)(2,1)}, f32[8,128]{1,0:T(8,128)}) custom-call(s32[16]{0:T(128)S(1)} %dynamic-slice_bitcast_fusion.offs_ref.refs_0_, bf16[128,1024]{1,0:T(8,128)(2,1)S(1)} %get-tuple-element.116.refs_1_, ...), custom_call_target="tpu_custom_call", output_to_operand_aliasing={{2}: (16, {})} | custom-call | flops 117440512 | bytes 917504 | tf_op jit(solution)/shard_map/pallas_call | solution.py:56
  78.3 0.3 collective-permute-done.27
  78.6 0.1 add_convert_fusion
  78.7 0.1 add_convert_fusion.1
  78.8 1.6 %collective-permute-start.29 = (bf16[128,1024]{1,0:T(8,128)(2,1)S(1)}, bf16[128,1024]{1,0:T(8,128)(2,1)S(1)}, u32[]{:S(2)}, u32[]{:S(2)}) collective-permute-start(bf16[128,1024]{1,0:T(8,128)(2,1)S(1)} %add_convert_fusion.1), channel_id=1, source_target_pairs={{0,2},{1,3},{2,6},{3,7},{6,10},{7,11},{10,14},{11,15},{14,12},{15,... | collective-permute-start | bytes 786440 | tf_op jit(solution)/shard_map/ppermute | solution.py:387
  80.5 0.4 collective-permute-start.30
  80.9 0.6 shard_map.132
  81.5 5.2 %shard_map.131 = (bf16[1024,16384]{1,0:T(8,128)(2,1)}, f32[8,128]{1,0:T(8,128)}) custom-call(s32[16]{0:T(128)S(1)} %dynamic-slice_bitcast_fusion.offs_ref.refs_0_, bf16[128,1024]{1,0:T(8,128)(2,1)S(1)} %get-tuple-element.116.refs_1_, bf16[1024,128]{1,0:T(8,128)(2,1)S(1)} %get-tuple-element.117.refs_2_, ...), custom_call_target="tpu_custom_call", output_to_operand_aliasing={{0}: (15, {})} | custom-call | flops 67108864 | bytes 524288 | tf_op jit(solution)/shard_map/pallas_call | solution.py:56
  86.8 0.1 collective-permute-done.29
  86.8 1.1 %collective-permute-done.30 = bf16[128,1024]{1,0:T(8,128)(2,1)S(1)} collective-permute-done((bf16[128,1024]{1,0:T(8,128)(2,1)S(1)}, bf16[128,1024]{1,0:T(8,128)(2,1)S(1)}, u32[]{:S(2)}, u32[]{:S(2)}) %collective-permute-start.30) | collective-permute-done | bytes 262176 | tf_op jit(solution)/shard_map/ppermute | solution.py:387
  87.9 1.0 %add_bitcast_fusion = f32[1,128,1024]{2,1,0:T(8,128)} fusion(bf16[128,1024]{1,0:T(8,128)(2,1)S(1)} %collective-permute-done.30, bf16[128,1024]{1,0:T(8,128)(2,1)S(1)} %collective-permute-done.29, f32[128,1024]{1,0:T(8,128)S(1)} %shard_map.132, f32[128,1024]{1,0:T(8,128)S(1)} %get-tuple-element.162, bf16[128,1024]{1,0:T(8,128)(2,1)S(1)} %collective-permute-done.31), kind=kLoop, calls=%fused_computation | loop fusion | flops 917504 | bytes 2359296 | tf_op jit(solution)/shard_map/reshape | solution.py:480
  (54 shorter events, 0.3 us)
Async XLA Ops:
  1.7 11.2 %collective-permute-start.1 = (bf16[128,1024]{1,0:T(8,128)(2,1)S(1)}, bf16[128,1024]{1,0:T(8,128)(2,1)S(1)}, u32[]{:S(2)}, u32[]{:S(2)}) collective-permute-start(bf16[128,1024]{1,0:T(8,128)(2,1)S(1)} %bitcast_convert_fusion.x_ref.refs_7_.refs_3_), channel_id=1, source_target_pairs={{0,4},{1,5},{2,0},{3,1},{6,2},{7,3},{10,6},{11,7},{14,10},{15,11},... | collective-permute-start | bytes 786440 | tf_op jit(solution)/shard_map/ppermute | solution.py:387
  4.8 8.1 %collective-permute-start = (bf16[128,1024]{1,0:T(8,128)(2,1)S(1)}, bf16[128,1024]{1,0:T(8,128)(2,1)}, u32[]{:S(2)}, u32[]{:S(2)}) collective-permute-start(bf16[128,1024]{1,0:T(8,128)(2,1)S(1)} %bitcast_convert_fusion.x_ref.refs_7_.refs_3_), channel_id=1, source_target_pairs={{0,2},{1,3},{2,6},{3,7},{6,10},{7,11},{10,14},{11,15},{14,12},{15,... | collective-permute-start | bytes 786440 | tf_op jit(solution)/shard_map/ppermute | solution.py:387
  4.8 10.7 %collective-permute-start.4 = (bf16[128,1024]{1,0:T(8,128)(2,1)S(1)}, bf16[128,1024]{1,0:T(8,128)(2,1)S(1)}, u32[]{:S(2)}, u32[]{:S(2)}) collective-permute-start(bf16[128,1024]{1,0:T(8,128)(2,1)S(1)} %bitcast_convert_fusion.x_ref.refs_7_.refs_3_), channel_id=1, source_target_pairs={{0,1},{1,0},{2,3},{3,2},{4,5},{5,4},{6,7},{7,6},{8,9},{9,8},{10,11... | collective-permute-start | bytes 786440 | tf_op jit(solution)/shard_map/ppermute | solution.py:390
  12.9 14.8 %collective-permute-start.2 = (bf16[128,1024]{1,0:T(8,128)(2,1)}, bf16[128,1024]{1,0:T(8,128)(2,1)S(1)}, u32[]{:S(2)}, u32[]{:S(2)}) collective-permute-start(bf16[128,1024]{1,0:T(8,128)(2,1)} %collective-permute-done.refs_9_.refs_3_), channel_id=1, source_target_pairs={{0,2},{1,3},{2,6},{3,7},{6,10},{7,11},{10,14},{11,15},{14,12},{15,... | collective-permute-start | bytes 786440 | tf_op jit(solution)/shard_map/ppermute | solution.py:387
  14.9 12.8 %collective-permute-start.3 = (bf16[128,1024]{1,0:T(8,128)(2,1)S(1)}, bf16[128,1024]{1,0:T(8,128)(2,1)S(1)}, u32[]{:S(2)}, u32[]{:S(2)}) collective-permute-start(bf16[128,1024]{1,0:T(8,128)(2,1)S(1)} %collective-permute-done.1.refs_10_.refs_4_), channel_id=1, source_target_pairs={{0,4},{1,5},{2,0},{3,1},{6,2},{7,3},{10,6},{11,7},{14,10},{15,11},... | collective-permute-start | bytes 786440 | tf_op jit(solution)/shard_map/ppermute | solution.py:387
  15.0 14.7 %collective-permute-start.7 = (bf16[128,1024]{1,0:T(8,128)(2,1)}, bf16[128,1024]{1,0:T(8,128)(2,1)S(1)}, u32[]{:S(2)}, u32[]{:S(2)}) collective-permute-start(bf16[128,1024]{1,0:T(8,128)(2,1)} %collective-permute-done.refs_9_.refs_3_), channel_id=1, source_target_pairs={{0,1},{1,0},{2,3},{3,2},{4,5},{5,4},{6,7},{7,6},{8,9},{9,8},{10,11... | collective-permute-start | bytes 786440 | tf_op jit(solution)/shard_map/ppermute | solution.py:390
  15.2 15.6 %collective-permute-start.8 = (bf16[128,1024]{1,0:T(8,128)(2,1)S(1)}, bf16[128,1024]{1,0:T(8,128)(2,1)S(1)}, u32[]{:S(2)}, u32[]{:S(2)}) collective-permute-start(bf16[128,1024]{1,0:T(8,128)(2,1)S(1)} %collective-permute-done.1.refs_10_.refs_4_), channel_id=1, source_target_pairs={{0,1},{1,0},{2,3},{3,2},{4,5},{5,4},{6,7},{7,6},{8,9},{9,8},{10,11... | collective-permute-start | bytes 786440 | tf_op jit(solution)/shard_map/ppermute | solution.py:390
  15.5 0.7 copy-start.3
  16.2 0.9 %copy-start.4 = (bf16[128,1024]{1,0:T(8,128)(2,1)S(1)}, bf16[128,1024]{1,0:T(8,128)(2,1)}, u32[]{:S(2)}) copy-start(bf16[128,1024]{1,0:T(8,128)(2,1)} %copy-done.3) | copy-start | bytes 786436
  17.2 13.1 %copy-start.2 = (f32[1,128,1024]{2,1,0:T(8,128)S(1)}, f32[1,128,1024]{2,1,0:T(8,128)}, u32[]{:S(2)}) copy-start(f32[1,128,1024]{2,1,0:T(8,128)} %param.8) | copy-start | bytes 1572868
  17.2 13.1 %copy-start.6 = (f32[128,128]{1,0:T(8,128)S(1)}, f32[128,128]{1,0:T(8,128)}, u32[]{:S(2)}) copy-start(f32[128,128]{1,0:T(8,128)} %constant.13.clone.cheb_ref) | copy-start | bytes 196612
  17.2 13.1 %copy-start.7 = (f32[16,1024]{1,0:T(8,128)S(1)}, f32[16,1024]{1,0:T(8,128)}, u32[]{:S(2)}) copy-start(f32[16,1024]{1,0:T(8,128)} %pert_ref.1) | copy-start | bytes 196612
  27.6 21.8 %copy-start = (bf16[128,16384]{1,0:T(8,128)(2,1)}, bf16[128,16384]{1,0:T(8,128)(2,1)S(1)}, u32[]{:S(2)}) copy-start(bf16[128,16384]{1,0:T(8,128)(2,1)S(1)} %get-tuple-element.101.refs_6_.refs_9_.refs_11_.refs_14_.refs_13_) | copy-start | bytes 12582916
  27.7 8.5 %collective-permute-start.5 = (bf16[128,1024]{1,0:T(8,128)(2,1)S(1)}, bf16[128,1024]{1,0:T(8,128)(2,1)S(1)}, u32[]{:S(2)}, u32[]{:S(2)}) collective-permute-start(bf16[128,1024]{1,0:T(8,128)(2,1)S(1)} %collective-permute-done.2.refs_10_.refs_7_), channel_id=1, source_target_pairs={{0,2},{1,3},{2,6},{3,7},{6,10},{7,11},{10,14},{11,15},{14,12},{15,... | collective-permute-start | bytes 786440 | tf_op jit(solution)/shard_map/ppermute | solution.py:387
  29.6 7.9 %collective-permute-start.6 = (bf16[128,1024]{1,0:T(8,128)(2,1)S(1)}, bf16[128,1024]{1,0:T(8,128)(2,1)S(1)}, u32[]{:S(2)}, u32[]{:S(2)}) collective-permute-start(bf16[128,1024]{1,0:T(8,128)(2,1)S(1)} %collective-permute-done.3.refs_11_.refs_3_), channel_id=1, source_target_pairs={{0,4},{1,5},{2,0},{3,1},{6,2},{7,3},{10,6},{11,7},{14,10},{15,11},... | collective-permute-start | bytes 786440 | tf_op jit(solution)/shard_map/ppermute | solution.py:387
  29.8 9.9 %collective-permute-start.11 = (bf16[128,1024]{1,0:T(8,128)(2,1)S(1)}, bf16[128,1024]{1,0:T(8,128)(2,1)S(1)}, u32[]{:S(2)}, u32[]{:S(2)}) collective-permute-start(bf16[128,1024]{1,0:T(8,128)(2,1)S(1)} %collective-permute-done.2.refs_10_.refs_7_), channel_id=1, source_target_pairs={{0,1},{1,0},{2,3},{3,2},{4,5},{5,4},{6,7},{7,6},{8,9},{9,8},{10,11... | collective-permute-start | bytes 786440 | tf_op jit(solution)/shard_map/ppermute | solution.py:390
  29.8 10.4 %collective-permute-start.12 = (bf16[128,1024]{1,0:T(8,128)(2,1)S(1)}, bf16[128,1024]{1,0:T(8,128)(2,1)S(1)}, u32[]{:S(2)}, u32[]{:S(2)}) collective-permute-start(bf16[128,1024]{1,0:T(8,128)(2,1)S(1)} %collective-permute-done.3.refs_11_.refs_3_), channel_id=1, source_target_pairs={{0,1},{1,0},{2,3},{3,2},{4,5},{5,4},{6,7},{7,6},{8,9},{9,8},{10,11... | collective-permute-start | bytes 786440 | tf_op jit(solution)/shard_map/ppermute | solution.py:390
  37.6 5.5 %collective-permute-start.10 = (bf16[64,1024]{1,0:T(8,128)(2,1)S(1)}, bf16[64,1024]{1,0:T(8,128)(2,1)S(1)}, u32[]{:S(2)}, u32[]{:S(2)}) collective-permute-start(bf16[64,1024]{1,0:T(8,128)(2,1)S(1)} %slice.27), channel_id=1, source_target_pairs={{0,4},{1,5},{2,0},{3,1},{6,2},{7,3},{10,6},{11,7},{14,10},{15,11},... | collective-permute-start | bytes 393224 | tf_op jit(solution)/shard_map/ppermute | solution.py:387
  38.0 5.0 %collective-permute-start.9 = (bf16[64,1024]{1,0:T(8,128)(2,1)S(1)}, bf16[64,1024]{1,0:T(8,128)(2,1)S(1)}, u32[]{:S(2)}, u32[]{:S(2)}) collective-permute-start(bf16[64,1024]{1,0:T(8,128)(2,1)S(1)} %slice.26), channel_id=1, source_target_pairs={{0,2},{1,3},{2,6},{3,7},{6,10},{7,11},{10,14},{11,15},{14,12},{15,... | collective-permute-start | bytes 393224 | tf_op jit(solution)/shard_map/ppermute | solution.py:387
  39.6 3.6 %collective-permute-start.14 = (bf16[128,1024]{1,0:T(8,128)(2,1)S(1)}, bf16[128,1024]{1,0:T(8,128)(2,1)S(1)}, u32[]{:S(2)}, u32[]{:S(2)}) collective-permute-start(bf16[128,1024]{1,0:T(8,128)(2,1)S(1)} %collective-permute-done.5.refs_10_.refs_6_), channel_id=1, source_target_pairs={{0,1},{1,0},{2,3},{3,2},{4,5},{5,4},{6,7},{7,6},{8,9},{9,8},{10,11... | collective-permute-start | bytes 786440 | tf_op jit(solution)/shard_map/ppermute | solution.py:390
  39.6 3.6 %collective-permute-start.15 = (bf16[128,1024]{1,0:T(8,128)(2,1)S(1)}, bf16[128,1024]{1,0:T(8,128)(2,1)S(1)}, u32[]{:S(2)}, u32[]{:S(2)}) collective-permute-start(bf16[128,1024]{1,0:T(8,128)(2,1)S(1)} %collective-permute-done.6.refs_11_.refs_7_), channel_id=1, source_target_pairs={{0,1},{1,0},{2,3},{3,2},{4,5},{5,4},{6,7},{7,6},{8,9},{9,8},{10,11... | collective-permute-start | bytes 786440 | tf_op jit(solution)/shard_map/ppermute | solution.py:390
  43.1 2.5 %copy-start.8 = (f32[1024]{0:T(1024)S(1)}, f32[1024]{0:T(1024)}, u32[]{:S(2)}) copy-start(f32[1024]{0:T(1024)} %param.12) | copy-start | bytes 12292
  43.1 2.5 %copy-start.9 = (f32[1024]{0:T(1024)S(1)}, f32[1024]{0:T(1024)}, u32[]{:S(2)}) copy-start(f32[1024]{0:T(1024)} %param.11) | copy-start | bytes 12292
  43.1 2.4 %collective-permute-start.13 = (bf16[128,1024]{1,0:T(8,128)(2,1)S(1)}, bf16[128,1024]{1,0:T(8,128)(2,1)S(1)}, u32[]{:S(2)}, u32[]{:S(2)}) collective-permute-start(bf16[128,1024]{1,0:T(8,128)(2,1)S(1)} %constant_dynamic-update-slice_fusion.refs_10_.refs_5_), channel_id=1, source_target_pairs={{0,1},{1,0},{2,3},{3,2},{4,5},{5,4},{6,7},{7,6},{8,9},{9,8},{10,11... | collective-permute-start | bytes 786440 | tf_op jit(solution)/shard_map/ppermute | solution.py:390
  48.9 3.0 %collective-permute-start.16 = (bf16[128,1024]{1,0:T(8,128)(2,1)S(1)}, bf16[128,1024]{1,0:T(8,128)(2,1)S(1)}, u32[]{:S(2)}, u32[]{:S(2)}) collective-permute-start(bf16[128,1024]{1,0:T(8,128)(2,1)S(1)} %get-tuple-element.119), channel_id=1, source_target_pairs={{0,1},{1,0},{2,3},{3,2},{4,5},{5,4},{6,7},{7,6},{8,9},{9,8},{10,11... | collective-permute-start | bytes 786440 | tf_op jit(solution)/shard_map/ppermute | solution.py:390
  51.3 3.0 %copy-start.1 = (bf16[128,16384]{1,0:T(8,128)(2,1)S(1)}, bf16[128,16384]{1,0:T(8,128)(2,1)}, u32[]{:S(2)}) copy-start(bf16[128,16384]{1,0:T(8,128)(2,1)} %copy-done) | copy-start | bytes 12582916
  51.3 3.0 %copy-start.5 = (bf16[128,1024]{1,0:T(8,128)(2,1)S(1)}, bf16[128,1024]{1,0:T(8,128)(2,1)}, u32[]{:S(2)}) copy-start(bf16[128,1024]{1,0:T(8,128)(2,1)} %copy-done.3) | copy-start | bytes 786436
  51.3 2.8 %collective-permute-start.17 = (bf16[128,1024]{1,0:T(8,128)(2,1)S(1)}, bf16[128,1024]{1,0:T(8,128)(2,1)S(1)}, u32[]{:S(2)}, u32[]{:S(2)}) collective-permute-start(bf16[128,1024]{1,0:T(8,128)(2,1)S(1)} %get-tuple-element.123), channel_id=1, source_target_pairs={{0,1},{1,0},{2,3},{3,2},{4,5},{5,4},{6,7},{7,6},{8,9},{9,8},{10,11... | collective-permute-start | bytes 786440 | tf_op jit(solution)/shard_map/ppermute | solution.py:390
  51.4 2.6 %collective-permute-start.20 = (bf16[128,1024]{1,0:T(8,128)(2,1)S(1)}, bf16[128,1024]{1,0:T(8,128)(2,1)S(1)}, u32[]{:S(2)}, u32[]{:S(2)}) collective-permute-start(bf16[128,1024]{1,0:T(8,128)(2,1)S(1)} %get-tuple-element.130), channel_id=1, source_target_pairs={{0,1},{1,0},{2,3},{3,2},{4,5},{5,4},{6,7},{7,6},{8,9},{9,8},{10,11... | collective-permute-start | bytes 786440 | tf_op jit(solution)/shard_map/ppermute | solution.py:390
  52.0 6.7 %collective-permute-start.19 = (bf16[64,1024]{1,0:T(8,128)(2,1)S(1)}, bf16[64,1024]{1,0:T(8,128)(2,1)S(1)}, u32[]{:S(2)}, u32[]{:S(2)}) collective-permute-start(bf16[64,1024]{1,0:T(8,128)(2,1)S(1)} %get-tuple-element.169), channel_id=1, source_target_pairs={{0,4},{1,5},{2,0},{3,1},{6,2},{7,3},{10,6},{11,7},{14,10},{15,11},... | collective-permute-start | bytes 393224 | tf_op jit(solution)/shard_map/ppermute | solution.py:387
  53.7 5.2 %collective-permute-start.18 = (bf16[64,1024]{1,0:T(8,128)(2,1)S(1)}, bf16[64,1024]{1,0:T(8,128)(2,1)S(1)}, u32[]{:S(2)}, u32[]{:S(2)}) collective-permute-start(bf16[64,1024]{1,0:T(8,128)(2,1)S(1)} %get-tuple-element.170), channel_id=1, source_target_pairs={{0,2},{1,3},{2,6},{3,7},{6,10},{7,11},{10,14},{11,15},{14,12},{15,... | collective-permute-start | bytes 393224 | tf_op jit(solution)/shard_map/ppermute | solution.py:387
  59.0 10.0 %collective-permute-start.21 = (bf16[128,1024]{1,0:T(8,128)(2,1)S(1)}, bf16[128,1024]{1,0:T(8,128)(2,1)S(1)}, u32[]{:S(2)}, u32[]{:S(2)}) collective-permute-start(bf16[128,1024]{1,0:T(8,128)(2,1)S(1)} %pad_maximum_fusion), channel_id=1, source_target_pairs={{0,2},{1,3},{2,6},{3,7},{6,10},{7,11},{10,14},{11,15},{14,12},{15,... | collective-permute-start | bytes 786440 | tf_op jit(solution)/shard_map/ppermute | solution.py:387
  60.4 8.6 %collective-permute-start.22 = (bf16[128,1024]{1,0:T(8,128)(2,1)S(1)}, bf16[128,1024]{1,0:T(8,128)(2,1)S(1)}, u32[]{:S(2)}, u32[]{:S(2)}) collective-permute-start(bf16[128,1024]{1,0:T(8,128)(2,1)S(1)} %pad_maximum_fusion.1), channel_id=1, source_target_pairs={{0,4},{1,5},{2,0},{3,1},{6,2},{7,3},{10,6},{11,7},{14,10},{15,11},... | collective-permute-start | bytes 786440 | tf_op jit(solution)/shard_map/ppermute | solution.py:387
  61.1 7.9 %collective-permute-start.24 = (bf16[128,1024]{1,0:T(8,128)(2,1)S(1)}, bf16[128,1024]{1,0:T(8,128)(2,1)S(1)}, u32[]{:S(2)}, u32[]{:S(2)}) collective-permute-start(bf16[128,1024]{1,0:T(8,128)(2,1)S(1)} %get-tuple-element.141), channel_id=1, source_target_pairs={{0,1},{1,0},{2,3},{3,2},{4,5},{5,4},{6,7},{7,6},{8,9},{9,8},{10,11... | collective-permute-start | bytes 786440 | tf_op jit(solution)/shard_map/ppermute | solution.py:390
  61.1 8.0 %collective-permute-start.25 = (bf16[128,1024]{1,0:T(8,128)(2,1)S(1)}, bf16[128,1024]{1,0:T(8,128)(2,1)S(1)}, u32[]{:S(2)}, u32[]{:S(2)}) collective-permute-start(bf16[128,1024]{1,0:T(8,128)(2,1)S(1)} %get-tuple-element.144), channel_id=1, source_target_pairs={{0,1},{1,0},{2,3},{3,2},{4,5},{5,4},{6,7},{7,6},{8,9},{9,8},{10,11... | collective-permute-start | bytes 786440 | tf_op jit(solution)/shard_map/ppermute | solution.py:390
  69.3 9.1 %collective-permute-start.26 = (bf16[128,1024]{1,0:T(8,128)(2,1)S(1)}, bf16[128,1024]{1,0:T(8,128)(2,1)S(1)}, u32[]{:S(2)}, u32[]{:S(2)}) collective-permute-start(bf16[128,1024]{1,0:T(8,128)(2,1)S(1)} %add_convert_fusion.3), channel_id=1, source_target_pairs={{0,2},{1,3},{2,6},{3,7},{6,10},{7,11},{10,14},{11,15},{14,12},{15,... | collective-permute-start | bytes 786440 | tf_op jit(solution)/shard_map/ppermute | solution.py:387
  70.7 7.9 %collective-permute-start.27 = (bf16[128,1024]{1,0:T(8,128)(2,1)S(1)}, bf16[128,1024]{1,0:T(8,128)(2,1)S(1)}, u32[]{:S(2)}, u32[]{:S(2)}) collective-permute-start(bf16[128,1024]{1,0:T(8,128)(2,1)S(1)} %add_convert_fusion.2), channel_id=1, source_target_pairs={{0,4},{1,5},{2,0},{3,1},{6,2},{7,3},{10,6},{11,7},{14,10},{15,11},... | collective-permute-start | bytes 786440 | tf_op jit(solution)/shard_map/ppermute | solution.py:387
  71.3 7.3 %collective-permute-start.28 = (bf16[128,1024]{1,0:T(8,128)(2,1)S(1)}, bf16[128,1024]{1,0:T(8,128)(2,1)S(1)}, u32[]{:S(2)}, u32[]{:S(2)}) collective-permute-start(bf16[128,1024]{1,0:T(8,128)(2,1)S(1)} %get-tuple-element.153), channel_id=1, source_target_pairs={{0,1},{1,0},{2,3},{3,2},{4,5},{5,4},{6,7},{7,6},{8,9},{9,8},{10,11... | collective-permute-start | bytes 786440 | tf_op jit(solution)/shard_map/ppermute | solution.py:390
  71.3 7.4 %collective-permute-start.23 = (bf16[128,1024]{1,0:T(8,128)(2,1)S(1)}, bf16[128,1024]{1,0:T(8,128)(2,1)S(1)}, u32[]{:S(2)}, u32[]{:S(2)}) collective-permute-start(bf16[128,1024]{1,0:T(8,128)(2,1)S(1)} %get-tuple-element.139), channel_id=1, source_target_pairs={{0,1},{1,0},{2,3},{3,2},{4,5},{5,4},{6,7},{7,6},{8,9},{9,8},{10,11... | collective-permute-start | bytes 786440 | tf_op jit(solution)/shard_map/ppermute | solution.py:390
  78.8 8.0 %collective-permute-start.29 = (bf16[128,1024]{1,0:T(8,128)(2,1)S(1)}, bf16[128,1024]{1,0:T(8,128)(2,1)S(1)}, u32[]{:S(2)}, u32[]{:S(2)}) collective-permute-start(bf16[128,1024]{1,0:T(8,128)(2,1)S(1)} %add_convert_fusion.1), channel_id=1, source_target_pairs={{0,2},{1,3},{2,6},{3,7},{6,10},{7,11},{10,14},{11,15},{14,12},{15,... | collective-permute-start | bytes 786440 | tf_op jit(solution)/shard_map/ppermute | solution.py:387
  80.5 7.4 %collective-permute-start.30 = (bf16[128,1024]{1,0:T(8,128)(2,1)S(1)}, bf16[128,1024]{1,0:T(8,128)(2,1)S(1)}, u32[]{:S(2)}, u32[]{:S(2)}) collective-permute-start(bf16[128,1024]{1,0:T(8,128)(2,1)S(1)} %add_convert_fusion), channel_id=1, source_target_pairs={{0,4},{1,5},{2,0},{3,1},{6,2},{7,3},{10,6},{11,7},{14,10},{15,11},... | collective-permute-start | bytes 786440 | tf_op jit(solution)/shard_map/ppermute | solution.py:387
  80.9 7.0 %collective-permute-start.31 = (bf16[128,1024]{1,0:T(8,128)(2,1)S(1)}, bf16[128,1024]{1,0:T(8,128)(2,1)S(1)}, u32[]{:S(2)}, u32[]{:S(2)}) collective-permute-start(bf16[128,1024]{1,0:T(8,128)(2,1)S(1)} %get-tuple-element.163), channel_id=1, source_target_pairs={{0,1},{1,0},{2,3},{3,2},{4,5},{5,4},{6,7},{7,6},{8,9},{9,8},{10,11... | collective-permute-start | bytes 786440 | tf_op jit(solution)/shard_map/ppermute | solution.py:390

commit v7 on v6

--- a/solution.py
+++ b/solution.py
@@ -9,9 +9,9 @@
 from jax.sharding import PartitionSpec as P
 
 SCALE = 2.0 / 1024.0
-VMEM_LIMIT = 4 * 2**20
+VMEM_LIMIT = 8 * 2**20
 BANDS = 8
-FIRST_BANDS = 4
+LOADS = (4, 2, 2)
 LONGEST_RING = 16
 
 
@@ -51,7 +51,7 @@
     )
 
 
-def call(kernel, out_shape, out_specs, scratch, costs, aliases=None, more=0):
+def call(kernel, out_shape, out_specs, scratch, costs, aliases=None):
     def run(operands, in_specs):
         return pl.pallas_call(
             kernel,
@@ -60,7 +60,7 @@
             out_specs=out_specs,
             scratch_shapes=scratch,
             input_output_aliases=aliases or {},
-            compiler_params=pltpu.CompilerParams(vmem_limit_bytes=VMEM_LIMIT + more),
+            compiler_params=pltpu.CompilerParams(vmem_limit_bytes=VMEM_LIMIT),
             cost_estimate=costs,
         )(*operands)
 
@@ -89,88 +89,60 @@
     )
 
 
-def first_kernel(base, offs_ref, perts_ref, w_ref, x_ref, out_ref, *refs):
-    bands, sems = refs[:-1], refs[-1]
-    here = columns_of(offs_ref, base, x_ref.shape[1])
-    tile = bands[0].shape[0]
-    for at, copy in enumerate(load_bands(w_ref, bands, sems, 0)):
-        copy.wait()
-        out_ref[pl.ds(at * tile, tile), :] = product(bands[at : at + 1], here, x_ref)
-
-
-def second_kernel(base, count, early, *refs):
-    offs_ref, w_ref, acc_ref = refs[:3]
-    bands, refs = refs[3 : 3 + early], refs[3 + early :]
-    xs, out_ref, late, sems = refs[:count], refs[count], refs[count + 1 : -1], refs[-1]
-    slab, tile = xs[0].shape[1], bands[0].shape[0]
-    copies = load_bands(w_ref, late, sems, early)
-    places = [columns_of(offs_ref, base + at, slab) for at in range(count)]
-    rows = pl.ds(0, early * tile)
-    total = acc_ref[rows, :]
-    for at in range(1, count):
-        total += product(bands, places[at], xs[at])
-    out_ref[rows, :] = total
+def pre_kernel(base, done, count, many, late, first, *refs):
+    offs_ref, refs = refs[0], refs[1:]
+    if first:
+        refs = refs[1:]
+    if late:
+        w_ref, refs = refs[0], refs[1:]
+    if many:
+        acc_ref, refs = refs[0], refs[1:]
+    bands, refs = refs[:many], refs[many:]
+    xs, refs = refs[: count + (done if late else 0)], refs[count + (done if late else 0) :]
+    out_ref, others, sems = refs[0], refs[1 : 1 + late], refs[-1]
+    slab = xs[0].shape[1]
+    tile = out_ref.shape[0] // BANDS
+    copies = load_bands(w_ref, others, sems, many) if late else []
+    places = [columns_of(offs_ref, base + at, slab) for at in range(done + count)]
+    for low in range(0, many, 2):
+        pair = bands[low : low + 2]
+        rows = pl.ds(low * tile, len(pair) * tile)
+        total = acc_ref[rows, :]
+        for at, x_ref in enumerate(xs[-count:]):
+            total += product(pair, places[done + at], x_ref)
+        out_ref[rows, :] = total
     for copy in copies:
         copy.wait()
-    total = product(late, places[0], xs[0])
-    for at in range(1, count):
-        total += product(late, places[at], xs[at])
-    out_ref[pl.ds(early * tile, len(late) * tile), :] = total
-
-
-def pre_kernel(base, count, many, offs_ref, acc_ref, *refs):
-    bands, xs, out_ref = refs[:many], refs[many:-1], refs[-1]
-    slab, tile = xs[0].shape[1], bands[0].shape[0]
-    for low in range(0, many, 4):
-        rows = pl.ds(low * tile, 4 * tile)
-        total = acc_ref[rows, :]
-        for at in range(count):
-            total += product(bands[low : low + 4], columns_of(offs_ref, base + at, slab), xs[at])
+    for low in range(0, late, 2):
+        pair = others[low : low + 2]
+        rows = pl.ds((many + low) * tile, len(pair) * tile)
+        total = product(pair, places[0], xs[0])
+        for at in range(1, len(xs)):
+            total += product(pair, places[at], xs[at])
         out_ref[rows, :] = total
 
 
-def band_shapes(count, weights):
-    return [pltpu.VMEM((weights.shape[0] // BANDS, weights.shape[1]), weights.dtype)] * count
-
-
-def first_products(offs, perts, base, x, weights):
-    (nodes, slab), rows = x.shape, weights.shape[0]
-    acc, *bands = call(
-        functools.partial(first_kernel, base),
-        [jax.ShapeDtypeStruct((rows, nodes), jnp.float32)] + band_shapes(FIRST_BANDS, weights),
-        [VMEM_REF] * (1 + FIRST_BANDS),
-        [pltpu.SemaphoreType.DMA((FIRST_BANDS,))],
-        cost(1, nodes, slab, rows),
-    )([offs, perts, weights, x], [SMEM_REF, SMEM_REF, HBM_REF, VMEM_REF])
-    return acc, bands
-
-
-def second_products(offs, base, xs, weights, acc, bands):
-    (nodes, slab), rows = xs[0].shape, weights.shape[0]
-    late = BANDS - len(bands)
+def add_products(offs, perts, weights, acc, bands, before, xs, late):
+    (nodes, slab), (rows, genes) = xs[0].shape, weights.shape
+    first, many, done, count = acc is None, len(bands), len(before), len(xs)
+    operands, specs = [offs], [SMEM_REF]
+    if first:
+        operands, specs = operands + [perts], specs + [SMEM_REF]
+    if late:
+        operands, specs = operands + [weights], specs + [HBM_REF]
+    if many:
+        operands, specs = operands + [acc], specs + [VMEM_REF]
+    operands += [*bands, *(before if late else []), *xs]
+    specs += [VMEM_REF] * (len(operands) - len(specs))
     acc, *others = call(
-        functools.partial(second_kernel, base, len(xs), len(bands)),
-        [jax.ShapeDtypeStruct((rows, nodes), jnp.float32)] + band_shapes(late, weights),
+        functools.partial(pre_kernel, 0, done, count, many, late, first),
+        [jax.ShapeDtypeStruct((rows, nodes), jnp.float32)]
+        + [pltpu.VMEM((rows // BANDS, genes), weights.dtype)] * late,
         [VMEM_REF] * (1 + late),
-        [pltpu.SemaphoreType.DMA((late,))],
-        cost(len(xs), nodes, slab, rows),
-    )(
-        [offs, weights, acc, *bands, *xs],
-        [SMEM_REF, HBM_REF] + [VMEM_REF] * (1 + len(bands) + len(xs)),
-    )
-    return acc, bands + others
-
-
-def add_products(offs, base, xs, acc, bands):
-    nodes, slab = xs[0].shape
-    rows, count = acc.shape[0], len(xs)
-    return call(
-        functools.partial(pre_kernel, base, count, len(bands)),
-        jax.ShapeDtypeStruct((rows, nodes), jnp.float32),
-        VMEM_REF,
-        [],
+        [pltpu.SemaphoreType.DMA((max(late, 1),))],
         cost(count, nodes, slab, rows),
-    )([offs, acc, *bands, *xs], [SMEM_REF] + [VMEM_REF] * (1 + len(bands) + count))
+    )(operands, specs)
+    return acc, [*bands, *others]
 
 
 def cheb_dot(turned, cheb_ref, array_ref):
@@ -323,7 +295,7 @@
     first = so_far is None
     shapes = [jax.ShapeDtypeStruct((nodes, slab), jnp.bfloat16)] * own
     shapes += [jax.ShapeDtypeStruct((nodes, slab), jnp.float32)] * own
-    specs, scratch, more = [VMEM_REF] * (2 * own), [], 0
+    specs, scratch = [VMEM_REF] * (2 * own), []
     if count:
         shapes += [
             jax.ShapeDtypeStruct(shape, jnp.bfloat16),
@@ -331,7 +303,6 @@
         ]
         specs += [ANY_REF, VMEM_REF]
         scratch = [pltpu.VMEM((4, tile, slab), jnp.bfloat16), pltpu.SemaphoreType.DMA((4,))]
-        more = 4 * 2 * tile * slab
     operands = [offs, delta, delta_t, *xs, *bands] + ([] if first else [so_far])
     outs = call(
         functools.partial(sums_kernel, base, count, places, len(bands), first),
@@ -340,7 +311,6 @@
         scratch,
         cost(count + 2 * own, nodes, slab, rows),
         {} if first else {len(operands) - 1: 2 * own},
-        more,
     )(
         operands,
         [SMEM_REF] + [VMEM_REF] * (2 + count + len(bands)) + ([] if first else [ANY_REF]),
@@ -398,6 +368,7 @@
 
     x = {(0, 0): xb}
     behind, ahead, base = xb, xb, 0
+    acc, bands, loads = None, [], list(LOADS)
     for step in range(1, half + 1):
         if step < half:
             behind, ahead = ring(behind, 1), ring(ahead, -1)
@@ -406,13 +377,11 @@
         for now in [0] if step == 1 else [1 - step, step - 1]:
             x[now, 1] = swap(x[now, 0])
         count = {1: 1, 2: 3}.get(step, 4)
-        xs = [x[key] for key in listing[base : base + count]]
-        if step == 1:
-            acc, bands = first_products(offs, perts, 0, xs[0], weights)
-        elif step == 2:
-            acc, bands = second_products(offs, 0, [x[0, 0], *xs], weights, acc, bands)
-        else:
-            acc = add_products(offs, base, xs, acc, bands)
+        late = loads.pop(0) if loads else 0
+        xs = [x[key] for key in listing[: base + count]]
+        acc, bands = add_products(
+            offs, perts, weights, acc, bands, xs[:base], xs[base:], late
+        )
         base += count
         if step == half - 1:
             derivs = derivatives(perts, cheb, flat, pert_table)
@@ -423,8 +392,8 @@
         else:
             x[half, 0] = jnp.concatenate([behind, ahead], axis=0)
     x[half, 1] = swap(x[half, 0])
-    xs = [x[key] for key in listing[base : base + 3]]
-    acc = add_products(offs, base, xs, acc, bands)
+    xs = [x[key] for key in listing[: base + 3]]
+    acc, _ = add_products(offs, perts, weights, acc, bands, xs[:base], xs[base:], 0)
     base += 3
 
     decay = decay.reshape(1, rows)

time: 89.2 us -> 88.9 us (level)
  waiting for transfers between devices: 5.49 us -> 3.61 us
  Pallas kernels: 55 us -> 56.4 us
    ppermute x16, waiting for transfers between devices: 5.45 us -> 3.57 us  [ring(): return lax.ppermute(array, 'row', pairs)]
    pallas_call x14, Pallas kernels: 55 us -> 56.4 us  [run(): pl.pallas_call(kernel, out_shape=out_shape, in_specs=in_specs, out_specs=...]
  transfers between devices with their start and end apart: 32 -> 32, of which waited for: 6 -> 7; matrix products, arithmetic and copies ran while one was open for 1% -> 1% of each run, Pallas kernels for 58% -> 60%
where the time goes in v7:
time: 88.9 us; the launch traced here: 88.6 us
  Pallas kernels  56.4 us (63%)
  starting transfers between devices  21.4 us (24%)
  waiting for transfers between devices  3.61 us (4%)
  other arithmetic  2.79 us (3%)
  local copies, waits for them, and re-layouts  2.72 us (3%)
  between operations  1.76 us (2%)
    pallas_call x14, Pallas kernels, run(): pl.pallas_call(kernel, out_shape=out_shape, in_specs=in_specs, out_specs=...  56.4 us
    ppermute x16, starting transfers between devices, ring(): return lax.ppermute(array, 'row', pairs)  17.6 us
    ppermute x16, starting transfers between devices, swap(): return lax.ppermute(array, 'row', [(i, i ^ 1) for i in range(2 * chips)])  3.75 us
    ppermute x16, waiting for transfers between devices, ring(): return lax.ppermute(array, 'row', pairs)  3.57 us
    unnamed x21, local copies, waits for them, and re-layouts  1.94 us
  transfers between devices with their start and end apart: 32, of which 7 were waited for; matrix products, arithmetic and copies ran while one was open for 1% of the time, Pallas kernels for 60%

profile of v7, /device:TPU:0, one launch (start us, length us, event | category | flops | bytes accessed | tf_op | source)
XLA Modules:
  0.0 88.6 jit_solution(3093200380276186867)
XLA Ops:
  0.6 1.1 %bitcast_convert_fusion.refs_3_.refs_7_.refs_9_ = bf16[128,1024]{1,0:T(8,128)(2,1)S(1)} fusion(f32[1,128,1024]{2,1,0:T(8,128)} %param.8), kind=kLoop, calls=%fused_computation.19 | loop fusion | flops 131072 | bytes 786432 | tf_op jit(solution)/shard_map/convert_element_type | solution.py:365
  1.7 3.1 %collective-permute-start.1 = (bf16[128,1024]{1,0:T(8,128)(2,1)S(1)}, bf16[128,1024]{1,0:T(8,128)(2,1)S(1)}, u32[]{:S(2)}, u32[]{:S(2)}) collective-permute-start(bf16[128,1024]{1,0:T(8,128)(2,1)S(1)} %bitcast_convert_fusion.refs_3_.refs_7_.refs_9_), channel_id=1, source_target_pairs={{0,4},{1,5},{2,0},{3,1},{6,2},{7,3},{10,6},{11,7},{14,10},{15,11},... | collective-permute-start | bytes 786440 | tf_op jit(solution)/shard_map/ppermute | solution.py:357
  4.8 0.0 collective-permute-start
  4.8 0.7 dynamic-slice_bitcast_fusion.refs_0_.offs_ref
  6.1 6.9 %shard_map.119 = (f32[1024,128]{1,0:T(8,128)S(1)}, bf16[128,16384]{1,0:T(8,128)(2,1)S(1)}, bf16[128,16384]{1,0:T(8,128)(2,1)S(1)}, bf16[128,16384]{1,0:T(8,128)(2,1)S(1)}, bf16[128,16384]{1,0:T(8,128)(2,1)S(1)}) custom-call(s32[16]{0:T(128)S(1)} %dynamic-slice_bitcast_fusion.refs_0_.offs_ref, s32[1]{0:T(128)S(6)} %copy.20.refs_1_.perts_ref, ...), custom_call_target="tpu_custom_call" | custom-call | flops 16777216 | bytes 131072 | tf_op jit(solution)/shard_map/pallas_call | solution.py:56
  13.0 0.0 collective-permute-done.1.refs_10_.refs_12_.refs_4_
  13.0 2.0 %collective-permute-start.2 = (bf16[128,1024]{1,0:T(8,128)(2,1)S(1)}, bf16[128,1024]{1,0:T(8,128)(2,1)S(1)}, u32[]{:S(2)}, u32[]{:S(2)}) collective-permute-start(bf16[128,1024]{1,0:T(8,128)(2,1)S(1)} %collective-permute-done.refs_9_.refs_11_.refs_3_), channel_id=1, source_target_pairs={{0,2},{1,3},{2,6},{3,7},{6,10},{7,11},{10,14},{11,15},{14,12},{15,... | collective-permute-start | bytes 786440 | tf_op jit(solution)/shard_map/ppermute | solution.py:357
  15.0 0.2 collective-permute-start.3
  15.2 0.2 collective-permute-start.7
  15.4 0.3 collective-permute-start.8
  15.7 0.0 collective-permute-done.4.refs_8_.refs_10_.refs_4_
  15.7 0.0 copy-start.7
  15.7 6.0 %shard_map.120 = (f32[1024,128]{1,0:T(8,128)S(1)}, bf16[128,16384]{1,0:T(8,128)(2,1)S(1)}, bf16[128,16384]{1,0:T(8,128)(2,1)S(1)}) custom-call(s32[16]{0:T(128)S(1)} %dynamic-slice_bitcast_fusion.refs_0_.offs_ref, bf16[1024,16384]{1,0:T(8,128)(2,1)} %refs_1_.4, f32[1024,128]{1,0:T(8,128)S(1)} %get-tuple-element.91.refs_2_, ...), custom_call_target="tpu_custom_call" | custom-call | flops 50331648 | bytes 393216 | tf_op jit(solution)/shard_map/pallas_call | solution.py:56
  21.7 0.4 collective-permute-done.2.refs_15_.refs_7_
  22.1 1.4 %collective-permute-done.3.refs_16_.refs_3_ = bf16[128,1024]{1,0:T(8,128)(2,1)S(1)} collective-permute-done((bf16[128,1024]{1,0:T(8,128)(2,1)S(1)}, bf16[128,1024]{1,0:T(8,128)(2,1)S(1)}, u32[]{:S(2)}, u32[]{:S(2)}) %collective-permute-start.3) | collective-permute-done | bytes 262176 | tf_op jit(solution)/shard_map/ppermute | solution.py:357
  23.5 1.6 %collective-permute-start.5 = (bf16[128,1024]{1,0:T(8,128)(2,1)S(1)}, bf16[128,1024]{1,0:T(8,128)(2,1)S(1)}, u32[]{:S(2)}, u32[]{:S(2)}) collective-permute-start(bf16[128,1024]{1,0:T(8,128)(2,1)S(1)} %collective-permute-done.2.refs_15_.refs_7_), channel_id=1, source_target_pairs={{0,2},{1,3},{2,6},{3,7},{6,10},{7,11},{10,14},{11,15},{14,12},{15,... | collective-permute-start | bytes 786440 | tf_op jit(solution)/shard_map/ppermute | solution.py:357
  25.0 0.4 collective-permute-start.6
  25.5 0.0 collective-permute-start.11
  25.5 0.5 collective-permute-start.12
  26.0 0.6 shard_map.122
  26.6 0.9 %copy-done.2 = bf16[128,1024]{1,0:T(8,128)(2,1)S(1)} copy-done((bf16[128,1024]{1,0:T(8,128)(2,1)S(1)}, bf16[128,1024]{1,0:T(8,128)(2,1)}, u32[]{:S(2)}) %copy-start.2) | copy-done | bytes 262168
  27.6 0.9 %copy-done.5 = bf16[128,1024]{1,0:T(8,128)(2,1)S(1)} copy-done((bf16[128,1024]{1,0:T(8,128)(2,1)S(1)}, bf16[128,1024]{1,0:T(8,128)(2,1)}, u32[]{:S(2)}) %copy-start.5) | copy-done | bytes 262168
  28.5 8.8 %shard_map.121 = (f32[1024,128]{1,0:T(8,128)S(1)}, bf16[128,16384]{1,0:T(8,128)(2,1)S(1)}, bf16[128,16384]{1,0:T(8,128)(2,1)S(1)}) custom-call(s32[16]{0:T(128)S(1)} %dynamic-slice_bitcast_fusion.refs_0_.offs_ref, bf16[1024,16384]{1,0:T(8,128)(2,1)} %refs_1_.4, f32[1024,128]{1,0:T(8,128)S(1)} %get-tuple-element.99.refs_2_, ...), custom_call_target="tpu_custom_call" | custom-call | flops 67108864 | bytes 524288 | tf_op jit(solution)/shard_map/pallas_call | solution.py:56
  37.4 0.5 collective-permute-start.10
  37.9 1.6 %collective-permute-start.9 = (bf16[64,1024]{1,0:T(8,128)(2,1)S(1)}, bf16[64,1024]{1,0:T(8,128)(2,1)S(1)}, u32[]{:S(2)}, u32[]{:S(2)}) collective-permute-start(bf16[64,1024]{1,0:T(8,128)(2,1)S(1)} %slice.26), channel_id=1, source_target_pairs={{0,2},{1,3},{2,6},{3,7},{6,10},{7,11},{10,14},{11,15},{14,12},{15,... | collective-permute-start | bytes 393224 | tf_op jit(solution)/shard_map/ppermute | solution.py:357
  39.5 0.5 collective-permute-start.15
  40.0 2.9 %shard_map.123.refs_1_ = f32[1024,128]{1,0:T(8,128)S(1)} custom-call(s32[16]{0:T(128)S(1)} %dynamic-slice_bitcast_fusion.refs_0_.offs_ref, f32[1024,128]{1,0:T(8,128)S(1)} %get-tuple-element.109.refs_1_, bf16[128,16384]{1,0:T(8,128)(2,1)S(1)} %get-tuple-element.92.refs_3_.refs_2_.refs_0_.refs_5_.refs_8_.refs_7_, ...), custom_call_target="tpu_custom_call" | custom-call | flops 67108864 | bytes 524288 | tf_op jit(solution)/shard_map/pallas_call | solution.py:56
  42.9 0.1 collective-permute-done.9
  43.0 0.0 copy-start.8
  43.1 0.0 copy-start.9
  43.1 0.1 collective-permute-start.13
  43.2 2.3 %shard_map.124.refs_8_ = f32[1024,128]{1,0:T(8,128)S(1)} custom-call(s32[16]{0:T(128)S(1)} %dynamic-slice_bitcast_fusion.refs_0_.offs_ref, f32[1024,128]{1,0:T(8,128)S(1)} %shard_map.123.refs_1_, bf16[128,16384]{1,0:T(8,128)(2,1)S(1)} %get-tuple-element.92.refs_3_.refs_2_.refs_0_.refs_5_.refs_8_.refs_7_, ...), custom_call_target="tpu_custom_call" | custom-call | flops 50331648 | bytes 393216 | tf_op jit(solution)/shard_map/pallas_call | solution.py:56
  45.5 2.1 %shard_map.125 = (f32[128,1024]{1,0:T(8,128)S(1)}, bf16[128,1024]{1,0:T(8,128)(2,1)S(1)}, bf16[1024,128]{1,0:T(8,128)(2,1)S(1)}, f32[16,1024]{1,0:T(8,128)}, f32[1,1024]{1,0:T(1,128)}, /*index=5*/f32[1,1024]{1,0:T(1,128)}) custom-call(s32[16]{0:T(128)S(1)} %dynamic-slice_bitcast_fusion.refs_0_.offs_ref, ...), custom_call_target="tpu_custom_call" | custom-call | flops 33554432 | bytes 262144 | tf_op jit(solution)/shard_map/pallas_call | solution.py:56
  47.6 1.3 %shard_map.126 = (bf16[128,1024]{1,0:T(8,128)(2,1)S(1)}, f32[128,1024]{1,0:T(8,128)S(1)}) custom-call(s32[16]{0:T(128)S(1)} %dynamic-slice_bitcast_fusion.refs_0_.offs_ref, bf16[128,1024]{1,0:T(8,128)(2,1)S(1)} %get-tuple-element.118.refs_1_, bf16[1024,128]{1,0:T(8,128)(2,1)S(1)} %get-tuple-element.119.refs_2_, ...), custom_call_target="tpu_custom_call" | custom-call | flops 33554432 | bytes 262144 | tf_op jit(solution)/shard_map/pallas_call | solution.py:56
  48.9 0.6 collective-permute-start.16
  49.5 1.9 %shard_map.127 = (bf16[128,1024]{1,0:T(8,128)(2,1)S(1)}, bf16[128,1024]{1,0:T(8,128)(2,1)S(1)}, f32[128,1024]{1,0:T(8,128)S(1)}, f32[128,1024]{1,0:T(8,128)S(1)}) custom-call(s32[16]{0:T(128)S(1)} %dynamic-slice_bitcast_fusion.refs_0_.offs_ref, bf16[128,1024]{1,0:T(8,128)(2,1)S(1)} %get-tuple-element.118.refs_1_, ...), custom_call_target="tpu_custom_call" | custom-call | flops 67108864 | bytes 524288 | tf_op jit(solution)/shard_map/pallas_call | solution.py:56
  51.3 0.1 collective-permute-start.17
  51.4 0.5 collective-permute-start.20
  51.9 0.1 add_convert_fusion.4
  52.0 1.7 %collective-permute-start.19 = (bf16[64,1024]{1,0:T(8,128)(2,1)S(1)}, bf16[64,1024]{1,0:T(8,128)(2,1)S(1)}, u32[]{:S(2)}, u32[]{:S(2)}) collective-permute-start(bf16[64,1024]{1,0:T(8,128)(2,1)S(1)} %get-tuple-element.171), channel_id=1, source_target_pairs={{0,4},{1,5},{2,0},{3,1},{6,2},{7,3},{10,6},{11,7},{14,10},{15,11},... | collective-permute-start | bytes 393224 | tf_op jit(solution)/shard_map/ppermute | solution.py:357
  53.8 0.3 collective-permute-start.18
  54.1 0.2 convert_add_fusion
  54.3 4.4 %shard_map.128 = (bf16[128,1024]{1,0:T(8,128)(2,1)S(1)}, bf16[128,1024]{1,0:T(8,128)(2,1)S(1)}, f32[128,1024]{1,0:T(8,128)S(1)}, f32[128,1024]{1,0:T(8,128)S(1)}...) custom-call(s32[16]{0:T(128)S(1)} %dynamic-slice_bitcast_fusion.refs_0_.offs_ref, ...), custom_call_target="tpu_custom_call" | custom-call | flops 100663296 | bytes 786432 | tf_op jit(solution)/shard_map/pallas_call | solution.py:56
  58.7 0.2 collective-permute-done.18
  59.1 1.4 %collective-permute-start.21 = (bf16[128,1024]{1,0:T(8,128)(2,1)S(1)}, bf16[128,1024]{1,0:T(8,128)(2,1)S(1)}, u32[]{:S(2)}, u32[]{:S(2)}) collective-permute-start(bf16[128,1024]{1,0:T(8,128)(2,1)S(1)} %pad_maximum_fusion), channel_id=1, source_target_pairs={{0,2},{1,3},{2,6},{3,7},{6,10},{7,11},{10,14},{11,15},{14,12},{15,... | collective-permute-start | bytes 786440 | tf_op jit(solution)/shard_map/ppermute | solution.py:357
  60.5 0.7 collective-permute-start.22
  61.2 0.5 collective-permute-start.25
  61.7 7.0 %shard_map.129 = (bf16[128,1024]{1,0:T(8,128)(2,1)S(1)}, bf16[128,1024]{1,0:T(8,128)(2,1)S(1)}, f32[128,1024]{1,0:T(8,128)S(1)}, f32[128,1024]{1,0:T(8,128)S(1)}...) custom-call(s32[16]{0:T(128)S(1)} %dynamic-slice_bitcast_fusion.refs_0_.offs_ref, ...), custom_call_target="tpu_custom_call", output_to_operand_aliasing={{4}: (16, {})} | custom-call | flops 150994944 | bytes 1179648 | tf_op jit(solution)/shard_map/pallas_call | solution.py:56
  68.7 0.1 add_convert_fusion.3
  68.9 0.1 add_convert_fusion.2
  69.0 1.4 %collective-permute-start.26 = (bf16[128,1024]{1,0:T(8,128)(2,1)S(1)}, bf16[128,1024]{1,0:T(8,128)(2,1)S(1)}, u32[]{:S(2)}, u32[]{:S(2)}) collective-permute-start(bf16[128,1024]{1,0:T(8,128)(2,1)S(1)} %add_convert_fusion.3), channel_id=1, source_target_pairs={{0,2},{1,3},{2,6},{3,7},{6,10},{7,11},{10,14},{11,15},{14,12},{15,... | collective-permute-start | bytes 786440 | tf_op jit(solution)/shard_map/ppermute | solution.py:357
  70.4 0.7 collective-permute-start.27
  71.1 0.5 collective-permute-start.23
  71.6 6.5 %shard_map.130 = (bf16[128,1024]{1,0:T(8,128)(2,1)S(1)}, f32[128,1024]{1,0:T(8,128)S(1)}, bf16[1024,16384]{1,0:T(8,128)(2,1)}, f32[8,128]{1,0:T(8,128)}) custom-call(s32[16]{0:T(128)S(1)} %dynamic-slice_bitcast_fusion.refs_0_.offs_ref, bf16[128,1024]{1,0:T(8,128)(2,1)S(1)} %get-tuple-element.118.refs_1_, ...), custom_call_target="tpu_custom_call", output_to_operand_aliasing={{2}: (16, {})} | custom-call | flops 117440512 | bytes 917504 | tf_op jit(solution)/shard_map/pallas_call | solution.py:56
  78.1 0.2 collective-permute-done.27
  78.3 0.1 add_convert_fusion
  78.4 0.1 add_convert_fusion.1
  78.5 1.6 %collective-permute-start.29 = (bf16[128,1024]{1,0:T(8,128)(2,1)S(1)}, bf16[128,1024]{1,0:T(8,128)(2,1)S(1)}, u32[]{:S(2)}, u32[]{:S(2)}) collective-permute-start(bf16[128,1024]{1,0:T(8,128)(2,1)S(1)} %add_convert_fusion.1), channel_id=1, source_target_pairs={{0,2},{1,3},{2,6},{3,7},{6,10},{7,11},{10,14},{11,15},{14,12},{15,... | collective-permute-start | bytes 786440 | tf_op jit(solution)/shard_map/ppermute | solution.py:357
  80.2 0.4 collective-permute-start.30
  80.6 0.6 shard_map.132
  81.3 5.2 %shard_map.131 = (bf16[1024,16384]{1,0:T(8,128)(2,1)}, f32[8,128]{1,0:T(8,128)}) custom-call(s32[16]{0:T(128)S(1)} %dynamic-slice_bitcast_fusion.refs_0_.offs_ref, bf16[128,1024]{1,0:T(8,128)(2,1)S(1)} %get-tuple-element.118.refs_1_, bf16[1024,128]{1,0:T(8,128)(2,1)S(1)} %get-tuple-element.119.refs_2_, ...), custom_call_target="tpu_custom_call", output_to_operand_aliasing={{0}: (15, {})} | custom-call | flops 67108864 | bytes 524288 | tf_op jit(solution)/shard_map/pallas_call | solution.py:56
  86.5 0.1 collective-permute-done.29
  86.6 1.1 %collective-permute-done.30 = bf16[128,1024]{1,0:T(8,128)(2,1)S(1)} collective-permute-done((bf16[128,1024]{1,0:T(8,128)(2,1)S(1)}, bf16[128,1024]{1,0:T(8,128)(2,1)S(1)}, u32[]{:S(2)}, u32[]{:S(2)}) %collective-permute-start.30) | collective-permute-done | bytes 262176 | tf_op jit(solution)/shard_map/ppermute | solution.py:357
  87.7 1.0 %add_bitcast_fusion = f32[1,128,1024]{2,1,0:T(8,128)} fusion(bf16[128,1024]{1,0:T(8,128)(2,1)S(1)} %collective-permute-done.30, bf16[128,1024]{1,0:T(8,128)(2,1)S(1)} %collective-permute-done.29, f32[128,1024]{1,0:T(8,128)S(1)} %shard_map.132, f32[128,1024]{1,0:T(8,128)S(1)} %get-tuple-element.164, bf16[128,1024]{1,0:T(8,128)(2,1)S(1)} %collective-permute-done.31), kind=kLoop, calls=%fused_computation | loop fusion | flops 917504 | bytes 2359296 | tf_op jit(solution)/shard_map/reshape | solution.py:449
  (54 shorter events, 0.3 us)
Async XLA Ops:
  1.7 11.3 %collective-permute-start.1 = (bf16[128,1024]{1,0:T(8,128)(2,1)S(1)}, bf16[128,1024]{1,0:T(8,128)(2,1)S(1)}, u32[]{:S(2)}, u32[]{:S(2)}) collective-permute-start(bf16[128,1024]{1,0:T(8,128)(2,1)S(1)} %bitcast_convert_fusion.refs_3_.refs_7_.refs_9_), channel_id=1, source_target_pairs={{0,4},{1,5},{2,0},{3,1},{6,2},{7,3},{10,6},{11,7},{14,10},{15,11},... | collective-permute-start | bytes 786440 | tf_op jit(solution)/shard_map/ppermute | solution.py:357
  4.8 8.2 %collective-permute-start = (bf16[128,1024]{1,0:T(8,128)(2,1)S(1)}, bf16[128,1024]{1,0:T(8,128)(2,1)S(1)}, u32[]{:S(2)}, u32[]{:S(2)}) collective-permute-start(bf16[128,1024]{1,0:T(8,128)(2,1)S(1)} %bitcast_convert_fusion.refs_3_.refs_7_.refs_9_), channel_id=1, source_target_pairs={{0,2},{1,3},{2,6},{3,7},{6,10},{7,11},{10,14},{11,15},{14,12},{15,... | collective-permute-start | bytes 786440 | tf_op jit(solution)/shard_map/ppermute | solution.py:357
  4.8 10.9 %collective-permute-start.4 = (bf16[128,1024]{1,0:T(8,128)(2,1)S(1)}, bf16[128,1024]{1,0:T(8,128)(2,1)S(1)}, u32[]{:S(2)}, u32[]{:S(2)}) collective-permute-start(bf16[128,1024]{1,0:T(8,128)(2,1)S(1)} %bitcast_convert_fusion.refs_3_.refs_7_.refs_9_), channel_id=1, source_target_pairs={{0,1},{1,0},{2,3},{3,2},{4,5},{5,4},{6,7},{7,6},{8,9},{9,8},{10,11... | collective-permute-start | bytes 786440 | tf_op jit(solution)/shard_map/ppermute | solution.py:360
  13.0 8.7 %copy-start.1 = (bf16[128,1024]{1,0:T(8,128)(2,1)}, bf16[128,1024]{1,0:T(8,128)(2,1)S(1)}, u32[]{:S(2)}) copy-start(bf16[128,1024]{1,0:T(8,128)(2,1)S(1)} %collective-permute-done.refs_9_.refs_11_.refs_3_) | copy-start | bytes 786436
  13.0 9.1 %collective-permute-start.2 = (bf16[128,1024]{1,0:T(8,128)(2,1)S(1)}, bf16[128,1024]{1,0:T(8,128)(2,1)S(1)}, u32[]{:S(2)}, u32[]{:S(2)}) collective-permute-start(bf16[128,1024]{1,0:T(8,128)(2,1)S(1)} %collective-permute-done.refs_9_.refs_11_.refs_3_), channel_id=1, source_target_pairs={{0,2},{1,3},{2,6},{3,7},{6,10},{7,11},{10,14},{11,15},{14,12},{15,... | collective-permute-start | bytes 786440 | tf_op jit(solution)/shard_map/ppermute | solution.py:357
  15.0 8.4 %collective-permute-start.3 = (bf16[128,1024]{1,0:T(8,128)(2,1)S(1)}, bf16[128,1024]{1,0:T(8,128)(2,1)S(1)}, u32[]{:S(2)}, u32[]{:S(2)}) collective-permute-start(bf16[128,1024]{1,0:T(8,128)(2,1)S(1)} %collective-permute-done.1.refs_10_.refs_12_.refs_4_), channel_id=1, source_target_pairs={{0,4},{1,5},{2,0},{3,1},{6,2},{7,3},{10,6},{11,7},{14,10},{15,11},... | collective-permute-start | bytes 786440 | tf_op jit(solution)/shard_map/ppermute | solution.py:357
  15.2 10.3 %collective-permute-start.7 = (bf16[128,1024]{1,0:T(8,128)(2,1)S(1)}, bf16[128,1024]{1,0:T(8,128)(2,1)S(1)}, u32[]{:S(2)}, u32[]{:S(2)}) collective-permute-start(bf16[128,1024]{1,0:T(8,128)(2,1)S(1)} %collective-permute-done.refs_9_.refs_11_.refs_3_), channel_id=1, source_target_pairs={{0,1},{1,0},{2,3},{3,2},{4,5},{5,4},{6,7},{7,6},{8,9},{9,8},{10,11... | collective-permute-start | bytes 786440 | tf_op jit(solution)/shard_map/ppermute | solution.py:360
  15.4 11.2 %collective-permute-start.8 = (bf16[128,1024]{1,0:T(8,128)(2,1)S(1)}, bf16[128,1024]{1,0:T(8,128)(2,1)S(1)}, u32[]{:S(2)}, u32[]{:S(2)}) collective-permute-start(bf16[128,1024]{1,0:T(8,128)(2,1)S(1)} %collective-permute-done.1.refs_10_.refs_12_.refs_4_), channel_id=1, source_target_pairs={{0,1},{1,0},{2,3},{3,2},{4,5},{5,4},{6,7},{7,6},{8,9},{9,8},{10,11... | collective-permute-start | bytes 786440 | tf_op jit(solution)/shard_map/ppermute | solution.py:360
  15.7 6.0 %copy-start.4 = (bf16[128,1024]{1,0:T(8,128)(2,1)}, bf16[128,1024]{1,0:T(8,128)(2,1)S(1)}, u32[]{:S(2)}) copy-start(bf16[128,1024]{1,0:T(8,128)(2,1)S(1)} %collective-permute-done.4.refs_8_.refs_10_.refs_4_) | copy-start | bytes 786436
  15.7 10.3 %copy-start = (f32[1,128,1024]{2,1,0:T(8,128)S(1)}, f32[1,128,1024]{2,1,0:T(8,128)}, u32[]{:S(2)}) copy-start(f32[1,128,1024]{2,1,0:T(8,128)} %param.8) | copy-start | bytes 1572868
  15.7 10.3 %copy-start.6 = (f32[128,128]{1,0:T(8,128)S(1)}, f32[128,128]{1,0:T(8,128)}, u32[]{:S(2)}) copy-start(f32[128,128]{1,0:T(8,128)} %constant.13.clone.cheb_ref) | copy-start | bytes 196612
  15.7 10.3 %copy-start.7 = (f32[16,1024]{1,0:T(8,128)S(1)}, f32[16,1024]{1,0:T(8,128)}, u32[]{:S(2)}) copy-start(f32[16,1024]{1,0:T(8,128)} %pert_ref.1) | copy-start | bytes 196612
  23.5 13.9 %collective-permute-start.5 = (bf16[128,1024]{1,0:T(8,128)(2,1)S(1)}, bf16[128,1024]{1,0:T(8,128)(2,1)S(1)}, u32[]{:S(2)}, u32[]{:S(2)}) collective-permute-start(bf16[128,1024]{1,0:T(8,128)(2,1)S(1)} %collective-permute-done.2.refs_15_.refs_7_), channel_id=1, source_target_pairs={{0,2},{1,3},{2,6},{3,7},{6,10},{7,11},{10,14},{11,15},{14,12},{15,... | collective-permute-start | bytes 786440 | tf_op jit(solution)/shard_map/ppermute | solution.py:357
  25.0 12.3 %collective-permute-start.6 = (bf16[128,1024]{1,0:T(8,128)(2,1)S(1)}, bf16[128,1024]{1,0:T(8,128)(2,1)S(1)}, u32[]{:S(2)}, u32[]{:S(2)}) collective-permute-start(bf16[128,1024]{1,0:T(8,128)(2,1)S(1)} %collective-permute-done.3.refs_16_.refs_3_), channel_id=1, source_target_pairs={{0,4},{1,5},{2,0},{3,1},{6,2},{7,3},{10,6},{11,7},{14,10},{15,11},... | collective-permute-start | bytes 786440 | tf_op jit(solution)/shard_map/ppermute | solution.py:357
  25.5 14.0 %collective-permute-start.11 = (bf16[128,1024]{1,0:T(8,128)(2,1)S(1)}, bf16[128,1024]{1,0:T(8,128)(2,1)S(1)}, u32[]{:S(2)}, u32[]{:S(2)}) collective-permute-start(bf16[128,1024]{1,0:T(8,128)(2,1)S(1)} %collective-permute-done.2.refs_15_.refs_7_), channel_id=1, source_target_pairs={{0,1},{1,0},{2,3},{3,2},{4,5},{5,4},{6,7},{7,6},{8,9},{9,8},{10,11... | collective-permute-start | bytes 786440 | tf_op jit(solution)/shard_map/ppermute | solution.py:360
  25.5 14.5 %collective-permute-start.12 = (bf16[128,1024]{1,0:T(8,128)(2,1)S(1)}, bf16[128,1024]{1,0:T(8,128)(2,1)S(1)}, u32[]{:S(2)}, u32[]{:S(2)}) collective-permute-start(bf16[128,1024]{1,0:T(8,128)(2,1)S(1)} %collective-permute-done.3.refs_16_.refs_3_), channel_id=1, source_target_pairs={{0,1},{1,0},{2,3},{3,2},{4,5},{5,4},{6,7},{7,6},{8,9},{9,8},{10,11... | collective-permute-start | bytes 786440 | tf_op jit(solution)/shard_map/ppermute | solution.py:360
  26.6 1.0 %copy-start.2 = (bf16[128,1024]{1,0:T(8,128)(2,1)S(1)}, bf16[128,1024]{1,0:T(8,128)(2,1)}, u32[]{:S(2)}) copy-start(bf16[128,1024]{1,0:T(8,128)(2,1)} %copy-done.1) | copy-start | bytes 786436
  27.6 0.9 %copy-start.5 = (bf16[128,1024]{1,0:T(8,128)(2,1)S(1)}, bf16[128,1024]{1,0:T(8,128)(2,1)}, u32[]{:S(2)}) copy-start(bf16[128,1024]{1,0:T(8,128)(2,1)} %copy-done.4) | copy-start | bytes 786436
  37.4 5.5 %collective-permute-start.10 = (bf16[64,1024]{1,0:T(8,128)(2,1)S(1)}, bf16[64,1024]{1,0:T(8,128)(2,1)S(1)}, u32[]{:S(2)}, u32[]{:S(2)}) collective-permute-start(bf16[64,1024]{1,0:T(8,128)(2,1)S(1)} %slice.27), channel_id=1, source_target_pairs={{0,4},{1,5},{2,0},{3,1},{6,2},{7,3},{10,6},{11,7},{14,10},{15,11},... | collective-permute-start | bytes 393224 | tf_op jit(solution)/shard_map/ppermute | solution.py:357
  37.9 5.1 %collective-permute-start.9 = (bf16[64,1024]{1,0:T(8,128)(2,1)S(1)}, bf16[64,1024]{1,0:T(8,128)(2,1)S(1)}, u32[]{:S(2)}, u32[]{:S(2)}) collective-permute-start(bf16[64,1024]{1,0:T(8,128)(2,1)S(1)} %slice.26), channel_id=1, source_target_pairs={{0,2},{1,3},{2,6},{3,7},{6,10},{7,11},{10,14},{11,15},{14,12},{15,... | collective-permute-start | bytes 393224 | tf_op jit(solution)/shard_map/ppermute | solution.py:357
  39.5 3.7 %collective-permute-start.14 = (bf16[128,1024]{1,0:T(8,128)(2,1)S(1)}, bf16[128,1024]{1,0:T(8,128)(2,1)S(1)}, u32[]{:S(2)}, u32[]{:S(2)}) collective-permute-start(bf16[128,1024]{1,0:T(8,128)(2,1)S(1)} %collective-permute-done.5.refs_12_.refs_6_), channel_id=1, source_target_pairs={{0,1},{1,0},{2,3},{3,2},{4,5},{5,4},{6,7},{7,6},{8,9},{9,8},{10,11... | collective-permute-start | bytes 786440 | tf_op jit(solution)/shard_map/ppermute | solution.py:360
  39.5 3.7 %collective-permute-start.15 = (bf16[128,1024]{1,0:T(8,128)(2,1)S(1)}, bf16[128,1024]{1,0:T(8,128)(2,1)S(1)}, u32[]{:S(2)}, u32[]{:S(2)}) collective-permute-start(bf16[128,1024]{1,0:T(8,128)(2,1)S(1)} %collective-permute-done.6.refs_13_.refs_7_), channel_id=1, source_target_pairs={{0,1},{1,0},{2,3},{3,2},{4,5},{5,4},{6,7},{7,6},{8,9},{9,8},{10,11... | collective-permute-start | bytes 786440 | tf_op jit(solution)/shard_map/ppermute | solution.py:360
  43.0 2.5 %copy-start.8 = (f32[1024]{0:T(1024)S(1)}, f32[1024]{0:T(1024)}, u32[]{:S(2)}) copy-start(f32[1024]{0:T(1024)} %param.12) | copy-start | bytes 12292
  43.1 2.5 %copy-start.9 = (f32[1024]{0:T(1024)S(1)}, f32[1024]{0:T(1024)}, u32[]{:S(2)}) copy-start(f32[1024]{0:T(1024)} %param.11) | copy-start | bytes 12292
  43.1 2.5 %collective-permute-start.13 = (bf16[128,1024]{1,0:T(8,128)(2,1)S(1)}, bf16[128,1024]{1,0:T(8,128)(2,1)S(1)}, u32[]{:S(2)}, u32[]{:S(2)}) collective-permute-start(bf16[128,1024]{1,0:T(8,128)(2,1)S(1)} %constant_dynamic-update-slice_fusion.refs_12_.refs_5_), channel_id=1, source_target_pairs={{0,1},{1,0},{2,3},{3,2},{4,5},{5,4},{6,7},{7,6},{8,9},{9,8},{10,11... | collective-permute-start | bytes 786440 | tf_op jit(solution)/shard_map/ppermute | solution.py:360
  48.9 3.0 %collective-permute-start.16 = (bf16[128,1024]{1,0:T(8,128)(2,1)S(1)}, bf16[128,1024]{1,0:T(8,128)(2,1)S(1)}, u32[]{:S(2)}, u32[]{:S(2)}) collective-permute-start(bf16[128,1024]{1,0:T(8,128)(2,1)S(1)} %get-tuple-element.121), channel_id=1, source_target_pairs={{0,1},{1,0},{2,3},{3,2},{4,5},{5,4},{6,7},{7,6},{8,9},{9,8},{10,11... | collective-permute-start | bytes 786440 | tf_op jit(solution)/shard_map/ppermute | solution.py:360
  51.3 2.8 %collective-permute-start.17 = (bf16[128,1024]{1,0:T(8,128)(2,1)S(1)}, bf16[128,1024]{1,0:T(8,128)(2,1)S(1)}, u32[]{:S(2)}, u32[]{:S(2)}) collective-permute-start(bf16[128,1024]{1,0:T(8,128)(2,1)S(1)} %get-tuple-element.125), channel_id=1, source_target_pairs={{0,1},{1,0},{2,3},{3,2},{4,5},{5,4},{6,7},{7,6},{8,9},{9,8},{10,11... | collective-permute-start | bytes 786440 | tf_op jit(solution)/shard_map/ppermute | solution.py:360
  51.4 2.7 %collective-permute-start.20 = (bf16[128,1024]{1,0:T(8,128)(2,1)S(1)}, bf16[128,1024]{1,0:T(8,128)(2,1)S(1)}, u32[]{:S(2)}, u32[]{:S(2)}) collective-permute-start(bf16[128,1024]{1,0:T(8,128)(2,1)S(1)} %get-tuple-element.132), channel_id=1, source_target_pairs={{0,1},{1,0},{2,3},{3,2},{4,5},{5,4},{6,7},{7,6},{8,9},{9,8},{10,11... | collective-permute-start | bytes 786440 | tf_op jit(solution)/shard_map/ppermute | solution.py:360
  52.0 6.7 %collective-permute-start.19 = (bf16[64,1024]{1,0:T(8,128)(2,1)S(1)}, bf16[64,1024]{1,0:T(8,128)(2,1)S(1)}, u32[]{:S(2)}, u32[]{:S(2)}) collective-permute-start(bf16[64,1024]{1,0:T(8,128)(2,1)S(1)} %get-tuple-element.171), channel_id=1, source_target_pairs={{0,4},{1,5},{2,0},{3,1},{6,2},{7,3},{10,6},{11,7},{14,10},{15,11},... | collective-permute-start | bytes 393224 | tf_op jit(solution)/shard_map/ppermute | solution.py:357
  53.8 5.2 %collective-permute-start.18 = (bf16[64,1024]{1,0:T(8,128)(2,1)S(1)}, bf16[64,1024]{1,0:T(8,128)(2,1)S(1)}, u32[]{:S(2)}, u32[]{:S(2)}) collective-permute-start(bf16[64,1024]{1,0:T(8,128)(2,1)S(1)} %get-tuple-element.172), channel_id=1, source_target_pairs={{0,2},{1,3},{2,6},{3,7},{6,10},{7,11},{10,14},{11,15},{14,12},{15,... | collective-permute-start | bytes 393224 | tf_op jit(solution)/shard_map/ppermute | solution.py:357
  54.3 7.4 %copy-start.3 = (bf16[128,1024]{1,0:T(8,128)(2,1)S(1)}, bf16[128,1024]{1,0:T(8,128)(2,1)}, u32[]{:S(2)}) copy-start(bf16[128,1024]{1,0:T(8,128)(2,1)} %copy-done.1) | copy-start | bytes 786436
  59.1 9.6 %collective-permute-start.21 = (bf16[128,1024]{1,0:T(8,128)(2,1)S(1)}, bf16[128,1024]{1,0:T(8,128)(2,1)S(1)}, u32[]{:S(2)}, u32[]{:S(2)}) collective-permute-start(bf16[128,1024]{1,0:T(8,128)(2,1)S(1)} %pad_maximum_fusion), channel_id=1, source_target_pairs={{0,2},{1,3},{2,6},{3,7},{6,10},{7,11},{10,14},{11,15},{14,12},{15,... | collective-permute-start | bytes 786440 | tf_op jit(solution)/shard_map/ppermute | solution.py:357
  60.5 8.2 %collective-permute-start.22 = (bf16[128,1024]{1,0:T(8,128)(2,1)S(1)}, bf16[128,1024]{1,0:T(8,128)(2,1)S(1)}, u32[]{:S(2)}, u32[]{:S(2)}) collective-permute-start(bf16[128,1024]{1,0:T(8,128)(2,1)S(1)} %pad_maximum_fusion.1), channel_id=1, source_target_pairs={{0,4},{1,5},{2,0},{3,1},{6,2},{7,3},{10,6},{11,7},{14,10},{15,11},... | collective-permute-start | bytes 786440 | tf_op jit(solution)/shard_map/ppermute | solution.py:357
  61.2 7.6 %collective-permute-start.24 = (bf16[128,1024]{1,0:T(8,128)(2,1)S(1)}, bf16[128,1024]{1,0:T(8,128)(2,1)S(1)}, u32[]{:S(2)}, u32[]{:S(2)}) collective-permute-start(bf16[128,1024]{1,0:T(8,128)(2,1)S(1)} %get-tuple-element.143), channel_id=1, source_target_pairs={{0,1},{1,0},{2,3},{3,2},{4,5},{5,4},{6,7},{7,6},{8,9},{9,8},{10,11... | collective-permute-start | bytes 786440 | tf_op jit(solution)/shard_map/ppermute | solution.py:360
  61.2 7.7 %collective-permute-start.25 = (bf16[128,1024]{1,0:T(8,128)(2,1)S(1)}, bf16[128,1024]{1,0:T(8,128)(2,1)S(1)}, u32[]{:S(2)}, u32[]{:S(2)}) collective-permute-start(bf16[128,1024]{1,0:T(8,128)(2,1)S(1)} %get-tuple-element.146), channel_id=1, source_target_pairs={{0,1},{1,0},{2,3},{3,2},{4,5},{5,4},{6,7},{7,6},{8,9},{9,8},{10,11... | collective-permute-start | bytes 786440 | tf_op jit(solution)/shard_map/ppermute | solution.py:360
  69.0 9.1 %collective-permute-start.26 = (bf16[128,1024]{1,0:T(8,128)(2,1)S(1)}, bf16[128,1024]{1,0:T(8,128)(2,1)S(1)}, u32[]{:S(2)}, u32[]{:S(2)}) collective-permute-start(bf16[128,1024]{1,0:T(8,128)(2,1)S(1)} %add_convert_fusion.3), channel_id=1, source_target_pairs={{0,2},{1,3},{2,6},{3,7},{6,10},{7,11},{10,14},{11,15},{14,12},{15,... | collective-permute-start | bytes 786440 | tf_op jit(solution)/shard_map/ppermute | solution.py:357
  70.4 7.9 %collective-permute-start.27 = (bf16[128,1024]{1,0:T(8,128)(2,1)S(1)}, bf16[128,1024]{1,0:T(8,128)(2,1)S(1)}, u32[]{:S(2)}, u32[]{:S(2)}) collective-permute-start(bf16[128,1024]{1,0:T(8,128)(2,1)S(1)} %add_convert_fusion.2), channel_id=1, source_target_pairs={{0,4},{1,5},{2,0},{3,1},{6,2},{7,3},{10,6},{11,7},{14,10},{15,11},... | collective-permute-start | bytes 786440 | tf_op jit(solution)/shard_map/ppermute | solution.py:357
  71.0 7.3 %collective-permute-start.28 = (bf16[128,1024]{1,0:T(8,128)(2,1)S(1)}, bf16[128,1024]{1,0:T(8,128)(2,1)S(1)}, u32[]{:S(2)}, u32[]{:S(2)}) collective-permute-start(bf16[128,1024]{1,0:T(8,128)(2,1)S(1)} %get-tuple-element.155), channel_id=1, source_target_pairs={{0,1},{1,0},{2,3},{3,2},{4,5},{5,4},{6,7},{7,6},{8,9},{9,8},{10,11... | collective-permute-start | bytes 786440 | tf_op jit(solution)/shard_map/ppermute | solution.py:360
  71.1 7.4 %collective-permute-start.23 = (bf16[128,1024]{1,0:T(8,128)(2,1)S(1)}, bf16[128,1024]{1,0:T(8,128)(2,1)S(1)}, u32[]{:S(2)}, u32[]{:S(2)}) collective-permute-start(bf16[128,1024]{1,0:T(8,128)(2,1)S(1)} %get-tuple-element.141), channel_id=1, source_target_pairs={{0,1},{1,0},{2,3},{3,2},{4,5},{5,4},{6,7},{7,6},{8,9},{9,8},{10,11... | collective-permute-start | bytes 786440 | tf_op jit(solution)/shard_map/ppermute | solution.py:360
  78.5 8.0 %collective-permute-start.29 = (bf16[128,1024]{1,0:T(8,128)(2,1)S(1)}, bf16[128,1024]{1,0:T(8,128)(2,1)S(1)}, u32[]{:S(2)}, u32[]{:S(2)}) collective-permute-start(bf16[128,1024]{1,0:T(8,128)(2,1)S(1)} %add_convert_fusion.1), channel_id=1, source_target_pairs={{0,2},{1,3},{2,6},{3,7},{6,10},{7,11},{10,14},{11,15},{14,12},{15,... | collective-permute-start | bytes 786440 | tf_op jit(solution)/shard_map/ppermute | solution.py:357
  80.2 7.5 %collective-permute-start.30 = (bf16[128,1024]{1,0:T(8,128)(2,1)S(1)}, bf16[128,1024]{1,0:T(8,128)(2,1)S(1)}, u32[]{:S(2)}, u32[]{:S(2)}) collective-permute-start(bf16[128,1024]{1,0:T(8,128)(2,1)S(1)} %add_convert_fusion), channel_id=1, source_target_pairs={{0,4},{1,5},{2,0},{3,1},{6,2},{7,3},{10,6},{11,7},{14,10},{15,11},... | collective-permute-start | bytes 786440 | tf_op jit(solution)/shard_map/ppermute | solution.py:357
  80.6 7.0 %collective-permute-start.31 = (bf16[128,1024]{1,0:T(8,128)(2,1)S(1)}, bf16[128,1024]{1,0:T(8,128)(2,1)S(1)}, u32[]{:S(2)}, u32[]{:S(2)}) collective-permute-start(bf16[128,1024]{1,0:T(8,128)(2,1)S(1)} %get-tuple-element.165), channel_id=1, source_target_pairs={{0,1},{1,0},{2,3},{3,2},{4,5},{5,4},{6,7},{7,6},{8,9},{9,8},{10,11... | collective-permute-start | bytes 786440 | tf_op jit(solution)/shard_map/ppermute | solution.py:360

commit v8 on v7

--- a/solution.py
+++ b/solution.py
@@ -10,8 +10,9 @@
 
 SCALE = 2.0 / 1024.0
 VMEM_LIMIT = 8 * 2**20
-BANDS = 8
-LOADS = (4, 2, 2)
+BANDS = 16
+GROUP = 4
+LOADS = (10, 6)
 LONGEST_RING = 16
 
 
@@ -84,8 +85,8 @@
 def product(bands, here, x_ref):
     rows = [band_ref[:, here] for band_ref in bands]
     return lax.dot_general(
-        rows[0] if len(rows) == 1 else jnp.concatenate(rows, axis=0),
-        x_ref[...], (((1,), (1,)), ((), ())), preferred_element_type=jnp.float32,
+        x_ref[...], rows[0] if len(rows) == 1 else jnp.concatenate(rows, axis=0),
+        (((1,), (1,)), ((), ())), preferred_element_type=jnp.float32,
     )
 
 
@@ -101,25 +102,25 @@
     xs, refs = refs[: count + (done if late else 0)], refs[count + (done if late else 0) :]
     out_ref, others, sems = refs[0], refs[1 : 1 + late], refs[-1]
     slab = xs[0].shape[1]
-    tile = out_ref.shape[0] // BANDS
+    tile = out_ref.shape[1] // BANDS
     copies = load_bands(w_ref, others, sems, many) if late else []
     places = [columns_of(offs_ref, base + at, slab) for at in range(done + count)]
-    for low in range(0, many, 2):
-        pair = bands[low : low + 2]
-        rows = pl.ds(low * tile, len(pair) * tile)
-        total = acc_ref[rows, :]
+    for low in range(0, many, GROUP):
+        group = bands[low : low + GROUP]
+        rows = pl.ds(low * tile, len(group) * tile)
+        total = acc_ref[:, rows]
         for at, x_ref in enumerate(xs[-count:]):
-            total += product(pair, places[done + at], x_ref)
-        out_ref[rows, :] = total
-    for copy in copies:
-        copy.wait()
-    for low in range(0, late, 2):
-        pair = others[low : low + 2]
-        rows = pl.ds((many + low) * tile, len(pair) * tile)
-        total = product(pair, places[0], xs[0])
+            total += product(group, places[done + at], x_ref)
+        out_ref[:, rows] = total
+    for low in range(0, late, GROUP):
+        for copy in copies[low : low + GROUP]:
+            copy.wait()
+        group = others[low : low + GROUP]
+        rows = pl.ds((many + low) * tile, len(group) * tile)
+        total = product(group, places[0], xs[0])
         for at in range(1, len(xs)):
-            total += product(pair, places[at], xs[at])
-        out_ref[rows, :] = total
+            total += product(group, places[at], xs[at])
+        out_ref[:, rows] = total
 
 
 def add_products(offs, perts, weights, acc, bands, before, xs, late):
@@ -136,7 +137,7 @@
     specs += [VMEM_REF] * (len(operands) - len(specs))
     acc, *others = call(
         functools.partial(pre_kernel, 0, done, count, many, late, first),
-        [jax.ShapeDtypeStruct((rows, nodes), jnp.float32)]
+        [jax.ShapeDtypeStruct((nodes, rows), jnp.float32)]
         + [pltpu.VMEM((rows // BANDS, genes), weights.dtype)] * late,
         [VMEM_REF] * (1 + late),
         [pltpu.SemaphoreType.DMA((max(late, 1),))],
@@ -192,13 +193,13 @@
     bands = refs[:many]
     acc_ref, deriv_ref, drive_ref, chosen_ref, states_ref, eps_ref, decay_ref = refs[many:-6]
     resid_ref, delta_ref, delta_t_ref, table_ref, sum_eps_ref, sum_decay_ref = refs[-6:]
-    tile = 2 * bands[0].shape[0]
+    tile = GROUP * bands[0].shape[0]
     here = columns_of(offs_ref, base, x_ref.shape[1])
-    for at in range(many // 2):
+    for at in range(many // GROUP):
         band = pl.ds(at * tile, tile)
-        part = acc_ref[band, :] + product(bands[2 * at : 2 * at + 2], here, x_ref)
+        part = acc_ref[:, band] + product(bands[at * GROUP : (at + 1) * GROUP], here, x_ref)
         states = states_ref[:, band]
-        act = jnp.tanh(part.T + drive_ref[:, band])
+        act = jnp.tanh(part + drive_ref[:, band])
         eps = eps_ref[:, band]
         resid = deriv_ref[:, band] - (eps * act - decay_ref[:, band] * states)
         delta = (-eps * (1.0 - act * act) * resid).astype(jnp.bfloat16)
@@ -213,7 +214,7 @@
 
 def middle(offs, base, x, bands, acc, derivs, states, eps, decay):
     nodes, slab = x.shape
-    rows = acc.shape[0]
+    rows = acc.shape[1]
     wide = functools.partial(jax.ShapeDtypeStruct, dtype=jnp.float32)
     return call(
         functools.partial(middle_kernel, base, len(bands)),
@@ -257,17 +258,18 @@
 
 
 def share_part(places, offs_ref, delta_ref, bands, outs):
-    depth = 2 * bands[0].shape[0]
+    depth = GROUP * bands[0].shape[0]
     for place, out_ref in zip(places, outs):
         slab = out_ref.shape[1]
         tile = max(slab // 2, 128)
         for col in range(0, slab, tile):
             there = pl.ds(pl.multiple_of(offs_ref[place] * slab + col, tile), tile)
             part = None
-            for low in range(0, len(bands), 2):
-                pair = jnp.concatenate([ref[:, there] for ref in bands[low : low + 2]], axis=0)
+            for at in range(len(bands) // GROUP):
+                group = bands[at * GROUP : (at + 1) * GROUP]
                 more = jnp.dot(
-                    delta_ref[:, low // 2 * depth : (low // 2 + 1) * depth], pair,
+                    delta_ref[:, at * depth : (at + 1) * depth],
+                    jnp.concatenate([ref[:, there] for ref in group], axis=0),
                     preferred_element_type=jnp.float32,
                 )
                 part = more if part is None else part + more
@@ -280,8 +282,7 @@
     refs = refs[3 + count + many + (0 if first else 1) :]
     outs, copies = refs[: len(places)], []
     if count:
-        out_ref, mark_ref, held, sems = refs[len(places) :]
-        mark_ref[...] = jnp.zeros_like(mark_ref)
+        out_ref, held, sems = refs[len(places) :]
         copies = grad_w_part(base, offs_ref, delta_t_ref, xs, out_ref, held, sems)
     share_part(places, offs_ref, delta_ref, bands, outs)
     for copy in copies:
@@ -299,9 +300,8 @@
     if count:
         shapes += [
             jax.ShapeDtypeStruct(shape, jnp.bfloat16),
-            jax.ShapeDtypeStruct((8, 128), jnp.float32),
         ]
-        specs += [ANY_REF, VMEM_REF]
+        specs += [ANY_REF]
         scratch = [pltpu.VMEM((4, tile, slab), jnp.bfloat16), pltpu.SemaphoreType.DMA((4,))]
     operands = [offs, delta, delta_t, *xs, *bands] + ([] if first else [so_far])
     outs = call(
@@ -409,23 +409,24 @@
         others, owns, rest = sums(
             offs, base, xs, places, delta, delta_t, bands, slab, grad_w, weights.shape
         )
-        grad_w, mark = rest if count else (grad_w, None)
-        return others, owns, grad_w, base + count, mark
+        if count:
+            (grad_w,) = rest
+        return others, owns, grad_w, base + count
 
     def joined(others, owns):
         return [own + swap(other).astype(jnp.float32) for other, own in zip(others, owns)]
 
-    counts = [2, 5, 5]
+    counts = [2, 4, 5]
     counts.append(len(listing) - sum(counts))
-    others, owns, _, _, _ = work(offs, 0, [half], None, 0)
+    others, owns, _, _ = work(offs, 0, [half], None, 0)
     (far,) = joined(others, owns)
-    others, owns, _, _, _ = work(offs, 0, [half - 1, 1 - half], None, 0)
+    others, owns, _, _ = work(offs, 0, [half - 1, 1 - half], None, 0)
     far, offs, *owns = gate((far.astype(jnp.bfloat16), offs, *owns))
     own_ahead, own_behind = joined(others, owns)
     ahead, behind = ring(far[:cut], 1), ring(far[cut:], -1)
     for step in range(half - 1, -1, -1):
         steps = [] if step == 0 else [0] if step == 1 else [step - 1, 1 - step]
-        others, owns, grad_w, base, mark = work(offs, counts.pop(0), steps, grad_w, base)
+        others, owns, grad_w, base = work(offs, counts.pop(0), steps, grad_w, base)
         if step == 0:
             break
         ahead, behind, *owns = gate((ahead, behind, *owns))

time: 88.9 us -> 85 us (0.956)
  Pallas kernels: 56.4 us -> 52.6 us
  waiting for transfers between devices: 3.61 us -> 5.53 us
  local copies, waits for them, and re-layouts: 2.72 us -> 0.81 us
    pallas_call x14, Pallas kernels: 56.4 us -> 52.6 us  [run(): pl.pallas_call(kernel, out_shape=out_shape, in_specs=in_specs, out_specs=...]
    ppermute x16, waiting for transfers between devices: 3.57 us -> 5.48 us  [ring(): return lax.ppermute(array, 'row', pairs)]
    unnamed x21 -> x11, local copies, waits for them, and re-layouts: 1.94 us -> 0.03 us
  transfers between devices with their start and end apart: 32 -> 32, of which waited for: 7 -> 7; matrix products, arithmetic and copies ran while one was open for 1% -> 1% of each run, Pallas kernels for 60% -> 58%
where the time goes in v8:
time: 85 us; the launch traced here: 84.8 us
  Pallas kernels  52.6 us (62%)
  starting transfers between devices  21.4 us (25%)
  waiting for transfers between devices  5.53 us (7%)
  other arithmetic  2.77 us (3%)
  between operations  1.68 us (2%)
    pallas_call x14, Pallas kernels, run(): pl.pallas_call(kernel, out_shape=out_shape, in_specs=in_specs, out_specs=...  52.6 us
    ppermute x16, starting transfers between devices, ring(): return lax.ppermute(array, 'row', pairs)  17.6 us
    ppermute x16, waiting for transfers between devices, ring(): return lax.ppermute(array, 'row', pairs)  5.48 us
    ppermute x16, starting transfers between devices, swap(): return lax.ppermute(array, 'row', [(i, i ^ 1) for i in range(2 * chips)])  3.75 us
  transfers between devices with their start and end apart: 32, of which 7 were waited for; matrix products, arithmetic and copies ran while one was open for 1% of the time, Pallas kernels for 58%

profile of v8, /device:TPU:0, one launch (start us, length us, event | category | flops | bytes accessed | tf_op | source)
XLA Modules:
  0.0 84.8 jit_solution(15582201387702604167)
XLA Ops:
  0.6 1.1 %bitcast_convert_fusion.refs_3_.refs_13_ = bf16[128,1024]{1,0:T(8,128)(2,1)S(1)} fusion(f32[1,128,1024]{2,1,0:T(8,128)} %param.8), kind=kLoop, calls=%fused_computation.19 | loop fusion | flops 131072 | bytes 786432 | tf_op jit(solution)/shard_map/convert_element_type | solution.py:365
  1.7 3.1 %collective-permute-start.1 = (bf16[128,1024]{1,0:T(8,128)(2,1)S(1)}, bf16[128,1024]{1,0:T(8,128)(2,1)S(1)}, u32[]{:S(2)}, u32[]{:S(2)}) collective-permute-start(bf16[128,1024]{1,0:T(8,128)(2,1)S(1)} %bitcast_convert_fusion.refs_3_.refs_13_), channel_id=1, source_target_pairs={{0,4},{1,5},{2,0},{3,1},{6,2},{7,3},{10,6},{11,7},{14,10},{15,11},... | collective-permute-start | bytes 786440 | tf_op jit(solution)/shard_map/ppermute | solution.py:357
  4.8 0.7 dynamic-slice_bitcast_fusion.refs_0_.offs_ref
  6.1 8.0 %shard_map.119 = (f32[128,1024]{1,0:T(8,128)S(1)}, bf16[64,16384]{1,0:T(8,128)(2,1)S(1)}, bf16[64,16384]{1,0:T(8,128)(2,1)S(1)}, bf16[64,16384]{1,0:T(8,128)(2,1...) custom-call(s32[16]{0:T(128)S(1)} %dynamic-slice_bitcast_fusion.refs, ...), custom_call_target="tpu_custom_call" | custom-call | flops 16777216 | bytes 131072 | tf_op jit(solution)/shard_map/pallas_call | solution.py:57
  14.1 0.0 collective-permute-done.refs_15_.refs_3_
  14.1 2.0 %collective-permute-start.2 = (bf16[128,1024]{1,0:T(8,128)(2,1)S(1)}, bf16[128,1024]{1,0:T(8,128)(2,1)S(1)}, u32[]{:S(2)}, u32[]{:S(2)}) collective-permute-start(bf16[128,1024]{1,0:T(8,128)(2,1)S(1)} %collective-permute-done.refs_15_.refs_3_), channel_id=1, source_target_pairs={{0,2},{1,3},{2,6},{3,7},{6,10},{7,11},{10,14},{11,15},{14,12},{15,... | collective-permute-start | bytes 786440 | tf_op jit(solution)/shard_map/ppermute | solution.py:357
  16.1 0.2 collective-permute-start.3
  16.3 0.2 collective-permute-start.7
  16.5 0.3 collective-permute-start.8
  16.8 0.0 collective-permute-done.4.refs_14_.refs_4_
  16.8 7.5 %shard_map.120 = (f32[128,1024]{1,0:T(8,128)S(1)}, bf16[64,16384]{1,0:T(8,128)(2,1)S(1)}, bf16[64,16384]{1,0:T(8,128)(2,1)S(1)}, bf16[64,16384]{1,0:T(8,128)(2,1...) custom-call(s32[16]{0:T(128)S(1)} %dynamic-slice_bitcast_fusion.refs_0_.offs_ref,, ...), custom_call_target="tpu_custom_call" | custom-call | flops 50331648 | bytes 393216 | tf_op jit(solution)/shard_map/pallas_call | solution.py:57
  24.3 0.0 collective-permute-done.2.refs_20_.refs_3_
  24.3 0.3 collective-permute-done.3.refs_21_.refs_4_
  24.6 1.7 %collective-permute-start.5 = (bf16[128,1024]{1,0:T(8,128)(2,1)S(1)}, bf16[128,1024]{1,0:T(8,128)(2,1)S(1)}, u32[]{:S(2)}, u32[]{:S(2)}) collective-permute-start(bf16[128,1024]{1,0:T(8,128)(2,1)S(1)} %collective-permute-done.2.refs_20_.refs_3_), channel_id=1, source_target_pairs={{0,2},{1,3},{2,6},{3,7},{6,10},{7,11},{10,14},{11,15},{14,12},{15,... | collective-permute-start | bytes 786440 | tf_op jit(solution)/shard_map/ppermute | solution.py:357
  26.2 0.4 collective-permute-start.6
  26.6 0.0 collective-permute-start.11
  26.6 0.5 collective-permute-start.12
  27.1 0.6 shard_map.122
  27.7 0.0 collective-permute-done.8.refs_19_.refs_6_
  27.7 3.5 %shard_map.121.refs_1_ = f32[128,1024]{1,0:T(8,128)S(1)} custom-call(s32[16]{0:T(128)S(1)} %dynamic-slice_bitcast_fusion.refs_0_.offs_ref, f32[128,1024]{1,0:T(8,128)S(1)} %get-tuple-element.111.refs_1_, bf16[64,16384]{1,0:T(8,128)(2,1)S(1)} %get-tuple-element.98.refs_3_.refs_2_.refs_0_.refs_5_.refs_7_.refs_8_, ...), custom_call_target="tpu_custom_call" | custom-call | flops 67108864 | bytes 524288 | tf_op jit(solution)/shard_map/pallas_call | solution.py:57
  31.2 1.6 %collective-permute-done.5.refs_20_.refs_7_ = bf16[128,1024]{1,0:T(8,128)(2,1)S(1)} collective-permute-done((bf16[128,1024]{1,0:T(8,128)(2,1)S(1)}, bf16[128,1024]{1,0:T(8,128)(2,1)S(1)}, u32[]{:S(2)}, u32[]{:S(2)}) %collective-permute-start.5) | collective-permute-done | bytes 262176 | tf_op jit(solution)/shard_map/ppermute | solution.py:357
  32.8 1.4 %collective-permute-done.6.refs_21_.refs_3_ = bf16[128,1024]{1,0:T(8,128)(2,1)S(1)} collective-permute-done((bf16[128,1024]{1,0:T(8,128)(2,1)S(1)}, bf16[128,1024]{1,0:T(8,128)(2,1)S(1)}, u32[]{:S(2)}, u32[]{:S(2)}) %collective-permute-start.6) | collective-permute-done | bytes 262176 | tf_op jit(solution)/shard_map/ppermute | solution.py:357
  34.2 0.5 collective-permute-start.10
  34.7 1.6 %collective-permute-start.9 = (bf16[64,1024]{1,0:T(8,128)(2,1)S(1)}, bf16[64,1024]{1,0:T(8,128)(2,1)S(1)}, u32[]{:S(2)}, u32[]{:S(2)}) collective-permute-start(bf16[64,1024]{1,0:T(8,128)(2,1)S(1)} %slice.26), channel_id=1, source_target_pairs={{0,2},{1,3},{2,6},{3,7},{6,10},{7,11},{10,14},{11,15},{14,12},{15,... | collective-permute-start | bytes 393224 | tf_op jit(solution)/shard_map/ppermute | solution.py:357
  36.3 0.0 collective-permute-start.14
  36.3 0.0 collective-permute-done.11.refs_18_.refs_5_
  36.3 0.5 collective-permute-start.15
  36.8 3.5 %shard_map.123.refs_1_ = f32[128,1024]{1,0:T(8,128)S(1)} custom-call(s32[16]{0:T(128)S(1)} %dynamic-slice_bitcast_fusion.refs_0_.offs_ref, f32[128,1024]{1,0:T(8,128)S(1)} %shard_map.121.refs_1_, bf16[64,16384]{1,0:T(8,128)(2,1)S(1)} %get-tuple-element.98.refs_3_.refs_2_.refs_0_.refs_5_.refs_7_.refs_8_, ...), custom_call_target="tpu_custom_call" | custom-call | flops 67108864 | bytes 524288 | tf_op jit(solution)/shard_map/pallas_call | solution.py:57
  40.4 0.0 copy-start.3
  40.4 0.0 copy-start.4
  40.4 0.1 collective-permute-start.13
  40.5 2.8 %shard_map.124.refs_16_ = f32[128,1024]{1,0:T(8,128)S(1)} custom-call(s32[16]{0:T(128)S(1)} %dynamic-slice_bitcast_fusion.refs_0_.offs_ref, f32[128,1024]{1,0:T(8,128)S(1)} %shard_map.123.refs_1_, bf16[64,16384]{1,0:T(8,128)(2,1)S(1)} %get-tuple-element.98.refs_3_.refs_2_.refs_0_.refs_5_.refs_7_.refs_8_, ...), custom_call_target="tpu_custom_call" | custom-call | flops 50331648 | bytes 393216 | tf_op jit(solution)/shard_map/pallas_call | solution.py:57
  43.3 2.3 %shard_map.125 = (f32[128,1024]{1,0:T(8,128)S(1)}, bf16[128,1024]{1,0:T(8,128)(2,1)S(1)}, bf16[1024,128]{1,0:T(8,128)(2,1)S(1)}, f32[16,1024]{1,0:T(8,128)}, f32[1,1024]{1,0:T(1,128)}, /*index=5*/f32[1,1024]{1,0:T(1,128)}) custom-call(s32[16]{0:T(128)S(1)} %dynamic-slice_bitcast_fusion.refs_0_.offs_ref, ...), custom_call_target="tpu_custom_call" | custom-call | flops 33554432 | bytes 262144 | tf_op jit(solution)/shard_map/pallas_call | solution.py:57
  45.6 1.3 %shard_map.126 = (bf16[128,1024]{1,0:T(8,128)(2,1)S(1)}, f32[128,1024]{1,0:T(8,128)S(1)}) custom-call(s32[16]{0:T(128)S(1)} %dynamic-slice_bitcast_fusion.refs_0_.offs_ref, bf16[128,1024]{1,0:T(8,128)(2,1)S(1)} %get-tuple-element.131.refs_1_, bf16[1024,128]{1,0:T(8,128)(2,1)S(1)} %get-tuple-element.132.refs_2_, ...), custom_call_target="tpu_custom_call" | custom-call | flops 33554432 | bytes 262144 | tf_op jit(solution)/shard_map/pallas_call | solution.py:57
  46.9 0.5 collective-permute-start.16
  47.4 1.8 %shard_map.127 = (bf16[128,1024]{1,0:T(8,128)(2,1)S(1)}, bf16[128,1024]{1,0:T(8,128)(2,1)S(1)}, f32[128,1024]{1,0:T(8,128)S(1)}, f32[128,1024]{1,0:T(8,128)S(1)}) custom-call(s32[16]{0:T(128)S(1)} %dynamic-slice_bitcast_fusion.refs_0_.offs_ref, bf16[128,1024]{1,0:T(8,128)(2,1)S(1)} %get-tuple-element.131.refs_1_, ...), custom_call_target="tpu_custom_call" | custom-call | flops 67108864 | bytes 524288 | tf_op jit(solution)/shard_map/pallas_call | solution.py:57
  49.3 0.1 collective-permute-start.17
  49.4 0.5 collective-permute-start.20
  49.9 0.1 add_convert_fusion.4
  50.0 1.1 %collective-permute-start.19 = (bf16[64,1024]{1,0:T(8,128)(2,1)S(1)}, bf16[64,1024]{1,0:T(8,128)(2,1)S(1)}, u32[]{:S(2)}, u32[]{:S(2)}) collective-permute-start(bf16[64,1024]{1,0:T(8,128)(2,1)S(1)} %get-tuple-element.183), channel_id=1, source_target_pairs={{0,4},{1,5},{2,0},{3,1},{6,2},{7,3},{10,6},{11,7},{14,10},{15,11},... | collective-permute-start | bytes 393224 | tf_op jit(solution)/shard_map/ppermute | solution.py:357
  51.0 1.0 %collective-permute-start.18 = (bf16[64,1024]{1,0:T(8,128)(2,1)S(1)}, bf16[64,1024]{1,0:T(8,128)(2,1)S(1)}, u32[]{:S(2)}, u32[]{:S(2)}) collective-permute-start(bf16[64,1024]{1,0:T(8,128)(2,1)S(1)} %get-tuple-element.184), channel_id=1, source_target_pairs={{0,2},{1,3},{2,6},{3,7},{6,10},{7,11},{10,14},{11,15},{14,12},{15,... | collective-permute-start | bytes 393224 | tf_op jit(solution)/shard_map/ppermute | solution.py:357
  52.0 0.1 convert_add_fusion
  52.2 3.8 %shard_map.128 = (bf16[128,1024]{1,0:T(8,128)(2,1)S(1)}, bf16[128,1024]{1,0:T(8,128)(2,1)S(1)}, f32[128,1024]{1,0:T(8,128)S(1)}, f32[128,1024]{1,0:T(8,128)S(1)}, bf16[1024,16384]{1,0:T(8,128)(2,1)}) custom-call(s32[16]{0:T(128)S(1)} %dynamic-slice_bitcast_fusion.refs_0_.offs_ref, bf16[128,1024]{1,0:T(8,128)(2,1)S(1)} %get-tuple-element.131.refs_1_, ...), custom_call_target="tpu_custom_call" | custom-call | flops 100663296 | bytes 786432 | tf_op jit(solution)/shard_map/pallas_call | solution.py:57
  56.0 0.2 collective-permute-done.18
  56.4 1.4 %collective-permute-start.21 = (bf16[128,1024]{1,0:T(8,128)(2,1)S(1)}, bf16[128,1024]{1,0:T(8,128)(2,1)S(1)}, u32[]{:S(2)}, u32[]{:S(2)}) collective-permute-start(bf16[128,1024]{1,0:T(8,128)(2,1)S(1)} %pad_maximum_fusion), channel_id=1, source_target_pairs={{0,2},{1,3},{2,6},{3,7},{6,10},{7,11},{10,14},{11,15},{14,12},{15,... | collective-permute-start | bytes 786440 | tf_op jit(solution)/shard_map/ppermute | solution.py:357
  57.8 0.6 collective-permute-start.22
  58.4 0.5 collective-permute-start.24
  58.9 5.6 %shard_map.129 = (bf16[128,1024]{1,0:T(8,128)(2,1)S(1)}, bf16[128,1024]{1,0:T(8,128)(2,1)S(1)}, f32[128,1024]{1,0:T(8,128)S(1)}, f32[128,1024]{1,0:T(8,128)S(1)}, bf16[1024,16384]{1,0:T(8,128)(2,1)}) custom-call(s32[16]{0:T(128)S(1)} %dynamic-slice_bitcast_fusion.refs_0_.offs_ref, ...), custom_call_target="tpu_custom_call", output_to_operand_aliasing={{4}: (23, {})} | custom-call | flops 134217728 | bytes 1048576 | tf_op jit(solution)/shard_map/pallas_call | solution.py:57
  64.6 0.7 collective-permute-done.22
  65.3 0.1 add_convert_fusion.2
  65.4 0.1 add_convert_fusion.3
  65.5 1.6 %collective-permute-start.26 = (bf16[128,1024]{1,0:T(8,128)(2,1)S(1)}, bf16[128,1024]{1,0:T(8,128)(2,1)S(1)}, u32[]{:S(2)}, u32[]{:S(2)}) collective-permute-start(bf16[128,1024]{1,0:T(8,128)(2,1)S(1)} %add_convert_fusion.3), channel_id=1, source_target_pairs={{0,2},{1,3},{2,6},{3,7},{6,10},{7,11},{10,14},{11,15},{14,12},{15,... | collective-permute-start | bytes 786440 | tf_op jit(solution)/shard_map/ppermute | solution.py:357
  67.1 0.4 collective-permute-start.27
  67.6 0.5 collective-permute-start.28
  68.1 5.9 %shard_map.130 = (bf16[128,1024]{1,0:T(8,128)(2,1)S(1)}, f32[128,1024]{1,0:T(8,128)S(1)}, bf16[1024,16384]{1,0:T(8,128)(2,1)}) custom-call(s32[16]{0:T(128)S(1)} %dynamic-slice_bitcast_fusion.refs_0_.offs_ref, bf16[128,1024]{1,0:T(8,128)(2,1)S(1)} %get-tuple-element.131.refs_1_, ...), custom_call_target="tpu_custom_call", output_to_operand_aliasing={{2}: (24, {})} | custom-call | flops 117440512 | bytes 917504 | tf_op jit(solution)/shard_map/pallas_call | solution.py:57
  74.0 0.2 collective-permute-done.27
  74.2 0.1 add_convert_fusion.1
  74.3 0.1 add_convert_fusion
  74.5 1.6 %collective-permute-start.29 = (bf16[128,1024]{1,0:T(8,128)(2,1)S(1)}, bf16[128,1024]{1,0:T(8,128)(2,1)S(1)}, u32[]{:S(2)}, u32[]{:S(2)}) collective-permute-start(bf16[128,1024]{1,0:T(8,128)(2,1)S(1)} %add_convert_fusion.1), channel_id=1, source_target_pairs={{0,2},{1,3},{2,6},{3,7},{6,10},{7,11},{10,14},{11,15},{14,12},{15,... | collective-permute-start | bytes 786440 | tf_op jit(solution)/shard_map/ppermute | solution.py:357
  76.1 0.4 collective-permute-start.30
  76.5 0.6 shard_map.132
  77.2 5.5 %shard_map.131 = bf16[1024,16384]{1,0:T(8,128)(2,1)} custom-call(s32[16]{0:T(128)S(1)} %dynamic-slice_bitcast_fusion.refs_0_.offs_ref, bf16[128,1024]{1,0:T(8,128)(2,1)S(1)} %get-tuple-element.131.refs_1_, bf16[1024,128]{1,0:T(8,128)(2,1)S(1)} %get-tuple-element.132.refs_2_, ...), custom_call_target="tpu_custom_call", output_to_operand_aliasing={{}: (24, {})} | custom-call | flops 83886080 | bytes 655360 | tf_op jit(solution)/shard_map/pallas_call | solution.py:57
  82.7 1.1 %collective-permute-done.30 = bf16[128,1024]{1,0:T(8,128)(2,1)S(1)} collective-permute-done((bf16[128,1024]{1,0:T(8,128)(2,1)S(1)}, bf16[128,1024]{1,0:T(8,128)(2,1)S(1)}, u32[]{:S(2)}, u32[]{:S(2)}) %collective-permute-start.30) | collective-permute-done | bytes 262176 | tf_op jit(solution)/shard_map/ppermute | solution.py:357
  83.8 1.0 %add_bitcast_fusion = f32[1,128,1024]{2,1,0:T(8,128)} fusion(bf16[128,1024]{1,0:T(8,128)(2,1)S(1)} %collective-permute-done.30, bf16[128,1024]{1,0:T(8,128)(2,1)S(1)} %collective-permute-done.29, f32[128,1024]{1,0:T(8,128)S(1)} %shard_map.132, f32[128,1024]{1,0:T(8,128)S(1)} %get-tuple-element.176, bf16[128,1024]{1,0:T(8,128)(2,1)S(1)} %collective-permute-done.31), kind=kLoop, calls=%fused_computation | loop fusion | flops 917504 | bytes 2359296 | tf_op jit(solution)/shard_map/reshape | solution.py:450
  (44 shorter events, 0.3 us)
Async XLA Ops:
  1.7 12.4 %collective-permute-start.1 = (bf16[128,1024]{1,0:T(8,128)(2,1)S(1)}, bf16[128,1024]{1,0:T(8,128)(2,1)S(1)}, u32[]{:S(2)}, u32[]{:S(2)}) collective-permute-start(bf16[128,1024]{1,0:T(8,128)(2,1)S(1)} %bitcast_convert_fusion.refs_3_.refs_13_), channel_id=1, source_target_pairs={{0,4},{1,5},{2,0},{3,1},{6,2},{7,3},{10,6},{11,7},{14,10},{15,11},... | collective-permute-start | bytes 786440 | tf_op jit(solution)/shard_map/ppermute | solution.py:357
  4.8 9.3 %collective-permute-start = (bf16[128,1024]{1,0:T(8,128)(2,1)S(1)}, bf16[128,1024]{1,0:T(8,128)(2,1)S(1)}, u32[]{:S(2)}, u32[]{:S(2)}) collective-permute-start(bf16[128,1024]{1,0:T(8,128)(2,1)S(1)} %bitcast_convert_fusion.refs_3_.refs_13_), channel_id=1, source_target_pairs={{0,2},{1,3},{2,6},{3,7},{6,10},{7,11},{10,14},{11,15},{14,12},{15,... | collective-permute-start | bytes 786440 | tf_op jit(solution)/shard_map/ppermute | solution.py:357
  4.8 12.0 %collective-permute-start.4 = (bf16[128,1024]{1,0:T(8,128)(2,1)S(1)}, bf16[128,1024]{1,0:T(8,128)(2,1)S(1)}, u32[]{:S(2)}, u32[]{:S(2)}) collective-permute-start(bf16[128,1024]{1,0:T(8,128)(2,1)S(1)} %bitcast_convert_fusion.refs_3_.refs_13_), channel_id=1, source_target_pairs={{0,1},{1,0},{2,3},{3,2},{4,5},{5,4},{6,7},{7,6},{8,9},{9,8},{10,11... | collective-permute-start | bytes 786440 | tf_op jit(solution)/shard_map/ppermute | solution.py:360
  14.1 10.1 %collective-permute-start.2 = (bf16[128,1024]{1,0:T(8,128)(2,1)S(1)}, bf16[128,1024]{1,0:T(8,128)(2,1)S(1)}, u32[]{:S(2)}, u32[]{:S(2)}) collective-permute-start(bf16[128,1024]{1,0:T(8,128)(2,1)S(1)} %collective-permute-done.refs_15_.refs_3_), channel_id=1, source_target_pairs={{0,2},{1,3},{2,6},{3,7},{6,10},{7,11},{10,14},{11,15},{14,12},{15,... | collective-permute-start | bytes 786440 | tf_op jit(solution)/shard_map/ppermute | solution.py:357
  16.1 8.4 %collective-permute-start.3 = (bf16[128,1024]{1,0:T(8,128)(2,1)S(1)}, bf16[128,1024]{1,0:T(8,128)(2,1)S(1)}, u32[]{:S(2)}, u32[]{:S(2)}) collective-permute-start(bf16[128,1024]{1,0:T(8,128)(2,1)S(1)} %collective-permute-done.1.refs_16_.refs_4_), channel_id=1, source_target_pairs={{0,4},{1,5},{2,0},{3,1},{6,2},{7,3},{10,6},{11,7},{14,10},{15,11},... | collective-permute-start | bytes 786440 | tf_op jit(solution)/shard_map/ppermute | solution.py:357
  16.3 10.3 %collective-permute-start.7 = (bf16[128,1024]{1,0:T(8,128)(2,1)S(1)}, bf16[128,1024]{1,0:T(8,128)(2,1)S(1)}, u32[]{:S(2)}, u32[]{:S(2)}) collective-permute-start(bf16[128,1024]{1,0:T(8,128)(2,1)S(1)} %collective-permute-done.refs_15_.refs_3_), channel_id=1, source_target_pairs={{0,1},{1,0},{2,3},{3,2},{4,5},{5,4},{6,7},{7,6},{8,9},{9,8},{10,11... | collective-permute-start | bytes 786440 | tf_op jit(solution)/shard_map/ppermute | solution.py:360
  16.5 11.2 %collective-permute-start.8 = (bf16[128,1024]{1,0:T(8,128)(2,1)S(1)}, bf16[128,1024]{1,0:T(8,128)(2,1)S(1)}, u32[]{:S(2)}, u32[]{:S(2)}) collective-permute-start(bf16[128,1024]{1,0:T(8,128)(2,1)S(1)} %collective-permute-done.1.refs_16_.refs_4_), channel_id=1, source_target_pairs={{0,1},{1,0},{2,3},{3,2},{4,5},{5,4},{6,7},{7,6},{8,9},{9,8},{10,11... | collective-permute-start | bytes 786440 | tf_op jit(solution)/shard_map/ppermute | solution.py:360
  16.8 10.3 %copy-start = (f32[1,128,1024]{2,1,0:T(8,128)S(1)}, f32[1,128,1024]{2,1,0:T(8,128)}, u32[]{:S(2)}) copy-start(f32[1,128,1024]{2,1,0:T(8,128)} %param.8) | copy-start | bytes 1572868
  16.8 10.3 %copy-start.1 = (f32[128,128]{1,0:T(8,128)S(1)}, f32[128,128]{1,0:T(8,128)}, u32[]{:S(2)}) copy-start(f32[128,128]{1,0:T(8,128)} %constant.13.clone.cheb_ref) | copy-start | bytes 196612
  16.8 10.3 %copy-start.2 = (f32[16,1024]{1,0:T(8,128)S(1)}, f32[16,1024]{1,0:T(8,128)}, u32[]{:S(2)}) copy-start(f32[16,1024]{1,0:T(8,128)} %pert_ref.1) | copy-start | bytes 196612
  24.6 8.2 %collective-permute-start.5 = (bf16[128,1024]{1,0:T(8,128)(2,1)S(1)}, bf16[128,1024]{1,0:T(8,128)(2,1)S(1)}, u32[]{:S(2)}, u32[]{:S(2)}) collective-permute-start(bf16[128,1024]{1,0:T(8,128)(2,1)S(1)} %collective-permute-done.2.refs_20_.refs_3_), channel_id=1, source_target_pairs={{0,2},{1,3},{2,6},{3,7},{6,10},{7,11},{10,14},{11,15},{14,12},{15,... | collective-permute-start | bytes 786440 | tf_op jit(solution)/shard_map/ppermute | solution.py:357
  26.2 7.9 %collective-permute-start.6 = (bf16[128,1024]{1,0:T(8,128)(2,1)S(1)}, bf16[128,1024]{1,0:T(8,128)(2,1)S(1)}, u32[]{:S(2)}, u32[]{:S(2)}) collective-permute-start(bf16[128,1024]{1,0:T(8,128)(2,1)S(1)} %collective-permute-done.3.refs_21_.refs_4_), channel_id=1, source_target_pairs={{0,4},{1,5},{2,0},{3,1},{6,2},{7,3},{10,6},{11,7},{14,10},{15,11},... | collective-permute-start | bytes 786440 | tf_op jit(solution)/shard_map/ppermute | solution.py:357
  26.6 9.7 %collective-permute-start.11 = (bf16[128,1024]{1,0:T(8,128)(2,1)S(1)}, bf16[128,1024]{1,0:T(8,128)(2,1)S(1)}, u32[]{:S(2)}, u32[]{:S(2)}) collective-permute-start(bf16[128,1024]{1,0:T(8,128)(2,1)S(1)} %collective-permute-done.2.refs_20_.refs_3_), channel_id=1, source_target_pairs={{0,1},{1,0},{2,3},{3,2},{4,5},{5,4},{6,7},{7,6},{8,9},{9,8},{10,11... | collective-permute-start | bytes 786440 | tf_op jit(solution)/shard_map/ppermute | solution.py:360
  26.6 10.2 %collective-permute-start.12 = (bf16[128,1024]{1,0:T(8,128)(2,1)S(1)}, bf16[128,1024]{1,0:T(8,128)(2,1)S(1)}, u32[]{:S(2)}, u32[]{:S(2)}) collective-permute-start(bf16[128,1024]{1,0:T(8,128)(2,1)S(1)} %collective-permute-done.3.refs_21_.refs_4_), channel_id=1, source_target_pairs={{0,1},{1,0},{2,3},{3,2},{4,5},{5,4},{6,7},{7,6},{8,9},{9,8},{10,11... | collective-permute-start | bytes 786440 | tf_op jit(solution)/shard_map/ppermute | solution.py:360
  34.2 6.1 %collective-permute-start.10 = (bf16[64,1024]{1,0:T(8,128)(2,1)S(1)}, bf16[64,1024]{1,0:T(8,128)(2,1)S(1)}, u32[]{:S(2)}, u32[]{:S(2)}) collective-permute-start(bf16[64,1024]{1,0:T(8,128)(2,1)S(1)} %slice.27), channel_id=1, source_target_pairs={{0,4},{1,5},{2,0},{3,1},{6,2},{7,3},{10,6},{11,7},{14,10},{15,11},... | collective-permute-start | bytes 393224 | tf_op jit(solution)/shard_map/ppermute | solution.py:357
  34.7 5.6 %collective-permute-start.9 = (bf16[64,1024]{1,0:T(8,128)(2,1)S(1)}, bf16[64,1024]{1,0:T(8,128)(2,1)S(1)}, u32[]{:S(2)}, u32[]{:S(2)}) collective-permute-start(bf16[64,1024]{1,0:T(8,128)(2,1)S(1)} %slice.26), channel_id=1, source_target_pairs={{0,2},{1,3},{2,6},{3,7},{6,10},{7,11},{10,14},{11,15},{14,12},{15,... | collective-permute-start | bytes 393224 | tf_op jit(solution)/shard_map/ppermute | solution.py:357
  36.3 4.2 %collective-permute-start.14 = (bf16[128,1024]{1,0:T(8,128)(2,1)S(1)}, bf16[128,1024]{1,0:T(8,128)(2,1)S(1)}, u32[]{:S(2)}, u32[]{:S(2)}) collective-permute-start(bf16[128,1024]{1,0:T(8,128)(2,1)S(1)} %collective-permute-done.5.refs_20_.refs_7_), channel_id=1, source_target_pairs={{0,1},{1,0},{2,3},{3,2},{4,5},{5,4},{6,7},{7,6},{8,9},{9,8},{10,11... | collective-permute-start | bytes 786440 | tf_op jit(solution)/shard_map/ppermute | solution.py:360
  36.3 4.2 %collective-permute-start.15 = (bf16[128,1024]{1,0:T(8,128)(2,1)S(1)}, bf16[128,1024]{1,0:T(8,128)(2,1)S(1)}, u32[]{:S(2)}, u32[]{:S(2)}) collective-permute-start(bf16[128,1024]{1,0:T(8,128)(2,1)S(1)} %collective-permute-done.6.refs_21_.refs_3_), channel_id=1, source_target_pairs={{0,1},{1,0},{2,3},{3,2},{4,5},{5,4},{6,7},{7,6},{8,9},{9,8},{10,11... | collective-permute-start | bytes 786440 | tf_op jit(solution)/shard_map/ppermute | solution.py:360
  40.4 3.0 %copy-start.3 = (f32[1024]{0:T(1024)S(1)}, f32[1024]{0:T(1024)}, u32[]{:S(2)}) copy-start(f32[1024]{0:T(1024)} %param.12) | copy-start | bytes 12292
  40.4 3.0 %copy-start.4 = (f32[1024]{0:T(1024)S(1)}, f32[1024]{0:T(1024)}, u32[]{:S(2)}) copy-start(f32[1024]{0:T(1024)} %param.11) | copy-start | bytes 12292
  40.4 2.9 %collective-permute-start.13 = (bf16[128,1024]{1,0:T(8,128)(2,1)S(1)}, bf16[128,1024]{1,0:T(8,128)(2,1)S(1)}, u32[]{:S(2)}, u32[]{:S(2)}) collective-permute-start(bf16[128,1024]{1,0:T(8,128)(2,1)S(1)} %constant_dynamic-update-slice_fusion.refs_20_.refs_6_), channel_id=1, source_target_pairs={{0,1},{1,0},{2,3},{3,2},{4,5},{5,4},{6,7},{7,6},{8,9},{9,8},{10,11... | collective-permute-start | bytes 786440 | tf_op jit(solution)/shard_map/ppermute | solution.py:360
  46.9 3.0 %collective-permute-start.16 = (bf16[128,1024]{1,0:T(8,128)(2,1)S(1)}, bf16[128,1024]{1,0:T(8,128)(2,1)S(1)}, u32[]{:S(2)}, u32[]{:S(2)}) collective-permute-start(bf16[128,1024]{1,0:T(8,128)(2,1)S(1)} %get-tuple-element.134), channel_id=1, source_target_pairs={{0,1},{1,0},{2,3},{3,2},{4,5},{5,4},{6,7},{7,6},{8,9},{9,8},{10,11... | collective-permute-start | bytes 786440 | tf_op jit(solution)/shard_map/ppermute | solution.py:360
  49.3 2.7 %collective-permute-start.17 = (bf16[128,1024]{1,0:T(8,128)(2,1)S(1)}, bf16[128,1024]{1,0:T(8,128)(2,1)S(1)}, u32[]{:S(2)}, u32[]{:S(2)}) collective-permute-start(bf16[128,1024]{1,0:T(8,128)(2,1)S(1)} %get-tuple-element.138), channel_id=1, source_target_pairs={{0,1},{1,0},{2,3},{3,2},{4,5},{5,4},{6,7},{7,6},{8,9},{9,8},{10,11... | collective-permute-start | bytes 786440 | tf_op jit(solution)/shard_map/ppermute | solution.py:360
  49.4 2.6 %collective-permute-start.20 = (bf16[128,1024]{1,0:T(8,128)(2,1)S(1)}, bf16[128,1024]{1,0:T(8,128)(2,1)S(1)}, u32[]{:S(2)}, u32[]{:S(2)}) collective-permute-start(bf16[128,1024]{1,0:T(8,128)(2,1)S(1)} %get-tuple-element.145), channel_id=1, source_target_pairs={{0,1},{1,0},{2,3},{3,2},{4,5},{5,4},{6,7},{7,6},{8,9},{9,8},{10,11... | collective-permute-start | bytes 786440 | tf_op jit(solution)/shard_map/ppermute | solution.py:360
  50.0 6.1 %collective-permute-start.19 = (bf16[64,1024]{1,0:T(8,128)(2,1)S(1)}, bf16[64,1024]{1,0:T(8,128)(2,1)S(1)}, u32[]{:S(2)}, u32[]{:S(2)}) collective-permute-start(bf16[64,1024]{1,0:T(8,128)(2,1)S(1)} %get-tuple-element.183), channel_id=1, source_target_pairs={{0,4},{1,5},{2,0},{3,1},{6,2},{7,3},{10,6},{11,7},{14,10},{15,11},... | collective-permute-start | bytes 393224 | tf_op jit(solution)/shard_map/ppermute | solution.py:357
  51.0 5.2 %collective-permute-start.18 = (bf16[64,1024]{1,0:T(8,128)(2,1)S(1)}, bf16[64,1024]{1,0:T(8,128)(2,1)S(1)}, u32[]{:S(2)}, u32[]{:S(2)}) collective-permute-start(bf16[64,1024]{1,0:T(8,128)(2,1)S(1)} %get-tuple-element.184), channel_id=1, source_target_pairs={{0,2},{1,3},{2,6},{3,7},{6,10},{7,11},{10,14},{11,15},{14,12},{15,... | collective-permute-start | bytes 393224 | tf_op jit(solution)/shard_map/ppermute | solution.py:357
  56.4 8.2 %collective-permute-start.21 = (bf16[128,1024]{1,0:T(8,128)(2,1)S(1)}, bf16[128,1024]{1,0:T(8,128)(2,1)S(1)}, u32[]{:S(2)}, u32[]{:S(2)}) collective-permute-start(bf16[128,1024]{1,0:T(8,128)(2,1)S(1)} %pad_maximum_fusion), channel_id=1, source_target_pairs={{0,2},{1,3},{2,6},{3,7},{6,10},{7,11},{10,14},{11,15},{14,12},{15,... | collective-permute-start | bytes 786440 | tf_op jit(solution)/shard_map/ppermute | solution.py:357
  57.8 7.5 %collective-permute-start.22 = (bf16[128,1024]{1,0:T(8,128)(2,1)S(1)}, bf16[128,1024]{1,0:T(8,128)(2,1)S(1)}, u32[]{:S(2)}, u32[]{:S(2)}) collective-permute-start(bf16[128,1024]{1,0:T(8,128)(2,1)S(1)} %pad_maximum_fusion.1), channel_id=1, source_target_pairs={{0,4},{1,5},{2,0},{3,1},{6,2},{7,3},{10,6},{11,7},{14,10},{15,11},... | collective-permute-start | bytes 786440 | tf_op jit(solution)/shard_map/ppermute | solution.py:357
  58.4 6.8 %collective-permute-start.25 = (bf16[128,1024]{1,0:T(8,128)(2,1)S(1)}, bf16[128,1024]{1,0:T(8,128)(2,1)S(1)}, u32[]{:S(2)}, u32[]{:S(2)}) collective-permute-start(bf16[128,1024]{1,0:T(8,128)(2,1)S(1)} %get-tuple-element.159), channel_id=1, source_target_pairs={{0,1},{1,0},{2,3},{3,2},{4,5},{5,4},{6,7},{7,6},{8,9},{9,8},{10,11... | collective-permute-start | bytes 786440 | tf_op jit(solution)/shard_map/ppermute | solution.py:360
  58.4 6.9 %collective-permute-start.24 = (bf16[128,1024]{1,0:T(8,128)(2,1)S(1)}, bf16[128,1024]{1,0:T(8,128)(2,1)S(1)}, u32[]{:S(2)}, u32[]{:S(2)}) collective-permute-start(bf16[128,1024]{1,0:T(8,128)(2,1)S(1)} %get-tuple-element.156), channel_id=1, source_target_pairs={{0,1},{1,0},{2,3},{3,2},{4,5},{5,4},{6,7},{7,6},{8,9},{9,8},{10,11... | collective-permute-start | bytes 786440 | tf_op jit(solution)/shard_map/ppermute | solution.py:360
  65.5 8.5 %collective-permute-start.26 = (bf16[128,1024]{1,0:T(8,128)(2,1)S(1)}, bf16[128,1024]{1,0:T(8,128)(2,1)S(1)}, u32[]{:S(2)}, u32[]{:S(2)}) collective-permute-start(bf16[128,1024]{1,0:T(8,128)(2,1)S(1)} %add_convert_fusion.3), channel_id=1, source_target_pairs={{0,2},{1,3},{2,6},{3,7},{6,10},{7,11},{10,14},{11,15},{14,12},{15,... | collective-permute-start | bytes 786440 | tf_op jit(solution)/shard_map/ppermute | solution.py:357
  67.1 7.1 %collective-permute-start.27 = (bf16[128,1024]{1,0:T(8,128)(2,1)S(1)}, bf16[128,1024]{1,0:T(8,128)(2,1)S(1)}, u32[]{:S(2)}, u32[]{:S(2)}) collective-permute-start(bf16[128,1024]{1,0:T(8,128)(2,1)S(1)} %add_convert_fusion.2), channel_id=1, source_target_pairs={{0,4},{1,5},{2,0},{3,1},{6,2},{7,3},{10,6},{11,7},{14,10},{15,11},... | collective-permute-start | bytes 786440 | tf_op jit(solution)/shard_map/ppermute | solution.py:357
  67.6 6.6 %collective-permute-start.23 = (bf16[128,1024]{1,0:T(8,128)(2,1)S(1)}, bf16[128,1024]{1,0:T(8,128)(2,1)S(1)}, u32[]{:S(2)}, u32[]{:S(2)}) collective-permute-start(bf16[128,1024]{1,0:T(8,128)(2,1)S(1)} %get-tuple-element.154), channel_id=1, source_target_pairs={{0,1},{1,0},{2,3},{3,2},{4,5},{5,4},{6,7},{7,6},{8,9},{9,8},{10,11... | collective-permute-start | bytes 786440 | tf_op jit(solution)/shard_map/ppermute | solution.py:360
  67.6 6.7 %collective-permute-start.28 = (bf16[128,1024]{1,0:T(8,128)(2,1)S(1)}, bf16[128,1024]{1,0:T(8,128)(2,1)S(1)}, u32[]{:S(2)}, u32[]{:S(2)}) collective-permute-start(bf16[128,1024]{1,0:T(8,128)(2,1)S(1)} %get-tuple-element.168), channel_id=1, source_target_pairs={{0,1},{1,0},{2,3},{3,2},{4,5},{5,4},{6,7},{7,6},{8,9},{9,8},{10,11... | collective-permute-start | bytes 786440 | tf_op jit(solution)/shard_map/ppermute | solution.py:360
  74.5 8.2 %collective-permute-start.29 = (bf16[128,1024]{1,0:T(8,128)(2,1)S(1)}, bf16[128,1024]{1,0:T(8,128)(2,1)S(1)}, u32[]{:S(2)}, u32[]{:S(2)}) collective-permute-start(bf16[128,1024]{1,0:T(8,128)(2,1)S(1)} %add_convert_fusion.1), channel_id=1, source_target_pairs={{0,2},{1,3},{2,6},{3,7},{6,10},{7,11},{10,14},{11,15},{14,12},{15,... | collective-permute-start | bytes 786440 | tf_op jit(solution)/shard_map/ppermute | solution.py:357
  76.1 7.7 %collective-permute-start.30 = (bf16[128,1024]{1,0:T(8,128)(2,1)S(1)}, bf16[128,1024]{1,0:T(8,128)(2,1)S(1)}, u32[]{:S(2)}, u32[]{:S(2)}) collective-permute-start(bf16[128,1024]{1,0:T(8,128)(2,1)S(1)} %add_convert_fusion), channel_id=1, source_target_pairs={{0,4},{1,5},{2,0},{3,1},{6,2},{7,3},{10,6},{11,7},{14,10},{15,11},... | collective-permute-start | bytes 786440 | tf_op jit(solution)/shard_map/ppermute | solution.py:357
  76.5 7.3 %collective-permute-start.31 = (bf16[128,1024]{1,0:T(8,128)(2,1)S(1)}, bf16[128,1024]{1,0:T(8,128)(2,1)S(1)}, u32[]{:S(2)}, u32[]{:S(2)}) collective-permute-start(bf16[128,1024]{1,0:T(8,128)(2,1)S(1)} %get-tuple-element.177), channel_id=1, source_target_pairs={{0,1},{1,0},{2,3},{3,2},{4,5},{5,4},{6,7},{7,6},{8,9},{9,8},{10,11... | collective-permute-start | bytes 786440 | tf_op jit(solution)/shard_map/ppermute | solution.py:360

commit v9 on v8

v9 whole, which is shorter than its diff:
```python
import functools

import jax
import jax.numpy as jnp
import numpy as np
from jax import lax
from jax.experimental import pallas as pl
from jax.experimental.pallas import tpu as pltpu
from jax.sharding import PartitionSpec as P

SCALE = 2.0 / 1024.0
VMEM_LIMIT = 8 * 2**20
BANDS = 16
GROUP = 4
LOADS = (10, 6)
PIECES = (2, 4, 5)
LONGEST_RING = 16


def cheb_matrix(count):
    index = np.arange(count)
    points = np.cos(np.pi * index / (count - 1))
    signs = np.where(index % 2 == 0, 1.0, -1.0)
    weight_c = signs * np.where((index == 0) | (index == count - 1), 2.0, 1.0)
    same = index[:, None] == index[None, :]
    spread = np.where(same, 1.0, points[:, None] - points[None, :])
    off = np.where(same, 0.0, weight_c[:, None] / weight_c[None, :] / spread)
    return jnp.asarray((off - np.diag(np.sum(off, axis=1))).astype(np.float32))


def chip_ring(chips):
    rows = 4
    cols = chips // rows
    cells = [(0, col) for col in range(cols)]
    for row in range(1, rows):
        span = range(1, cols)
        cells += [(row, col) for col in (reversed(span) if row % 2 else span)]
    cells += [(row, 0) for row in range(rows - 1, 0, -1)]
    return [row * cols + col for row, col in cells]


VMEM_REF = pl.BlockSpec(memory_space=pltpu.VMEM)
SMEM_REF = pl.BlockSpec(memory_space=pltpu.SMEM)
ANY_REF = pl.BlockSpec(memory_space=pl.ANY)
HBM_REF = pl.BlockSpec(memory_space=pltpu.HBM)


def cost(products, nodes, slab, rows):
    return pl.CostEstimate(
        flops=2 * products * nodes * slab * rows // 16,
        bytes_accessed=2 * products * slab * rows // 16,
        transcendentals=0,
    )


def call(kernel, out_shape, out_specs, scratch, costs, aliases=None):
    def run(operands, in_specs):
        return pl.pallas_call(
            kernel,
            out_shape=out_shape,
            in_specs=in_specs,
            out_specs=out_specs,
            scratch_shapes=scratch,
            input_output_aliases=aliases or {},
            compiler_params=pltpu.CompilerParams(vmem_limit_bytes=VMEM_LIMIT),
            cost_estimate=costs,
        )(*operands)

    return run


def columns_of(offs_ref, at, slab):
    return pl.ds(pl.multiple_of(offs_ref[at] * slab, slab), slab)


def load_bands(w_ref, bands, sems, first):
    copies = []
    for at, band_ref in enumerate(bands):
        tile = band_ref.shape[0]
        rows = pl.ds((first + at) * tile, tile)
        copies.append(pltpu.make_async_copy(w_ref.at[rows, :], band_ref, sems.at[at]))
        copies[-1].start()
    return copies


def product(bands, here, x_ref):
    return lax.dot_general(
        jnp.concatenate([band_ref[:, here] for band_ref in bands], axis=0), x_ref[...],
        (((1,), (1,)), ((), ())), preferred_element_type=jnp.float32,
    )


def split_pieces(pieces):
    arrays, found = [], []
    for array, index in pieces:
        at = [place for place, other in enumerate(arrays) if other is array]
        if not at:
            arrays.append(array)
        found.append((at[0] if at else len(arrays) - 1, index))
    return arrays, found


def load_kernel(offs_ref, perts_ref, w_ref, mark_ref, *refs):
    mark_ref[...] = jnp.zeros_like(mark_ref)
    for copy in load_bands(w_ref, refs[:-1], refs[-1], 0):
        copy.wait()


def band_shapes(count, weights):
    return [pltpu.VMEM((weights.shape[0] // BANDS, weights.shape[1]), weights.dtype)] * count


def load_first(offs, perts, weights, count):
    mark, *bands = call(
        load_kernel,
        [jax.ShapeDtypeStruct((8, 128), jnp.float32)] + band_shapes(count, weights),
        [VMEM_REF] * (1 + count),
        [pltpu.SemaphoreType.DMA((count,))],
        cost(1, 128, 128, 1024),
    )([offs, perts, weights], [SMEM_REF, SMEM_REF, HBM_REF])
    return mark, bands


def pre_kernel(found, count, many, fresh, late, offs_ref, acc_ref, *refs):
    if late:
        w_ref, refs = refs[0], refs[1:]
    bands, refs = refs[:many], refs[many:]
    arrays = 1 + max(at for at, _ in found)
    xs, out_ref, others, sems = refs[:arrays], refs[arrays], refs[arrays + 1 : -1], refs[-1]
    slab = xs[0].shape[-1]
    tile = out_ref.shape[0] // BANDS
    copies = load_bands(w_ref, others, sems, many) if late else []
    for low in [*range(0, many - fresh, GROUP), *range(many - fresh, many, GROUP)]:
        old = low < many - fresh
        group = bands[low : min(low + GROUP, many - fresh if old else many)]
        rows = pl.ds(low * tile, len(group) * tile)
        total = acc_ref[rows, :] if old else None
        for place in range(len(found) - count if old else 0, len(found)):
            at, index = found[place]
            part = product(group, columns_of(offs_ref, place, slab), xs[at].at[index])
            total = part if total is None else total + part
        out_ref[rows, :] = total
    for copy in copies:
        copy.wait()


def add_products(offs, weights, acc, bands, pieces, count, fresh, late):
    arrays, found = split_pieces(pieces if fresh else pieces[-count:])
    if not fresh:
        found = [(0, 0)] * (len(pieces) - count) + found
    (_, nodes, slab), rows, many = arrays[0].shape, weights.shape[0], len(bands)
    operands = [offs, acc] + ([weights] if late else []) + [*bands, *arrays]
    acc, *others = call(
        functools.partial(pre_kernel, found, count, many, fresh, late),
        [jax.ShapeDtypeStruct((rows, nodes), jnp.float32)] + band_shapes(late, weights),
        [VMEM_REF] * (1 + late),
        [pltpu.SemaphoreType.DMA((max(late, 1),))],
        cost(count, nodes, slab, rows),
    )(
        operands,
        [SMEM_REF, VMEM_REF] + ([HBM_REF] if late else [])
        + [VMEM_REF] * (many + len(arrays)),
    )
    return acc, [*bands, *others]


def cheb_dot(turned, cheb_ref, array_ref):
    return SCALE * lax.dot_general(
        cheb_ref[...], array_ref[...], (((0 if turned else 1,), (0,)), ((), ())),
        precision=lax.Precision.HIGHEST, preferred_element_type=jnp.float32,
    )


def deriv_kernel(perts_ref, cheb_ref, states_ref, pert_ref, deriv_ref, drive_ref, chosen_ref):
    pert = perts_ref[0]
    deriv_ref[...] = cheb_dot(False, cheb_ref, states_ref)
    drive_ref[...] = pert_ref[pl.ds(pert, 1), :]
    rows = lax.broadcasted_iota(jnp.int32, chosen_ref.shape, 0)
    chosen_ref[...] = (rows == pert).astype(jnp.float32)


def derivatives(perts, cheb, states, pert_table):
    return call(
        deriv_kernel,
        [
            jax.ShapeDtypeStruct(states.shape, jnp.float32),
            jax.ShapeDtypeStruct((1, states.shape[1]), jnp.float32),
            jax.ShapeDtypeStruct(pert_table.shape, jnp.float32),
        ],
        [VMEM_REF] * 3,
        [],
        cost(1, *states.shape, states.shape[0]),
    )([perts, cheb, states, pert_table], [SMEM_REF] + [VMEM_REF] * 3)


def local_kernel(cheb_ref, resid_ref, decay_ref, out_ref):
    out_ref[...] = cheb_dot(True, cheb_ref, resid_ref) + decay_ref[...] * resid_ref[...]


def local_terms(cheb, resid, decay):
    return call(
        local_kernel,
        jax.ShapeDtypeStruct(resid.shape, jnp.float32),
        VMEM_REF,
        [],
        cost(1, *resid.shape, resid.shape[0]),
    )([cheb, resid, decay], [VMEM_REF] * 3)


def middle_kernel(base, many, offs_ref, x_ref, *refs):
    bands = refs[:many]
    acc_ref, deriv_ref, drive_ref, chosen_ref, states_ref, eps_ref, decay_ref = refs[many:-6]
    resid_ref, delta_ref, delta_t_ref, table_ref, sum_eps_ref, sum_decay_ref = refs[-6:]
    tile = GROUP * bands[0].shape[0]
    here = columns_of(offs_ref, base, x_ref.shape[-1])
    for at in range(many // GROUP):
        band = pl.ds(at * tile, tile)
        part = acc_ref[band, :] + product(bands[at * GROUP : (at + 1) * GROUP], here, x_ref.at[0])
        states = states_ref[:, band]
        act = jnp.tanh(part.T + drive_ref[:, band])
        eps = eps_ref[:, band]
        resid = deriv_ref[:, band] - (eps * act - decay_ref[:, band] * states)
        delta = (-eps * (1.0 - act * act) * resid).astype(jnp.bfloat16)
        wide = delta.astype(jnp.float32)
        resid_ref[:, band] = resid
        delta_ref[:, band] = delta
        delta_t_ref[band, :] = wide.T.astype(jnp.bfloat16)
        table_ref[:, band] = chosen_ref[:, band] * jnp.sum(wide, axis=0, keepdims=True)
        sum_eps_ref[:, band] = -jnp.sum(act * resid, axis=0, keepdims=True)
        sum_decay_ref[:, band] = jnp.sum(states * resid, axis=0, keepdims=True)


def middle(offs, base, x, bands, acc, derivs, states, eps, decay):
    _, nodes, slab = x.shape
    rows = acc.shape[0]
    wide = functools.partial(jax.ShapeDtypeStruct, dtype=jnp.float32)
    return call(
        functools.partial(middle_kernel, base, len(bands)),
        [
            wide((nodes, rows)),
            jax.ShapeDtypeStruct((nodes, rows), jnp.bfloat16),
            jax.ShapeDtypeStruct((rows, nodes), jnp.bfloat16),
            wide(derivs[2].shape),
            wide((1, rows)),
            wide((1, rows)),
        ],
        [VMEM_REF] * 6,
        [],
        cost(2, nodes, slab, rows),
    )(
        [offs, x, *bands, acc, *derivs, states, eps, decay],
        [SMEM_REF] + [VMEM_REF] * (8 + len(bands)),
    )


def grad_w_part(base, offs_ref, delta_t_ref, xs, out_ref, held, sems):
    rows, slab = delta_t_ref.shape[0], held.shape[2]
    slots, tile = held.shape[:2]
    step = min(256, slab)
    copies = []
    for at, x_ref in enumerate(xs):
        for start in range(0, rows, tile):
            slot, band = len(copies) % slots, pl.ds(start, tile)
            if len(copies) >= slots:
                copies[-slots].wait()
            for col in range(0, slab, step):
                held[slot, :, col : col + step] = jnp.dot(
                    delta_t_ref[band, :], x_ref[:, col : col + step],
                    preferred_element_type=jnp.float32,
                ).astype(held.dtype)
            there = columns_of(offs_ref, base + at, slab)
            copy = pltpu.make_async_copy(held.at[slot], out_ref.at[band, there], sems.at[slot])
            copy.start()
            copies.append(copy)
    return copies[-slots:]


def share_part(places, offs_ref, delta_ref, bands, out_ref):
    depth, slab = GROUP * bands[0].shape[0], out_ref.shape[2]
    tile = max(slab // 2, 128)
    for index, place in enumerate(places):
        for col in range(0, slab, tile):
            there = pl.ds(pl.multiple_of(offs_ref[place] * slab + col, tile), tile)
            part = None
            for at in range(len(bands) // GROUP):
                group = bands[at * GROUP : (at + 1) * GROUP]
                more = jnp.dot(
                    delta_ref[:, at * depth : (at + 1) * depth],
                    jnp.concatenate([ref[:, there] for ref in group], axis=0),
                    preferred_element_type=jnp.float32,
                )
                part = more if part is None else part + more
            out_ref[index, :, pl.ds(col, tile)] = part.astype(out_ref.dtype)


def sums_kernel(base, found, arrays, sent, kept, many, first, *refs):
    offs_ref, delta_ref, delta_t_ref = refs[:3]
    xs, bands = refs[3 : 3 + arrays], refs[3 + arrays : 3 + arrays + many]
    refs = refs[3 + arrays + many + (0 if first else 1) :]
    copies = []
    if found:
        out_ref, held, sems = refs[-3:]
        views = [xs[at].at[index] for at, index in found]
        copies = grad_w_part(base, offs_ref, delta_t_ref, views, out_ref, held, sems)
    if sent:
        share_part(sent, offs_ref, delta_ref, bands, refs[0])
        share_part(kept, offs_ref, delta_ref, bands, refs[1])
    for copy in copies:
        copy.wait()


def sums(offs, base, pieces, sent, kept, delta, delta_t, bands, slab, so_far, shape):
    nodes, rows = delta.shape
    arrays, found = split_pieces(pieces)
    first = so_far is None
    tile = rows // 2
    shapes, scratch = [], []
    if sent:
        shapes = [
            jax.ShapeDtypeStruct((len(sent), nodes, slab), jnp.bfloat16),
            jax.ShapeDtypeStruct((len(kept), nodes, slab), jnp.float32),
        ]
    specs = [VMEM_REF] * len(shapes)
    if found:
        shapes, specs = shapes + [jax.ShapeDtypeStruct(shape, jnp.bfloat16)], specs + [ANY_REF]
        scratch = [pltpu.VMEM((4, tile, slab), jnp.bfloat16), pltpu.SemaphoreType.DMA((4,))]
    operands = [offs, delta, delta_t, *arrays, *bands] + ([] if first else [so_far])
    outs = call(
        functools.partial(
            sums_kernel, base, found, len(arrays), sent, kept, len(bands), first
        ),
        shapes,
        specs,
        scratch,
        cost(len(found) + len(sent) + len(kept), nodes, slab, rows),
        {} if first else {len(operands) - 1: len(shapes) - 1},
    )(
        operands,
        [SMEM_REF] + [VMEM_REF] * (2 + len(arrays) + len(bands))
        + ([] if first else [ANY_REF]),
    )
    others, owns = outs[:2] if sent else (None, None)
    return others, owns, outs[-1] if found else so_far


def ring_body(chips, states, weights, pert_table, eps_gain, decay, perts):
    _, nodes, slab = states.shape
    rows = weights.shape[0]
    order = chip_ring(chips)
    place = np.argsort(order)
    half = chips // 2

    listing = [(0, 0), (0, 1)]
    for step in range(1, half):
        listing += [(step, 0), (step, 1), (-step, 1), (-step, 0)]
    listing += [(half, 0), (half, 1)]
    sides = {key: at for at, key in enumerate(listing)}
    table = np.array(
        [
            [
                2 * order[(place[device // 2] + (step if device % 2 else -step)) % chips]
                + (device % 2 ^ side)
                for step, side in listing
            ]
            for device in range(2 * chips)
        ],
        dtype=np.int32,
    )
    me = lax.axis_index("row")
    offs = lax.dynamic_slice(jnp.asarray(table), (me, 0), (1, 2 * chips)).reshape(-1)

    def passed(array, way=1, cross=0):
        pairs = []
        for at, chip in enumerate(order):
            pairs.append((2 * chip, 2 * order[(at + way) % chips] + cross))
            pairs.append((2 * chip + 1, 2 * order[(at - way) % chips] + 1 - cross))
        return lax.ppermute(array, "row", pairs)

    def swap(array):
        return lax.ppermute(array, "row", [(i, i ^ 1) for i in range(2 * chips)])

    gate = lax.optimization_barrier
    weights = pltpu.with_memory_space_constraint(weights, pltpu.HBM)
    cheb = cheb_matrix(nodes)
    flat = states.reshape(nodes, slab)
    xb = states.astype(jnp.bfloat16)

    near, over = passed(xb), passed(xb, -1, 1)
    other = swap(xb)
    mark, bands = load_first(offs, perts, weights, LOADS[0])
    near, over, other, mark = gate((near, over, other, mark))
    x = {(0, 0): (xb, 0), (0, 1): (other, 0)}
    flow = jnp.concatenate([near, over], axis=0)
    acc, seen = mark, 0
    for step in range(1, half + 1):
        if step < half:
            x[step, 0], x[step, 1] = (flow, 0), (flow, 1)
            other = flow
        else:
            x[half, 0], other = (flow, 0), flow
        if step < half:
            flow = passed(flow if step < half - 1 else flow[:1])
        other = swap(other)
        if step < half:
            x[-step, 1], x[-step, 0] = (other, 0), (other, 1)
        else:
            x[half, 1] = (other, 0)
        count = 3 if step == half else 4
        late = LOADS[1] if step == 1 else 0
        acc, bands = add_products(
            offs, weights, acc, bands, [x[key] for key in listing[: seen + count]], count,
            LOADS[1] if step == 2 else len(bands) if step == 1 else 0, late,
        )
        seen += count
        if step == half - 2:
            derivs = derivatives(perts, cheb, flat, pert_table)
            acc, *derivs = gate((acc, *derivs))
        if step < half:
            flow, acc = gate((flow, acc))

    decay = decay.reshape(1, rows)
    resid, delta, delta_t, grad_table, grad_eps, grad_decay = middle(
        offs, seen, x[half, 1][0], bands, acc, derivs, flat, eps_gain.reshape(1, rows), decay
    )

    grad_w, base = None, 0

    def work(offs, count, step, grad_w, base):
        if step is None:
            sent, kept = [], []
        elif step in (0, half):
            sent, kept = [sides[step, 1]], [sides[step, 0]]
        else:
            sent = [sides[step, 1], sides[step, 0]]
            kept = [sides[-step, 0], sides[-step, 1]]
        others, owns, grad_w = sums(
            offs, base, [x[key] for key in listing[base : base + count]], sent, kept,
            delta, delta_t, bands, slab, grad_w, weights.shape,
        )
        return others, owns, grad_w, base + count

    def joined(others, owns):
        return owns + swap(others).astype(jnp.float32)

    counts = list(PIECES)
    others, owns, _, _ = work(offs, 0, half, None, 0)
    far = joined(others, owns).astype(jnp.bfloat16)
    others, owns, _, _ = work(offs, 0, half - 1, None, 0)
    far, offs, owns = gate((far, offs, owns))
    share = joined(others, owns)
    flow = passed(far)
    for step in range(half - 1, 0, -1):
        others, owns, grad_w, base = work(offs, counts.pop(0), step - 1, grad_w, base)
        flow, owns = gate((flow, owns))
        flow = flow.astype(jnp.float32)
        if step == half - 1:
            total = jnp.concatenate([share[:1] + flow, share[1:]], axis=0)
        else:
            total = share + flow
        total = total.astype(jnp.bfloat16)
        share = joined(others, owns)
        total, offs = gate((total, offs))
        if step > 1:
            flow = passed(total)
        else:
            near, over = passed(total[:1]), passed(total[1:], 1, 1)
    _, _, grad_w, base = work(offs, len(listing) - base, None, grad_w, base)
    local = local_terms(cheb, resid, decay)
    near, over, local = gate((near, over, local))
    grad_x = local + share[0] + near[0].astype(jnp.float32) + over[0].astype(jnp.float32)
    grad_x = grad_x.reshape(states.shape)
    return (grad_w, grad_x, grad_table, grad_eps.reshape(rows), grad_decay.reshape(rows))


def plain_body(states, weights, pert_table, eps_gain, decay, perts):
    traj, nodes, slab = states.shape
    total = traj * nodes
    cheb = cheb_matrix(nodes)
    xb = states.astype(jnp.bfloat16).reshape(total, slab)
    full = lax.all_gather(xb, "row", axis=1, tiled=True)
    pre = lax.dot_general(
        full, weights, (((1,), (1,)), ((), ())), preferred_element_type=jnp.float32
    )
    onehot = (perts[:, None] == jnp.arange(pert_table.shape[0], dtype=jnp.int32)[None, :]).astype(
        jnp.float32
    )
    drive = jnp.dot(onehot, pert_table, precision=lax.Precision.HIGHEST)
    act = jnp.tanh(pre.reshape(traj, nodes, slab) + drive[:, None, :])
    deriv = SCALE * jnp.einsum("kl,clg->ckg", cheb, states, precision=lax.Precision.HIGHEST)
    resid = deriv - (eps_gain * act - decay * states)
    delta = (-eps_gain * (1.0 - act * act) * resid).astype(jnp.bfloat16)
    dflat = delta.reshape(total, slab)
    grad_w = lax.dot_general(
        dflat, full, (((0,), (0,)), ((), ())), preferred_element_type=jnp.float32
    ).astype(jnp.bfloat16)
    back = jnp.dot(dflat, weights, preferred_element_type=jnp.float32)
    back = lax.psum_scatter(back, "row", scatter_dimension=1, tiled=True)
    grad_x = (
        SCALE * jnp.einsum("lk,clg->ckg", cheb, resid, precision=lax.Precision.HIGHEST)
        + decay * resid
        + back.reshape(traj, nodes, slab)
    )
    node_sums = jnp.sum(delta.astype(jnp.float32), axis=1)
    grad_table = jnp.dot(onehot.T, node_sums, precision=lax.Precision.HIGHEST)
    grad_eps = -jnp.sum(act * resid, axis=(0, 1))
    grad_decay = jnp.sum(states * resid, axis=(0, 1))
    return (grad_w, grad_x, grad_table, grad_eps, grad_decay)


def solution(mesh):
    chips = mesh.shape["row"] // 2
    in_specs = (
        P("rep", None, "row"),
        P(("rep", "row"), None),
        P("rep", "row"),
        P(("rep", "row")),
        P(("rep", "row")),
        P("rep"),
    )
    out_specs = (
        P(("rep", "row"), None),
        P("rep", None, "row"),
        P("rep", "row"),
        P(("rep", "row")),
        P(("rep", "row")),
    )

    def run(states, *others):
        if states.shape[0] == 1 and chips <= LONGEST_RING:
            return ring_body(chips, states, *others)
        return plain_body(states, *others)

    return jax.shard_map(run, mesh=mesh, in_specs=in_specs, out_specs=out_specs, check_vma=False)
```

time: 85 us -> 84.1 us (0.989)
  waiting for transfers between devices: 5.53 us -> 8.66 us
  Pallas kernels: 52.6 us -> 50.5 us
  starting transfers between devices: 21.4 us -> 19.4 us
    ppermute x16 -> x10, waiting for transfers between devices: 5.48 us -> 8.63 us  [passed(): return lax.ppermute(array, 'row', pairs)]
    pallas_call x14, Pallas kernels: 52.6 us -> 50.5 us  [run(): pl.pallas_call(kernel, out_shape=out_shape, in_specs=in_specs, out_specs=...]
    ppermute x16 -> x10, starting transfers between devices: 3.75 us -> 2.42 us  [swap(): return lax.ppermute(array, 'row', [(i, i ^ 1) for i in range(2 * chips)])]
    ppermute x16 -> x10, starting transfers between devices: 17.6 us -> 17 us  [passed(): return lax.ppermute(array, 'row', pairs)]
  transfers between devices with their start and end apart: 32 -> 20, of which waited for: 7 -> 6; matrix products, arithmetic and copies ran while one was open for 1% -> 1% of each run, Pallas kernels for 58% -> 56%
where the time goes in v9:
time: 84.1 us; the launch traced here: 83.9 us
  Pallas kernels  50.5 us (60%)
  starting transfers between devices  19.4 us (23%)
  waiting for transfers between devices  8.66 us (10%)
  other arithmetic  2.92 us (3%)
  between operations  1.6 us (2%)
  local copies, waits for them, and re-layouts  0.85 us (1%)
    pallas_call x14, Pallas kernels, run(): pl.pallas_call(kernel, out_shape=out_shape, in_specs=in_specs, out_specs=...  50.5 us
    ppermute x10, starting transfers between devices, passed(): return lax.ppermute(array, 'row', pairs)  17 us
    ppermute x10, waiting for transfers between devices, passed(): return lax.ppermute(array, 'row', pairs)  8.63 us
    ppermute x10, starting transfers between devices, swap(): return lax.ppermute(array, 'row', [(i, i ^ 1) for i in range(2 * chips)])  2.42 us
  transfers between devices with their start and end apart: 20, of which 6 were waited for; matrix products, arithmetic and copies ran while one was open for 1% of the time, Pallas kernels for 56%

profile of v9, /device:TPU:0, one launch (start us, length us, event | category | flops | bytes accessed | tf_op | source)
XLA Modules:
  0.0 83.9 jit_solution(3850216683490079475)
XLA Ops:
  0.6 1.1 %convert_element_type.49.refs_11_.refs_16_.refs_3_ = bf16[1,128,1024]{2,1,0:T(8,128)(2,1)S(1)} convert(f32[1,128,1024]{2,1,0:T(8,128)} %param.8) | non-fusion elementwise | flops 131072 | bytes 786432 | tf_op jit(solution)/shard_map/convert_element_type | solution.py:386
  1.7 0.5 collective-permute-start.2
  2.2 2.7 %collective-permute-start.1 = (bf16[1,128,1024]{2,1,0:T(8,128)(2,1)S(1)}, bf16[1,128,1024]{2,1,0:T(8,128)(2,1)S(1)}, u32[]{:S(2)}, u32[]{:S(2)}) collective-permute-start(bf16[1,128,1024]{2,1,0:T(8,128)(2,1)S(1)} %convert_element_type.49.refs_11_.refs_16_.refs_3_), channel_id=1, source_target_pairs={{0,5},{1,2},{2,1},{3,6},{6,3},{7,10},{10,7},{11,14},{14,11},{15,12... | collective-permute-start | bytes 786440 | tf_op jit(solution)/shard_map/ppermute | solution.py:377
  4.9 0.0 collective-permute-start
  5.6 0.7 dynamic-slice_bitcast_fusion.offs_ref.refs_0_
  6.3 7.7 %shard_map.119 = (f32[8,128]{1,0:T(8,128)S(1)}, bf16[64,16384]{1,0:T(8,128)(2,1)S(1)}, bf16[64,16384]{1,0:T(8,128)(2,1)S(1)}, bf16[64,16384]{1,0:T(8,128)(2,1)S(...) custom-call(s32[16]{0:T(128)S(1)} %dynamic-slice_bitcast_fusion.offs, ...), custom_call_target="tpu_custom_call" | custom-call | flops 2097152 | bytes 16384 | tf_op jit(solution)/shard_map/pallas_call | solution.py:58
  14.0 0.0 collective-permute-done.2.refs_12_.refs_17_.refs_4_
  14.0 0.0 collective-permute-done.1
  14.0 0.0 collective-permute-done
  14.0 2.0 %collective-permute-start.3 = (bf16[2,128,1024]{2,1,0:T(8,128)(2,1)S(1)}, bf16[2,128,1024]{2,1,0:T(8,128)(2,1)S(1)}, u32[]{:S(2)}, u32[]{:S(2)}) collective-permute-start(bf16[2,128,1024]{2,1,0:T(8,128)(2,1)S(1)} %constant_dynamic-update-slice_fusion.refs_13_.refs_18_.refs_3_), channel_id=1, source_target_pairs={{0,2},{1,5},{2,6},{3,1},{6,10},{7,3},{10,14},{11,7},{14,12},{15,11... | collective-permute-start | bytes 1572872 | tf_op jit(solution)/shard_map/ppermute | solution.py:377
  16.0 0.0 collective-permute-start.5
  16.0 6.7 %shard_map.120 = (f32[1024,128]{1,0:T(8,128)S(1)}, bf16[64,16384]{1,0:T(8,128)(2,1)S(1)}, bf16[64,16384]{1,0:T(8,128)(2,1)S(1)}, bf16[64,16384]{1,0:T(8,128)(2,1...) custom-call(s32[16]{0:T(128)S(1)} %dynamic-slice_bitcast_fusion.offs_ref.refs_0_,, ...), custom_call_target="tpu_custom_call" | custom-call | flops 67108864 | bytes 524288 | tf_op jit(solution)/shard_map/pallas_call | solution.py:58
  22.7 0.6 collective-permute-done.3.refs_20_.refs_3_
  23.3 1.9 %collective-permute-start.4 = (bf16[2,128,1024]{2,1,0:T(8,128)(2,1)S(1)}, bf16[2,128,1024]{2,1,0:T(8,128)(2,1)S(1)}, u32[]{:S(2)}, u32[]{:S(2)}) collective-permute-start(bf16[2,128,1024]{2,1,0:T(8,128)(2,1)S(1)} %collective-permute-done.3.refs_20_.refs_3_), channel_id=1, source_target_pairs={{0,2},{1,5},{2,6},{3,1},{6,10},{7,3},{10,14},{11,7},{14,12},{15,11... | collective-permute-start | bytes 1572872 | tf_op jit(solution)/shard_map/ppermute | solution.py:377
  25.2 0.0 collective-permute-start.7
  25.2 0.6 shard_map.122
  25.8 0.0 collective-permute-done.5.refs_19_.refs_4_
  25.8 3.7 %shard_map.121.acc_ref = f32[1024,128]{1,0:T(8,128)S(1)} custom-call(s32[16]{0:T(128)S(1)} %dynamic-slice_bitcast_fusion.offs_ref.refs_0_, f32[1024,128]{1,0:T(8,128)S(1)} %get-tuple-element.94.acc_ref, bf16[64,16384]{1,0:T(8,128)(2,1)S(1)} %get-tuple-element.81.refs_1_.refs_0_.refs_3_.refs_5_.refs_6_.refs_7_, ...), custom_call_target="tpu_custom_call" | custom-call | flops 67108864 | bytes 524288 | tf_op jit(solution)/shard_map/pallas_call | solution.py:58
  29.6 2.9 %collective-permute-done.4.refs_17_.refs_5_.refs_3_ = bf16[2,128,1024]{2,1,0:T(8,128)(2,1)S(1)} collective-permute-done((bf16[2,128,1024]{2,1,0:T(8,128)(2,1)S(1)}, bf16[2,128,1024]{2,1,0:T(8,128)(2,1)S(1)}, u32[]{:S(2)}, u32[]{:S(2)}) %collective-permute-start.4) | collective-permute-done | bytes 524320 | tf_op jit(solution)/shard_map/ppermute | solution.py:377
  32.5 0.0 collective-permute-start.9
  32.5 2.0 %collective-permute-start.6 = (bf16[1,128,1024]{2,1,0:T(8,128)(2,1)S(1)}, bf16[1,128,1024]{2,1,0:T(8,128)(2,1)S(1)}, u32[]{:S(2)}, u32[]{:S(2)}) collective-permute-start(bf16[1,128,1024]{2,1,0:T(8,128)(2,1)S(1)} %slice.16), channel_id=1, source_target_pairs={{0,2},{1,5},{2,6},{3,1},{6,10},{7,3},{10,14},{11,7},{14,12},{15,11... | collective-permute-start | bytes 786440 | tf_op jit(solution)/shard_map/ppermute | solution.py:377
  34.5 0.0 collective-permute-done.7.refs_16_.refs_4_
  34.5 2.9 %shard_map.123.acc_ref = f32[1024,128]{1,0:T(8,128)S(1)} custom-call(s32[16]{0:T(128)S(1)} %dynamic-slice_bitcast_fusion.offs_ref.refs_0_, f32[1024,128]{1,0:T(8,128)S(1)} %shard_map.121.acc_ref, bf16[64,16384]{1,0:T(8,128)(2,1)S(1)} %get-tuple-element.81.refs_1_.refs_0_.refs_3_.refs_5_.refs_6_.refs_7_, ...), custom_call_target="tpu_custom_call" | custom-call | flops 67108864 | bytes 524288 | tf_op jit(solution)/shard_map/pallas_call | solution.py:58
  37.4 0.0 copy-start.3
  37.4 0.0 copy-start.4
  37.4 1.5 %collective-permute-done.6.refs_17_.refs_5_ = bf16[1,128,1024]{2,1,0:T(8,128)(2,1)S(1)} collective-permute-done((bf16[1,128,1024]{2,1,0:T(8,128)(2,1)S(1)}, bf16[1,128,1024]{2,1,0:T(8,128)(2,1)S(1)}, u32[]{:S(2)}, u32[]{:S(2)}) %collective-permute-start.6) | collective-permute-done | bytes 262176 | tf_op jit(solution)/shard_map/ppermute | solution.py:377
  38.9 0.0 collective-permute-start.8
  38.9 0.0 collective-permute-done.9.refs_16_.refs_4_
  38.9 2.3 %shard_map.124.refs_16_ = f32[1024,128]{1,0:T(8,128)S(1)} custom-call(s32[16]{0:T(128)S(1)} %dynamic-slice_bitcast_fusion.offs_ref.refs_0_, f32[1024,128]{1,0:T(8,128)S(1)} %shard_map.123.acc_ref, bf16[64,16384]{1,0:T(8,128)(2,1)S(1)} %get-tuple-element.81.refs_1_.refs_0_.refs_3_.refs_5_.refs_6_.refs_7_, ...), custom_call_target="tpu_custom_call" | custom-call | flops 50331648 | bytes 393216 | tf_op jit(solution)/shard_map/pallas_call | solution.py:58
  41.3 0.0 collective-permute-done.8.x_ref.refs_6_
  41.3 2.1 %shard_map.125 = (f32[128,1024]{1,0:T(8,128)S(1)}, bf16[128,1024]{1,0:T(8,128)(2,1)S(1)}, bf16[1024,128]{1,0:T(8,128)(2,1)S(1)}, f32[16,1024]{1,0:T(8,128)}, f32[1,1024]{1,0:T(1,128)}, /*index=5*/f32[1,1024]{1,0:T(1,128)}) custom-call(s32[16]{0:T(128)S(1)} %dynamic-slice_bitcast_fusion.offs_ref.refs_0_, ...), custom_call_target="tpu_custom_call" | custom-call | flops 33554432 | bytes 262144 | tf_op jit(solution)/shard_map/pallas_call | solution.py:58
  43.4 1.3 %shard_map.126 = (bf16[1,128,1024]{2,1,0:T(8,128)(2,1)S(1)}, f32[1,128,1024]{2,1,0:T(8,128)S(1)}) custom-call(s32[16]{0:T(128)S(1)} %dynamic-slice_bitcast_fusion.offs_ref.refs_0_, bf16[128,1024]{1,0:T(8,128)(2,1)S(1)} %get-tuple-element.112.refs_1_, bf16[1024,128]{1,0:T(8,128)(2,1)S(1)} %get-tuple-element.113.refs_2_, ...), custom_call_target="tpu_custom_call" | custom-call | flops 33554432 | bytes 262144 | tf_op jit(solution)/shard_map/pallas_call | solution.py:58
  44.7 0.6 collective-permute-start.10
  45.3 1.8 %shard_map.127 = (bf16[2,128,1024]{2,1,0:T(8,128)(2,1)S(1)}, f32[2,128,1024]{2,1,0:T(8,128)S(1)}) custom-call(s32[16]{0:T(128)S(1)} %dynamic-slice_bitcast_fusion.offs_ref.refs_0_, bf16[128,1024]{1,0:T(8,128)(2,1)S(1)} %get-tuple-element.112.refs_1_, bf16[1024,128]{1,0:T(8,128)(2,1)S(1)} %get-tuple-element.113.refs_2_, ...), custom_call_target="tpu_custom_call" | custom-call | flops 67108864 | bytes 524288 | tf_op jit(solution)/shard_map/pallas_call | solution.py:58
  47.1 0.1 collective-permute-start.11
  47.2 0.0 collective-permute-done.10
  47.2 0.1 add_convert_fusion.2
  47.3 2.2 %collective-permute-start.12 = (bf16[1,128,1024]{2,1,0:T(8,128)(2,1)S(1)}, bf16[1,128,1024]{2,1,0:T(8,128)(2,1)S(1)}, u32[]{:S(2)}, u32[]{:S(2)}) collective-permute-start(bf16[1,128,1024]{2,1,0:T(8,128)(2,1)S(1)} %add_convert_fusion.2), channel_id=1, source_target_pairs={{0,2},{1,5},{2,6},{3,1},{6,10},{7,3},{10,14},{11,7},{14,12},{15,11... | collective-permute-start | bytes 786440 | tf_op jit(solution)/shard_map/ppermute | solution.py:377
  49.4 3.8 %shard_map.128 = (bf16[2,128,1024]{2,1,0:T(8,128)(2,1)S(1)}, f32[2,128,1024]{2,1,0:T(8,128)S(1)}, bf16[1024,16384]{1,0:T(8,128)(2,1)}) custom-call(s32[16]{0:T(128)S(1)} %dynamic-slice_bitcast_fusion.offs_ref.refs_0_, bf16[128,1024]{1,0:T(8,128)(2,1)S(1)} %get-tuple-element.112.refs_1_, bf16[1024,128]{1,0:T(8,128)(2,1)S(1)} %get-tuple-element.113.refs_2_, ...), custom_call_target="tpu_custom_call" | custom-call | flops 100663296 | bytes 786432 | tf_op jit(solution)/shard_map/pallas_call | solution.py:58
  53.2 0.7 collective-permute-done.12
  53.9 0.0 collective-permute-done.11
  53.9 0.2 convert_add_fusion
  54.1 0.1 fusion
  54.2 0.1 pad_maximum_fusion
  54.3 2.0 %collective-permute-start.13 = (bf16[2,128,1024]{2,1,0:T(8,128)(2,1)S(1)}, bf16[2,128,1024]{2,1,0:T(8,128)(2,1)S(1)}, u32[]{:S(2)}, u32[]{:S(2)}) collective-permute-start(bf16[2,128,1024]{2,1,0:T(8,128)(2,1)S(1)} %pad_maximum_fusion), channel_id=1, source_target_pairs={{0,2},{1,5},{2,6},{3,1},{6,10},{7,3},{10,14},{11,7},{14,12},{15,11... | collective-permute-start | bytes 1572872 | tf_op jit(solution)/shard_map/ppermute | solution.py:377
  56.2 0.0 collective-permute-start.15
  56.2 5.6 %shard_map.129 = (bf16[2,128,1024]{2,1,0:T(8,128)(2,1)S(1)}, f32[2,128,1024]{2,1,0:T(8,128)S(1)}, bf16[1024,16384]{1,0:T(8,128)(2,1)}) custom-call(s32[16]{0:T(128)S(1)} %dynamic-slice_bitcast_fusion.offs_ref.refs_0_, bf16[128,1024]{1,0:T(8,128)(2,1)S(1)} %get-tuple-element.112.refs_1_, ...), custom_call_target="tpu_custom_call", output_to_operand_aliasing={{2}: (21, {})} | custom-call | flops 134217728 | bytes 1048576 | tf_op jit(solution)/shard_map/pallas_call | solution.py:58
  61.9 1.6 %collective-permute-done.13 = bf16[2,128,1024]{2,1,0:T(8,128)(2,1)S(1)} collective-permute-done((bf16[2,128,1024]{2,1,0:T(8,128)(2,1)S(1)}, bf16[2,128,1024]{2,1,0:T(8,128)(2,1)S(1)}, u32[]{:S(2)}, u32[]{:S(2)}) %collective-permute-start.13) | collective-permute-done | bytes 524320 | tf_op jit(solution)/shard_map/ppermute | solution.py:377
  63.5 0.0 collective-permute-done.15
  63.5 0.3 add_convert_fusion.1
  63.7 2.0 %collective-permute-start.16 = (bf16[2,128,1024]{2,1,0:T(8,128)(2,1)S(1)}, bf16[2,128,1024]{2,1,0:T(8,128)(2,1)S(1)}, u32[]{:S(2)}, u32[]{:S(2)}) collective-permute-start(bf16[2,128,1024]{2,1,0:T(8,128)(2,1)S(1)} %add_convert_fusion.1), channel_id=1, source_target_pairs={{0,2},{1,5},{2,6},{3,1},{6,10},{7,3},{10,14},{11,7},{14,12},{15,11... | collective-permute-start | bytes 1572872 | tf_op jit(solution)/shard_map/ppermute | solution.py:377
  65.7 0.0 collective-permute-start.14
  65.7 5.9 %shard_map.130 = (bf16[1,128,1024]{2,1,0:T(8,128)(2,1)S(1)}, f32[1,128,1024]{2,1,0:T(8,128)S(1)}, bf16[1024,16384]{1,0:T(8,128)(2,1)}) custom-call(s32[16]{0:T(128)S(1)} %dynamic-slice_bitcast_fusion.offs_ref.refs_0_, bf16[128,1024]{1,0:T(8,128)(2,1)S(1)} %get-tuple-element.112.refs_1_, ...), custom_call_target="tpu_custom_call", output_to_operand_aliasing={{2}: (22, {})} | custom-call | flops 117440512 | bytes 917504 | tf_op jit(solution)/shard_map/pallas_call | solution.py:58
  71.6 1.4 %collective-permute-done.16 = bf16[2,128,1024]{2,1,0:T(8,128)(2,1)S(1)} collective-permute-done((bf16[2,128,1024]{2,1,0:T(8,128)(2,1)S(1)}, bf16[2,128,1024]{2,1,0:T(8,128)(2,1)S(1)}, u32[]{:S(2)}, u32[]{:S(2)}) %collective-permute-start.16) | collective-permute-done | bytes 524320 | tf_op jit(solution)/shard_map/ppermute | solution.py:377
  73.0 0.0 collective-permute-done.14
  73.0 0.3 add_convert_fusion
  73.3 0.4 collective-permute-start.18
  73.7 1.9 %collective-permute-start.17 = (bf16[1,128,1024]{2,1,0:T(8,128)(2,1)S(1)}, bf16[1,128,1024]{2,1,0:T(8,128)(2,1)S(1)}, u32[]{:S(2)}, u32[]{:S(2)}) collective-permute-start(bf16[1,128,1024]{2,1,0:T(8,128)(2,1)S(1)} %get-tuple-element.150), channel_id=1, source_target_pairs={{0,2},{1,5},{2,6},{3,1},{6,10},{7,3},{10,14},{11,7},{14,12},{15,11... | collective-permute-start | bytes 786440 | tf_op jit(solution)/shard_map/ppermute | solution.py:377
  75.6 1.2 %collective-permute-start.19 = (bf16[1,128,1024]{2,1,0:T(8,128)(2,1)S(1)}, bf16[1,128,1024]{2,1,0:T(8,128)(2,1)S(1)}, u32[]{:S(2)}, u32[]{:S(2)}) collective-permute-start(bf16[1,128,1024]{2,1,0:T(8,128)(2,1)S(1)} %get-tuple-element.143), channel_id=1, source_target_pairs={{0,1},{1,0},{2,3},{3,2},{4,5},{5,4},{6,7},{7,6},{8,9},{9,8},{10,11... | collective-permute-start | bytes 786440 | tf_op jit(solution)/shard_map/ppermute | solution.py:380
  76.8 0.6 shard_map.132
  77.4 5.5 %shard_map.131 = bf16[1024,16384]{1,0:T(8,128)(2,1)} custom-call(s32[16]{0:T(128)S(1)} %dynamic-slice_bitcast_fusion.offs_ref.refs_0_, bf16[128,1024]{1,0:T(8,128)(2,1)S(1)} %get-tuple-element.112.refs_1_, bf16[1024,128]{1,0:T(8,128)(2,1)S(1)} %get-tuple-element.113.refs_2_, ...), custom_call_target="tpu_custom_call", output_to_operand_aliasing={{}: (23, {})} | custom-call | flops 83886080 | bytes 655360 | tf_op jit(solution)/shard_map/pallas_call | solution.py:58
  82.9 0.0 collective-permute-done.17
  82.9 0.0 collective-permute-done.19
  83.0 1.0 %fusion.1 = f32[1,128,1024]{2,1,0:T(8,128)} fusion(f32[128,1024]{1,0:T(8,128)S(1)} %shard_map.132, f32[1,128,1024]{2,1,0:T(8,128)S(1)} %get-tuple-element.142, bf16[1,128,1024]{2,1,0:T(8,128)(2,1)S(1)} %collective-permute-done.19, bf16[1,128,1024]{2,1,0:T(8,128)(2,1)S(1)} %collective-permute-done.18, bf16[1,128,1024]{2,1,0:T(8,128)(2,1)S(1)} %collective-permute-done.17), kind=kLoop, calls=%fused_computation.8 | loop fusion | flops 917504 | bytes 2359296 | tf_op jit(solution)/shard_map/reshape | solution.py:471
  (14 shorter events, 0.1 us)
Async XLA Ops:
  1.7 12.2 %collective-permute-start.2 = (bf16[1,128,1024]{2,1,0:T(8,128)(2,1)S(1)}, bf16[1,128,1024]{2,1,0:T(8,128)(2,1)S(1)}, u32[]{:S(2)}, u32[]{:S(2)}) collective-permute-start(bf16[1,128,1024]{2,1,0:T(8,128)(2,1)S(1)} %convert_element_type.49.refs_11_.refs_16_.refs_3_), channel_id=1, source_target_pairs={{0,1},{1,0},{2,3},{3,2},{4,5},{5,4},{6,7},{7,6},{8,9},{9,8},{10,11... | collective-permute-start | bytes 786440 | tf_op jit(solution)/shard_map/ppermute | solution.py:380
  2.2 11.7 %collective-permute-start.1 = (bf16[1,128,1024]{2,1,0:T(8,128)(2,1)S(1)}, bf16[1,128,1024]{2,1,0:T(8,128)(2,1)S(1)}, u32[]{:S(2)}, u32[]{:S(2)}) collective-permute-start(bf16[1,128,1024]{2,1,0:T(8,128)(2,1)S(1)} %convert_element_type.49.refs_11_.refs_16_.refs_3_), channel_id=1, source_target_pairs={{0,5},{1,2},{2,1},{3,6},{6,3},{7,10},{10,7},{11,14},{14,11},{15,12... | collective-permute-start | bytes 786440 | tf_op jit(solution)/shard_map/ppermute | solution.py:377
  4.9 9.1 %collective-permute-start = (bf16[1,128,1024]{2,1,0:T(8,128)(2,1)S(1)}, bf16[1,128,1024]{2,1,0:T(8,128)(2,1)S(1)}, u32[]{:S(2)}, u32[]{:S(2)}) collective-permute-start(bf16[1,128,1024]{2,1,0:T(8,128)(2,1)S(1)} %convert_element_type.49.refs_11_.refs_16_.refs_3_), channel_id=1, source_target_pairs={{0,2},{1,5},{2,6},{3,1},{6,10},{7,3},{10,14},{11,7},{14,12},{15,11... | collective-permute-start | bytes 786440 | tf_op jit(solution)/shard_map/ppermute | solution.py:377
  14.0 9.2 %collective-permute-start.3 = (bf16[2,128,1024]{2,1,0:T(8,128)(2,1)S(1)}, bf16[2,128,1024]{2,1,0:T(8,128)(2,1)S(1)}, u32[]{:S(2)}, u32[]{:S(2)}) collective-permute-start(bf16[2,128,1024]{2,1,0:T(8,128)(2,1)S(1)} %constant_dynamic-update-slice_fusion.refs_13_.refs_18_.refs_3_), channel_id=1, source_target_pairs={{0,2},{1,5},{2,6},{3,1},{6,10},{7,3},{10,14},{11,7},{14,12},{15,11... | collective-permute-start | bytes 1572872 | tf_op jit(solution)/shard_map/ppermute | solution.py:377
  16.0 9.8 %collective-permute-start.5 = (bf16[2,128,1024]{2,1,0:T(8,128)(2,1)S(1)}, bf16[2,128,1024]{2,1,0:T(8,128)(2,1)S(1)}, u32[]{:S(2)}, u32[]{:S(2)}) collective-permute-start(bf16[2,128,1024]{2,1,0:T(8,128)(2,1)S(1)} %constant_dynamic-update-slice_fusion.refs_13_.refs_18_.refs_3_), channel_id=1, source_target_pairs={{0,1},{1,0},{2,3},{3,2},{4,5},{5,4},{6,7},{7,6},{8,9},{9,8},{10,11... | collective-permute-start | bytes 1572872 | tf_op jit(solution)/shard_map/ppermute | solution.py:380
  16.0 9.2 %copy-start = (f32[1,128,1024]{2,1,0:T(8,128)S(1)}, f32[1,128,1024]{2,1,0:T(8,128)}, u32[]{:S(2)}) copy-start(f32[1,128,1024]{2,1,0:T(8,128)} %param.8) | copy-start | bytes 1572868
  16.0 9.2 %copy-start.1 = (f32[128,128]{1,0:T(8,128)S(1)}, f32[128,128]{1,0:T(8,128)}, u32[]{:S(2)}) copy-start(f32[128,128]{1,0:T(8,128)} %constant.13.clone.cheb_ref) | copy-start | bytes 196612
  16.0 9.2 %copy-start.2 = (f32[16,1024]{1,0:T(8,128)S(1)}, f32[16,1024]{1,0:T(8,128)}, u32[]{:S(2)}) copy-start(f32[16,1024]{1,0:T(8,128)} %pert_ref.1) | copy-start | bytes 196612
  23.3 9.2 %collective-permute-start.4 = (bf16[2,128,1024]{2,1,0:T(8,128)(2,1)S(1)}, bf16[2,128,1024]{2,1,0:T(8,128)(2,1)S(1)}, u32[]{:S(2)}, u32[]{:S(2)}) collective-permute-start(bf16[2,128,1024]{2,1,0:T(8,128)(2,1)S(1)} %collective-permute-done.3.refs_20_.refs_3_), channel_id=1, source_target_pairs={{0,2},{1,5},{2,6},{3,1},{6,10},{7,3},{10,14},{11,7},{14,12},{15,11... | collective-permute-start | bytes 1572872 | tf_op jit(solution)/shard_map/ppermute | solution.py:377
  25.2 9.3 %collective-permute-start.7 = (bf16[2,128,1024]{2,1,0:T(8,128)(2,1)S(1)}, bf16[2,128,1024]{2,1,0:T(8,128)(2,1)S(1)}, u32[]{:S(2)}, u32[]{:S(2)}) collective-permute-start(bf16[2,128,1024]{2,1,0:T(8,128)(2,1)S(1)} %collective-permute-done.3.refs_20_.refs_3_), channel_id=1, source_target_pairs={{0,1},{1,0},{2,3},{3,2},{4,5},{5,4},{6,7},{7,6},{8,9},{9,8},{10,11... | collective-permute-start | bytes 1572872 | tf_op jit(solution)/shard_map/ppermute | solution.py:380
  32.5 6.5 %collective-permute-start.9 = (bf16[2,128,1024]{2,1,0:T(8,128)(2,1)S(1)}, bf16[2,128,1024]{2,1,0:T(8,128)(2,1)S(1)}, u32[]{:S(2)}, u32[]{:S(2)}) collective-permute-start(bf16[2,128,1024]{2,1,0:T(8,128)(2,1)S(1)} %collective-permute-done.4.refs_17_.refs_5_.refs_3_), channel_id=1, source_target_pairs={{0,1},{1,0},{2,3},{3,2},{4,5},{5,4},{6,7},{7,6},{8,9},{9,8},{10,11... | collective-permute-start | bytes 1572872 | tf_op jit(solution)/shard_map/ppermute | solution.py:380
  32.5 6.4 %collective-permute-start.6 = (bf16[1,128,1024]{2,1,0:T(8,128)(2,1)S(1)}, bf16[1,128,1024]{2,1,0:T(8,128)(2,1)S(1)}, u32[]{:S(2)}, u32[]{:S(2)}) collective-permute-start(bf16[1,128,1024]{2,1,0:T(8,128)(2,1)S(1)} %slice.16), channel_id=1, source_target_pairs={{0,2},{1,5},{2,6},{3,1},{6,10},{7,3},{10,14},{11,7},{14,12},{15,11... | collective-permute-start | bytes 786440 | tf_op jit(solution)/shard_map/ppermute | solution.py:377
  37.4 3.9 %copy-start.3 = (f32[1024]{0:T(1024)S(1)}, f32[1024]{0:T(1024)}, u32[]{:S(2)}) copy-start(f32[1024]{0:T(1024)} %param.12) | copy-start | bytes 12292
  37.4 3.9 %copy-start.4 = (f32[1024]{0:T(1024)S(1)}, f32[1024]{0:T(1024)}, u32[]{:S(2)}) copy-start(f32[1024]{0:T(1024)} %param.11) | copy-start | bytes 12292
  38.9 2.4 %collective-permute-start.8 = (bf16[1,128,1024]{2,1,0:T(8,128)(2,1)S(1)}, bf16[1,128,1024]{2,1,0:T(8,128)(2,1)S(1)}, u32[]{:S(2)}, u32[]{:S(2)}) collective-permute-start(bf16[1,128,1024]{2,1,0:T(8,128)(2,1)S(1)} %collective-permute-done.6.refs_17_.refs_5_), channel_id=1, source_target_pairs={{0,1},{1,0},{2,3},{3,2},{4,5},{5,4},{6,7},{7,6},{8,9},{9,8},{10,11... | collective-permute-start | bytes 786440 | tf_op jit(solution)/shard_map/ppermute | solution.py:380
  44.7 2.5 %collective-permute-start.10 = (bf16[1,128,1024]{2,1,0:T(8,128)(2,1)S(1)}, bf16[1,128,1024]{2,1,0:T(8,128)(2,1)S(1)}, u32[]{:S(2)}, u32[]{:S(2)}) collective-permute-start(bf16[1,128,1024]{2,1,0:T(8,128)(2,1)S(1)} %get-tuple-element.115), channel_id=1, source_target_pairs={{0,1},{1,0},{2,3},{3,2},{4,5},{5,4},{6,7},{7,6},{8,9},{9,8},{10,11... | collective-permute-start | bytes 786440 | tf_op jit(solution)/shard_map/ppermute | solution.py:380
  47.1 6.8 %collective-permute-start.11 = (bf16[2,128,1024]{2,1,0:T(8,128)(2,1)S(1)}, bf16[2,128,1024]{2,1,0:T(8,128)(2,1)S(1)}, u32[]{:S(2)}, u32[]{:S(2)}) collective-permute-start(bf16[2,128,1024]{2,1,0:T(8,128)(2,1)S(1)} %get-tuple-element.118), channel_id=1, source_target_pairs={{0,1},{1,0},{2,3},{3,2},{4,5},{5,4},{6,7},{7,6},{8,9},{9,8},{10,11... | collective-permute-start | bytes 1572872 | tf_op jit(solution)/shard_map/ppermute | solution.py:380
  47.3 6.6 %collective-permute-start.12 = (bf16[1,128,1024]{2,1,0:T(8,128)(2,1)S(1)}, bf16[1,128,1024]{2,1,0:T(8,128)(2,1)S(1)}, u32[]{:S(2)}, u32[]{:S(2)}) collective-permute-start(bf16[1,128,1024]{2,1,0:T(8,128)(2,1)S(1)} %add_convert_fusion.2), channel_id=1, source_target_pairs={{0,2},{1,5},{2,6},{3,1},{6,10},{7,3},{10,14},{11,7},{14,12},{15,11... | collective-permute-start | bytes 786440 | tf_op jit(solution)/shard_map/ppermute | solution.py:377
  54.3 9.2 %collective-permute-start.13 = (bf16[2,128,1024]{2,1,0:T(8,128)(2,1)S(1)}, bf16[2,128,1024]{2,1,0:T(8,128)(2,1)S(1)}, u32[]{:S(2)}, u32[]{:S(2)}) collective-permute-start(bf16[2,128,1024]{2,1,0:T(8,128)(2,1)S(1)} %pad_maximum_fusion), channel_id=1, source_target_pairs={{0,2},{1,5},{2,6},{3,1},{6,10},{7,3},{10,14},{11,7},{14,12},{15,11... | collective-permute-start | bytes 1572872 | tf_op jit(solution)/shard_map/ppermute | solution.py:377
  56.2 7.3 %collective-permute-start.15 = (bf16[2,128,1024]{2,1,0:T(8,128)(2,1)S(1)}, bf16[2,128,1024]{2,1,0:T(8,128)(2,1)S(1)}, u32[]{:S(2)}, u32[]{:S(2)}) collective-permute-start(bf16[2,128,1024]{2,1,0:T(8,128)(2,1)S(1)} %get-tuple-element.130), channel_id=1, source_target_pairs={{0,1},{1,0},{2,3},{3,2},{4,5},{5,4},{6,7},{7,6},{8,9},{9,8},{10,11... | collective-permute-start | bytes 1572872 | tf_op jit(solution)/shard_map/ppermute | solution.py:380
  63.7 9.2 %collective-permute-start.16 = (bf16[2,128,1024]{2,1,0:T(8,128)(2,1)S(1)}, bf16[2,128,1024]{2,1,0:T(8,128)(2,1)S(1)}, u32[]{:S(2)}, u32[]{:S(2)}) collective-permute-start(bf16[2,128,1024]{2,1,0:T(8,128)(2,1)S(1)} %add_convert_fusion.1), channel_id=1, source_target_pairs={{0,2},{1,5},{2,6},{3,1},{6,10},{7,3},{10,14},{11,7},{14,12},{15,11... | collective-permute-start | bytes 1572872 | tf_op jit(solution)/shard_map/ppermute | solution.py:377
  65.7 7.3 %collective-permute-start.14 = (bf16[2,128,1024]{2,1,0:T(8,128)(2,1)S(1)}, bf16[2,128,1024]{2,1,0:T(8,128)(2,1)S(1)}, u32[]{:S(2)}, u32[]{:S(2)}) collective-permute-start(bf16[2,128,1024]{2,1,0:T(8,128)(2,1)S(1)} %get-tuple-element.128), channel_id=1, source_target_pairs={{0,1},{1,0},{2,3},{3,2},{4,5},{5,4},{6,7},{7,6},{8,9},{9,8},{10,11... | collective-permute-start | bytes 1572872 | tf_op jit(solution)/shard_map/ppermute | solution.py:380
  73.3 9.6 %collective-permute-start.18 = (bf16[1,128,1024]{2,1,0:T(8,128)(2,1)S(1)}, bf16[1,128,1024]{2,1,0:T(8,128)(2,1)S(1)}, u32[]{:S(2)}, u32[]{:S(2)}) collective-permute-start(bf16[1,128,1024]{2,1,0:T(8,128)(2,1)S(1)} %get-tuple-element.149), channel_id=1, source_target_pairs={{0,3},{1,4},{2,7},{3,0},{6,11},{7,2},{10,15},{11,6},{14,13},{15,10... | collective-permute-start | bytes 786440 | tf_op jit(solution)/shard_map/ppermute | solution.py:377
  73.7 9.2 %collective-permute-start.17 = (bf16[1,128,1024]{2,1,0:T(8,128)(2,1)S(1)}, bf16[1,128,1024]{2,1,0:T(8,128)(2,1)S(1)}, u32[]{:S(2)}, u32[]{:S(2)}) collective-permute-start(bf16[1,128,1024]{2,1,0:T(8,128)(2,1)S(1)} %get-tuple-element.150), channel_id=1, source_target_pairs={{0,2},{1,5},{2,6},{3,1},{6,10},{7,3},{10,14},{11,7},{14,12},{15,11... | collective-permute-start | bytes 786440 | tf_op jit(solution)/shard_map/ppermute | solution.py:377
  75.6 7.4 %collective-permute-start.19 = (bf16[1,128,1024]{2,1,0:T(8,128)(2,1)S(1)}, bf16[1,128,1024]{2,1,0:T(8,128)(2,1)S(1)}, u32[]{:S(2)}, u32[]{:S(2)}) collective-permute-start(bf16[1,128,1024]{2,1,0:T(8,128)(2,1)S(1)} %get-tuple-element.143), channel_id=1, source_target_pairs={{0,1},{1,0},{2,3},{3,2},{4,5},{5,4},{6,7},{7,6},{8,9},{9,8},{10,11... | collective-permute-start | bytes 786440 | tf_op jit(solution)/shard_map/ppermute | solution.py:380

commit v10 on v9

--- a/solution.py
+++ b/solution.py
@@ -12,9 +12,8 @@
 VMEM_LIMIT = 8 * 2**20
 BANDS = 16
 GROUP = 4
-LOADS = (10, 6)
-PIECES = (2, 4, 5)
-LONGEST_RING = 16
+LOADS = (8, 6, 2)
+PIECES = (0, 5, 6)
 
 
 def cheb_matrix(count):
@@ -121,7 +120,7 @@
     return mark, bands
 
 
-def pre_kernel(found, count, many, fresh, late, offs_ref, acc_ref, *refs):
+def pre_kernel(found, count, many, fresh, late, ripe, offs_ref, acc_ref, *refs):
     if late:
         w_ref, refs = refs[0], refs[1:]
     bands, refs = refs[:many], refs[many:]
@@ -142,16 +141,22 @@
         out_ref[rows, :] = total
     for copy in copies:
         copy.wait()
-
-
-def add_products(offs, weights, acc, bands, pieces, count, fresh, late):
+    if ripe:
+        rows, total = pl.ds(many * tile, late * tile), None
+        for place, (at, index) in enumerate(found):
+            part = product(others, columns_of(offs_ref, place, slab), xs[at].at[index])
+            total = part if total is None else total + part
+        out_ref[rows, :] = total
+
+
+def add_products(offs, weights, acc, bands, pieces, count, fresh, late, ripe):
     arrays, found = split_pieces(pieces if fresh else pieces[-count:])
     if not fresh:
         found = [(0, 0)] * (len(pieces) - count) + found
     (_, nodes, slab), rows, many = arrays[0].shape, weights.shape[0], len(bands)
     operands = [offs, acc] + ([weights] if late else []) + [*bands, *arrays]
     acc, *others = call(
-        functools.partial(pre_kernel, found, count, many, fresh, late),
+        functools.partial(pre_kernel, found, count, many, fresh, late, ripe),
         [jax.ShapeDtypeStruct((rows, nodes), jnp.float32)] + band_shapes(late, weights),
         [VMEM_REF] * (1 + late),
         [pltpu.SemaphoreType.DMA((max(late, 1),))],
@@ -304,6 +309,7 @@
         copies = grad_w_part(base, offs_ref, delta_t_ref, views, out_ref, held, sems)
     if sent:
         share_part(sent, offs_ref, delta_ref, bands, refs[0])
+    if kept:
         share_part(kept, offs_ref, delta_ref, bands, refs[1])
     for copy in copies:
         copy.wait()
@@ -316,10 +322,9 @@
     tile = rows // 2
     shapes, scratch = [], []
     if sent:
-        shapes = [
-            jax.ShapeDtypeStruct((len(sent), nodes, slab), jnp.bfloat16),
-            jax.ShapeDtypeStruct((len(kept), nodes, slab), jnp.float32),
-        ]
+        shapes.append(jax.ShapeDtypeStruct((len(sent), nodes, slab), jnp.bfloat16))
+    if kept:
+        shapes.append(jax.ShapeDtypeStruct((len(kept), nodes, slab), jnp.float32))
     specs = [VMEM_REF] * len(shapes)
     if found:
         shapes, specs = shapes + [jax.ShapeDtypeStruct(shape, jnp.bfloat16)], specs + [ANY_REF]
@@ -339,7 +344,7 @@
         [SMEM_REF] + [VMEM_REF] * (2 + len(arrays) + len(bands))
         + ([] if first else [ANY_REF]),
     )
-    others, owns = outs[:2] if sent else (None, None)
+    others, owns = outs[0] if sent else None, outs[1] if kept else None
     return others, owns, outs[-1] if found else so_far
 
 
@@ -405,11 +410,12 @@
             x[-step, 1], x[-step, 0] = (other, 0), (other, 1)
         else:
             x[half, 1] = (other, 0)
-        count = 3 if step == half else 4
-        late = LOADS[1] if step == 1 else 0
+        count = 1 if step == half else 6 if step == half - 1 else 4
+        fresh = [LOADS[0], LOADS[1], 0][min(step, 3) - 1]
+        late = [LOADS[1], LOADS[2], 0][min(step, 3) - 1]
         acc, bands = add_products(
             offs, weights, acc, bands, [x[key] for key in listing[: seen + count]], count,
-            LOADS[1] if step == 2 else len(bands) if step == 1 else 0, late,
+            fresh, late, step == 2,
         )
         seen += count
         if step == half - 2:
@@ -425,14 +431,13 @@
 
     grad_w, base = None, 0
 
-    def work(offs, count, step, grad_w, base):
-        if step is None:
-            sent, kept = [], []
-        elif step in (0, half):
-            sent, kept = [sides[step, 1]], [sides[step, 0]]
-        else:
-            sent = [sides[step, 1], sides[step, 0]]
-            kept = [sides[-step, 0], sides[-step, 1]]
+    def sent(step):
+        return [sides[step, 1]] if step in (0, half) else [sides[step, 1], sides[step, 0]]
+
+    def kept(step):
+        return [sides[step, 0]] if step in (0, half) else [sides[-step, 0], sides[-step, 1]]
+
+    def work(offs, count, sent, kept, grad_w, base):
         others, owns, grad_w = sums(
             offs, base, [x[key] for key in listing[base : base + count]], sent, kept,
             delta, delta_t, bands, slab, grad_w, weights.shape,
@@ -443,17 +448,20 @@
         return owns + swap(others).astype(jnp.float32)
 
     counts = list(PIECES)
-    others, owns, _, _ = work(offs, 0, half, None, 0)
+    others, owns, _, _ = work(offs, 0, sent(half), kept(half), None, 0)
     far = joined(others, owns).astype(jnp.bfloat16)
-    others, owns, _, _ = work(offs, 0, half - 1, None, 0)
-    far, offs, owns = gate((far, offs, owns))
-    share = joined(others, owns)
-    flow = passed(far)
+    others, _, _, _ = work(offs, 0, sent(half - 1), [], None, 0)
+    far, offs, others = gate((far, offs, others))
+    ready, flow = swap(others), passed(far)
     for step in range(half - 1, 0, -1):
-        others, owns, grad_w, base = work(offs, counts.pop(0), step - 1, grad_w, base)
+        late = kept(step) if step == half - 1 else []
+        others, owns, grad_w, base = work(
+            offs, counts.pop(0), sent(step - 1), late + kept(step - 1), grad_w, base
+        )
         flow, owns = gate((flow, owns))
         flow = flow.astype(jnp.float32)
-        if step == half - 1:
+        if late:
+            share, owns = owns[:2] + ready.astype(jnp.float32), owns[2:]
             total = jnp.concatenate([share[:1] + flow, share[1:]], axis=0)
         else:
             total = share + flow
@@ -464,7 +472,7 @@
             flow = passed(total)
         else:
             near, over = passed(total[:1]), passed(total[1:], 1, 1)
-    _, _, grad_w, base = work(offs, len(listing) - base, None, grad_w, base)
+    _, _, grad_w, base = work(offs, len(listing) - base, [], [], grad_w, base)
     local = local_terms(cheb, resid, decay)
     near, over, local = gate((near, over, local))
     grad_x = local + share[0] + near[0].astype(jnp.float32) + over[0].astype(jnp.float32)
@@ -526,7 +534,7 @@
     )
 
     def run(states, *others):
-        if states.shape[0] == 1 and chips <= LONGEST_RING:
+        if states.shape[0] == 1 and chips // 2 == len(PIECES) + 1:
             return ring_body(chips, states, *others)
         return plain_body(states, *others)
 

time: 84.1 us -> 81.5 us (0.969)
  waiting for transfers between devices: 8.66 us -> 6.47 us
  starting transfers between devices: 19.4 us -> 17.4 us
  Pallas kernels: 50.5 us -> 52.1 us
    ppermute x10, waiting for transfers between devices: 8.63 us -> 6.19 us  [passed(): return lax.ppermute(array, 'row', pairs)]
    pallas_call x14, Pallas kernels: 50.5 us -> 52.1 us  [run(): pl.pallas_call(kernel, out_shape=out_shape, in_specs=in_specs, out_specs=...]
    ppermute x10, starting transfers between devices: 17 us -> 15.5 us  [passed(): return lax.ppermute(array, 'row', pairs)]
  transfers between devices with their start and end apart: 20 -> 20, of which waited for: 6 -> 6; matrix products, arithmetic and copies ran while one was open for 1% -> 1% of each run, Pallas kernels for 56% -> 60%
where the time goes in v10:
time: 81.5 us; the launch traced here: 81.2 us
  Pallas kernels  52.1 us (64%)
  starting transfers between devices  17.4 us (21%)
  waiting for transfers between devices  6.47 us (8%)
  other arithmetic  2.91 us (4%)
  between operations  1.59 us (2%)
  local copies, waits for them, and re-layouts  0.85 us (1%)
    pallas_call x14, Pallas kernels, run(): pl.pallas_call(kernel, out_shape=out_shape, in_specs=in_specs, out_specs=...  52.1 us
    ppermute x10, starting transfers between devices, passed(): return lax.ppermute(array, 'row', pairs)  15.5 us
    ppermute x10, waiting for transfers between devices, passed(): return lax.ppermute(array, 'row', pairs)  6.19 us
    ppermute x10, starting transfers between devices, swap(): return lax.ppermute(array, 'row', [(i, i ^ 1) for i in range(2 * chips)])  1.83 us
  transfers between devices with their start and end apart: 20, of which 6 were waited for; matrix products, arithmetic and copies ran while one was open for 1% of the time, Pallas kernels for 60%

profile of v10, /device:TPU:0, one launch (start us, length us, event | category | flops | bytes accessed | tf_op | source)
XLA Modules:
  0.0 81.2 jit_solution(10930835110365956311)
XLA Ops:
  0.6 1.1 %convert_element_type.49.refs_9_.refs_15_.refs_3_ = bf16[1,128,1024]{2,1,0:T(8,128)(2,1)S(1)} convert(f32[1,128,1024]{2,1,0:T(8,128)} %param.8) | non-fusion elementwise | flops 131072 | bytes 786432 | tf_op jit(solution)/shard_map/convert_element_type | solution.py:391
  1.7 0.5 collective-permute-start.2
  2.2 2.7 %collective-permute-start.1 = (bf16[1,128,1024]{2,1,0:T(8,128)(2,1)S(1)}, bf16[1,128,1024]{2,1,0:T(8,128)(2,1)S(1)}, u32[]{:S(2)}, u32[]{:S(2)}) collective-permute-start(bf16[1,128,1024]{2,1,0:T(8,128)(2,1)S(1)} %convert_element_type.49.refs_9_.refs_15_.refs_3_), channel_id=1, source_target_pairs={{0,5},{1,2},{2,1},{3,6},{6,3},{7,10},{10,7},{11,14},{14,11},{15,12... | collective-permute-start | bytes 786440 | tf_op jit(solution)/shard_map/ppermute | solution.py:382
  4.9 0.0 collective-permute-start
  5.6 0.7 dynamic-slice_bitcast_fusion.offs_ref.refs_0_
  6.3 6.5 %shard_map.119 = (f32[8,128]{1,0:T(8,128)S(1)}, bf16[64,16384]{1,0:T(8,128)(2,1)S(1)}, bf16[64,16384]{1,0:T(8,128)(2,1)S(1)}, bf16[64,16384]{1,0:T(8,128)(2,1)S(...) custom-call(s32[16]{0:T(128)S(1)} %dynamic-slice_bitcast_fusion.offs, ...), custom_call_target="tpu_custom_call" | custom-call | flops 2097152 | bytes 16384 | tf_op jit(solution)/shard_map/pallas_call | solution.py:57
  12.7 0.0 collective-permute-done.2.refs_10_.refs_16_.refs_4_
  12.8 0.0 collective-permute-done.1
  12.8 0.0 collective-permute-done
  12.8 2.0 %collective-permute-start.3 = (bf16[2,128,1024]{2,1,0:T(8,128)(2,1)S(1)}, bf16[2,128,1024]{2,1,0:T(8,128)(2,1)S(1)}, u32[]{:S(2)}, u32[]{:S(2)}) collective-permute-start(bf16[2,128,1024]{2,1,0:T(8,128)(2,1)S(1)} %constant_dynamic-update-slice_fusion.refs_11_.refs_17_.refs_5_), channel_id=1, source_target_pairs={{0,2},{1,5},{2,6},{3,1},{6,10},{7,3},{10,14},{11,7},{14,12},{15,11... | collective-permute-start | bytes 1572872 | tf_op jit(solution)/shard_map/ppermute | solution.py:382
  14.8 0.0 collective-permute-start.5
  14.8 6.3 %shard_map.120 = (f32[1024,128]{1,0:T(8,128)S(1)}, bf16[64,16384]{1,0:T(8,128)(2,1)S(1)}, bf16[64,16384]{1,0:T(8,128)(2,1)S(1)}, bf16[64,16384]{1,0:T(8,128)(2,1...) custom-call(s32[16]{0:T(128)S(1)} %dynamic-slice_bitcast_fusion.offs_ref.refs_0_,, ...), custom_call_target="tpu_custom_call" | custom-call | flops 67108864 | bytes 524288 | tf_op jit(solution)/shard_map/pallas_call | solution.py:57
  21.2 0.9 %collective-permute-done.3.refs_19_.refs_4_ = bf16[2,128,1024]{2,1,0:T(8,128)(2,1)S(1)} collective-permute-done((bf16[2,128,1024]{2,1,0:T(8,128)(2,1)S(1)}, bf16[2,128,1024]{2,1,0:T(8,128)(2,1)S(1)}, u32[]{:S(2)}, u32[]{:S(2)}) %collective-permute-start.3) | collective-permute-done | bytes 524320 | tf_op jit(solution)/shard_map/ppermute | solution.py:382
  22.1 1.9 %collective-permute-start.4 = (bf16[2,128,1024]{2,1,0:T(8,128)(2,1)S(1)}, bf16[2,128,1024]{2,1,0:T(8,128)(2,1)S(1)}, u32[]{:S(2)}, u32[]{:S(2)}) collective-permute-start(bf16[2,128,1024]{2,1,0:T(8,128)(2,1)S(1)} %collective-permute-done.3.refs_19_.refs_4_), channel_id=1, source_target_pairs={{0,2},{1,5},{2,6},{3,1},{6,10},{7,3},{10,14},{11,7},{14,12},{15,11... | collective-permute-start | bytes 1572872 | tf_op jit(solution)/shard_map/ppermute | solution.py:382
  24.0 0.6 shard_map.122
  24.6 0.1 collective-permute-start.7
  24.7 0.0 collective-permute-done.5.refs_18_.refs_6_.refs_3_
  24.7 7.2 %shard_map.121 = (f32[1024,128]{1,0:T(8,128)S(1)}, bf16[64,16384]{1,0:T(8,128)(2,1)S(1)}, bf16[64,16384]{1,0:T(8,128)(2,1)S(1)}) custom-call(s32[16]{0:T(128)S(1)} %dynamic-slice_bitcast_fusion.offs_ref.refs_0_, f32[1024,128]{1,0:T(8,128)S(1)} %get-tuple-element.90.acc_ref, bf16[1024,16384]{1,0:T(8,128)(2,1)} %refs_0_.3, ...), custom_call_target="tpu_custom_call" | custom-call | flops 67108864 | bytes 524288 | tf_op jit(solution)/shard_map/pallas_call | solution.py:57
  31.9 0.0 collective-permute-done.4.refs_17_.refs_6_.refs_3_
  31.9 0.5 collective-permute-start.8
  32.5 1.6 %collective-permute-start.6 = (bf16[1,128,1024]{2,1,0:T(8,128)(2,1)S(1)}, bf16[1,128,1024]{2,1,0:T(8,128)(2,1)S(1)}, u32[]{:S(2)}, u32[]{:S(2)}) collective-permute-start(bf16[1,128,1024]{2,1,0:T(8,128)(2,1)S(1)} %slice.22), channel_id=1, source_target_pairs={{0,2},{1,5},{2,6},{3,1},{6,10},{7,3},{10,14},{11,7},{14,12},{15,11... | collective-permute-start | bytes 786440 | tf_op jit(solution)/shard_map/ppermute | solution.py:382
  34.1 0.0 collective-permute-done.7.refs_16_.refs_5_
  34.1 0.0 collective-permute-done.8.refs_18_.refs_4_
  34.1 4.0 %shard_map.123.acc_ref = f32[1024,128]{1,0:T(8,128)S(1)} custom-call(s32[16]{0:T(128)S(1)} %dynamic-slice_bitcast_fusion.offs_ref.refs_0_, f32[1024,128]{1,0:T(8,128)S(1)} %get-tuple-element.103.acc_ref, bf16[64,16384]{1,0:T(8,128)(2,1)S(1)} %get-tuple-element.79.refs_1_.refs_0_.refs_3_.refs_7_, ...), custom_call_target="tpu_custom_call" | custom-call | flops 100663296 | bytes 786432 | tf_op jit(solution)/shard_map/pallas_call | solution.py:57
  38.1 0.0 copy-start.3
  38.1 0.0 copy-start.4
  38.1 0.8 collective-permute-done.6.refs_16_.refs_5_
  38.9 0.0 collective-permute-start.9
  38.9 1.3 %shard_map.124.refs_16_ = f32[1024,128]{1,0:T(8,128)S(1)} custom-call(s32[16]{0:T(128)S(1)} %dynamic-slice_bitcast_fusion.offs_ref.refs_0_, f32[1024,128]{1,0:T(8,128)S(1)} %shard_map.123.acc_ref, bf16[64,16384]{1,0:T(8,128)(2,1)S(1)} %get-tuple-element.79.refs_1_.refs_0_.refs_3_.refs_7_, ...), custom_call_target="tpu_custom_call" | custom-call | flops 16777216 | bytes 131072 | tf_op jit(solution)/shard_map/pallas_call | solution.py:57
  40.2 0.3 collective-permute-done.9.x_ref.refs_6_
  40.5 2.1 %shard_map.125 = (f32[128,1024]{1,0:T(8,128)S(1)}, bf16[128,1024]{1,0:T(8,128)(2,1)S(1)}, bf16[1024,128]{1,0:T(8,128)(2,1)S(1)}, f32[16,1024]{1,0:T(8,128)}, f32[1,1024]{1,0:T(1,128)}, /*index=5*/f32[1,1024]{1,0:T(1,128)}) custom-call(s32[16]{0:T(128)S(1)} %dynamic-slice_bitcast_fusion.offs_ref.refs_0_, ...), custom_call_target="tpu_custom_call" | custom-call | flops 33554432 | bytes 262144 | tf_op jit(solution)/shard_map/pallas_call | solution.py:57
  42.5 1.3 %shard_map.126 = (bf16[1,128,1024]{2,1,0:T(8,128)(2,1)S(1)}, f32[1,128,1024]{2,1,0:T(8,128)S(1)}) custom-call(s32[16]{0:T(128)S(1)} %dynamic-slice_bitcast_fusion.offs_ref.refs_0_, bf16[128,1024]{1,0:T(8,128)(2,1)S(1)} %get-tuple-element.111.refs_1_, bf16[1024,128]{1,0:T(8,128)(2,1)S(1)} %get-tuple-element.112.refs_2_, ...), custom_call_target="tpu_custom_call" | custom-call | flops 33554432 | bytes 262144 | tf_op jit(solution)/shard_map/pallas_call | solution.py:57
  43.8 0.4 collective-permute-start.10
  44.2 1.3 %shard_map.127 = bf16[2,128,1024]{2,1,0:T(8,128)(2,1)S(1)} custom-call(s32[16]{0:T(128)S(1)} %dynamic-slice_bitcast_fusion.offs_ref.refs_0_, bf16[128,1024]{1,0:T(8,128)(2,1)S(1)} %get-tuple-element.111.refs_1_, bf16[1024,128]{1,0:T(8,128)(2,1)S(1)} %get-tuple-element.112.refs_2_, bf16[64,16384]{1,0:T(8,128)(2,1)S(1)} %get-tuple-element.79.refs_1_.refs_0_.refs_3_.refs_7_, ...), custom_call_target="tpu_custom_call" | custom-call | flops 33554432 | bytes 262144 | tf_op jit(solution)/shard_map/pallas_call | solution.py:57
  45.5 0.0 collective-permute-done.10
  45.5 0.1 add_convert_fusion.2
  45.5 0.3 collective-permute-start.12
  45.9 1.6 %collective-permute-start.11 = (bf16[1,128,1024]{2,1,0:T(8,128)(2,1)S(1)}, bf16[1,128,1024]{2,1,0:T(8,128)(2,1)S(1)}, u32[]{:S(2)}, u32[]{:S(2)}) collective-permute-start(bf16[1,128,1024]{2,1,0:T(8,128)(2,1)S(1)} %add_convert_fusion.2), channel_id=1, source_target_pairs={{0,2},{1,5},{2,6},{3,1},{6,10},{7,3},{10,14},{11,7},{14,12},{15,11... | collective-permute-start | bytes 786440 | tf_op jit(solution)/shard_map/ppermute | solution.py:382
  47.4 2.4 %shard_map.128 = (bf16[2,128,1024]{2,1,0:T(8,128)(2,1)S(1)}, f32[4,128,1024]{2,1,0:T(8,128)S(1)}) custom-call(s32[16]{0:T(128)S(1)} %dynamic-slice_bitcast_fusion.offs_ref.refs_0_, bf16[128,1024]{1,0:T(8,128)(2,1)S(1)} %get-tuple-element.111.refs_1_, bf16[1024,128]{1,0:T(8,128)(2,1)S(1)} %get-tuple-element.112.refs_2_, ...), custom_call_target="tpu_custom_call" | custom-call | flops 100663296 | bytes 786432 | tf_op jit(solution)/shard_map/pallas_call | solution.py:57
  49.8 2.4 %collective-permute-done.11 = bf16[1,128,1024]{2,1,0:T(8,128)(2,1)S(1)} collective-permute-done((bf16[1,128,1024]{2,1,0:T(8,128)(2,1)S(1)}, bf16[1,128,1024]{2,1,0:T(8,128)(2,1)S(1)}, u32[]{:S(2)}, u32[]{:S(2)}) %collective-permute-start.11) | collective-permute-done | bytes 262176 | tf_op jit(solution)/shard_map/ppermute | solution.py:382
  52.2 0.0 collective-permute-done.12
  52.2 0.2 convert_add_fusion
  52.5 0.1 fusion
  52.5 0.1 pad_maximum_fusion
  52.6 1.6 %collective-permute-start.13 = (bf16[2,128,1024]{2,1,0:T(8,128)(2,1)S(1)}, bf16[2,128,1024]{2,1,0:T(8,128)(2,1)S(1)}, u32[]{:S(2)}, u32[]{:S(2)}) collective-permute-start(bf16[2,128,1024]{2,1,0:T(8,128)(2,1)S(1)} %pad_maximum_fusion), channel_id=1, source_target_pairs={{0,2},{1,5},{2,6},{3,1},{6,10},{7,3},{10,14},{11,7},{14,12},{15,11... | collective-permute-start | bytes 1572872 | tf_op jit(solution)/shard_map/ppermute | solution.py:382
  54.2 0.0 collective-permute-start.15
  54.2 6.4 %shard_map.129 = (bf16[2,128,1024]{2,1,0:T(8,128)(2,1)S(1)}, f32[2,128,1024]{2,1,0:T(8,128)S(1)}, bf16[1024,16384]{1,0:T(8,128)(2,1)}) custom-call(s32[16]{0:T(128)S(1)} %dynamic-slice_bitcast_fusion.offs_ref.refs_0_, bf16[128,1024]{1,0:T(8,128)(2,1)S(1)} %get-tuple-element.111.refs_1_, bf16[1024,128]{1,0:T(8,128)(2,1)S(1)} %get-tuple-element.112.refs_2_, ...), custom_call_target="tpu_custom_call" | custom-call | flops 150994944 | bytes 1179648 | tf_op jit(solution)/shard_map/pallas_call | solution.py:57
  60.7 1.2 %collective-permute-done.13 = bf16[2,128,1024]{2,1,0:T(8,128)(2,1)S(1)} collective-permute-done((bf16[2,128,1024]{2,1,0:T(8,128)(2,1)S(1)}, bf16[2,128,1024]{2,1,0:T(8,128)(2,1)S(1)}, u32[]{:S(2)}, u32[]{:S(2)}) %collective-permute-start.13) | collective-permute-done | bytes 524320 | tf_op jit(solution)/shard_map/ppermute | solution.py:382
  61.8 0.0 collective-permute-done.15
  61.8 0.3 add_convert_fusion.1
  62.1 1.6 %collective-permute-start.16 = (bf16[2,128,1024]{2,1,0:T(8,128)(2,1)S(1)}, bf16[2,128,1024]{2,1,0:T(8,128)(2,1)S(1)}, u32[]{:S(2)}, u32[]{:S(2)}) collective-permute-start(bf16[2,128,1024]{2,1,0:T(8,128)(2,1)S(1)} %add_convert_fusion.1), channel_id=1, source_target_pairs={{0,2},{1,5},{2,6},{3,1},{6,10},{7,3},{10,14},{11,7},{14,12},{15,11... | collective-permute-start | bytes 1572872 | tf_op jit(solution)/shard_map/ppermute | solution.py:382
  63.7 0.0 collective-permute-start.14
  63.7 6.7 %shard_map.130 = (bf16[1,128,1024]{2,1,0:T(8,128)(2,1)S(1)}, f32[1,128,1024]{2,1,0:T(8,128)S(1)}, bf16[1024,16384]{1,0:T(8,128)(2,1)}) custom-call(s32[16]{0:T(128)S(1)} %dynamic-slice_bitcast_fusion.offs_ref.refs_0_, bf16[128,1024]{1,0:T(8,128)(2,1)S(1)} %get-tuple-element.111.refs_1_, ...), custom_call_target="tpu_custom_call", output_to_operand_aliasing={{2}: (23, {})} | custom-call | flops 134217728 | bytes 1048576 | tf_op jit(solution)/shard_map/pallas_call | solution.py:57
  70.4 0.9 %collective-permute-done.16 = bf16[2,128,1024]{2,1,0:T(8,128)(2,1)S(1)} collective-permute-done((bf16[2,128,1024]{2,1,0:T(8,128)(2,1)S(1)}, bf16[2,128,1024]{2,1,0:T(8,128)(2,1)S(1)}, u32[]{:S(2)}, u32[]{:S(2)}) %collective-permute-start.16) | collective-permute-done | bytes 524320 | tf_op jit(solution)/shard_map/ppermute | solution.py:382
  71.3 0.0 collective-permute-done.14
  71.3 0.3 add_convert_fusion
  71.6 0.9 %collective-permute-start.18 = (bf16[1,128,1024]{2,1,0:T(8,128)(2,1)S(1)}, bf16[1,128,1024]{2,1,0:T(8,128)(2,1)S(1)}, u32[]{:S(2)}, u32[]{:S(2)}) collective-permute-start(bf16[1,128,1024]{2,1,0:T(8,128)(2,1)S(1)} %get-tuple-element.145), channel_id=1, source_target_pairs={{0,3},{1,4},{2,7},{3,0},{6,11},{7,2},{10,15},{11,6},{14,13},{15,10... | collective-permute-start | bytes 786440 | tf_op jit(solution)/shard_map/ppermute | solution.py:382
  72.5 1.6 %collective-permute-start.17 = (bf16[1,128,1024]{2,1,0:T(8,128)(2,1)S(1)}, bf16[1,128,1024]{2,1,0:T(8,128)(2,1)S(1)}, u32[]{:S(2)}, u32[]{:S(2)}) collective-permute-start(bf16[1,128,1024]{2,1,0:T(8,128)(2,1)S(1)} %get-tuple-element.146), channel_id=1, source_target_pairs={{0,2},{1,5},{2,6},{3,1},{6,10},{7,3},{10,14},{11,7},{14,12},{15,11... | collective-permute-start | bytes 786440 | tf_op jit(solution)/shard_map/ppermute | solution.py:382
  74.1 0.0 collective-permute-start.19
  74.1 0.6 shard_map.132
  74.7 5.5 %shard_map.131 = bf16[1024,16384]{1,0:T(8,128)(2,1)} custom-call(s32[16]{0:T(128)S(1)} %dynamic-slice_bitcast_fusion.offs_ref.refs_0_, bf16[128,1024]{1,0:T(8,128)(2,1)S(1)} %get-tuple-element.111.refs_1_, bf16[1024,128]{1,0:T(8,128)(2,1)S(1)} %get-tuple-element.112.refs_2_, ...), custom_call_target="tpu_custom_call", output_to_operand_aliasing={{}: (23, {})} | custom-call | flops 83886080 | bytes 655360 | tf_op jit(solution)/shard_map/pallas_call | solution.py:57
  80.2 0.0 collective-permute-done.18
  80.3 0.0 collective-permute-done.17
  80.3 1.0 %fusion.1 = f32[1,128,1024]{2,1,0:T(8,128)} fusion(f32[128,1024]{1,0:T(8,128)S(1)} %shard_map.132, f32[1,128,1024]{2,1,0:T(8,128)S(1)} %get-tuple-element.138, bf16[1,128,1024]{2,1,0:T(8,128)(2,1)S(1)} %collective-permute-done.19, bf16[1,128,1024]{2,1,0:T(8,128)(2,1)S(1)} %collective-permute-done.18, bf16[1,128,1024]{2,1,0:T(8,128)(2,1)S(1)} %collective-permute-done.17), kind=kLoop, calls=%fused_computation.8 | loop fusion | flops 917504 | bytes 2359296 | tf_op jit(solution)/shard_map/reshape | solution.py:479
  (14 shorter events, 0.1 us)
Async XLA Ops:
  1.7 11.0 %collective-permute-start.2 = (bf16[1,128,1024]{2,1,0:T(8,128)(2,1)S(1)}, bf16[1,128,1024]{2,1,0:T(8,128)(2,1)S(1)}, u32[]{:S(2)}, u32[]{:S(2)}) collective-permute-start(bf16[1,128,1024]{2,1,0:T(8,128)(2,1)S(1)} %convert_element_type.49.refs_9_.refs_15_.refs_3_), channel_id=1, source_target_pairs={{0,1},{1,0},{2,3},{3,2},{4,5},{5,4},{6,7},{7,6},{8,9},{9,8},{10,11... | collective-permute-start | bytes 786440 | tf_op jit(solution)/shard_map/ppermute | solution.py:385
  2.2 10.5 %collective-permute-start.1 = (bf16[1,128,1024]{2,1,0:T(8,128)(2,1)S(1)}, bf16[1,128,1024]{2,1,0:T(8,128)(2,1)S(1)}, u32[]{:S(2)}, u32[]{:S(2)}) collective-permute-start(bf16[1,128,1024]{2,1,0:T(8,128)(2,1)S(1)} %convert_element_type.49.refs_9_.refs_15_.refs_3_), channel_id=1, source_target_pairs={{0,5},{1,2},{2,1},{3,6},{6,3},{7,10},{10,7},{11,14},{14,11},{15,12... | collective-permute-start | bytes 786440 | tf_op jit(solution)/shard_map/ppermute | solution.py:382
  4.9 7.8 %collective-permute-start = (bf16[1,128,1024]{2,1,0:T(8,128)(2,1)S(1)}, bf16[1,128,1024]{2,1,0:T(8,128)(2,1)S(1)}, u32[]{:S(2)}, u32[]{:S(2)}) collective-permute-start(bf16[1,128,1024]{2,1,0:T(8,128)(2,1)S(1)} %convert_element_type.49.refs_9_.refs_15_.refs_3_), channel_id=1, source_target_pairs={{0,2},{1,5},{2,6},{3,1},{6,10},{7,3},{10,14},{11,7},{14,12},{15,11... | collective-permute-start | bytes 786440 | tf_op jit(solution)/shard_map/ppermute | solution.py:382
  12.8 9.2 %collective-permute-start.3 = (bf16[2,128,1024]{2,1,0:T(8,128)(2,1)S(1)}, bf16[2,128,1024]{2,1,0:T(8,128)(2,1)S(1)}, u32[]{:S(2)}, u32[]{:S(2)}) collective-permute-start(bf16[2,128,1024]{2,1,0:T(8,128)(2,1)S(1)} %constant_dynamic-update-slice_fusion.refs_11_.refs_17_.refs_5_), channel_id=1, source_target_pairs={{0,2},{1,5},{2,6},{3,1},{6,10},{7,3},{10,14},{11,7},{14,12},{15,11... | collective-permute-start | bytes 1572872 | tf_op jit(solution)/shard_map/ppermute | solution.py:382
  14.8 9.9 %collective-permute-start.5 = (bf16[2,128,1024]{2,1,0:T(8,128)(2,1)S(1)}, bf16[2,128,1024]{2,1,0:T(8,128)(2,1)S(1)}, u32[]{:S(2)}, u32[]{:S(2)}) collective-permute-start(bf16[2,128,1024]{2,1,0:T(8,128)(2,1)S(1)} %constant_dynamic-update-slice_fusion.refs_11_.refs_17_.refs_5_), channel_id=1, source_target_pairs={{0,1},{1,0},{2,3},{3,2},{4,5},{5,4},{6,7},{7,6},{8,9},{9,8},{10,11... | collective-permute-start | bytes 1572872 | tf_op jit(solution)/shard_map/ppermute | solution.py:385
  14.8 9.2 %copy-start = (f32[1,128,1024]{2,1,0:T(8,128)S(1)}, f32[1,128,1024]{2,1,0:T(8,128)}, u32[]{:S(2)}) copy-start(f32[1,128,1024]{2,1,0:T(8,128)} %param.8) | copy-start | bytes 1572868
  14.8 9.2 %copy-start.1 = (f32[128,128]{1,0:T(8,128)S(1)}, f32[128,128]{1,0:T(8,128)}, u32[]{:S(2)}) copy-start(f32[128,128]{1,0:T(8,128)} %constant.13.clone.cheb_ref) | copy-start | bytes 196612
  14.8 9.2 %copy-start.2 = (f32[16,1024]{1,0:T(8,128)S(1)}, f32[16,1024]{1,0:T(8,128)}, u32[]{:S(2)}) copy-start(f32[16,1024]{1,0:T(8,128)} %pert_ref.1) | copy-start | bytes 196612
  22.1 9.9 %collective-permute-start.4 = (bf16[2,128,1024]{2,1,0:T(8,128)(2,1)S(1)}, bf16[2,128,1024]{2,1,0:T(8,128)(2,1)S(1)}, u32[]{:S(2)}, u32[]{:S(2)}) collective-permute-start(bf16[2,128,1024]{2,1,0:T(8,128)(2,1)S(1)} %collective-permute-done.3.refs_19_.refs_4_), channel_id=1, source_target_pairs={{0,2},{1,5},{2,6},{3,1},{6,10},{7,3},{10,14},{11,7},{14,12},{15,11... | collective-permute-start | bytes 1572872 | tf_op jit(solution)/shard_map/ppermute | solution.py:382
  24.6 9.5 %collective-permute-start.7 = (bf16[2,128,1024]{2,1,0:T(8,128)(2,1)S(1)}, bf16[2,128,1024]{2,1,0:T(8,128)(2,1)S(1)}, u32[]{:S(2)}, u32[]{:S(2)}) collective-permute-start(bf16[2,128,1024]{2,1,0:T(8,128)(2,1)S(1)} %collective-permute-done.3.refs_19_.refs_4_), channel_id=1, source_target_pairs={{0,1},{1,0},{2,3},{3,2},{4,5},{5,4},{6,7},{7,6},{8,9},{9,8},{10,11... | collective-permute-start | bytes 1572872 | tf_op jit(solution)/shard_map/ppermute | solution.py:385
  31.9 2.2 %collective-permute-start.8 = (bf16[2,128,1024]{2,1,0:T(8,128)(2,1)S(1)}, bf16[2,128,1024]{2,1,0:T(8,128)(2,1)S(1)}, u32[]{:S(2)}, u32[]{:S(2)}) collective-permute-start(bf16[2,128,1024]{2,1,0:T(8,128)(2,1)S(1)} %collective-permute-done.4.refs_17_.refs_6_.refs_3_), channel_id=1, source_target_pairs={{0,1},{1,0},{2,3},{3,2},{4,5},{5,4},{6,7},{7,6},{8,9},{9,8},{10,11... | collective-permute-start | bytes 1572872 | tf_op jit(solution)/shard_map/ppermute | solution.py:385
  32.5 6.4 %collective-permute-start.6 = (bf16[1,128,1024]{2,1,0:T(8,128)(2,1)S(1)}, bf16[1,128,1024]{2,1,0:T(8,128)(2,1)S(1)}, u32[]{:S(2)}, u32[]{:S(2)}) collective-permute-start(bf16[1,128,1024]{2,1,0:T(8,128)(2,1)S(1)} %slice.22), channel_id=1, source_target_pairs={{0,2},{1,5},{2,6},{3,1},{6,10},{7,3},{10,14},{11,7},{14,12},{15,11... | collective-permute-start | bytes 786440 | tf_op jit(solution)/shard_map/ppermute | solution.py:382
  38.1 2.4 %copy-start.3 = (f32[1024]{0:T(1024)S(1)}, f32[1024]{0:T(1024)}, u32[]{:S(2)}) copy-start(f32[1024]{0:T(1024)} %param.12) | copy-start | bytes 12292
  38.1 2.4 %copy-start.4 = (f32[1024]{0:T(1024)S(1)}, f32[1024]{0:T(1024)}, u32[]{:S(2)}) copy-start(f32[1024]{0:T(1024)} %param.11) | copy-start | bytes 12292
  38.9 1.5 %collective-permute-start.9 = (bf16[1,128,1024]{2,1,0:T(8,128)(2,1)S(1)}, bf16[1,128,1024]{2,1,0:T(8,128)(2,1)S(1)}, u32[]{:S(2)}, u32[]{:S(2)}) collective-permute-start(bf16[1,128,1024]{2,1,0:T(8,128)(2,1)S(1)} %collective-permute-done.6.refs_16_.refs_5_), channel_id=1, source_target_pairs={{0,1},{1,0},{2,3},{3,2},{4,5},{5,4},{6,7},{7,6},{8,9},{9,8},{10,11... | collective-permute-start | bytes 786440 | tf_op jit(solution)/shard_map/ppermute | solution.py:385
  43.8 1.7 %collective-permute-start.10 = (bf16[1,128,1024]{2,1,0:T(8,128)(2,1)S(1)}, bf16[1,128,1024]{2,1,0:T(8,128)(2,1)S(1)}, u32[]{:S(2)}, u32[]{:S(2)}) collective-permute-start(bf16[1,128,1024]{2,1,0:T(8,128)(2,1)S(1)} %get-tuple-element.114), channel_id=1, source_target_pairs={{0,1},{1,0},{2,3},{3,2},{4,5},{5,4},{6,7},{7,6},{8,9},{9,8},{10,11... | collective-permute-start | bytes 786440 | tf_op jit(solution)/shard_map/ppermute | solution.py:385
  45.5 6.7 %collective-permute-start.12 = (bf16[2,128,1024]{2,1,0:T(8,128)(2,1)S(1)}, bf16[2,128,1024]{2,1,0:T(8,128)(2,1)S(1)}, u32[]{:S(2)}, u32[]{:S(2)}) collective-permute-start(bf16[2,128,1024]{2,1,0:T(8,128)(2,1)S(1)} %shard_map.127), channel_id=1, source_target_pairs={{0,1},{1,0},{2,3},{3,2},{4,5},{5,4},{6,7},{7,6},{8,9},{9,8},{10,11... | collective-permute-start | bytes 1572872 | tf_op jit(solution)/shard_map/ppermute | solution.py:385
  45.9 6.4 %collective-permute-start.11 = (bf16[1,128,1024]{2,1,0:T(8,128)(2,1)S(1)}, bf16[1,128,1024]{2,1,0:T(8,128)(2,1)S(1)}, u32[]{:S(2)}, u32[]{:S(2)}) collective-permute-start(bf16[1,128,1024]{2,1,0:T(8,128)(2,1)S(1)} %add_convert_fusion.2), channel_id=1, source_target_pairs={{0,2},{1,5},{2,6},{3,1},{6,10},{7,3},{10,14},{11,7},{14,12},{15,11... | collective-permute-start | bytes 786440 | tf_op jit(solution)/shard_map/ppermute | solution.py:382
  52.6 9.2 %collective-permute-start.13 = (bf16[2,128,1024]{2,1,0:T(8,128)(2,1)S(1)}, bf16[2,128,1024]{2,1,0:T(8,128)(2,1)S(1)}, u32[]{:S(2)}, u32[]{:S(2)}) collective-permute-start(bf16[2,128,1024]{2,1,0:T(8,128)(2,1)S(1)} %pad_maximum_fusion), channel_id=1, source_target_pairs={{0,2},{1,5},{2,6},{3,1},{6,10},{7,3},{10,14},{11,7},{14,12},{15,11... | collective-permute-start | bytes 1572872 | tf_op jit(solution)/shard_map/ppermute | solution.py:382
  54.2 7.6 %collective-permute-start.15 = (bf16[2,128,1024]{2,1,0:T(8,128)(2,1)S(1)}, bf16[2,128,1024]{2,1,0:T(8,128)(2,1)S(1)}, u32[]{:S(2)}, u32[]{:S(2)}) collective-permute-start(bf16[2,128,1024]{2,1,0:T(8,128)(2,1)S(1)} %get-tuple-element.126), channel_id=1, source_target_pairs={{0,1},{1,0},{2,3},{3,2},{4,5},{5,4},{6,7},{7,6},{8,9},{9,8},{10,11... | collective-permute-start | bytes 1572872 | tf_op jit(solution)/shard_map/ppermute | solution.py:385
  62.1 9.2 %collective-permute-start.16 = (bf16[2,128,1024]{2,1,0:T(8,128)(2,1)S(1)}, bf16[2,128,1024]{2,1,0:T(8,128)(2,1)S(1)}, u32[]{:S(2)}, u32[]{:S(2)}) collective-permute-start(bf16[2,128,1024]{2,1,0:T(8,128)(2,1)S(1)} %add_convert_fusion.1), channel_id=1, source_target_pairs={{0,2},{1,5},{2,6},{3,1},{6,10},{7,3},{10,14},{11,7},{14,12},{15,11... | collective-permute-start | bytes 1572872 | tf_op jit(solution)/shard_map/ppermute | solution.py:382
  63.7 7.6 %collective-permute-start.14 = (bf16[2,128,1024]{2,1,0:T(8,128)(2,1)S(1)}, bf16[2,128,1024]{2,1,0:T(8,128)(2,1)S(1)}, u32[]{:S(2)}, u32[]{:S(2)}) collective-permute-start(bf16[2,128,1024]{2,1,0:T(8,128)(2,1)S(1)} %get-tuple-element.125), channel_id=1, source_target_pairs={{0,1},{1,0},{2,3},{3,2},{4,5},{5,4},{6,7},{7,6},{8,9},{9,8},{10,11... | collective-permute-start | bytes 1572872 | tf_op jit(solution)/shard_map/ppermute | solution.py:385
  71.6 8.6 %collective-permute-start.18 = (bf16[1,128,1024]{2,1,0:T(8,128)(2,1)S(1)}, bf16[1,128,1024]{2,1,0:T(8,128)(2,1)S(1)}, u32[]{:S(2)}, u32[]{:S(2)}) collective-permute-start(bf16[1,128,1024]{2,1,0:T(8,128)(2,1)S(1)} %get-tuple-element.145), channel_id=1, source_target_pairs={{0,3},{1,4},{2,7},{3,0},{6,11},{7,2},{10,15},{11,6},{14,13},{15,10... | collective-permute-start | bytes 786440 | tf_op jit(solution)/shard_map/ppermute | solution.py:382
  72.5 7.7 %collective-permute-start.17 = (bf16[1,128,1024]{2,1,0:T(8,128)(2,1)S(1)}, bf16[1,128,1024]{2,1,0:T(8,128)(2,1)S(1)}, u32[]{:S(2)}, u32[]{:S(2)}) collective-permute-start(bf16[1,128,1024]{2,1,0:T(8,128)(2,1)S(1)} %get-tuple-element.146), channel_id=1, source_target_pairs={{0,2},{1,5},{2,6},{3,1},{6,10},{7,3},{10,14},{11,7},{14,12},{15,11... | collective-permute-start | bytes 786440 | tf_op jit(solution)/shard_map/ppermute | solution.py:382
  74.1 6.2 %collective-permute-start.19 = (bf16[1,128,1024]{2,1,0:T(8,128)(2,1)S(1)}, bf16[1,128,1024]{2,1,0:T(8,128)(2,1)S(1)}, u32[]{:S(2)}, u32[]{:S(2)}) collective-permute-start(bf16[1,128,1024]{2,1,0:T(8,128)(2,1)S(1)} %get-tuple-element.139), channel_id=1, source_target_pairs={{0,1},{1,0},{2,3},{3,2},{4,5},{5,4},{6,7},{7,6},{8,9},{9,8},{10,11... | collective-permute-start | bytes 786440 | tf_op jit(solution)/shard_map/ppermute | solution.py:385

commit v11 on v10

--- a/solution.py
+++ b/solution.py
@@ -12,8 +12,8 @@
 VMEM_LIMIT = 8 * 2**20
 BANDS = 16
 GROUP = 4
-LOADS = (8, 6, 2)
-PIECES = (0, 5, 6)
+LOADS = (7, 6, 3)
+PIECES = (2, 5, 6)
 
 
 def cheb_matrix(count):
@@ -129,9 +129,10 @@
     slab = xs[0].shape[-1]
     tile = out_ref.shape[0] // BANDS
     copies = load_bands(w_ref, others, sems, many) if late else []
-    for low in [*range(0, many - fresh, GROUP), *range(many - fresh, many, GROUP)]:
+    rest = fresh % GROUP if ripe else 0
+    for low in [*range(0, many - fresh, GROUP), *range(many - fresh, many - rest, GROUP)]:
         old = low < many - fresh
-        group = bands[low : min(low + GROUP, many - fresh if old else many)]
+        group = bands[low : min(low + GROUP, many - fresh if old else many - rest)]
         rows = pl.ds(low * tile, len(group) * tile)
         total = acc_ref[rows, :] if old else None
         for place in range(len(found) - count if old else 0, len(found)):
@@ -142,11 +143,11 @@
     for copy in copies:
         copy.wait()
     if ripe:
-        rows, total = pl.ds(many * tile, late * tile), None
+        group, total = [*bands[many - rest :], *others], None
         for place, (at, index) in enumerate(found):
-            part = product(others, columns_of(offs_ref, place, slab), xs[at].at[index])
+            part = product(group, columns_of(offs_ref, place, slab), xs[at].at[index])
             total = part if total is None else total + part
-        out_ref[rows, :] = total
+        out_ref[pl.ds((many - rest) * tile, len(group) * tile), :] = total
 
 
 def add_products(offs, weights, acc, bands, pieces, count, fresh, late, ripe):
@@ -212,10 +213,10 @@
     )([cheb, resid, decay], [VMEM_REF] * 3)
 
 
-def middle_kernel(base, many, offs_ref, x_ref, *refs):
+def middle_kernel(base, sent, many, offs_ref, x_ref, *refs):
     bands = refs[:many]
-    acc_ref, deriv_ref, drive_ref, chosen_ref, states_ref, eps_ref, decay_ref = refs[many:-6]
-    resid_ref, delta_ref, delta_t_ref, table_ref, sum_eps_ref, sum_decay_ref = refs[-6:]
+    acc_ref, deriv_ref, drive_ref, chosen_ref, states_ref, eps_ref, decay_ref = refs[many:-7]
+    resid_ref, delta_ref, delta_t_ref, table_ref, sum_eps_ref, sum_decay_ref = refs[-7:-1]
     tile = GROUP * bands[0].shape[0]
     here = columns_of(offs_ref, base, x_ref.shape[-1])
     for at in range(many // GROUP):
@@ -233,14 +234,15 @@
         table_ref[:, band] = chosen_ref[:, band] * jnp.sum(wide, axis=0, keepdims=True)
         sum_eps_ref[:, band] = -jnp.sum(act * resid, axis=0, keepdims=True)
         sum_decay_ref[:, band] = jnp.sum(states * resid, axis=0, keepdims=True)
-
-
-def middle(offs, base, x, bands, acc, derivs, states, eps, decay):
+    share_part(sent, offs_ref, delta_ref, bands, refs[-1])
+
+
+def middle(offs, base, sent, x, bands, acc, derivs, states, eps, decay):
     _, nodes, slab = x.shape
     rows = acc.shape[0]
     wide = functools.partial(jax.ShapeDtypeStruct, dtype=jnp.float32)
     return call(
-        functools.partial(middle_kernel, base, len(bands)),
+        functools.partial(middle_kernel, base, sent, len(bands)),
         [
             wide((nodes, rows)),
             jax.ShapeDtypeStruct((nodes, rows), jnp.bfloat16),
@@ -248,8 +250,9 @@
             wide(derivs[2].shape),
             wide((1, rows)),
             wide((1, rows)),
+            jax.ShapeDtypeStruct((len(sent), nodes, slab), jnp.bfloat16),
         ],
-        [VMEM_REF] * 6,
+        [VMEM_REF] * 7,
         [],
         cost(2, nodes, slab, rows),
     )(
@@ -425,8 +428,9 @@
             flow, acc = gate((flow, acc))
 
     decay = decay.reshape(1, rows)
-    resid, delta, delta_t, grad_table, grad_eps, grad_decay = middle(
-        offs, seen, x[half, 1][0], bands, acc, derivs, flat, eps_gain.reshape(1, rows), decay
+    resid, delta, delta_t, grad_table, grad_eps, grad_decay, others = middle(
+        offs, seen, [sides[half, 1]], x[half, 1][0], bands, acc, derivs, flat,
+        eps_gain.reshape(1, rows), decay,
     )
 
     grad_w, base = None, 0
@@ -448,9 +452,10 @@
         return owns + swap(others).astype(jnp.float32)
 
     counts = list(PIECES)
-    others, owns, _, _ = work(offs, 0, sent(half), kept(half), None, 0)
-    far = joined(others, owns).astype(jnp.bfloat16)
-    others, _, _, _ = work(offs, 0, sent(half - 1), [], None, 0)
+    others, offs = gate((others, offs))
+    far = swap(others)
+    others, owns, _, _ = work(offs, 0, sent(half - 1), kept(half), None, 0)
+    far = (owns + far.astype(jnp.float32)).astype(jnp.bfloat16)
     far, offs, others = gate((far, offs, others))
     ready, flow = swap(others), passed(far)
     for step in range(half - 1, 0, -1):
@@ -458,6 +463,9 @@
         others, owns, grad_w, base = work(
             offs, counts.pop(0), sent(step - 1), late + kept(step - 1), grad_w, base
         )
+        if late:
+            local = local_terms(cheb, resid, decay)
+            owns, local = gate((owns, local))
         flow, owns = gate((flow, owns))
         flow = flow.astype(jnp.float32)
         if late:
@@ -473,8 +481,6 @@
         else:
             near, over = passed(total[:1]), passed(total[1:], 1, 1)
     _, _, grad_w, base = work(offs, len(listing) - base, [], [], grad_w, base)
-    local = local_terms(cheb, resid, decay)
-    near, over, local = gate((near, over, local))
     grad_x = local + share[0] + near[0].astype(jnp.float32) + over[0].astype(jnp.float32)
     grad_x = grad_x.reshape(states.shape)
     return (grad_w, grad_x, grad_table, grad_eps.reshape(rows), grad_decay.reshape(rows))

time: 81.5 us -> 82.1 us (level)
    pallas_call x14 -> x13, Pallas kernels: 52.1 us -> 52.6 us  [run(): pl.pallas_call(kernel, out_shape=out_shape, in_specs=in_specs, out_specs=...]
  transfers between devices with their start and end apart: 20 -> 20, of which waited for: 6 -> 7; matrix products, arithmetic and copies ran while one was open for 1% -> 1% of each run, Pallas kernels for 60% -> 62%
where the time goes in v11:
time: 82.1 us; the launch traced here: 81.6 us
  Pallas kernels  52.6 us (64%)
  starting transfers between devices  17.3 us (21%)
  waiting for transfers between devices  6.4 us (8%)
  other arithmetic  2.9 us (4%)
  between operations  1.58 us (2%)
  local copies, waits for them, and re-layouts  0.85 us (1%)
    pallas_call x13, Pallas kernels, run(): pl.pallas_call(kernel, out_shape=out_shape, in_specs=in_specs, out_specs=...  52.6 us
    ppermute x10, starting transfers between devices, passed(): return lax.ppermute(array, 'row', pairs)  15 us
    ppermute x10, waiting for transfers between devices, passed(): return lax.ppermute(array, 'row', pairs)  6.11 us
    ppermute x10, starting transfers between devices, swap(): return lax.ppermute(array, 'row', [(i, i ^ 1) for i in range(2 * chips)])  2.29 us
  transfers between devices with their start and end apart: 20, of which 7 were waited for; matrix products, arithmetic and copies ran while one was open for 1% of the time, Pallas kernels for 62%

profile of v11, /device:TPU:0, one launch (start us, length us, event | category | flops | bytes accessed | tf_op | source)
XLA Modules:
  0.0 81.6 jit_solution(17217054961580768888)
XLA Ops:
  0.6 1.1 %convert_element_type.49.refs_8_.refs_14_.refs_3_ = bf16[1,128,1024]{2,1,0:T(8,128)(2,1)S(1)} convert(f32[1,128,1024]{2,1,0:T(8,128)} %param.8) | non-fusion elementwise | flops 131072 | bytes 786432 | tf_op jit(solution)/shard_map/convert_element_type | solution.py:394
  1.7 0.5 collective-permute-start.2
  2.2 2.7 %collective-permute-start.1 = (bf16[1,128,1024]{2,1,0:T(8,128)(2,1)S(1)}, bf16[1,128,1024]{2,1,0:T(8,128)(2,1)S(1)}, u32[]{:S(2)}, u32[]{:S(2)}) collective-permute-start(bf16[1,128,1024]{2,1,0:T(8,128)(2,1)S(1)} %convert_element_type.49.refs_8_.refs_14_.refs_3_), channel_id=1, source_target_pairs={{0,5},{1,2},{2,1},{3,6},{6,3},{7,10},{10,7},{11,14},{14,11},{15,12... | collective-permute-start | bytes 786440 | tf_op jit(solution)/shard_map/ppermute | solution.py:385
  4.9 0.0 collective-permute-start
  5.6 0.7 dynamic-slice_bitcast_fusion.offs_ref.refs_0_
  6.3 5.9 %shard_map.119 = (f32[8,128]{1,0:T(8,128)S(1)}, bf16[64,16384]{1,0:T(8,128)(2,1)S(1)}, bf16[64,16384]{1,0:T(8,128)(2,1)S(1)}, bf16[64,16384]{1,0:T(8,128)(2,1)S(...) custom-call(s32[16]{0:T(128)S(1)} %dynamic-slice_bitcast_fusion.offs, ...), custom_call_target="tpu_custom_call" | custom-call | flops 2097152 | bytes 16384 | tf_op jit(solution)/shard_map/pallas_call | solution.py:57
  12.1 0.0 collective-permute-done.2.refs_9_.refs_15_.refs_4_
  12.1 0.0 collective-permute-done.1
  12.2 0.0 collective-permute-done
  12.2 2.0 %collective-permute-start.3 = (bf16[2,128,1024]{2,1,0:T(8,128)(2,1)S(1)}, bf16[2,128,1024]{2,1,0:T(8,128)(2,1)S(1)}, u32[]{:S(2)}, u32[]{:S(2)}) collective-permute-start(bf16[2,128,1024]{2,1,0:T(8,128)(2,1)S(1)} %constant_dynamic-update-slice_fusion.refs_10_.refs_16_.refs_3_), channel_id=1, source_target_pairs={{0,2},{1,5},{2,6},{3,1},{6,10},{7,3},{10,14},{11,7},{14,12},{15,11... | collective-permute-start | bytes 1572872 | tf_op jit(solution)/shard_map/ppermute | solution.py:385
  14.2 0.0 collective-permute-start.5
  14.2 6.2 %shard_map.120 = (f32[1024,128]{1,0:T(8,128)S(1)}, bf16[64,16384]{1,0:T(8,128)(2,1)S(1)}, bf16[64,16384]{1,0:T(8,128)(2,1)S(1)}, bf16[64,16384]{1,0:T(8,128)(2,1...) custom-call(s32[16]{0:T(128)S(1)} %dynamic-slice_bitcast_fusion.offs_ref.refs_0_,, ...), custom_call_target="tpu_custom_call" | custom-call | flops 67108864 | bytes 524288 | tf_op jit(solution)/shard_map/pallas_call | solution.py:57
  20.5 1.0 %collective-permute-done.3.refs_18_.refs_5_.refs_3_ = bf16[2,128,1024]{2,1,0:T(8,128)(2,1)S(1)} collective-permute-done((bf16[2,128,1024]{2,1,0:T(8,128)(2,1)S(1)}, bf16[2,128,1024]{2,1,0:T(8,128)(2,1)S(1)}, u32[]{:S(2)}, u32[]{:S(2)}) %collective-permute-start.3) | collective-permute-done | bytes 524320 | tf_op jit(solution)/shard_map/ppermute | solution.py:385
  21.5 1.9 %collective-permute-start.4 = (bf16[2,128,1024]{2,1,0:T(8,128)(2,1)S(1)}, bf16[2,128,1024]{2,1,0:T(8,128)(2,1)S(1)}, u32[]{:S(2)}, u32[]{:S(2)}) collective-permute-start(bf16[2,128,1024]{2,1,0:T(8,128)(2,1)S(1)} %collective-permute-done.3.refs_18_.refs_5_.refs_3_), channel_id=1, source_target_pairs={{0,2},{1,5},{2,6},{3,1},{6,10},{7,3},{10,14},{11,7},{14,12},{15,11... | collective-permute-start | bytes 1572872 | tf_op jit(solution)/shard_map/ppermute | solution.py:385
  23.4 0.6 shard_map.122
  24.0 0.1 collective-permute-start.7
  24.1 0.0 collective-permute-done.5.refs_17_.refs_4_
  24.1 9.0 %shard_map.121 = (f32[1024,128]{1,0:T(8,128)S(1)}, bf16[64,16384]{1,0:T(8,128)(2,1)S(1)}, bf16[64,16384]{1,0:T(8,128)(2,1)S(1)}, bf16[64,16384]{1,0:T(8,128)(2,1)S(1)}) custom-call(s32[16]{0:T(128)S(1)} %dynamic-slice_bitcast_fusion.offs_ref.refs_0_, f32[1024,128]{1,0:T(8,128)S(1)} %get-tuple-element.92.acc_ref, bf16[1024,16384]{1,0:T(8,128)(2,1)} %refs_0_.3, ...), custom_call_target="tpu_custom_call" | custom-call | flops 67108864 | bytes 524288 | tf_op jit(solution)/shard_map/pallas_call | solution.py:57
  33.0 0.0 collective-permute-done.4.refs_17_.refs_5_
  33.0 0.5 collective-permute-start.8
  33.6 1.6 %collective-permute-start.6 = (bf16[1,128,1024]{2,1,0:T(8,128)(2,1)S(1)}, bf16[1,128,1024]{2,1,0:T(8,128)(2,1)S(1)}, u32[]{:S(2)}, u32[]{:S(2)}) collective-permute-start(bf16[1,128,1024]{2,1,0:T(8,128)(2,1)S(1)} %slice.22), channel_id=1, source_target_pairs={{0,2},{1,5},{2,6},{3,1},{6,10},{7,3},{10,14},{11,7},{14,12},{15,11... | collective-permute-start | bytes 786440 | tf_op jit(solution)/shard_map/ppermute | solution.py:385
  35.2 0.0 collective-permute-done.7.refs_16_.refs_4_
  35.2 0.0 collective-permute-done.8.refs_18_.refs_6_.refs_3_
  35.2 4.0 %shard_map.123.acc_ref = f32[1024,128]{1,0:T(8,128)S(1)} custom-call(s32[16]{0:T(128)S(1)} %dynamic-slice_bitcast_fusion.offs_ref.refs_0_, f32[1024,128]{1,0:T(8,128)S(1)} %get-tuple-element.105.acc_ref, bf16[64,16384]{1,0:T(8,128)(2,1)S(1)} %get-tuple-element.82.refs_1_.refs_0_.refs_3_.refs_5_.refs_6_.refs_7_, ...), custom_call_target="tpu_custom_call" | custom-call | flops 100663296 | bytes 786432 | tf_op jit(solution)/shard_map/pallas_call | solution.py:57
  39.2 0.0 copy-start.3
  39.2 0.0 copy-start.4
  39.2 0.8 collective-permute-done.6.refs_16_.refs_4_
  40.0 0.0 collective-permute-start.9
  40.0 1.3 %shard_map.124.refs_16_ = f32[1024,128]{1,0:T(8,128)S(1)} custom-call(s32[16]{0:T(128)S(1)} %dynamic-slice_bitcast_fusion.offs_ref.refs_0_, f32[1024,128]{1,0:T(8,128)S(1)} %shard_map.123.acc_ref, bf16[64,16384]{1,0:T(8,128)(2,1)S(1)} %get-tuple-element.82.refs_1_.refs_0_.refs_3_.refs_5_.refs_6_.refs_7_, ...), custom_call_target="tpu_custom_call" | custom-call | flops 16777216 | bytes 131072 | tf_op jit(solution)/shard_map/pallas_call | solution.py:57
  41.3 0.3 collective-permute-done.9.x_ref.refs_5_
  41.6 2.3 %shard_map.125 = (f32[128,1024]{1,0:T(8,128)S(1)}, bf16[128,1024]{1,0:T(8,128)(2,1)S(1)}, bf16[1024,128]{1,0:T(8,128)(2,1)S(1)}, f32[16,1024]{1,0:T(8,128)}, f32...) custom-call(s32[16]{0:T(128)S(1)} %dynamic-slice_bitcast_fusion.offs_ref.refs_0_, ...), custom_call_target="tpu_custom_call" | custom-call | flops 33554432 | bytes 262144 | tf_op jit(solution)/shard_map/pallas_call | solution.py:57
  43.8 0.3 collective-permute-start.10
  44.2 1.6 %shard_map.126 = (bf16[2,128,1024]{2,1,0:T(8,128)(2,1)S(1)}, f32[1,128,1024]{2,1,0:T(8,128)S(1)}) custom-call(s32[16]{0:T(128)S(1)} %dynamic-slice_bitcast_fusion.offs_ref.refs_0_, bf16[128,1024]{1,0:T(8,128)(2,1)S(1)} %get-tuple-element.116.refs_1_, bf16[1024,128]{1,0:T(8,128)(2,1)S(1)} %get-tuple-element.117.refs_2_, ...), custom_call_target="tpu_custom_call" | custom-call | flops 50331648 | bytes 393216 | tf_op jit(solution)/shard_map/pallas_call | solution.py:57
  45.7 0.0 collective-permute-done.10
  45.7 0.1 add_convert_fusion.2
  45.8 0.3 collective-permute-start.12
  46.0 1.6 %collective-permute-start.11 = (bf16[1,128,1024]{2,1,0:T(8,128)(2,1)S(1)}, bf16[1,128,1024]{2,1,0:T(8,128)(2,1)S(1)}, u32[]{:S(2)}, u32[]{:S(2)}) collective-permute-start(bf16[1,128,1024]{2,1,0:T(8,128)(2,1)S(1)} %add_convert_fusion.2), channel_id=1, source_target_pairs={{0,2},{1,5},{2,6},{3,1},{6,10},{7,3},{10,14},{11,7},{14,12},{15,11... | collective-permute-start | bytes 786440 | tf_op jit(solution)/shard_map/ppermute | solution.py:385
  47.7 0.6 shard_map.128
  48.3 4.3 %shard_map.127 = (bf16[2,128,1024]{2,1,0:T(8,128)(2,1)S(1)}, f32[4,128,1024]{2,1,0:T(8,128)S(1)}, bf16[1024,16384]{1,0:T(8,128)(2,1)}) custom-call(s32[16]{0:T(128)S(1)} %dynamic-slice_bitcast_fusion.offs_ref.refs_0_, bf16[128,1024]{1,0:T(8,128)(2,1)S(1)} %get-tuple-element.116.refs_1_, bf16[1024,128]{1,0:T(8,128)(2,1)S(1)} %get-tuple-element.117.refs_2_, ...), custom_call_target="tpu_custom_call" | custom-call | flops 134217728 | bytes 1048576 | tf_op jit(solution)/shard_map/pallas_call | solution.py:57
  52.7 0.0 collective-permute-done.11
  52.7 0.0 collective-permute-done.12
  52.7 0.2 convert_add_fusion
  52.9 0.1 fusion
  53.0 0.1 pad_maximum_fusion
  53.0 1.6 %collective-permute-start.13 = (bf16[2,128,1024]{2,1,0:T(8,128)(2,1)S(1)}, bf16[2,128,1024]{2,1,0:T(8,128)(2,1)S(1)}, u32[]{:S(2)}, u32[]{:S(2)}) collective-permute-start(bf16[2,128,1024]{2,1,0:T(8,128)(2,1)S(1)} %pad_maximum_fusion), channel_id=1, source_target_pairs={{0,2},{1,5},{2,6},{3,1},{6,10},{7,3},{10,14},{11,7},{14,12},{15,11... | collective-permute-start | bytes 1572872 | tf_op jit(solution)/shard_map/ppermute | solution.py:385
  54.6 0.0 collective-permute-start.15
  54.6 6.4 %shard_map.129 = (bf16[2,128,1024]{2,1,0:T(8,128)(2,1)S(1)}, f32[2,128,1024]{2,1,0:T(8,128)S(1)}, bf16[1024,16384]{1,0:T(8,128)(2,1)}) custom-call(s32[16]{0:T(128)S(1)} %dynamic-slice_bitcast_fusion.offs_ref.refs_0_, bf16[128,1024]{1,0:T(8,128)(2,1)S(1)} %get-tuple-element.116.refs_1_, ...), custom_call_target="tpu_custom_call", output_to_operand_aliasing={{2}: (22, {})} | custom-call | flops 150994944 | bytes 1179648 | tf_op jit(solution)/shard_map/pallas_call | solution.py:57
  61.1 1.1 %collective-permute-done.13 = bf16[2,128,1024]{2,1,0:T(8,128)(2,1)S(1)} collective-permute-done((bf16[2,128,1024]{2,1,0:T(8,128)(2,1)S(1)}, bf16[2,128,1024]{2,1,0:T(8,128)(2,1)S(1)}, u32[]{:S(2)}, u32[]{:S(2)}) %collective-permute-start.13) | collective-permute-done | bytes 524320 | tf_op jit(solution)/shard_map/ppermute | solution.py:385
  62.2 0.0 collective-permute-done.15
  62.2 0.3 add_convert_fusion.1
  62.5 1.8 %collective-permute-start.16 = (bf16[2,128,1024]{2,1,0:T(8,128)(2,1)S(1)}, bf16[2,128,1024]{2,1,0:T(8,128)(2,1)S(1)}, u32[]{:S(2)}, u32[]{:S(2)}) collective-permute-start(bf16[2,128,1024]{2,1,0:T(8,128)(2,1)S(1)} %add_convert_fusion.1), channel_id=1, source_target_pairs={{0,2},{1,5},{2,6},{3,1},{6,10},{7,3},{10,14},{11,7},{14,12},{15,11... | collective-permute-start | bytes 1572872 | tf_op jit(solution)/shard_map/ppermute | solution.py:385
  64.4 0.0 collective-permute-start.14
  64.4 6.7 %shard_map.130 = (bf16[1,128,1024]{2,1,0:T(8,128)(2,1)S(1)}, f32[1,128,1024]{2,1,0:T(8,128)S(1)}, bf16[1024,16384]{1,0:T(8,128)(2,1)}) custom-call(s32[16]{0:T(128)S(1)} %dynamic-slice_bitcast_fusion.offs_ref.refs_0_, bf16[128,1024]{1,0:T(8,128)(2,1)S(1)} %get-tuple-element.116.refs_1_, ...), custom_call_target="tpu_custom_call", output_to_operand_aliasing={{2}: (23, {})} | custom-call | flops 134217728 | bytes 1048576 | tf_op jit(solution)/shard_map/pallas_call | solution.py:57
  71.1 0.6 collective-permute-start.17
  71.7 0.3 collective-permute-done.16
  72.0 0.0 collective-permute-done.14
  72.0 0.3 add_convert_fusion
  72.3 1.6 %collective-permute-start.18 = (bf16[1,128,1024]{2,1,0:T(8,128)(2,1)S(1)}, bf16[1,128,1024]{2,1,0:T(8,128)(2,1)S(1)}, u32[]{:S(2)}, u32[]{:S(2)}) collective-permute-start(bf16[1,128,1024]{2,1,0:T(8,128)(2,1)S(1)} %get-tuple-element.151), channel_id=1, source_target_pairs={{0,2},{1,5},{2,6},{3,1},{6,10},{7,3},{10,14},{11,7},{14,12},{15,11... | collective-permute-start | bytes 786440 | tf_op jit(solution)/shard_map/ppermute | solution.py:385
  73.9 0.0 collective-permute-start.19
  73.9 3.8 %shard_map.131 = bf16[1024,16384]{1,0:T(8,128)(2,1)} custom-call(s32[16]{0:T(128)S(1)} %dynamic-slice_bitcast_fusion.offs_ref.refs_0_, bf16[128,1024]{1,0:T(8,128)(2,1)S(1)} %get-tuple-element.116.refs_1_, bf16[1024,128]{1,0:T(8,128)(2,1)S(1)} %get-tuple-element.117.refs_2_, ...), custom_call_target="tpu_custom_call", output_to_operand_aliasing={{}: (22, {})} | custom-call | flops 50331648 | bytes 393216 | tf_op jit(solution)/shard_map/pallas_call | solution.py:57
  77.7 0.0 collective-permute-done.17
  77.7 1.0 %collective-permute-done.18 = bf16[1,128,1024]{2,1,0:T(8,128)(2,1)S(1)} collective-permute-done((bf16[1,128,1024]{2,1,0:T(8,128)(2,1)S(1)}, bf16[1,128,1024]{2,1,0:T(8,128)(2,1)S(1)}, u32[]{:S(2)}, u32[]{:S(2)}) %collective-permute-start.18) | collective-permute-done | bytes 262176 | tf_op jit(solution)/shard_map/ppermute | solution.py:385
  78.7 1.9 %collective-permute-done.19 = bf16[1,128,1024]{2,1,0:T(8,128)(2,1)S(1)} collective-permute-done((bf16[1,128,1024]{2,1,0:T(8,128)(2,1)S(1)}, bf16[1,128,1024]{2,1,0:T(8,128)(2,1)S(1)}, u32[]{:S(2)}, u32[]{:S(2)}) %collective-permute-start.19) | collective-permute-done | bytes 262176 | tf_op jit(solution)/shard_map/ppermute | solution.py:385
  80.6 1.0 %fusion.1 = f32[1,128,1024]{2,1,0:T(8,128)} fusion(f32[128,1024]{1,0:T(8,128)S(1)} %shard_map.128, f32[1,128,1024]{2,1,0:T(8,128)S(1)} %get-tuple-element.145, bf16[1,128,1024]{2,1,0:T(8,128)(2,1)S(1)} %collective-permute-done.17, bf16[1,128,1024]{2,1,0:T(8,128)(2,1)S(1)} %collective-permute-done.19, bf16[1,128,1024]{2,1,0:T(8,128)(2,1)S(1)} %collective-permute-done.18), kind=kLoop, calls=%fused_computation.8 | loop fusion | flops 917504 | bytes 2359296 | tf_op jit(solution)/shard_map/reshape | solution.py:485
  (13 shorter events, 0.1 us)
Async XLA Ops:
  1.7 10.4 %collective-permute-start.2 = (bf16[1,128,1024]{2,1,0:T(8,128)(2,1)S(1)}, bf16[1,128,1024]{2,1,0:T(8,128)(2,1)S(1)}, u32[]{:S(2)}, u32[]{:S(2)}) collective-permute-start(bf16[1,128,1024]{2,1,0:T(8,128)(2,1)S(1)} %convert_element_type.49.refs_8_.refs_14_.refs_3_), channel_id=1, source_target_pairs={{0,1},{1,0},{2,3},{3,2},{4,5},{5,4},{6,7},{7,6},{8,9},{9,8},{10,11... | collective-permute-start | bytes 786440 | tf_op jit(solution)/shard_map/ppermute | solution.py:388
  2.2 9.9 %collective-permute-start.1 = (bf16[1,128,1024]{2,1,0:T(8,128)(2,1)S(1)}, bf16[1,128,1024]{2,1,0:T(8,128)(2,1)S(1)}, u32[]{:S(2)}, u32[]{:S(2)}) collective-permute-start(bf16[1,128,1024]{2,1,0:T(8,128)(2,1)S(1)} %convert_element_type.49.refs_8_.refs_14_.refs_3_), channel_id=1, source_target_pairs={{0,5},{1,2},{2,1},{3,6},{6,3},{7,10},{10,7},{11,14},{14,11},{15,12... | collective-permute-start | bytes 786440 | tf_op jit(solution)/shard_map/ppermute | solution.py:385
  4.9 7.2 %collective-permute-start = (bf16[1,128,1024]{2,1,0:T(8,128)(2,1)S(1)}, bf16[1,128,1024]{2,1,0:T(8,128)(2,1)S(1)}, u32[]{:S(2)}, u32[]{:S(2)}) collective-permute-start(bf16[1,128,1024]{2,1,0:T(8,128)(2,1)S(1)} %convert_element_type.49.refs_8_.refs_14_.refs_3_), channel_id=1, source_target_pairs={{0,2},{1,5},{2,6},{3,1},{6,10},{7,3},{10,14},{11,7},{14,12},{15,11... | collective-permute-start | bytes 786440 | tf_op jit(solution)/shard_map/ppermute | solution.py:385
  12.2 9.2 %collective-permute-start.3 = (bf16[2,128,1024]{2,1,0:T(8,128)(2,1)S(1)}, bf16[2,128,1024]{2,1,0:T(8,128)(2,1)S(1)}, u32[]{:S(2)}, u32[]{:S(2)}) collective-permute-start(bf16[2,128,1024]{2,1,0:T(8,128)(2,1)S(1)} %constant_dynamic-update-slice_fusion.refs_10_.refs_16_.refs_3_), channel_id=1, source_target_pairs={{0,2},{1,5},{2,6},{3,1},{6,10},{7,3},{10,14},{11,7},{14,12},{15,11... | collective-permute-start | bytes 1572872 | tf_op jit(solution)/shard_map/ppermute | solution.py:385
  14.2 9.9 %collective-permute-start.5 = (bf16[2,128,1024]{2,1,0:T(8,128)(2,1)S(1)}, bf16[2,128,1024]{2,1,0:T(8,128)(2,1)S(1)}, u32[]{:S(2)}, u32[]{:S(2)}) collective-permute-start(bf16[2,128,1024]{2,1,0:T(8,128)(2,1)S(1)} %constant_dynamic-update-slice_fusion.refs_10_.refs_16_.refs_3_), channel_id=1, source_target_pairs={{0,1},{1,0},{2,3},{3,2},{4,5},{5,4},{6,7},{7,6},{8,9},{9,8},{10,11... | collective-permute-start | bytes 1572872 | tf_op jit(solution)/shard_map/ppermute | solution.py:388
  14.2 9.2 %copy-start = (f32[1,128,1024]{2,1,0:T(8,128)S(1)}, f32[1,128,1024]{2,1,0:T(8,128)}, u32[]{:S(2)}) copy-start(f32[1,128,1024]{2,1,0:T(8,128)} %param.8) | copy-start | bytes 1572868
  14.2 9.2 %copy-start.1 = (f32[128,128]{1,0:T(8,128)S(1)}, f32[128,128]{1,0:T(8,128)}, u32[]{:S(2)}) copy-start(f32[128,128]{1,0:T(8,128)} %constant.13.clone.cheb_ref) | copy-start | bytes 196612
  14.2 9.2 %copy-start.2 = (f32[16,1024]{1,0:T(8,128)S(1)}, f32[16,1024]{1,0:T(8,128)}, u32[]{:S(2)}) copy-start(f32[16,1024]{1,0:T(8,128)} %pert_ref.1) | copy-start | bytes 196612
  21.5 11.6 %collective-permute-start.4 = (bf16[2,128,1024]{2,1,0:T(8,128)(2,1)S(1)}, bf16[2,128,1024]{2,1,0:T(8,128)(2,1)S(1)}, u32[]{:S(2)}, u32[]{:S(2)}) collective-permute-start(bf16[2,128,1024]{2,1,0:T(8,128)(2,1)S(1)} %collective-permute-done.3.refs_18_.refs_5_.refs_3_), channel_id=1, source_target_pairs={{0,2},{1,5},{2,6},{3,1},{6,10},{7,3},{10,14},{11,7},{14,12},{15,11... | collective-permute-start | bytes 1572872 | tf_op jit(solution)/shard_map/ppermute | solution.py:385
  24.0 11.2 %collective-permute-start.7 = (bf16[2,128,1024]{2,1,0:T(8,128)(2,1)S(1)}, bf16[2,128,1024]{2,1,0:T(8,128)(2,1)S(1)}, u32[]{:S(2)}, u32[]{:S(2)}) collective-permute-start(bf16[2,128,1024]{2,1,0:T(8,128)(2,1)S(1)} %collective-permute-done.3.refs_18_.refs_5_.refs_3_), channel_id=1, source_target_pairs={{0,1},{1,0},{2,3},{3,2},{4,5},{5,4},{6,7},{7,6},{8,9},{9,8},{10,11... | collective-permute-start | bytes 1572872 | tf_op jit(solution)/shard_map/ppermute | solution.py:388
  33.0 2.2 %collective-permute-start.8 = (bf16[2,128,1024]{2,1,0:T(8,128)(2,1)S(1)}, bf16[2,128,1024]{2,1,0:T(8,128)(2,1)S(1)}, u32[]{:S(2)}, u32[]{:S(2)}) collective-permute-start(bf16[2,128,1024]{2,1,0:T(8,128)(2,1)S(1)} %collective-permute-done.4.refs_17_.refs_5_), channel_id=1, source_target_pairs={{0,1},{1,0},{2,3},{3,2},{4,5},{5,4},{6,7},{7,6},{8,9},{9,8},{10,11... | collective-permute-start | bytes 1572872 | tf_op jit(solution)/shard_map/ppermute | solution.py:388
  33.6 6.4 %collective-permute-start.6 = (bf16[1,128,1024]{2,1,0:T(8,128)(2,1)S(1)}, bf16[1,128,1024]{2,1,0:T(8,128)(2,1)S(1)}, u32[]{:S(2)}, u32[]{:S(2)}) collective-permute-start(bf16[1,128,1024]{2,1,0:T(8,128)(2,1)S(1)} %slice.22), channel_id=1, source_target_pairs={{0,2},{1,5},{2,6},{3,1},{6,10},{7,3},{10,14},{11,7},{14,12},{15,11... | collective-permute-start | bytes 786440 | tf_op jit(solution)/shard_map/ppermute | solution.py:385
  39.2 2.4 %copy-start.3 = (f32[1024]{0:T(1024)S(1)}, f32[1024]{0:T(1024)}, u32[]{:S(2)}) copy-start(f32[1024]{0:T(1024)} %param.12) | copy-start | bytes 12292
  39.2 2.3 %copy-start.4 = (f32[1024]{0:T(1024)S(1)}, f32[1024]{0:T(1024)}, u32[]{:S(2)}) copy-start(f32[1024]{0:T(1024)} %param.11) | copy-start | bytes 12292
  40.0 1.5 %collective-permute-start.9 = (bf16[1,128,1024]{2,1,0:T(8,128)(2,1)S(1)}, bf16[1,128,1024]{2,1,0:T(8,128)(2,1)S(1)}, u32[]{:S(2)}, u32[]{:S(2)}) collective-permute-start(bf16[1,128,1024]{2,1,0:T(8,128)(2,1)S(1)} %collective-permute-done.6.refs_16_.refs_4_), channel_id=1, source_target_pairs={{0,1},{1,0},{2,3},{3,2},{4,5},{5,4},{6,7},{7,6},{8,9},{9,8},{10,11... | collective-permute-start | bytes 786440 | tf_op jit(solution)/shard_map/ppermute | solution.py:388
  43.8 1.9 %collective-permute-start.10 = (bf16[1,128,1024]{2,1,0:T(8,128)(2,1)S(1)}, bf16[1,128,1024]{2,1,0:T(8,128)(2,1)S(1)}, u32[]{:S(2)}, u32[]{:S(2)}) collective-permute-start(bf16[1,128,1024]{2,1,0:T(8,128)(2,1)S(1)} %get-tuple-element.119), channel_id=1, source_target_pairs={{0,1},{1,0},{2,3},{3,2},{4,5},{5,4},{6,7},{7,6},{8,9},{9,8},{10,11... | collective-permute-start | bytes 786440 | tf_op jit(solution)/shard_map/ppermute | solution.py:388
  45.8 6.9 %collective-permute-start.12 = (bf16[2,128,1024]{2,1,0:T(8,128)(2,1)S(1)}, bf16[2,128,1024]{2,1,0:T(8,128)(2,1)S(1)}, u32[]{:S(2)}, u32[]{:S(2)}) collective-permute-start(bf16[2,128,1024]{2,1,0:T(8,128)(2,1)S(1)} %get-tuple-element.127), channel_id=1, source_target_pairs={{0,1},{1,0},{2,3},{3,2},{4,5},{5,4},{6,7},{7,6},{8,9},{9,8},{10,11... | collective-permute-start | bytes 1572872 | tf_op jit(solution)/shard_map/ppermute | solution.py:388
  46.0 6.6 %collective-permute-start.11 = (bf16[1,128,1024]{2,1,0:T(8,128)(2,1)S(1)}, bf16[1,128,1024]{2,1,0:T(8,128)(2,1)S(1)}, u32[]{:S(2)}, u32[]{:S(2)}) collective-permute-start(bf16[1,128,1024]{2,1,0:T(8,128)(2,1)S(1)} %add_convert_fusion.2), channel_id=1, source_target_pairs={{0,2},{1,5},{2,6},{3,1},{6,10},{7,3},{10,14},{11,7},{14,12},{15,11... | collective-permute-start | bytes 786440 | tf_op jit(solution)/shard_map/ppermute | solution.py:385
  53.0 9.2 %collective-permute-start.13 = (bf16[2,128,1024]{2,1,0:T(8,128)(2,1)S(1)}, bf16[2,128,1024]{2,1,0:T(8,128)(2,1)S(1)}, u32[]{:S(2)}, u32[]{:S(2)}) collective-permute-start(bf16[2,128,1024]{2,1,0:T(8,128)(2,1)S(1)} %pad_maximum_fusion), channel_id=1, source_target_pairs={{0,2},{1,5},{2,6},{3,1},{6,10},{7,3},{10,14},{11,7},{14,12},{15,11... | collective-permute-start | bytes 1572872 | tf_op jit(solution)/shard_map/ppermute | solution.py:385
  54.6 7.6 %collective-permute-start.15 = (bf16[2,128,1024]{2,1,0:T(8,128)(2,1)S(1)}, bf16[2,128,1024]{2,1,0:T(8,128)(2,1)S(1)}, u32[]{:S(2)}, u32[]{:S(2)}) collective-permute-start(bf16[2,128,1024]{2,1,0:T(8,128)(2,1)S(1)} %get-tuple-element.135), channel_id=1, source_target_pairs={{0,1},{1,0},{2,3},{3,2},{4,5},{5,4},{6,7},{7,6},{8,9},{9,8},{10,11... | collective-permute-start | bytes 1572872 | tf_op jit(solution)/shard_map/ppermute | solution.py:388
  62.5 9.5 %collective-permute-start.16 = (bf16[2,128,1024]{2,1,0:T(8,128)(2,1)S(1)}, bf16[2,128,1024]{2,1,0:T(8,128)(2,1)S(1)}, u32[]{:S(2)}, u32[]{:S(2)}) collective-permute-start(bf16[2,128,1024]{2,1,0:T(8,128)(2,1)S(1)} %add_convert_fusion.1), channel_id=1, source_target_pairs={{0,2},{1,5},{2,6},{3,1},{6,10},{7,3},{10,14},{11,7},{14,12},{15,11... | collective-permute-start | bytes 1572872 | tf_op jit(solution)/shard_map/ppermute | solution.py:385
  64.4 7.6 %collective-permute-start.14 = (bf16[2,128,1024]{2,1,0:T(8,128)(2,1)S(1)}, bf16[2,128,1024]{2,1,0:T(8,128)(2,1)S(1)}, u32[]{:S(2)}, u32[]{:S(2)}) collective-permute-start(bf16[2,128,1024]{2,1,0:T(8,128)(2,1)S(1)} %get-tuple-element.134), channel_id=1, source_target_pairs={{0,1},{1,0},{2,3},{3,2},{4,5},{5,4},{6,7},{7,6},{8,9},{9,8},{10,11... | collective-permute-start | bytes 1572872 | tf_op jit(solution)/shard_map/ppermute | solution.py:388
  71.1 6.6 %collective-permute-start.17 = (bf16[1,128,1024]{2,1,0:T(8,128)(2,1)S(1)}, bf16[1,128,1024]{2,1,0:T(8,128)(2,1)S(1)}, u32[]{:S(2)}, u32[]{:S(2)}) collective-permute-start(bf16[1,128,1024]{2,1,0:T(8,128)(2,1)S(1)} %get-tuple-element.146), channel_id=1, source_target_pairs={{0,1},{1,0},{2,3},{3,2},{4,5},{5,4},{6,7},{7,6},{8,9},{9,8},{10,11... | collective-permute-start | bytes 786440 | tf_op jit(solution)/shard_map/ppermute | solution.py:388
  72.3 6.4 %collective-permute-start.18 = (bf16[1,128,1024]{2,1,0:T(8,128)(2,1)S(1)}, bf16[1,128,1024]{2,1,0:T(8,128)(2,1)S(1)}, u32[]{:S(2)}, u32[]{:S(2)}) collective-permute-start(bf16[1,128,1024]{2,1,0:T(8,128)(2,1)S(1)} %get-tuple-element.151), channel_id=1, source_target_pairs={{0,2},{1,5},{2,6},{3,1},{6,10},{7,3},{10,14},{11,7},{14,12},{15,11... | collective-permute-start | bytes 786440 | tf_op jit(solution)/shard_map/ppermute | solution.py:385
  73.9 6.7 %collective-permute-start.19 = (bf16[1,128,1024]{2,1,0:T(8,128)(2,1)S(1)}, bf16[1,128,1024]{2,1,0:T(8,128)(2,1)S(1)}, u32[]{:S(2)}, u32[]{:S(2)}) collective-permute-start(bf16[1,128,1024]{2,1,0:T(8,128)(2,1)S(1)} %get-tuple-element.152), channel_id=1, source_target_pairs={{0,3},{1,4},{2,7},{3,0},{6,11},{7,2},{10,15},{11,6},{14,13},{15,10... | collective-permute-start | bytes 786440 | tf_op jit(solution)/shard_map/ppermute | solution.py:385

commit v12 on v11

--- a/solution.py
+++ b/solution.py
@@ -12,8 +12,8 @@
 VMEM_LIMIT = 8 * 2**20
 BANDS = 16
 GROUP = 4
-LOADS = (7, 6, 3)
-PIECES = (2, 5, 6)
+LOADS = (8, 8)
+PIECES = (2, 4, 5)
 
 
 def cheb_matrix(count):
@@ -72,13 +72,12 @@
     return pl.ds(pl.multiple_of(offs_ref[at] * slab, slab), slab)
 
 
-def load_bands(w_ref, bands, sems, first):
+def band_copies(w_ref, bands, sems, first):
     copies = []
     for at, band_ref in enumerate(bands):
         tile = band_ref.shape[0]
         rows = pl.ds((first + at) * tile, tile)
         copies.append(pltpu.make_async_copy(w_ref.at[rows, :], band_ref, sems.at[at]))
-        copies[-1].start()
     return copies
 
 
@@ -101,7 +100,10 @@
 
 def load_kernel(offs_ref, perts_ref, w_ref, mark_ref, *refs):
     mark_ref[...] = jnp.zeros_like(mark_ref)
-    for copy in load_bands(w_ref, refs[:-1], refs[-1], 0):
+    copies = band_copies(w_ref, refs[:-1], refs[-1], 0)
+    for copy in copies:
+        copy.start()
+    for copy in copies:
         copy.wait()
 
 
@@ -120,7 +122,7 @@
     return mark, bands
 
 
-def pre_kernel(found, count, many, fresh, late, ripe, offs_ref, acc_ref, *refs):
+def pre_kernel(found, count, many, fresh, late, offs_ref, acc_ref, *refs):
     if late:
         w_ref, refs = refs[0], refs[1:]
     bands, refs = refs[:many], refs[many:]
@@ -128,36 +130,34 @@
     xs, out_ref, others, sems = refs[:arrays], refs[arrays], refs[arrays + 1 : -1], refs[-1]
     slab = xs[0].shape[-1]
     tile = out_ref.shape[0] // BANDS
-    copies = load_bands(w_ref, others, sems, many) if late else []
-    rest = fresh % GROUP if ripe else 0
-    for low in [*range(0, many - fresh, GROUP), *range(many - fresh, many - rest, GROUP)]:
+    copies = band_copies(w_ref, others, sems, many) if late else []
+    waiting = list(copies)
+    for low in [*range(0, many - fresh, GROUP), *range(many - fresh, many, GROUP)]:
         old = low < many - fresh
-        group = bands[low : min(low + GROUP, many - fresh if old else many - rest)]
+        group = bands[low : min(low + GROUP, many - fresh if old else many)]
         rows = pl.ds(low * tile, len(group) * tile)
         total = acc_ref[rows, :] if old else None
         for place in range(len(found) - count if old else 0, len(found)):
+            if waiting:
+                waiting.pop(0).start()
             at, index = found[place]
             part = product(group, columns_of(offs_ref, place, slab), xs[at].at[index])
             total = part if total is None else total + part
         out_ref[rows, :] = total
+    for copy in waiting:
+        copy.start()
     for copy in copies:
         copy.wait()
-    if ripe:
-        group, total = [*bands[many - rest :], *others], None
-        for place, (at, index) in enumerate(found):
-            part = product(group, columns_of(offs_ref, place, slab), xs[at].at[index])
-            total = part if total is None else total + part
-        out_ref[pl.ds((many - rest) * tile, len(group) * tile), :] = total
-
-
-def add_products(offs, weights, acc, bands, pieces, count, fresh, late, ripe):
+
+
+def add_products(offs, weights, acc, bands, pieces, count, fresh, late):
     arrays, found = split_pieces(pieces if fresh else pieces[-count:])
     if not fresh:
         found = [(0, 0)] * (len(pieces) - count) + found
     (_, nodes, slab), rows, many = arrays[0].shape, weights.shape[0], len(bands)
     operands = [offs, acc] + ([weights] if late else []) + [*bands, *arrays]
     acc, *others = call(
-        functools.partial(pre_kernel, found, count, many, fresh, late, ripe),
+        functools.partial(pre_kernel, found, count, many, fresh, late),
         [jax.ShapeDtypeStruct((rows, nodes), jnp.float32)] + band_shapes(late, weights),
         [VMEM_REF] * (1 + late),
         [pltpu.SemaphoreType.DMA((max(late, 1),))],
@@ -414,11 +414,11 @@
         else:
             x[half, 1] = (other, 0)
         count = 1 if step == half else 6 if step == half - 1 else 4
-        fresh = [LOADS[0], LOADS[1], 0][min(step, 3) - 1]
-        late = [LOADS[1], LOADS[2], 0][min(step, 3) - 1]
+        fresh = LOADS[step - 1] if step <= 2 else 0
+        late = LOADS[1] if step == 1 else 0
         acc, bands = add_products(
             offs, weights, acc, bands, [x[key] for key in listing[: seen + count]], count,
-            fresh, late, step == 2,
+            fresh, late,
         )
         seen += count
         if step == half - 2:

time: 82.1 us -> 80.1 us (0.976)
  Pallas kernels: 52.6 us -> 49.5 us
  waiting for transfers between devices: 6.4 us -> 8.33 us
  starting transfers between devices: 17.3 us -> 16.4 us
    pallas_call x13, Pallas kernels: 52.6 us -> 49.5 us  [run(): pl.pallas_call(kernel, out_shape=out_shape, in_specs=in_specs, out_specs=...]
    ppermute x10, waiting for transfers between devices: 6.11 us -> 7.8 us  [passed(): return lax.ppermute(array, 'row', pairs)]
  transfers between devices with their start and end apart: 20 -> 20, of which waited for: 7 -> 7; matrix products, arithmetic and copies ran while one was open for 1% -> 1% of each run, Pallas kernels for 62% -> 59%
where the time goes in v12:
time: 80.1 us; the launch traced here: 79.7 us
  Pallas kernels  49.5 us (62%)
  starting transfers between devices  16.4 us (20%)
  waiting for transfers between devices  8.33 us (10%)
  other arithmetic  2.92 us (4%)
  between operations  1.59 us (2%)
  local copies, waits for them, and re-layouts  0.85 us (1%)
    pallas_call x13, Pallas kernels, run(): pl.pallas_call(kernel, out_shape=out_shape, in_specs=in_specs, out_specs=...  49.5 us
    ppermute x10, starting transfers between devices, passed(): return lax.ppermute(array, 'row', pairs)  14.7 us
    ppermute x10, waiting for transfers between devices, passed(): return lax.ppermute(array, 'row', pairs)  7.8 us
    ppermute x10, starting transfers between devices, swap(): return lax.ppermute(array, 'row', [(i, i ^ 1) for i in range(2 * chips)])  1.75 us
  transfers between devices with their start and end apart: 20, of which 7 were waited for; matrix products, arithmetic and copies ran while one was open for 1% of the time, Pallas kernels for 59%

profile of v12, /device:TPU:0, one launch (start us, length us, event | category | flops | bytes accessed | tf_op | source)
XLA Modules:
  0.0 79.7 jit_solution(14358285465073811699)
XLA Ops:
  0.6 1.1 %convert_element_type.49.refs_9_.refs_16_.refs_3_ = bf16[1,128,1024]{2,1,0:T(8,128)(2,1)S(1)} convert(f32[1,128,1024]{2,1,0:T(8,128)} %param.8) | non-fusion elementwise | flops 131072 | bytes 786432 | tf_op jit(solution)/shard_map/convert_element_type | solution.py:394
  1.7 0.5 collective-permute-start.2
  2.2 2.7 %collective-permute-start.1 = (bf16[1,128,1024]{2,1,0:T(8,128)(2,1)S(1)}, bf16[1,128,1024]{2,1,0:T(8,128)(2,1)S(1)}, u32[]{:S(2)}, u32[]{:S(2)}) collective-permute-start(bf16[1,128,1024]{2,1,0:T(8,128)(2,1)S(1)} %convert_element_type.49.refs_9_.refs_16_.refs_3_), channel_id=1, source_target_pairs={{0,5},{1,2},{2,1},{3,6},{6,3},{7,10},{10,7},{11,14},{14,11},{15,12... | collective-permute-start | bytes 786440 | tf_op jit(solution)/shard_map/ppermute | solution.py:385
  4.9 0.0 collective-permute-start
  5.6 0.7 dynamic-slice_bitcast_fusion.offs_ref.refs_0_
  6.3 6.5 %shard_map.119 = (f32[8,128]{1,0:T(8,128)S(1)}, bf16[64,16384]{1,0:T(8,128)(2,1)S(1)}, bf16[64,16384]{1,0:T(8,128)(2,1)S(1)}, bf16[64,16384]{1,0:T(8,128)(2,1)S(...) custom-call(s32[16]{0:T(128)S(1)} %dynamic-slice_bitcast_fusion.offs, ...), custom_call_target="tpu_custom_call" | custom-call | flops 2097152 | bytes 16384 | tf_op jit(solution)/shard_map/pallas_call | solution.py:57
  12.7 0.0 collective-permute-done.2.refs_10_.refs_17_.refs_4_
  12.8 0.0 collective-permute-done.1
  12.8 0.0 collective-permute-done
  12.8 2.0 %collective-permute-start.3 = (bf16[2,128,1024]{2,1,0:T(8,128)(2,1)S(1)}, bf16[2,128,1024]{2,1,0:T(8,128)(2,1)S(1)}, u32[]{:S(2)}, u32[]{:S(2)}) collective-permute-start(bf16[2,128,1024]{2,1,0:T(8,128)(2,1)S(1)} %constant_dynamic-update-slice_fusion.refs_11_.refs_18_.refs_3_), channel_id=1, source_target_pairs={{0,2},{1,5},{2,6},{3,1},{6,10},{7,3},{10,14},{11,7},{14,12},{15,11... | collective-permute-start | bytes 1572872 | tf_op jit(solution)/shard_map/ppermute | solution.py:385
  14.8 0.0 collective-permute-start.5
  14.8 7.5 %shard_map.120 = (f32[1024,128]{1,0:T(8,128)S(1)}, bf16[64,16384]{1,0:T(8,128)(2,1)S(1)}, bf16[64,16384]{1,0:T(8,128)(2,1)S(1)}, bf16[64,16384]{1,0:T(8,128)(2,1...) custom-call(s32[16]{0:T(128)S(1)} %dynamic-slice_bitcast_fusion.offs, ...), custom_call_target="tpu_custom_call" | custom-call | flops 67108864 | bytes 524288 | tf_op jit(solution)/shard_map/pallas_call | solution.py:57
  22.4 0.0 collective-permute-done.3.refs_20_.refs_3_
  22.4 1.6 %collective-permute-start.4 = (bf16[2,128,1024]{2,1,0:T(8,128)(2,1)S(1)}, bf16[2,128,1024]{2,1,0:T(8,128)(2,1)S(1)}, u32[]{:S(2)}, u32[]{:S(2)}) collective-permute-start(bf16[2,128,1024]{2,1,0:T(8,128)(2,1)S(1)} %collective-permute-done.3.refs_20_.refs_3_), channel_id=1, source_target_pairs={{0,2},{1,5},{2,6},{3,1},{6,10},{7,3},{10,14},{11,7},{14,12},{15,11... | collective-permute-start | bytes 1572872 | tf_op jit(solution)/shard_map/ppermute | solution.py:385
  24.0 0.6 shard_map.122
  24.6 0.1 collective-permute-start.7
  24.7 0.0 collective-permute-done.5.refs_19_.refs_4_
  24.7 4.0 %shard_map.121.acc_ref = f32[1024,128]{1,0:T(8,128)S(1)} custom-call(s32[16]{0:T(128)S(1)} %dynamic-slice_bitcast_fusion.offs_ref.refs_0_, f32[1024,128]{1,0:T(8,128)S(1)} %get-tuple-element.92.acc_ref, bf16[64,16384]{1,0:T(8,128)(2,1)S(1)} %get-tuple-element.81.refs_1_.refs_0_.refs_3_.refs_5_.refs_6_.refs_7_, ...), custom_call_target="tpu_custom_call" | custom-call | flops 67108864 | bytes 524288 | tf_op jit(solution)/shard_map/pallas_call | solution.py:57
  28.7 2.9 %collective-permute-done.4.refs_17_.refs_5_.refs_3_ = bf16[2,128,1024]{2,1,0:T(8,128)(2,1)S(1)} collective-permute-done((bf16[2,128,1024]{2,1,0:T(8,128)(2,1)S(1)}, bf16[2,128,1024]{2,1,0:T(8,128)(2,1)S(1)}, u32[]{:S(2)}, u32[]{:S(2)}) %collective-permute-start.4) | collective-permute-done | bytes 524320 | tf_op jit(solution)/shard_map/ppermute | solution.py:385
  31.6 0.0 collective-permute-start.8
  31.6 1.6 %collective-permute-start.6 = (bf16[1,128,1024]{2,1,0:T(8,128)(2,1)S(1)}, bf16[1,128,1024]{2,1,0:T(8,128)(2,1)S(1)}, u32[]{:S(2)}, u32[]{:S(2)}) collective-permute-start(bf16[1,128,1024]{2,1,0:T(8,128)(2,1)S(1)} %slice.22), channel_id=1, source_target_pairs={{0,2},{1,5},{2,6},{3,1},{6,10},{7,3},{10,14},{11,7},{14,12},{15,11... | collective-permute-start | bytes 786440 | tf_op jit(solution)/shard_map/ppermute | solution.py:385
  33.3 0.0 collective-permute-done.7.refs_16_.refs_4_
  33.3 0.3 collective-permute-done.8.refs_18_.refs_4_
  33.5 4.0 %shard_map.123.acc_ref = f32[1024,128]{1,0:T(8,128)S(1)} custom-call(s32[16]{0:T(128)S(1)} %dynamic-slice_bitcast_fusion.offs_ref.refs_0_, f32[1024,128]{1,0:T(8,128)S(1)} %shard_map.121.acc_ref, bf16[64,16384]{1,0:T(8,128)(2,1)S(1)} %get-tuple-element.81.refs_1_.refs_0_.refs_3_.refs_5_.refs_6_.refs_7_, ...), custom_call_target="tpu_custom_call" | custom-call | flops 100663296 | bytes 786432 | tf_op jit(solution)/shard_map/pallas_call | solution.py:57
  37.5 0.0 copy-start.3
  37.5 0.0 copy-start.4
  37.5 0.5 collective-permute-done.6.refs_16_.refs_5_
  38.1 0.0 collective-permute-start.9
  38.1 1.3 %shard_map.124.refs_16_ = f32[1024,128]{1,0:T(8,128)S(1)} custom-call(s32[16]{0:T(128)S(1)} %dynamic-slice_bitcast_fusion.offs_ref.refs_0_, f32[1024,128]{1,0:T(8,128)S(1)} %shard_map.123.acc_ref, bf16[64,16384]{1,0:T(8,128)(2,1)S(1)} %get-tuple-element.81.refs_1_.refs_0_.refs_3_.refs_5_.refs_6_.refs_7_, ...), custom_call_target="tpu_custom_call" | custom-call | flops 16777216 | bytes 131072 | tf_op jit(solution)/shard_map/pallas_call | solution.py:57
  39.3 0.3 collective-permute-done.9.x_ref.refs_6_
  39.6 2.3 %shard_map.125 = (f32[128,1024]{1,0:T(8,128)S(1)}, bf16[128,1024]{1,0:T(8,128)(2,1)S(1)}, bf16[1024,128]{1,0:T(8,128)(2,1)S(1)}, f32[16,1024]{1,0:T(8,128)}, f32...) custom-call(s32[16]{0:T(128)S(1)} %dynamic-slice_bitcast_fusion.offs_ref.refs_0_, ...), custom_call_target="tpu_custom_call" | custom-call | flops 33554432 | bytes 262144 | tf_op jit(solution)/shard_map/pallas_call | solution.py:57
  41.9 0.3 collective-permute-start.10
  42.2 1.6 %shard_map.126 = (bf16[2,128,1024]{2,1,0:T(8,128)(2,1)S(1)}, f32[1,128,1024]{2,1,0:T(8,128)S(1)}) custom-call(s32[16]{0:T(128)S(1)} %dynamic-slice_bitcast_fusion.offs_ref.refs_0_, bf16[128,1024]{1,0:T(8,128)(2,1)S(1)} %get-tuple-element.114.refs_1_, bf16[1024,128]{1,0:T(8,128)(2,1)S(1)} %get-tuple-element.115.refs_2_, ...), custom_call_target="tpu_custom_call" | custom-call | flops 50331648 | bytes 393216 | tf_op jit(solution)/shard_map/pallas_call | solution.py:57
  43.8 0.0 collective-permute-done.10
  43.8 0.1 add_convert_fusion.2
  43.9 0.3 collective-permute-start.12
  44.1 1.6 %collective-permute-start.11 = (bf16[1,128,1024]{2,1,0:T(8,128)(2,1)S(1)}, bf16[1,128,1024]{2,1,0:T(8,128)(2,1)S(1)}, u32[]{:S(2)}, u32[]{:S(2)}) collective-permute-start(bf16[1,128,1024]{2,1,0:T(8,128)(2,1)S(1)} %add_convert_fusion.2), channel_id=1, source_target_pairs={{0,2},{1,5},{2,6},{3,1},{6,10},{7,3},{10,14},{11,7},{14,12},{15,11... | collective-permute-start | bytes 786440 | tf_op jit(solution)/shard_map/ppermute | solution.py:385
  45.7 0.6 shard_map.128
  46.4 4.3 %shard_map.127 = (bf16[2,128,1024]{2,1,0:T(8,128)(2,1)S(1)}, f32[4,128,1024]{2,1,0:T(8,128)S(1)}, bf16[1024,16384]{1,0:T(8,128)(2,1)}) custom-call(s32[16]{0:T(128)S(1)} %dynamic-slice_bitcast_fusion.offs_ref.refs_0_, bf16[128,1024]{1,0:T(8,128)(2,1)S(1)} %get-tuple-element.114.refs_1_, bf16[1024,128]{1,0:T(8,128)(2,1)S(1)} %get-tuple-element.115.refs_2_, ...), custom_call_target="tpu_custom_call" | custom-call | flops 134217728 | bytes 1048576 | tf_op jit(solution)/shard_map/pallas_call | solution.py:57
  50.7 0.0 collective-permute-done.11
  50.7 0.0 collective-permute-done.12
  50.7 0.2 convert_add_fusion
  51.0 0.1 fusion
  51.0 0.1 pad_maximum_fusion
  51.1 1.6 %collective-permute-start.13 = (bf16[2,128,1024]{2,1,0:T(8,128)(2,1)S(1)}, bf16[2,128,1024]{2,1,0:T(8,128)(2,1)S(1)}, u32[]{:S(2)}, u32[]{:S(2)}) collective-permute-start(bf16[2,128,1024]{2,1,0:T(8,128)(2,1)S(1)} %pad_maximum_fusion), channel_id=1, source_target_pairs={{0,2},{1,5},{2,6},{3,1},{6,10},{7,3},{10,14},{11,7},{14,12},{15,11... | collective-permute-start | bytes 1572872 | tf_op jit(solution)/shard_map/ppermute | solution.py:385
  52.7 0.0 collective-permute-start.15
  52.7 5.6 %shard_map.129 = (bf16[2,128,1024]{2,1,0:T(8,128)(2,1)S(1)}, f32[2,128,1024]{2,1,0:T(8,128)S(1)}, bf16[1024,16384]{1,0:T(8,128)(2,1)}) custom-call(s32[16]{0:T(128)S(1)} %dynamic-slice_bitcast_fusion.offs_ref.refs_0_, bf16[128,1024]{1,0:T(8,128)(2,1)S(1)} %get-tuple-element.114.refs_1_, ...), custom_call_target="tpu_custom_call", output_to_operand_aliasing={{2}: (21, {})} | custom-call | flops 134217728 | bytes 1048576 | tf_op jit(solution)/shard_map/pallas_call | solution.py:57
  58.3 2.0 %collective-permute-done.13 = bf16[2,128,1024]{2,1,0:T(8,128)(2,1)S(1)} collective-permute-done((bf16[2,128,1024]{2,1,0:T(8,128)(2,1)S(1)}, bf16[2,128,1024]{2,1,0:T(8,128)(2,1)S(1)}, u32[]{:S(2)}, u32[]{:S(2)}) %collective-permute-start.13) | collective-permute-done | bytes 524320 | tf_op jit(solution)/shard_map/ppermute | solution.py:385
  60.3 0.0 collective-permute-done.15
  60.3 0.3 add_convert_fusion.1
  60.6 1.6 %collective-permute-start.16 = (bf16[2,128,1024]{2,1,0:T(8,128)(2,1)S(1)}, bf16[2,128,1024]{2,1,0:T(8,128)(2,1)S(1)}, u32[]{:S(2)}, u32[]{:S(2)}) collective-permute-start(bf16[2,128,1024]{2,1,0:T(8,128)(2,1)S(1)} %add_convert_fusion.1), channel_id=1, source_target_pairs={{0,2},{1,5},{2,6},{3,1},{6,10},{7,3},{10,14},{11,7},{14,12},{15,11... | collective-permute-start | bytes 1572872 | tf_op jit(solution)/shard_map/ppermute | solution.py:385
  62.2 0.0 collective-permute-start.14
  62.2 5.9 %shard_map.130 = (bf16[1,128,1024]{2,1,0:T(8,128)(2,1)S(1)}, f32[1,128,1024]{2,1,0:T(8,128)S(1)}, bf16[1024,16384]{1,0:T(8,128)(2,1)}) custom-call(s32[16]{0:T(128)S(1)} %dynamic-slice_bitcast_fusion.offs_ref.refs_0_, bf16[128,1024]{1,0:T(8,128)(2,1)S(1)} %get-tuple-element.114.refs_1_, ...), custom_call_target="tpu_custom_call", output_to_operand_aliasing={{2}: (22, {})} | custom-call | flops 117440512 | bytes 917504 | tf_op jit(solution)/shard_map/pallas_call | solution.py:57
  68.1 0.6 collective-permute-start.17
  68.7 1.1 %collective-permute-done.16 = bf16[2,128,1024]{2,1,0:T(8,128)(2,1)S(1)} collective-permute-done((bf16[2,128,1024]{2,1,0:T(8,128)(2,1)S(1)}, bf16[2,128,1024]{2,1,0:T(8,128)(2,1)S(1)}, u32[]{:S(2)}, u32[]{:S(2)}) %collective-permute-start.16) | collective-permute-done | bytes 524320 | tf_op jit(solution)/shard_map/ppermute | solution.py:385
  69.8 0.0 collective-permute-done.14
  69.8 0.3 add_convert_fusion
  70.1 1.9 %collective-permute-start.18 = (bf16[1,128,1024]{2,1,0:T(8,128)(2,1)S(1)}, bf16[1,128,1024]{2,1,0:T(8,128)(2,1)S(1)}, u32[]{:S(2)}, u32[]{:S(2)}) collective-permute-start(bf16[1,128,1024]{2,1,0:T(8,128)(2,1)S(1)} %get-tuple-element.149), channel_id=1, source_target_pairs={{0,2},{1,5},{2,6},{3,1},{6,10},{7,3},{10,14},{11,7},{14,12},{15,11... | collective-permute-start | bytes 786440 | tf_op jit(solution)/shard_map/ppermute | solution.py:385
  72.0 0.0 collective-permute-start.19
  72.0 5.5 %shard_map.131 = bf16[1024,16384]{1,0:T(8,128)(2,1)} custom-call(s32[16]{0:T(128)S(1)} %dynamic-slice_bitcast_fusion.offs_ref.refs_0_, bf16[128,1024]{1,0:T(8,128)(2,1)S(1)} %get-tuple-element.114.refs_1_, bf16[1024,128]{1,0:T(8,128)(2,1)S(1)} %get-tuple-element.115.refs_2_, ...), custom_call_target="tpu_custom_call", output_to_operand_aliasing={{}: (23, {})} | custom-call | flops 83886080 | bytes 655360 | tf_op jit(solution)/shard_map/pallas_call | solution.py:57
  77.5 0.0 collective-permute-done.17
  77.5 0.0 collective-permute-done.18
  77.5 1.2 %collective-permute-done.19 = bf16[1,128,1024]{2,1,0:T(8,128)(2,1)S(1)} collective-permute-done((bf16[1,128,1024]{2,1,0:T(8,128)(2,1)S(1)}, bf16[1,128,1024]{2,1,0:T(8,128)(2,1)S(1)}, u32[]{:S(2)}, u32[]{:S(2)}) %collective-permute-start.19) | collective-permute-done | bytes 262176 | tf_op jit(solution)/shard_map/ppermute | solution.py:385
  78.7 1.0 %fusion.1 = f32[1,128,1024]{2,1,0:T(8,128)} fusion(f32[128,1024]{1,0:T(8,128)S(1)} %shard_map.128, f32[1,128,1024]{2,1,0:T(8,128)S(1)} %get-tuple-element.143, bf16[1,128,1024]{2,1,0:T(8,128)(2,1)S(1)} %collective-permute-done.17, bf16[1,128,1024]{2,1,0:T(8,128)(2,1)S(1)} %collective-permute-done.19, bf16[1,128,1024]{2,1,0:T(8,128)(2,1)S(1)} %collective-permute-done.18), kind=kLoop, calls=%fused_computation.8 | loop fusion | flops 917504 | bytes 2359296 | tf_op jit(solution)/shard_map/reshape | solution.py:485
  (13 shorter events, 0.1 us)
Async XLA Ops:
  1.7 11.0 %collective-permute-start.2 = (bf16[1,128,1024]{2,1,0:T(8,128)(2,1)S(1)}, bf16[1,128,1024]{2,1,0:T(8,128)(2,1)S(1)}, u32[]{:S(2)}, u32[]{:S(2)}) collective-permute-start(bf16[1,128,1024]{2,1,0:T(8,128)(2,1)S(1)} %convert_element_type.49.refs_9_.refs_16_.refs_3_), channel_id=1, source_target_pairs={{0,1},{1,0},{2,3},{3,2},{4,5},{5,4},{6,7},{7,6},{8,9},{9,8},{10,11... | collective-permute-start | bytes 786440 | tf_op jit(solution)/shard_map/ppermute | solution.py:388
  2.2 10.5 %collective-permute-start.1 = (bf16[1,128,1024]{2,1,0:T(8,128)(2,1)S(1)}, bf16[1,128,1024]{2,1,0:T(8,128)(2,1)S(1)}, u32[]{:S(2)}, u32[]{:S(2)}) collective-permute-start(bf16[1,128,1024]{2,1,0:T(8,128)(2,1)S(1)} %convert_element_type.49.refs_9_.refs_16_.refs_3_), channel_id=1, source_target_pairs={{0,5},{1,2},{2,1},{3,6},{6,3},{7,10},{10,7},{11,14},{14,11},{15,12... | collective-permute-start | bytes 786440 | tf_op jit(solution)/shard_map/ppermute | solution.py:385
  4.9 7.8 %collective-permute-start = (bf16[1,128,1024]{2,1,0:T(8,128)(2,1)S(1)}, bf16[1,128,1024]{2,1,0:T(8,128)(2,1)S(1)}, u32[]{:S(2)}, u32[]{:S(2)}) collective-permute-start(bf16[1,128,1024]{2,1,0:T(8,128)(2,1)S(1)} %convert_element_type.49.refs_9_.refs_16_.refs_3_), channel_id=1, source_target_pairs={{0,2},{1,5},{2,6},{3,1},{6,10},{7,3},{10,14},{11,7},{14,12},{15,11... | collective-permute-start | bytes 786440 | tf_op jit(solution)/shard_map/ppermute | solution.py:385
  12.8 9.6 %collective-permute-start.3 = (bf16[2,128,1024]{2,1,0:T(8,128)(2,1)S(1)}, bf16[2,128,1024]{2,1,0:T(8,128)(2,1)S(1)}, u32[]{:S(2)}, u32[]{:S(2)}) collective-permute-start(bf16[2,128,1024]{2,1,0:T(8,128)(2,1)S(1)} %constant_dynamic-update-slice_fusion.refs_11_.refs_18_.refs_3_), channel_id=1, source_target_pairs={{0,2},{1,5},{2,6},{3,1},{6,10},{7,3},{10,14},{11,7},{14,12},{15,11... | collective-permute-start | bytes 1572872 | tf_op jit(solution)/shard_map/ppermute | solution.py:385
  14.8 9.9 %collective-permute-start.5 = (bf16[2,128,1024]{2,1,0:T(8,128)(2,1)S(1)}, bf16[2,128,1024]{2,1,0:T(8,128)(2,1)S(1)}, u32[]{:S(2)}, u32[]{:S(2)}) collective-permute-start(bf16[2,128,1024]{2,1,0:T(8,128)(2,1)S(1)} %constant_dynamic-update-slice_fusion.refs_11_.refs_18_.refs_3_), channel_id=1, source_target_pairs={{0,1},{1,0},{2,3},{3,2},{4,5},{5,4},{6,7},{7,6},{8,9},{9,8},{10,11... | collective-permute-start | bytes 1572872 | tf_op jit(solution)/shard_map/ppermute | solution.py:388
  14.8 9.2 %copy-start = (f32[1,128,1024]{2,1,0:T(8,128)S(1)}, f32[1,128,1024]{2,1,0:T(8,128)}, u32[]{:S(2)}) copy-start(f32[1,128,1024]{2,1,0:T(8,128)} %param.8) | copy-start | bytes 1572868
  14.8 9.2 %copy-start.1 = (f32[128,128]{1,0:T(8,128)S(1)}, f32[128,128]{1,0:T(8,128)}, u32[]{:S(2)}) copy-start(f32[128,128]{1,0:T(8,128)} %constant.13.clone.cheb_ref) | copy-start | bytes 196612
  14.8 9.2 %copy-start.2 = (f32[16,1024]{1,0:T(8,128)S(1)}, f32[16,1024]{1,0:T(8,128)}, u32[]{:S(2)}) copy-start(f32[16,1024]{1,0:T(8,128)} %pert_ref.1) | copy-start | bytes 196612
  22.4 9.2 %collective-permute-start.4 = (bf16[2,128,1024]{2,1,0:T(8,128)(2,1)S(1)}, bf16[2,128,1024]{2,1,0:T(8,128)(2,1)S(1)}, u32[]{:S(2)}, u32[]{:S(2)}) collective-permute-start(bf16[2,128,1024]{2,1,0:T(8,128)(2,1)S(1)} %collective-permute-done.3.refs_20_.refs_3_), channel_id=1, source_target_pairs={{0,2},{1,5},{2,6},{3,1},{6,10},{7,3},{10,14},{11,7},{14,12},{15,11... | collective-permute-start | bytes 1572872 | tf_op jit(solution)/shard_map/ppermute | solution.py:385
  24.6 8.7 %collective-permute-start.7 = (bf16[2,128,1024]{2,1,0:T(8,128)(2,1)S(1)}, bf16[2,128,1024]{2,1,0:T(8,128)(2,1)S(1)}, u32[]{:S(2)}, u32[]{:S(2)}) collective-permute-start(bf16[2,128,1024]{2,1,0:T(8,128)(2,1)S(1)} %collective-permute-done.3.refs_20_.refs_3_), channel_id=1, source_target_pairs={{0,1},{1,0},{2,3},{3,2},{4,5},{5,4},{6,7},{7,6},{8,9},{9,8},{10,11... | collective-permute-start | bytes 1572872 | tf_op jit(solution)/shard_map/ppermute | solution.py:388
  31.6 1.9 %collective-permute-start.8 = (bf16[2,128,1024]{2,1,0:T(8,128)(2,1)S(1)}, bf16[2,128,1024]{2,1,0:T(8,128)(2,1)S(1)}, u32[]{:S(2)}, u32[]{:S(2)}) collective-permute-start(bf16[2,128,1024]{2,1,0:T(8,128)(2,1)S(1)} %collective-permute-done.4.refs_17_.refs_5_.refs_3_), channel_id=1, source_target_pairs={{0,1},{1,0},{2,3},{3,2},{4,5},{5,4},{6,7},{7,6},{8,9},{9,8},{10,11... | collective-permute-start | bytes 1572872 | tf_op jit(solution)/shard_map/ppermute | solution.py:388
  31.6 6.4 %collective-permute-start.6 = (bf16[1,128,1024]{2,1,0:T(8,128)(2,1)S(1)}, bf16[1,128,1024]{2,1,0:T(8,128)(2,1)S(1)}, u32[]{:S(2)}, u32[]{:S(2)}) collective-permute-start(bf16[1,128,1024]{2,1,0:T(8,128)(2,1)S(1)} %slice.22), channel_id=1, source_target_pairs={{0,2},{1,5},{2,6},{3,1},{6,10},{7,3},{10,14},{11,7},{14,12},{15,11... | collective-permute-start | bytes 786440 | tf_op jit(solution)/shard_map/ppermute | solution.py:385
  37.5 2.1 %copy-start.3 = (f32[1024]{0:T(1024)S(1)}, f32[1024]{0:T(1024)}, u32[]{:S(2)}) copy-start(f32[1024]{0:T(1024)} %param.12) | copy-start | bytes 12292
  37.5 2.1 %copy-start.4 = (f32[1024]{0:T(1024)S(1)}, f32[1024]{0:T(1024)}, u32[]{:S(2)}) copy-start(f32[1024]{0:T(1024)} %param.11) | copy-start | bytes 12292
  38.1 1.5 %collective-permute-start.9 = (bf16[1,128,1024]{2,1,0:T(8,128)(2,1)S(1)}, bf16[1,128,1024]{2,1,0:T(8,128)(2,1)S(1)}, u32[]{:S(2)}, u32[]{:S(2)}) collective-permute-start(bf16[1,128,1024]{2,1,0:T(8,128)(2,1)S(1)} %collective-permute-done.6.refs_16_.refs_5_), channel_id=1, source_target_pairs={{0,1},{1,0},{2,3},{3,2},{4,5},{5,4},{6,7},{7,6},{8,9},{9,8},{10,11... | collective-permute-start | bytes 786440 | tf_op jit(solution)/shard_map/ppermute | solution.py:388
  41.9 1.9 %collective-permute-start.10 = (bf16[1,128,1024]{2,1,0:T(8,128)(2,1)S(1)}, bf16[1,128,1024]{2,1,0:T(8,128)(2,1)S(1)}, u32[]{:S(2)}, u32[]{:S(2)}) collective-permute-start(bf16[1,128,1024]{2,1,0:T(8,128)(2,1)S(1)} %get-tuple-element.117), channel_id=1, source_target_pairs={{0,1},{1,0},{2,3},{3,2},{4,5},{5,4},{6,7},{7,6},{8,9},{9,8},{10,11... | collective-permute-start | bytes 786440 | tf_op jit(solution)/shard_map/ppermute | solution.py:388
  43.9 6.9 %collective-permute-start.12 = (bf16[2,128,1024]{2,1,0:T(8,128)(2,1)S(1)}, bf16[2,128,1024]{2,1,0:T(8,128)(2,1)S(1)}, u32[]{:S(2)}, u32[]{:S(2)}) collective-permute-start(bf16[2,128,1024]{2,1,0:T(8,128)(2,1)S(1)} %get-tuple-element.125), channel_id=1, source_target_pairs={{0,1},{1,0},{2,3},{3,2},{4,5},{5,4},{6,7},{7,6},{8,9},{9,8},{10,11... | collective-permute-start | bytes 1572872 | tf_op jit(solution)/shard_map/ppermute | solution.py:388
  44.1 6.6 %collective-permute-start.11 = (bf16[1,128,1024]{2,1,0:T(8,128)(2,1)S(1)}, bf16[1,128,1024]{2,1,0:T(8,128)(2,1)S(1)}, u32[]{:S(2)}, u32[]{:S(2)}) collective-permute-start(bf16[1,128,1024]{2,1,0:T(8,128)(2,1)S(1)} %add_convert_fusion.2), channel_id=1, source_target_pairs={{0,2},{1,5},{2,6},{3,1},{6,10},{7,3},{10,14},{11,7},{14,12},{15,11... | collective-permute-start | bytes 786440 | tf_op jit(solution)/shard_map/ppermute | solution.py:385
  51.1 9.2 %collective-permute-start.13 = (bf16[2,128,1024]{2,1,0:T(8,128)(2,1)S(1)}, bf16[2,128,1024]{2,1,0:T(8,128)(2,1)S(1)}, u32[]{:S(2)}, u32[]{:S(2)}) collective-permute-start(bf16[2,128,1024]{2,1,0:T(8,128)(2,1)S(1)} %pad_maximum_fusion), channel_id=1, source_target_pairs={{0,2},{1,5},{2,6},{3,1},{6,10},{7,3},{10,14},{11,7},{14,12},{15,11... | collective-permute-start | bytes 1572872 | tf_op jit(solution)/shard_map/ppermute | solution.py:385
  52.7 7.6 %collective-permute-start.15 = (bf16[2,128,1024]{2,1,0:T(8,128)(2,1)S(1)}, bf16[2,128,1024]{2,1,0:T(8,128)(2,1)S(1)}, u32[]{:S(2)}, u32[]{:S(2)}) collective-permute-start(bf16[2,128,1024]{2,1,0:T(8,128)(2,1)S(1)} %get-tuple-element.133), channel_id=1, source_target_pairs={{0,1},{1,0},{2,3},{3,2},{4,5},{5,4},{6,7},{7,6},{8,9},{9,8},{10,11... | collective-permute-start | bytes 1572872 | tf_op jit(solution)/shard_map/ppermute | solution.py:388
  60.6 9.2 %collective-permute-start.16 = (bf16[2,128,1024]{2,1,0:T(8,128)(2,1)S(1)}, bf16[2,128,1024]{2,1,0:T(8,128)(2,1)S(1)}, u32[]{:S(2)}, u32[]{:S(2)}) collective-permute-start(bf16[2,128,1024]{2,1,0:T(8,128)(2,1)S(1)} %add_convert_fusion.1), channel_id=1, source_target_pairs={{0,2},{1,5},{2,6},{3,1},{6,10},{7,3},{10,14},{11,7},{14,12},{15,11... | collective-permute-start | bytes 1572872 | tf_op jit(solution)/shard_map/ppermute | solution.py:385
  62.2 7.6 %collective-permute-start.14 = (bf16[2,128,1024]{2,1,0:T(8,128)(2,1)S(1)}, bf16[2,128,1024]{2,1,0:T(8,128)(2,1)S(1)}, u32[]{:S(2)}, u32[]{:S(2)}) collective-permute-start(bf16[2,128,1024]{2,1,0:T(8,128)(2,1)S(1)} %get-tuple-element.132), channel_id=1, source_target_pairs={{0,1},{1,0},{2,3},{3,2},{4,5},{5,4},{6,7},{7,6},{8,9},{9,8},{10,11... | collective-permute-start | bytes 1572872 | tf_op jit(solution)/shard_map/ppermute | solution.py:388
  68.1 9.3 %collective-permute-start.17 = (bf16[1,128,1024]{2,1,0:T(8,128)(2,1)S(1)}, bf16[1,128,1024]{2,1,0:T(8,128)(2,1)S(1)}, u32[]{:S(2)}, u32[]{:S(2)}) collective-permute-start(bf16[1,128,1024]{2,1,0:T(8,128)(2,1)S(1)} %get-tuple-element.144), channel_id=1, source_target_pairs={{0,1},{1,0},{2,3},{3,2},{4,5},{5,4},{6,7},{7,6},{8,9},{9,8},{10,11... | collective-permute-start | bytes 786440 | tf_op jit(solution)/shard_map/ppermute | solution.py:388
  70.1 7.4 %collective-permute-start.18 = (bf16[1,128,1024]{2,1,0:T(8,128)(2,1)S(1)}, bf16[1,128,1024]{2,1,0:T(8,128)(2,1)S(1)}, u32[]{:S(2)}, u32[]{:S(2)}) collective-permute-start(bf16[1,128,1024]{2,1,0:T(8,128)(2,1)S(1)} %get-tuple-element.149), channel_id=1, source_target_pairs={{0,2},{1,5},{2,6},{3,1},{6,10},{7,3},{10,14},{11,7},{14,12},{15,11... | collective-permute-start | bytes 786440 | tf_op jit(solution)/shard_map/ppermute | solution.py:385
  72.0 6.7 %collective-permute-start.19 = (bf16[1,128,1024]{2,1,0:T(8,128)(2,1)S(1)}, bf16[1,128,1024]{2,1,0:T(8,128)(2,1)S(1)}, u32[]{:S(2)}, u32[]{:S(2)}) collective-permute-start(bf16[1,128,1024]{2,1,0:T(8,128)(2,1)S(1)} %get-tuple-element.150), channel_id=1, source_target_pairs={{0,3},{1,4},{2,7},{3,0},{6,11},{7,2},{10,15},{11,6},{14,13},{15,10... | collective-permute-start | bytes 786440 | tf_op jit(solution)/shard_map/ppermute | solution.py:385

commit v13 on v12

--- a/solution.py
+++ b/solution.py
@@ -13,7 +13,8 @@
 BANDS = 16
 GROUP = 4
 LOADS = (8, 8)
-PIECES = (2, 4, 5)
+COUNTS = (2, 6, 6, 1)
+PIECES = (1, 5, 5)
 
 
 def cheb_matrix(count):
@@ -413,7 +414,7 @@
             x[-step, 1], x[-step, 0] = (other, 0), (other, 1)
         else:
             x[half, 1] = (other, 0)
-        count = 1 if step == half else 6 if step == half - 1 else 4
+        count = COUNTS[step - 1]
         fresh = LOADS[step - 1] if step <= 2 else 0
         late = LOADS[1] if step == 1 else 0
         acc, bands = add_products(
@@ -463,7 +464,7 @@
         others, owns, grad_w, base = work(
             offs, counts.pop(0), sent(step - 1), late + kept(step - 1), grad_w, base
         )
-        if late:
+        if step == 1:
             local = local_terms(cheb, resid, decay)
             owns, local = gate((owns, local))
         flow, owns = gate((flow, owns))
@@ -481,7 +482,8 @@
         else:
             near, over = passed(total[:1]), passed(total[1:], 1, 1)
     _, _, grad_w, base = work(offs, len(listing) - base, [], [], grad_w, base)
-    grad_x = local + share[0] + near[0].astype(jnp.float32) + over[0].astype(jnp.float32)
+    near, over, local = gate((near, over, local + share[0]))
+    grad_x = local + near[0].astype(jnp.float32) + over[0].astype(jnp.float32)
     grad_x = grad_x.reshape(states.shape)
     return (grad_w, grad_x, grad_table, grad_eps.reshape(rows), grad_decay.reshape(rows))
 

time: 80.1 us -> 80 us (level)
  waiting for transfers between devices: 8.33 us -> 5.5 us
  starting transfers between devices: 16.4 us -> 19.1 us
    ppermute x10, starting transfers between devices: 14.7 us -> 17.4 us  [passed(): return lax.ppermute(array, 'row', pairs)]
    ppermute x10, waiting for transfers between devices: 7.8 us -> 5.22 us  [passed(): return lax.ppermute(array, 'row', pairs)]
  transfers between devices with their start and end apart: 20 -> 20, of which waited for: 7 -> 8; matrix products, arithmetic and copies ran while one was open for 1% -> 1% of each run, Pallas kernels for 59% -> 60%
where the time goes in v13:
time: 80 us; the launch traced here: 79.8 us
  Pallas kernels  49.8 us (62%)
  starting transfers between devices  19.1 us (24%)
  waiting for transfers between devices  5.5 us (7%)
  other arithmetic  2.93 us (4%)
  between operations  1.57 us (2%)
  local copies, waits for them, and re-layouts  0.85 us (1%)
    pallas_call x13, Pallas kernels, run(): pl.pallas_call(kernel, out_shape=out_shape, in_specs=in_specs, out_specs=...  49.8 us
    ppermute x10, starting transfers between devices, passed(): return lax.ppermute(array, 'row', pairs)  17.4 us
    ppermute x10, waiting for transfers between devices, passed(): return lax.ppermute(array, 'row', pairs)  5.22 us
    ppermute x10, starting transfers between devices, swap(): return lax.ppermute(array, 'row', [(i, i ^ 1) for i in range(2 * chips)])  1.74 us
  transfers between devices with their start and end apart: 20, of which 8 were waited for; matrix products, arithmetic and copies ran while one was open for 1% of the time, Pallas kernels for 60%

profile of v13, /device:TPU:0, one launch (start us, length us, event | category | flops | bytes accessed | tf_op | source)
XLA Modules:
  0.0 79.8 jit_solution(3362636350413119023)
XLA Ops:
  0.6 1.1 %convert_element_type.49.refs_9_.refs_16_.refs_3_ = bf16[1,128,1024]{2,1,0:T(8,128)(2,1)S(1)} convert(f32[1,128,1024]{2,1,0:T(8,128)} %param.8) | non-fusion elementwise | flops 131072 | bytes 786432 | tf_op jit(solution)/shard_map/convert_element_type | solution.py:395
  1.7 0.5 collective-permute-start.2
  2.2 2.7 %collective-permute-start.1 = (bf16[1,128,1024]{2,1,0:T(8,128)(2,1)S(1)}, bf16[1,128,1024]{2,1,0:T(8,128)(2,1)S(1)}, u32[]{:S(2)}, u32[]{:S(2)}) collective-permute-start(bf16[1,128,1024]{2,1,0:T(8,128)(2,1)S(1)} %convert_element_type.49.refs_9_.refs_16_.refs_3_), channel_id=1, source_target_pairs={{0,5},{1,2},{2,1},{3,6},{6,3},{7,10},{10,7},{11,14},{14,11},{15,12... | collective-permute-start | bytes 786440 | tf_op jit(solution)/shard_map/ppermute | solution.py:386
  4.9 0.0 collective-permute-start
  5.6 0.7 dynamic-slice_bitcast_fusion.offs_ref.refs_0_
  6.3 6.5 %shard_map.119 = (f32[8,128]{1,0:T(8,128)S(1)}, bf16[64,16384]{1,0:T(8,128)(2,1)S(1)}, bf16[64,16384]{1,0:T(8,128)(2,1)S(1)}, bf16[64,16384]{1,0:T(8,128)(2,1)S(...) custom-call(s32[16]{0:T(128)S(1)} %dynamic-slice_bitcast_fusion.offs, ...), custom_call_target="tpu_custom_call" | custom-call | flops 2097152 | bytes 16384 | tf_op jit(solution)/shard_map/pallas_call | solution.py:58
  12.7 0.0 collective-permute-done.2.refs_10_.refs_17_.refs_3_
  12.8 0.0 collective-permute-done.1
  12.8 0.0 collective-permute-done
  12.8 2.0 %collective-permute-start.3 = (bf16[2,128,1024]{2,1,0:T(8,128)(2,1)S(1)}, bf16[2,128,1024]{2,1,0:T(8,128)(2,1)S(1)}, u32[]{:S(2)}, u32[]{:S(2)}) collective-permute-start(bf16[2,128,1024]{2,1,0:T(8,128)(2,1)S(1)} %constant_dynamic-update-slice_fusion.refs_18_.refs_4_), channel_id=1, source_target_pairs={{0,2},{1,5},{2,6},{3,1},{6,10},{7,3},{10,14},{11,7},{14,12},{15,11... | collective-permute-start | bytes 1572872 | tf_op jit(solution)/shard_map/ppermute | solution.py:386
  14.8 0.0 collective-permute-start.5
  14.8 7.0 %shard_map.120 = (f32[1024,128]{1,0:T(8,128)S(1)}, bf16[64,16384]{1,0:T(8,128)(2,1)S(1)}, bf16[64,16384]{1,0:T(8,128)(2,1)S(1)}, bf16[64,16384]{1,0:T(8,128)(2,1...) custom-call(s32[16]{0:T(128)S(1)} %dynamic-slice_bitcast_fusion.offs, ...), custom_call_target="tpu_custom_call" | custom-call | flops 33554432 | bytes 262144 | tf_op jit(solution)/shard_map/pallas_call | solution.py:58
  21.8 0.2 collective-permute-done.3.refs_20_.refs_3_
  22.1 1.9 %collective-permute-start.4 = (bf16[2,128,1024]{2,1,0:T(8,128)(2,1)S(1)}, bf16[2,128,1024]{2,1,0:T(8,128)(2,1)S(1)}, u32[]{:S(2)}, u32[]{:S(2)}) collective-permute-start(bf16[2,128,1024]{2,1,0:T(8,128)(2,1)S(1)} %collective-permute-done.3.refs_20_.refs_3_), channel_id=1, source_target_pairs={{0,2},{1,5},{2,6},{3,1},{6,10},{7,3},{10,14},{11,7},{14,12},{15,11... | collective-permute-start | bytes 1572872 | tf_op jit(solution)/shard_map/ppermute | solution.py:386
  24.0 0.6 shard_map.122
  24.6 0.1 collective-permute-start.7
  24.7 0.0 collective-permute-done.5.refs_19_.refs_5_
  24.7 4.5 %shard_map.121.acc_ref = f32[1024,128]{1,0:T(8,128)S(1)} custom-call(s32[16]{0:T(128)S(1)} %dynamic-slice_bitcast_fusion.offs_ref.refs_0_, f32[1024,128]{1,0:T(8,128)S(1)} %get-tuple-element.95.acc_ref, bf16[64,16384]{1,0:T(8,128)(2,1)S(1)} %get-tuple-element.84.refs_1_.refs_0_.refs_3_.refs_4_.refs_6_.refs_7_, ...), custom_call_target="tpu_custom_call" | custom-call | flops 100663296 | bytes 786432 | tf_op jit(solution)/shard_map/pallas_call | solution.py:58
  29.2 2.1 %collective-permute-done.4.refs_17_.refs_5_.refs_3_ = bf16[2,128,1024]{2,1,0:T(8,128)(2,1)S(1)} collective-permute-done((bf16[2,128,1024]{2,1,0:T(8,128)(2,1)S(1)}, bf16[2,128,1024]{2,1,0:T(8,128)(2,1)S(1)}, u32[]{:S(2)}, u32[]{:S(2)}) %collective-permute-start.4) | collective-permute-done | bytes 524320 | tf_op jit(solution)/shard_map/ppermute | solution.py:386
  31.2 0.0 collective-permute-start.8
  31.3 2.0 %collective-permute-start.6 = (bf16[1,128,1024]{2,1,0:T(8,128)(2,1)S(1)}, bf16[1,128,1024]{2,1,0:T(8,128)(2,1)S(1)}, u32[]{:S(2)}, u32[]{:S(2)}) collective-permute-start(bf16[1,128,1024]{2,1,0:T(8,128)(2,1)S(1)} %slice.22), channel_id=1, source_target_pairs={{0,2},{1,5},{2,6},{3,1},{6,10},{7,3},{10,14},{11,7},{14,12},{15,11... | collective-permute-start | bytes 786440 | tf_op jit(solution)/shard_map/ppermute | solution.py:386
  33.3 0.0 collective-permute-done.7.refs_16_.refs_4_
  33.3 0.0 collective-permute-done.8.refs_18_.refs_4_
  33.3 4.0 %shard_map.123.acc_ref = f32[1024,128]{1,0:T(8,128)S(1)} custom-call(s32[16]{0:T(128)S(1)} %dynamic-slice_bitcast_fusion.offs_ref.refs_0_, f32[1024,128]{1,0:T(8,128)S(1)} %shard_map.121.acc_ref, bf16[64,16384]{1,0:T(8,128)(2,1)S(1)} %get-tuple-element.84.refs_1_.refs_0_.refs_3_.refs_4_.refs_6_.refs_7_, ...), custom_call_target="tpu_custom_call" | custom-call | flops 100663296 | bytes 786432 | tf_op jit(solution)/shard_map/pallas_call | solution.py:58
  37.2 0.0 copy-start.3
  37.2 0.0 copy-start.4
  37.2 0.4 collective-permute-done.6.refs_16_.refs_5_
  37.7 0.0 collective-permute-start.9
  37.7 1.3 %shard_map.124.refs_16_ = f32[1024,128]{1,0:T(8,128)S(1)} custom-call(s32[16]{0:T(128)S(1)} %dynamic-slice_bitcast_fusion.offs_ref.refs_0_, f32[1024,128]{1,0:T(8,128)S(1)} %shard_map.123.acc_ref, bf16[64,16384]{1,0:T(8,128)(2,1)S(1)} %get-tuple-element.84.refs_1_.refs_0_.refs_3_.refs_4_.refs_6_.refs_7_, ...), custom_call_target="tpu_custom_call" | custom-call | flops 16777216 | bytes 131072 | tf_op jit(solution)/shard_map/pallas_call | solution.py:58
  39.0 0.3 collective-permute-done.9.x_ref.refs_6_
  39.2 2.3 %shard_map.125 = (f32[128,1024]{1,0:T(8,128)S(1)}, bf16[128,1024]{1,0:T(8,128)(2,1)S(1)}, bf16[1024,128]{1,0:T(8,128)(2,1)S(1)}, f32[16,1024]{1,0:T(8,128)}, f32...) custom-call(s32[16]{0:T(128)S(1)} %dynamic-slice_bitcast_fusion.offs_ref.refs_0_, ...), custom_call_target="tpu_custom_call" | custom-call | flops 33554432 | bytes 262144 | tf_op jit(solution)/shard_map/pallas_call | solution.py:58
  41.5 0.3 collective-permute-start.10
  41.8 1.6 %shard_map.126 = (bf16[2,128,1024]{2,1,0:T(8,128)(2,1)S(1)}, f32[1,128,1024]{2,1,0:T(8,128)S(1)}) custom-call(s32[16]{0:T(128)S(1)} %dynamic-slice_bitcast_fusion.offs_ref.refs_0_, bf16[128,1024]{1,0:T(8,128)(2,1)S(1)} %get-tuple-element.117.refs_1_, bf16[1024,128]{1,0:T(8,128)(2,1)S(1)} %get-tuple-element.118.refs_2_, ...), custom_call_target="tpu_custom_call" | custom-call | flops 50331648 | bytes 393216 | tf_op jit(solution)/shard_map/pallas_call | solution.py:58
  43.4 0.0 collective-permute-done.10
  43.4 0.1 add_convert_fusion.2
  43.5 0.3 collective-permute-start.12
  43.7 1.9 %collective-permute-start.11 = (bf16[1,128,1024]{2,1,0:T(8,128)(2,1)S(1)}, bf16[1,128,1024]{2,1,0:T(8,128)(2,1)S(1)}, u32[]{:S(2)}, u32[]{:S(2)}) collective-permute-start(bf16[1,128,1024]{2,1,0:T(8,128)(2,1)S(1)} %add_convert_fusion.2), channel_id=1, source_target_pairs={{0,2},{1,5},{2,6},{3,1},{6,10},{7,3},{10,14},{11,7},{14,12},{15,11... | collective-permute-start | bytes 786440 | tf_op jit(solution)/shard_map/ppermute | solution.py:386
  45.7 3.8 %shard_map.127 = (bf16[2,128,1024]{2,1,0:T(8,128)(2,1)S(1)}, f32[4,128,1024]{2,1,0:T(8,128)S(1)}, bf16[1024,16384]{1,0:T(8,128)(2,1)}) custom-call(s32[16]{0:T(128)S(1)} %dynamic-slice_bitcast_fusion.offs_ref.refs_0_, bf16[128,1024]{1,0:T(8,128)(2,1)S(1)} %get-tuple-element.117.refs_1_, bf16[1024,128]{1,0:T(8,128)(2,1)S(1)} %get-tuple-element.118.refs_2_, ...), custom_call_target="tpu_custom_call" | custom-call | flops 117440512 | bytes 917504 | tf_op jit(solution)/shard_map/pallas_call | solution.py:58
  49.4 0.7 collective-permute-done.11
  50.1 0.0 collective-permute-done.12
  50.1 0.2 convert_add_fusion
  50.3 0.1 fusion
  50.4 0.1 pad_maximum_fusion
  50.4 2.2 %collective-permute-start.13 = (bf16[2,128,1024]{2,1,0:T(8,128)(2,1)S(1)}, bf16[2,128,1024]{2,1,0:T(8,128)(2,1)S(1)}, u32[]{:S(2)}, u32[]{:S(2)}) collective-permute-start(bf16[2,128,1024]{2,1,0:T(8,128)(2,1)S(1)} %pad_maximum_fusion), channel_id=1, source_target_pairs={{0,2},{1,5},{2,6},{3,1},{6,10},{7,3},{10,14},{11,7},{14,12},{15,11... | collective-permute-start | bytes 1572872 | tf_op jit(solution)/shard_map/ppermute | solution.py:386
  52.6 0.0 collective-permute-start.15
  52.6 6.5 %shard_map.128 = (bf16[2,128,1024]{2,1,0:T(8,128)(2,1)S(1)}, f32[2,128,1024]{2,1,0:T(8,128)S(1)}, bf16[1024,16384]{1,0:T(8,128)(2,1)}) custom-call(s32[16]{0:T(128)S(1)} %dynamic-slice_bitcast_fusion.offs_ref.refs_0_, bf16[128,1024]{1,0:T(8,128)(2,1)S(1)} %get-tuple-element.117.refs_1_, ...), custom_call_target="tpu_custom_call", output_to_operand_aliasing={{2}: (22, {})} | custom-call | flops 150994944 | bytes 1179648 | tf_op jit(solution)/shard_map/pallas_call | solution.py:58
  59.1 0.8 collective-permute-done.13
  59.9 0.0 collective-permute-done.15
  59.9 0.3 add_convert_fusion.1
  60.1 2.0 %collective-permute-start.16 = (bf16[2,128,1024]{2,1,0:T(8,128)(2,1)S(1)}, bf16[2,128,1024]{2,1,0:T(8,128)(2,1)S(1)}, u32[]{:S(2)}, u32[]{:S(2)}) collective-permute-start(bf16[2,128,1024]{2,1,0:T(8,128)(2,1)S(1)} %add_convert_fusion.1), channel_id=1, source_target_pairs={{0,2},{1,5},{2,6},{3,1},{6,10},{7,3},{10,14},{11,7},{14,12},{15,11... | collective-permute-start | bytes 1572872 | tf_op jit(solution)/shard_map/ppermute | solution.py:386
  62.1 0.0 collective-permute-start.14
  62.1 0.6 shard_map.130
  62.8 5.9 %shard_map.129 = (bf16[1,128,1024]{2,1,0:T(8,128)(2,1)S(1)}, f32[1,128,1024]{2,1,0:T(8,128)S(1)}, bf16[1024,16384]{1,0:T(8,128)(2,1)}) custom-call(s32[16]{0:T(128)S(1)} %dynamic-slice_bitcast_fusion.offs_ref.refs_0_, bf16[128,1024]{1,0:T(8,128)(2,1)S(1)} %get-tuple-element.117.refs_1_, ...), custom_call_target="tpu_custom_call", output_to_operand_aliasing={{2}: (22, {})} | custom-call | flops 117440512 | bytes 917504 | tf_op jit(solution)/shard_map/pallas_call | solution.py:58
  68.7 0.6 collective-permute-start.19
  69.2 0.1 collective-permute-done.16
  69.4 0.3 add_convert_fusion
  69.7 1.2 %collective-permute-start.18 = (bf16[1,128,1024]{2,1,0:T(8,128)(2,1)S(1)}, bf16[1,128,1024]{2,1,0:T(8,128)(2,1)S(1)}, u32[]{:S(2)}, u32[]{:S(2)}) collective-permute-start(bf16[1,128,1024]{2,1,0:T(8,128)(2,1)S(1)} %get-tuple-element.155), channel_id=1, source_target_pairs={{0,3},{1,4},{2,7},{3,0},{6,11},{7,2},{10,15},{11,6},{14,13},{15,10... | collective-permute-start | bytes 786440 | tf_op jit(solution)/shard_map/ppermute | solution.py:386
  70.8 1.6 %collective-permute-start.17 = (bf16[1,128,1024]{2,1,0:T(8,128)(2,1)S(1)}, bf16[1,128,1024]{2,1,0:T(8,128)(2,1)S(1)}, u32[]{:S(2)}, u32[]{:S(2)}) collective-permute-start(bf16[1,128,1024]{2,1,0:T(8,128)(2,1)S(1)} %get-tuple-element.156), channel_id=1, source_target_pairs={{0,2},{1,5},{2,6},{3,1},{6,10},{7,3},{10,14},{11,7},{14,12},{15,11... | collective-permute-start | bytes 786440 | tf_op jit(solution)/shard_map/ppermute | solution.py:386
  72.4 5.5 %shard_map.131 = bf16[1024,16384]{1,0:T(8,128)(2,1)} custom-call(s32[16]{0:T(128)S(1)} %dynamic-slice_bitcast_fusion.offs_ref.refs_0_, bf16[128,1024]{1,0:T(8,128)(2,1)S(1)} %get-tuple-element.117.refs_1_, bf16[1024,128]{1,0:T(8,128)(2,1)S(1)} %get-tuple-element.118.refs_2_, ...), custom_call_target="tpu_custom_call", output_to_operand_aliasing={{}: (23, {})} | custom-call | flops 83886080 | bytes 655360 | tf_op jit(solution)/shard_map/pallas_call | solution.py:58
  77.9 0.0 collective-permute-done.19
  77.9 0.1 bitcast_add_fusion
  78.0 0.0 collective-permute-done.18
  78.0 0.9 %collective-permute-done.17 = bf16[1,128,1024]{2,1,0:T(8,128)(2,1)S(1)} collective-permute-done((bf16[1,128,1024]{2,1,0:T(8,128)(2,1)S(1)}, bf16[1,128,1024]{2,1,0:T(8,128)(2,1)S(1)}, u32[]{:S(2)}, u32[]{:S(2)}) %collective-permute-start.17) | collective-permute-done | bytes 262176 | tf_op jit(solution)/shard_map/ppermute | solution.py:386
  78.9 0.9 %fusion.1 = f32[1,128,1024]{2,1,0:T(8,128)} fusion(f32[128,1024]{1,0:T(8,128)S(1)} %bitcast_add_fusion, bf16[1,128,1024]{2,1,0:T(8,128)(2,1)S(1)} %collective-permute-done.18, bf16[1,128,1024]{2,1,0:T(8,128)(2,1)S(1)} %collective-permute-done.17), kind=kLoop, calls=%fused_computation.8 | loop fusion | flops 524288 | bytes 1572864 | tf_op jit(solution)/shard_map/reshape | solution.py:487
  (14 shorter events, 0.1 us)
Async XLA Ops:
  1.7 11.0 %collective-permute-start.2 = (bf16[1,128,1024]{2,1,0:T(8,128)(2,1)S(1)}, bf16[1,128,1024]{2,1,0:T(8,128)(2,1)S(1)}, u32[]{:S(2)}, u32[]{:S(2)}) collective-permute-start(bf16[1,128,1024]{2,1,0:T(8,128)(2,1)S(1)} %convert_element_type.49.refs_9_.refs_16_.refs_3_), channel_id=1, source_target_pairs={{0,1},{1,0},{2,3},{3,2},{4,5},{5,4},{6,7},{7,6},{8,9},{9,8},{10,11... | collective-permute-start | bytes 786440 | tf_op jit(solution)/shard_map/ppermute | solution.py:389
  2.2 10.5 %collective-permute-start.1 = (bf16[1,128,1024]{2,1,0:T(8,128)(2,1)S(1)}, bf16[1,128,1024]{2,1,0:T(8,128)(2,1)S(1)}, u32[]{:S(2)}, u32[]{:S(2)}) collective-permute-start(bf16[1,128,1024]{2,1,0:T(8,128)(2,1)S(1)} %convert_element_type.49.refs_9_.refs_16_.refs_3_), channel_id=1, source_target_pairs={{0,5},{1,2},{2,1},{3,6},{6,3},{7,10},{10,7},{11,14},{14,11},{15,12... | collective-permute-start | bytes 786440 | tf_op jit(solution)/shard_map/ppermute | solution.py:386
  4.9 7.8 %collective-permute-start = (bf16[1,128,1024]{2,1,0:T(8,128)(2,1)S(1)}, bf16[1,128,1024]{2,1,0:T(8,128)(2,1)S(1)}, u32[]{:S(2)}, u32[]{:S(2)}) collective-permute-start(bf16[1,128,1024]{2,1,0:T(8,128)(2,1)S(1)} %convert_element_type.49.refs_9_.refs_16_.refs_3_), channel_id=1, source_target_pairs={{0,2},{1,5},{2,6},{3,1},{6,10},{7,3},{10,14},{11,7},{14,12},{15,11... | collective-permute-start | bytes 786440 | tf_op jit(solution)/shard_map/ppermute | solution.py:386
  12.8 9.2 %collective-permute-start.3 = (bf16[2,128,1024]{2,1,0:T(8,128)(2,1)S(1)}, bf16[2,128,1024]{2,1,0:T(8,128)(2,1)S(1)}, u32[]{:S(2)}, u32[]{:S(2)}) collective-permute-start(bf16[2,128,1024]{2,1,0:T(8,128)(2,1)S(1)} %constant_dynamic-update-slice_fusion.refs_18_.refs_4_), channel_id=1, source_target_pairs={{0,2},{1,5},{2,6},{3,1},{6,10},{7,3},{10,14},{11,7},{14,12},{15,11... | collective-permute-start | bytes 1572872 | tf_op jit(solution)/shard_map/ppermute | solution.py:386
  14.8 9.9 %collective-permute-start.5 = (bf16[2,128,1024]{2,1,0:T(8,128)(2,1)S(1)}, bf16[2,128,1024]{2,1,0:T(8,128)(2,1)S(1)}, u32[]{:S(2)}, u32[]{:S(2)}) collective-permute-start(bf16[2,128,1024]{2,1,0:T(8,128)(2,1)S(1)} %constant_dynamic-update-slice_fusion.refs_18_.refs_4_), channel_id=1, source_target_pairs={{0,1},{1,0},{2,3},{3,2},{4,5},{5,4},{6,7},{7,6},{8,9},{9,8},{10,11... | collective-permute-start | bytes 1572872 | tf_op jit(solution)/shard_map/ppermute | solution.py:389
  14.8 9.2 %copy-start = (f32[1,128,1024]{2,1,0:T(8,128)S(1)}, f32[1,128,1024]{2,1,0:T(8,128)}, u32[]{:S(2)}) copy-start(f32[1,128,1024]{2,1,0:T(8,128)} %param.8) | copy-start | bytes 1572868
  14.8 9.2 %copy-start.1 = (f32[128,128]{1,0:T(8,128)S(1)}, f32[128,128]{1,0:T(8,128)}, u32[]{:S(2)}) copy-start(f32[128,128]{1,0:T(8,128)} %constant.13.clone.cheb_ref) | copy-start | bytes 196612
  14.8 9.2 %copy-start.2 = (f32[16,1024]{1,0:T(8,128)S(1)}, f32[16,1024]{1,0:T(8,128)}, u32[]{:S(2)}) copy-start(f32[16,1024]{1,0:T(8,128)} %pert_ref.1) | copy-start | bytes 196612
  22.1 9.2 %collective-permute-start.4 = (bf16[2,128,1024]{2,1,0:T(8,128)(2,1)S(1)}, bf16[2,128,1024]{2,1,0:T(8,128)(2,1)S(1)}, u32[]{:S(2)}, u32[]{:S(2)}) collective-permute-start(bf16[2,128,1024]{2,1,0:T(8,128)(2,1)S(1)} %collective-permute-done.3.refs_20_.refs_3_), channel_id=1, source_target_pairs={{0,2},{1,5},{2,6},{3,1},{6,10},{7,3},{10,14},{11,7},{14,12},{15,11... | collective-permute-start | bytes 1572872 | tf_op jit(solution)/shard_map/ppermute | solution.py:386
  24.6 8.7 %collective-permute-start.7 = (bf16[2,128,1024]{2,1,0:T(8,128)(2,1)S(1)}, bf16[2,128,1024]{2,1,0:T(8,128)(2,1)S(1)}, u32[]{:S(2)}, u32[]{:S(2)}) collective-permute-start(bf16[2,128,1024]{2,1,0:T(8,128)(2,1)S(1)} %collective-permute-done.3.refs_20_.refs_3_), channel_id=1, source_target_pairs={{0,1},{1,0},{2,3},{3,2},{4,5},{5,4},{6,7},{7,6},{8,9},{9,8},{10,11... | collective-permute-start | bytes 1572872 | tf_op jit(solution)/shard_map/ppermute | solution.py:389
  31.2 2.0 %collective-permute-start.8 = (bf16[2,128,1024]{2,1,0:T(8,128)(2,1)S(1)}, bf16[2,128,1024]{2,1,0:T(8,128)(2,1)S(1)}, u32[]{:S(2)}, u32[]{:S(2)}) collective-permute-start(bf16[2,128,1024]{2,1,0:T(8,128)(2,1)S(1)} %collective-permute-done.4.refs_17_.refs_5_.refs_3_), channel_id=1, source_target_pairs={{0,1},{1,0},{2,3},{3,2},{4,5},{5,4},{6,7},{7,6},{8,9},{9,8},{10,11... | collective-permute-start | bytes 1572872 | tf_op jit(solution)/shard_map/ppermute | solution.py:389
  31.3 6.4 %collective-permute-start.6 = (bf16[1,128,1024]{2,1,0:T(8,128)(2,1)S(1)}, bf16[1,128,1024]{2,1,0:T(8,128)(2,1)S(1)}, u32[]{:S(2)}, u32[]{:S(2)}) collective-permute-start(bf16[1,128,1024]{2,1,0:T(8,128)(2,1)S(1)} %slice.22), channel_id=1, source_target_pairs={{0,2},{1,5},{2,6},{3,1},{6,10},{7,3},{10,14},{11,7},{14,12},{15,11... | collective-permute-start | bytes 786440 | tf_op jit(solution)/shard_map/ppermute | solution.py:386
  37.2 2.0 %copy-start.3 = (f32[1024]{0:T(1024)S(1)}, f32[1024]{0:T(1024)}, u32[]{:S(2)}) copy-start(f32[1024]{0:T(1024)} %param.12) | copy-start | bytes 12292
  37.2 2.0 %copy-start.4 = (f32[1024]{0:T(1024)S(1)}, f32[1024]{0:T(1024)}, u32[]{:S(2)}) copy-start(f32[1024]{0:T(1024)} %param.11) | copy-start | bytes 12292
  37.7 1.5 %collective-permute-start.9 = (bf16[1,128,1024]{2,1,0:T(8,128)(2,1)S(1)}, bf16[1,128,1024]{2,1,0:T(8,128)(2,1)S(1)}, u32[]{:S(2)}, u32[]{:S(2)}) collective-permute-start(bf16[1,128,1024]{2,1,0:T(8,128)(2,1)S(1)} %collective-permute-done.6.refs_16_.refs_5_), channel_id=1, source_target_pairs={{0,1},{1,0},{2,3},{3,2},{4,5},{5,4},{6,7},{7,6},{8,9},{9,8},{10,11... | collective-permute-start | bytes 786440 | tf_op jit(solution)/shard_map/ppermute | solution.py:389
  41.5 1.9 %collective-permute-start.10 = (bf16[1,128,1024]{2,1,0:T(8,128)(2,1)S(1)}, bf16[1,128,1024]{2,1,0:T(8,128)(2,1)S(1)}, u32[]{:S(2)}, u32[]{:S(2)}) collective-permute-start(bf16[1,128,1024]{2,1,0:T(8,128)(2,1)S(1)} %get-tuple-element.120), channel_id=1, source_target_pairs={{0,1},{1,0},{2,3},{3,2},{4,5},{5,4},{6,7},{7,6},{8,9},{9,8},{10,11... | collective-permute-start | bytes 786440 | tf_op jit(solution)/shard_map/ppermute | solution.py:389
  43.5 6.6 %collective-permute-start.12 = (bf16[2,128,1024]{2,1,0:T(8,128)(2,1)S(1)}, bf16[2,128,1024]{2,1,0:T(8,128)(2,1)S(1)}, u32[]{:S(2)}, u32[]{:S(2)}) collective-permute-start(bf16[2,128,1024]{2,1,0:T(8,128)(2,1)S(1)} %get-tuple-element.126), channel_id=1, source_target_pairs={{0,1},{1,0},{2,3},{3,2},{4,5},{5,4},{6,7},{7,6},{8,9},{9,8},{10,11... | collective-permute-start | bytes 1572872 | tf_op jit(solution)/shard_map/ppermute | solution.py:389
  43.7 6.4 %collective-permute-start.11 = (bf16[1,128,1024]{2,1,0:T(8,128)(2,1)S(1)}, bf16[1,128,1024]{2,1,0:T(8,128)(2,1)S(1)}, u32[]{:S(2)}, u32[]{:S(2)}) collective-permute-start(bf16[1,128,1024]{2,1,0:T(8,128)(2,1)S(1)} %add_convert_fusion.2), channel_id=1, source_target_pairs={{0,2},{1,5},{2,6},{3,1},{6,10},{7,3},{10,14},{11,7},{14,12},{15,11... | collective-permute-start | bytes 786440 | tf_op jit(solution)/shard_map/ppermute | solution.py:386
  50.4 9.4 %collective-permute-start.13 = (bf16[2,128,1024]{2,1,0:T(8,128)(2,1)S(1)}, bf16[2,128,1024]{2,1,0:T(8,128)(2,1)S(1)}, u32[]{:S(2)}, u32[]{:S(2)}) collective-permute-start(bf16[2,128,1024]{2,1,0:T(8,128)(2,1)S(1)} %pad_maximum_fusion), channel_id=1, source_target_pairs={{0,2},{1,5},{2,6},{3,1},{6,10},{7,3},{10,14},{11,7},{14,12},{15,11... | collective-permute-start | bytes 1572872 | tf_op jit(solution)/shard_map/ppermute | solution.py:386
  52.6 7.3 %collective-permute-start.15 = (bf16[2,128,1024]{2,1,0:T(8,128)(2,1)S(1)}, bf16[2,128,1024]{2,1,0:T(8,128)(2,1)S(1)}, u32[]{:S(2)}, u32[]{:S(2)}) collective-permute-start(bf16[2,128,1024]{2,1,0:T(8,128)(2,1)S(1)} %get-tuple-element.134), channel_id=1, source_target_pairs={{0,1},{1,0},{2,3},{3,2},{4,5},{5,4},{6,7},{7,6},{8,9},{9,8},{10,11... | collective-permute-start | bytes 1572872 | tf_op jit(solution)/shard_map/ppermute | solution.py:389
  60.1 9.2 %collective-permute-start.16 = (bf16[2,128,1024]{2,1,0:T(8,128)(2,1)S(1)}, bf16[2,128,1024]{2,1,0:T(8,128)(2,1)S(1)}, u32[]{:S(2)}, u32[]{:S(2)}) collective-permute-start(bf16[2,128,1024]{2,1,0:T(8,128)(2,1)S(1)} %add_convert_fusion.1), channel_id=1, source_target_pairs={{0,2},{1,5},{2,6},{3,1},{6,10},{7,3},{10,14},{11,7},{14,12},{15,11... | collective-permute-start | bytes 1572872 | tf_op jit(solution)/shard_map/ppermute | solution.py:386
  62.1 7.3 %collective-permute-start.14 = (bf16[2,128,1024]{2,1,0:T(8,128)(2,1)S(1)}, bf16[2,128,1024]{2,1,0:T(8,128)(2,1)S(1)}, u32[]{:S(2)}, u32[]{:S(2)}) collective-permute-start(bf16[2,128,1024]{2,1,0:T(8,128)(2,1)S(1)} %get-tuple-element.133), channel_id=1, source_target_pairs={{0,1},{1,0},{2,3},{3,2},{4,5},{5,4},{6,7},{7,6},{8,9},{9,8},{10,11... | collective-permute-start | bytes 1572872 | tf_op jit(solution)/shard_map/ppermute | solution.py:389
  68.7 9.2 %collective-permute-start.19 = (bf16[1,128,1024]{2,1,0:T(8,128)(2,1)S(1)}, bf16[1,128,1024]{2,1,0:T(8,128)(2,1)S(1)}, u32[]{:S(2)}, u32[]{:S(2)}) collective-permute-start(bf16[1,128,1024]{2,1,0:T(8,128)(2,1)S(1)} %get-tuple-element.148), channel_id=1, source_target_pairs={{0,1},{1,0},{2,3},{3,2},{4,5},{5,4},{6,7},{7,6},{8,9},{9,8},{10,11... | collective-permute-start | bytes 786440 | tf_op jit(solution)/shard_map/ppermute | solution.py:389
  69.7 8.3 %collective-permute-start.18 = (bf16[1,128,1024]{2,1,0:T(8,128)(2,1)S(1)}, bf16[1,128,1024]{2,1,0:T(8,128)(2,1)S(1)}, u32[]{:S(2)}, u32[]{:S(2)}) collective-permute-start(bf16[1,128,1024]{2,1,0:T(8,128)(2,1)S(1)} %get-tuple-element.155), channel_id=1, source_target_pairs={{0,3},{1,4},{2,7},{3,0},{6,11},{7,2},{10,15},{11,6},{14,13},{15,10... | collective-permute-start | bytes 786440 | tf_op jit(solution)/shard_map/ppermute | solution.py:386
  70.8 8.1 %collective-permute-start.17 = (bf16[1,128,1024]{2,1,0:T(8,128)(2,1)S(1)}, bf16[1,128,1024]{2,1,0:T(8,128)(2,1)S(1)}, u32[]{:S(2)}, u32[]{:S(2)}) collective-permute-start(bf16[1,128,1024]{2,1,0:T(8,128)(2,1)S(1)} %get-tuple-element.156), channel_id=1, source_target_pairs={{0,2},{1,5},{2,6},{3,1},{6,10},{7,3},{10,14},{11,7},{14,12},{15,11... | collective-permute-start | bytes 786440 | tf_op jit(solution)/shard_map/ppermute | solution.py:386

commit v14 on v13

--- a/solution.py
+++ b/solution.py
@@ -99,7 +99,7 @@
     return arrays, found
 
 
-def load_kernel(offs_ref, perts_ref, w_ref, mark_ref, *refs):
+def load_kernel(offs_ref, w_ref, mark_ref, *refs):
     mark_ref[...] = jnp.zeros_like(mark_ref)
     copies = band_copies(w_ref, refs[:-1], refs[-1], 0)
     for copy in copies:
@@ -112,14 +112,14 @@
     return [pltpu.VMEM((weights.shape[0] // BANDS, weights.shape[1]), weights.dtype)] * count
 
 
-def load_first(offs, perts, weights, count):
+def load_first(offs, weights, count):
     mark, *bands = call(
         load_kernel,
         [jax.ShapeDtypeStruct((8, 128), jnp.float32)] + band_shapes(count, weights),
         [VMEM_REF] * (1 + count),
         [pltpu.SemaphoreType.DMA((count,))],
         cost(1, 128, 128, 1024),
-    )([offs, perts, weights], [SMEM_REF, SMEM_REF, HBM_REF])
+    )([offs, weights], [SMEM_REF, HBM_REF])
     return mark, bands
 
 
@@ -179,11 +179,11 @@
 
 
 def deriv_kernel(perts_ref, cheb_ref, states_ref, pert_ref, deriv_ref, drive_ref, chosen_ref):
-    pert = perts_ref[0]
     deriv_ref[...] = cheb_dot(False, cheb_ref, states_ref)
-    drive_ref[...] = pert_ref[pl.ds(pert, 1), :]
     rows = lax.broadcasted_iota(jnp.int32, chosen_ref.shape, 0)
-    chosen_ref[...] = (rows == pert).astype(jnp.float32)
+    chosen = rows == jnp.broadcast_to(perts_ref[...], chosen_ref.shape)
+    drive_ref[...] = jnp.sum(jnp.where(chosen, pert_ref[...], 0.0), axis=0, keepdims=True)
+    chosen_ref[...] = jnp.where(chosen, 1.0, 0.0)
 
 
 def derivatives(perts, cheb, states, pert_table):
@@ -197,7 +197,7 @@
         [VMEM_REF] * 3,
         [],
         cost(1, *states.shape, states.shape[0]),
-    )([perts, cheb, states, pert_table], [SMEM_REF] + [VMEM_REF] * 3)
+    )([perts.reshape(1, 1), cheb, states, pert_table], [VMEM_REF] * 4)
 
 
 def local_kernel(cheb_ref, resid_ref, decay_ref, out_ref):
@@ -396,7 +396,7 @@
 
     near, over = passed(xb), passed(xb, -1, 1)
     other = swap(xb)
-    mark, bands = load_first(offs, perts, weights, LOADS[0])
+    mark, bands = load_first(offs, weights, LOADS[0])
     near, over, other, mark = gate((near, over, other, mark))
     x = {(0, 0): (xb, 0), (0, 1): (other, 0)}
     flow = jnp.concatenate([near, over], axis=0)

time: 80 us -> 79.4 us (level)
  no operation moved by 1% of the time
where the time goes in v14:
time: 79.4 us; the launch traced here: 79.2 us
  Pallas kernels  49.8 us (63%)
  starting transfers between devices  19.2 us (24%)
  waiting for transfers between devices  4.81 us (6%)
  other arithmetic  2.93 us (4%)
  between operations  1.59 us (2%)
  local copies, waits for them, and re-layouts  0.84 us (1%)
    pallas_call x13, Pallas kernels, run(): pl.pallas_call(kernel, out_shape=out_shape, in_specs=in_specs, out_specs=...  49.8 us
    ppermute x10, starting transfers between devices, passed(): return lax.ppermute(array, 'row', pairs)  17.4 us
    ppermute x10, waiting for transfers between devices, passed(): return lax.ppermute(array, 'row', pairs)  4.52 us
    ppermute x10, starting transfers between devices, swap(): return lax.ppermute(array, 'row', [(i, i ^ 1) for i in range(2 * chips)])  1.76 us
  transfers between devices with their start and end apart: 20, of which 8 were waited for; matrix products, arithmetic and copies ran while one was open for 1% of the time, Pallas kernels for 60%

profile of v14, /device:TPU:0, one launch (start us, length us, event | category | flops | bytes accessed | tf_op | source)
XLA Modules:
  0.0 79.2 jit_solution(12069552418153069911)
XLA Ops:
  0.6 1.1 %convert_element_type.49.refs_9_.refs_16_.refs_3_ = bf16[1,128,1024]{2,1,0:T(8,128)(2,1)S(1)} convert(f32[1,128,1024]{2,1,0:T(8,128)} %param.8) | non-fusion elementwise | flops 131072 | bytes 786432 | tf_op jit(solution)/shard_map/convert_element_type | solution.py:395
  1.7 0.5 collective-permute-start.2
  2.2 2.7 %collective-permute-start.1 = (bf16[1,128,1024]{2,1,0:T(8,128)(2,1)S(1)}, bf16[1,128,1024]{2,1,0:T(8,128)(2,1)S(1)}, u32[]{:S(2)}, u32[]{:S(2)}) collective-permute-start(bf16[1,128,1024]{2,1,0:T(8,128)(2,1)S(1)} %convert_element_type.49.refs_9_.refs_16_.refs_3_), channel_id=1, source_target_pairs={{0,5},{1,2},{2,1},{3,6},{6,3},{7,10},{10,7},{11,14},{14,11},{15,12... | collective-permute-start | bytes 786440 | tf_op jit(solution)/shard_map/ppermute | solution.py:386
  4.9 0.0 collective-permute-start
  4.9 0.7 dynamic-slice_bitcast_fusion.offs_ref.refs_0_
  5.6 6.5 %shard_map.119 = (f32[8,128]{1,0:T(8,128)S(1)}, bf16[64,16384]{1,0:T(8,128)(2,1)S(1)}, bf16[64,16384]{1,0:T(8,128)(2,1)S(1)}, bf16[64,16384]{1,0:T(8,128)(2,1)S(...) custom-call(s32[16]{0:T(128)S(1)} %dynamic-slice_bitcast_fusion.offs, ...), custom_call_target="tpu_custom_call" | custom-call | flops 2097152 | bytes 16384 | tf_op jit(solution)/shard_map/pallas_call | solution.py:58
  12.1 0.0 collective-permute-done.2.refs_10_.refs_17_.refs_3_
  12.1 0.0 collective-permute-done.1
  12.1 0.0 collective-permute-done
  12.2 2.0 %collective-permute-start.3 = (bf16[2,128,1024]{2,1,0:T(8,128)(2,1)S(1)}, bf16[2,128,1024]{2,1,0:T(8,128)(2,1)S(1)}, u32[]{:S(2)}, u32[]{:S(2)}) collective-permute-start(bf16[2,128,1024]{2,1,0:T(8,128)(2,1)S(1)} %constant_dynamic-update-slice_fusion.refs_18_.refs_4_), channel_id=1, source_target_pairs={{0,2},{1,5},{2,6},{3,1},{6,10},{7,3},{10,14},{11,7},{14,12},{15,11... | collective-permute-start | bytes 1572872 | tf_op jit(solution)/shard_map/ppermute | solution.py:386
  14.2 0.0 collective-permute-start.5
  14.2 7.0 %shard_map.120 = (f32[1024,128]{1,0:T(8,128)S(1)}, bf16[64,16384]{1,0:T(8,128)(2,1)S(1)}, bf16[64,16384]{1,0:T(8,128)(2,1)S(1)}, bf16[64,16384]{1,0:T(8,128)(2,1...) custom-call(s32[16]{0:T(128)S(1)} %dynamic-slice_bitcast_fusion.offs, ...), custom_call_target="tpu_custom_call" | custom-call | flops 33554432 | bytes 262144 | tf_op jit(solution)/shard_map/pallas_call | solution.py:58
  21.2 0.2 collective-permute-done.3.refs_20_.refs_3_
  21.4 1.9 %collective-permute-start.4 = (bf16[2,128,1024]{2,1,0:T(8,128)(2,1)S(1)}, bf16[2,128,1024]{2,1,0:T(8,128)(2,1)S(1)}, u32[]{:S(2)}, u32[]{:S(2)}) collective-permute-start(bf16[2,128,1024]{2,1,0:T(8,128)(2,1)S(1)} %collective-permute-done.3.refs_20_.refs_3_), channel_id=1, source_target_pairs={{0,2},{1,5},{2,6},{3,1},{6,10},{7,3},{10,14},{11,7},{14,12},{15,11... | collective-permute-start | bytes 1572872 | tf_op jit(solution)/shard_map/ppermute | solution.py:386
  24.0 0.6 shard_map.122
  24.6 0.1 collective-permute-start.7
  24.7 0.0 collective-permute-done.5.refs_19_.refs_5_
  24.7 4.5 %shard_map.121.acc_ref = f32[1024,128]{1,0:T(8,128)S(1)} custom-call(s32[16]{0:T(128)S(1)} %dynamic-slice_bitcast_fusion.offs_ref.refs_0_, f32[1024,128]{1,0:T(8,128)S(1)} %get-tuple-element.95.acc_ref, bf16[64,16384]{1,0:T(8,128)(2,1)S(1)} %get-tuple-element.84.refs_1_.refs_0_.refs_3_.refs_4_.refs_6_.refs_7_, ...), custom_call_target="tpu_custom_call" | custom-call | flops 100663296 | bytes 786432 | tf_op jit(solution)/shard_map/pallas_call | solution.py:58
  29.2 1.4 %collective-permute-done.4.refs_17_.refs_5_.refs_3_ = bf16[2,128,1024]{2,1,0:T(8,128)(2,1)S(1)} collective-permute-done((bf16[2,128,1024]{2,1,0:T(8,128)(2,1)S(1)}, bf16[2,128,1024]{2,1,0:T(8,128)(2,1)S(1)}, u32[]{:S(2)}, u32[]{:S(2)}) %collective-permute-start.4) | collective-permute-done | bytes 524320 | tf_op jit(solution)/shard_map/ppermute | solution.py:386
  30.6 0.0 collective-permute-start.8
  30.6 2.0 %collective-permute-start.6 = (bf16[1,128,1024]{2,1,0:T(8,128)(2,1)S(1)}, bf16[1,128,1024]{2,1,0:T(8,128)(2,1)S(1)}, u32[]{:S(2)}, u32[]{:S(2)}) collective-permute-start(bf16[1,128,1024]{2,1,0:T(8,128)(2,1)S(1)} %slice.22), channel_id=1, source_target_pairs={{0,2},{1,5},{2,6},{3,1},{6,10},{7,3},{10,14},{11,7},{14,12},{15,11... | collective-permute-start | bytes 786440 | tf_op jit(solution)/shard_map/ppermute | solution.py:386
  32.6 0.0 collective-permute-done.7.refs_16_.refs_4_
  32.6 0.0 collective-permute-done.8.refs_18_.refs_4_
  32.6 4.0 %shard_map.123.acc_ref = f32[1024,128]{1,0:T(8,128)S(1)} custom-call(s32[16]{0:T(128)S(1)} %dynamic-slice_bitcast_fusion.offs_ref.refs_0_, f32[1024,128]{1,0:T(8,128)S(1)} %shard_map.121.acc_ref, bf16[64,16384]{1,0:T(8,128)(2,1)S(1)} %get-tuple-element.84.refs_1_.refs_0_.refs_3_.refs_4_.refs_6_.refs_7_, ...), custom_call_target="tpu_custom_call" | custom-call | flops 100663296 | bytes 786432 | tf_op jit(solution)/shard_map/pallas_call | solution.py:58
  36.6 0.0 copy-start.3
  36.6 0.0 copy-start.4
  36.6 0.4 collective-permute-done.6.refs_16_.refs_5_
  37.0 0.0 collective-permute-start.9
  37.0 1.3 %shard_map.124.refs_16_ = f32[1024,128]{1,0:T(8,128)S(1)} custom-call(s32[16]{0:T(128)S(1)} %dynamic-slice_bitcast_fusion.offs_ref.refs_0_, f32[1024,128]{1,0:T(8,128)S(1)} %shard_map.123.acc_ref, bf16[64,16384]{1,0:T(8,128)(2,1)S(1)} %get-tuple-element.84.refs_1_.refs_0_.refs_3_.refs_4_.refs_6_.refs_7_, ...), custom_call_target="tpu_custom_call" | custom-call | flops 16777216 | bytes 131072 | tf_op jit(solution)/shard_map/pallas_call | solution.py:58
  38.3 0.3 collective-permute-done.9.x_ref.refs_6_
  38.6 2.3 %shard_map.125 = (f32[128,1024]{1,0:T(8,128)S(1)}, bf16[128,1024]{1,0:T(8,128)(2,1)S(1)}, bf16[1024,128]{1,0:T(8,128)(2,1)S(1)}, f32[16,1024]{1,0:T(8,128)}, f32...) custom-call(s32[16]{0:T(128)S(1)} %dynamic-slice_bitcast_fusion.offs_ref.refs_0_, ...), custom_call_target="tpu_custom_call" | custom-call | flops 33554432 | bytes 262144 | tf_op jit(solution)/shard_map/pallas_call | solution.py:58
  40.9 0.3 collective-permute-start.10
  41.2 1.5 %shard_map.126 = (bf16[2,128,1024]{2,1,0:T(8,128)(2,1)S(1)}, f32[1,128,1024]{2,1,0:T(8,128)S(1)}) custom-call(s32[16]{0:T(128)S(1)} %dynamic-slice_bitcast_fusion.offs_ref.refs_0_, bf16[128,1024]{1,0:T(8,128)(2,1)S(1)} %get-tuple-element.117.refs_1_, bf16[1024,128]{1,0:T(8,128)(2,1)S(1)} %get-tuple-element.118.refs_2_, ...), custom_call_target="tpu_custom_call" | custom-call | flops 50331648 | bytes 393216 | tf_op jit(solution)/shard_map/pallas_call | solution.py:58
  42.7 0.0 collective-permute-done.10
  42.7 0.1 add_convert_fusion.2
  42.8 0.3 collective-permute-start.12
  43.1 1.9 %collective-permute-start.11 = (bf16[1,128,1024]{2,1,0:T(8,128)(2,1)S(1)}, bf16[1,128,1024]{2,1,0:T(8,128)(2,1)S(1)}, u32[]{:S(2)}, u32[]{:S(2)}) collective-permute-start(bf16[1,128,1024]{2,1,0:T(8,128)(2,1)S(1)} %add_convert_fusion.2), channel_id=1, source_target_pairs={{0,2},{1,5},{2,6},{3,1},{6,10},{7,3},{10,14},{11,7},{14,12},{15,11... | collective-permute-start | bytes 786440 | tf_op jit(solution)/shard_map/ppermute | solution.py:386
  45.0 3.8 %shard_map.127 = (bf16[2,128,1024]{2,1,0:T(8,128)(2,1)S(1)}, f32[4,128,1024]{2,1,0:T(8,128)S(1)}, bf16[1024,16384]{1,0:T(8,128)(2,1)}) custom-call(s32[16]{0:T(128)S(1)} %dynamic-slice_bitcast_fusion.offs_ref.refs_0_, bf16[128,1024]{1,0:T(8,128)(2,1)S(1)} %get-tuple-element.117.refs_1_, bf16[1024,128]{1,0:T(8,128)(2,1)S(1)} %get-tuple-element.118.refs_2_, ...), custom_call_target="tpu_custom_call" | custom-call | flops 117440512 | bytes 917504 | tf_op jit(solution)/shard_map/pallas_call | solution.py:58
  48.8 0.7 collective-permute-done.11
  49.4 0.0 collective-permute-done.12
  49.4 0.2 convert_add_fusion
  49.7 0.1 fusion
  49.7 0.1 pad_maximum_fusion
  49.8 2.2 %collective-permute-start.13 = (bf16[2,128,1024]{2,1,0:T(8,128)(2,1)S(1)}, bf16[2,128,1024]{2,1,0:T(8,128)(2,1)S(1)}, u32[]{:S(2)}, u32[]{:S(2)}) collective-permute-start(bf16[2,128,1024]{2,1,0:T(8,128)(2,1)S(1)} %pad_maximum_fusion), channel_id=1, source_target_pairs={{0,2},{1,5},{2,6},{3,1},{6,10},{7,3},{10,14},{11,7},{14,12},{15,11... | collective-permute-start | bytes 1572872 | tf_op jit(solution)/shard_map/ppermute | solution.py:386
  52.0 0.0 collective-permute-start.15
  52.0 6.5 %shard_map.128 = (bf16[2,128,1024]{2,1,0:T(8,128)(2,1)S(1)}, f32[2,128,1024]{2,1,0:T(8,128)S(1)}, bf16[1024,16384]{1,0:T(8,128)(2,1)}) custom-call(s32[16]{0:T(128)S(1)} %dynamic-slice_bitcast_fusion.offs_ref.refs_0_, bf16[128,1024]{1,0:T(8,128)(2,1)S(1)} %get-tuple-element.117.refs_1_, ...), custom_call_target="tpu_custom_call", output_to_operand_aliasing={{2}: (22, {})} | custom-call | flops 150994944 | bytes 1179648 | tf_op jit(solution)/shard_map/pallas_call | solution.py:58
  58.4 0.8 collective-permute-done.13
  59.2 0.0 collective-permute-done.15
  59.2 0.3 add_convert_fusion.1
  59.5 2.0 %collective-permute-start.16 = (bf16[2,128,1024]{2,1,0:T(8,128)(2,1)S(1)}, bf16[2,128,1024]{2,1,0:T(8,128)(2,1)S(1)}, u32[]{:S(2)}, u32[]{:S(2)}) collective-permute-start(bf16[2,128,1024]{2,1,0:T(8,128)(2,1)S(1)} %add_convert_fusion.1), channel_id=1, source_target_pairs={{0,2},{1,5},{2,6},{3,1},{6,10},{7,3},{10,14},{11,7},{14,12},{15,11... | collective-permute-start | bytes 1572872 | tf_op jit(solution)/shard_map/ppermute | solution.py:386
  61.5 0.0 collective-permute-start.14
  61.5 0.6 shard_map.130
  62.1 5.9 %shard_map.129 = (bf16[1,128,1024]{2,1,0:T(8,128)(2,1)S(1)}, f32[1,128,1024]{2,1,0:T(8,128)S(1)}, bf16[1024,16384]{1,0:T(8,128)(2,1)}) custom-call(s32[16]{0:T(128)S(1)} %dynamic-slice_bitcast_fusion.offs_ref.refs_0_, bf16[128,1024]{1,0:T(8,128)(2,1)S(1)} %get-tuple-element.117.refs_1_, ...), custom_call_target="tpu_custom_call", output_to_operand_aliasing={{2}: (22, {})} | custom-call | flops 117440512 | bytes 917504 | tf_op jit(solution)/shard_map/pallas_call | solution.py:58
  68.0 0.6 collective-permute-start.19
  68.6 0.1 collective-permute-done.16
  68.7 0.0 collective-permute-done.14
  68.7 0.3 add_convert_fusion
  69.0 1.2 %collective-permute-start.18 = (bf16[1,128,1024]{2,1,0:T(8,128)(2,1)S(1)}, bf16[1,128,1024]{2,1,0:T(8,128)(2,1)S(1)}, u32[]{:S(2)}, u32[]{:S(2)}) collective-permute-start(bf16[1,128,1024]{2,1,0:T(8,128)(2,1)S(1)} %get-tuple-element.155), channel_id=1, source_target_pairs={{0,3},{1,4},{2,7},{3,0},{6,11},{7,2},{10,15},{11,6},{14,13},{15,10... | collective-permute-start | bytes 786440 | tf_op jit(solution)/shard_map/ppermute | solution.py:386
  70.2 1.6 %collective-permute-start.17 = (bf16[1,128,1024]{2,1,0:T(8,128)(2,1)S(1)}, bf16[1,128,1024]{2,1,0:T(8,128)(2,1)S(1)}, u32[]{:S(2)}, u32[]{:S(2)}) collective-permute-start(bf16[1,128,1024]{2,1,0:T(8,128)(2,1)S(1)} %get-tuple-element.156), channel_id=1, source_target_pairs={{0,2},{1,5},{2,6},{3,1},{6,10},{7,3},{10,14},{11,7},{14,12},{15,11... | collective-permute-start | bytes 786440 | tf_op jit(solution)/shard_map/ppermute | solution.py:386
  71.8 5.5 %shard_map.131 = bf16[1024,16384]{1,0:T(8,128)(2,1)} custom-call(s32[16]{0:T(128)S(1)} %dynamic-slice_bitcast_fusion.offs_ref.refs_0_, bf16[128,1024]{1,0:T(8,128)(2,1)S(1)} %get-tuple-element.117.refs_1_, bf16[1024,128]{1,0:T(8,128)(2,1)S(1)} %get-tuple-element.118.refs_2_, ...), custom_call_target="tpu_custom_call", output_to_operand_aliasing={{}: (23, {})} | custom-call | flops 83886080 | bytes 655360 | tf_op jit(solution)/shard_map/pallas_call | solution.py:58
  77.2 0.1 bitcast_add_fusion
  77.4 0.0 collective-permute-done.18
  77.4 0.9 %collective-permute-done.17 = bf16[1,128,1024]{2,1,0:T(8,128)(2,1)S(1)} collective-permute-done((bf16[1,128,1024]{2,1,0:T(8,128)(2,1)S(1)}, bf16[1,128,1024]{2,1,0:T(8,128)(2,1)S(1)}, u32[]{:S(2)}, u32[]{:S(2)}) %collective-permute-start.17) | collective-permute-done | bytes 262176 | tf_op jit(solution)/shard_map/ppermute | solution.py:386
  78.3 0.9 %fusion.1 = f32[1,128,1024]{2,1,0:T(8,128)} fusion(f32[128,1024]{1,0:T(8,128)S(1)} %bitcast_add_fusion, bf16[1,128,1024]{2,1,0:T(8,128)(2,1)S(1)} %collective-permute-done.18, bf16[1,128,1024]{2,1,0:T(8,128)(2,1)S(1)} %collective-permute-done.17), kind=kLoop, calls=%fused_computation.8 | loop fusion | flops 524288 | bytes 1572864 | tf_op jit(solution)/shard_map/reshape | solution.py:487
  (14 shorter events, 0.1 us)
Async XLA Ops:
  1.7 10.4 %collective-permute-start.2 = (bf16[1,128,1024]{2,1,0:T(8,128)(2,1)S(1)}, bf16[1,128,1024]{2,1,0:T(8,128)(2,1)S(1)}, u32[]{:S(2)}, u32[]{:S(2)}) collective-permute-start(bf16[1,128,1024]{2,1,0:T(8,128)(2,1)S(1)} %convert_element_type.49.refs_9_.refs_16_.refs_3_), channel_id=1, source_target_pairs={{0,1},{1,0},{2,3},{3,2},{4,5},{5,4},{6,7},{7,6},{8,9},{9,8},{10,11... | collective-permute-start | bytes 786440 | tf_op jit(solution)/shard_map/ppermute | solution.py:389
  2.2 9.9 %collective-permute-start.1 = (bf16[1,128,1024]{2,1,0:T(8,128)(2,1)S(1)}, bf16[1,128,1024]{2,1,0:T(8,128)(2,1)S(1)}, u32[]{:S(2)}, u32[]{:S(2)}) collective-permute-start(bf16[1,128,1024]{2,1,0:T(8,128)(2,1)S(1)} %convert_element_type.49.refs_9_.refs_16_.refs_3_), channel_id=1, source_target_pairs={{0,5},{1,2},{2,1},{3,6},{6,3},{7,10},{10,7},{11,14},{14,11},{15,12... | collective-permute-start | bytes 786440 | tf_op jit(solution)/shard_map/ppermute | solution.py:386
  4.9 7.2 %collective-permute-start = (bf16[1,128,1024]{2,1,0:T(8,128)(2,1)S(1)}, bf16[1,128,1024]{2,1,0:T(8,128)(2,1)S(1)}, u32[]{:S(2)}, u32[]{:S(2)}) collective-permute-start(bf16[1,128,1024]{2,1,0:T(8,128)(2,1)S(1)} %convert_element_type.49.refs_9_.refs_16_.refs_3_), channel_id=1, source_target_pairs={{0,2},{1,5},{2,6},{3,1},{6,10},{7,3},{10,14},{11,7},{14,12},{15,11... | collective-permute-start | bytes 786440 | tf_op jit(solution)/shard_map/ppermute | solution.py:386
  12.2 9.2 %collective-permute-start.3 = (bf16[2,128,1024]{2,1,0:T(8,128)(2,1)S(1)}, bf16[2,128,1024]{2,1,0:T(8,128)(2,1)S(1)}, u32[]{:S(2)}, u32[]{:S(2)}) collective-permute-start(bf16[2,128,1024]{2,1,0:T(8,128)(2,1)S(1)} %constant_dynamic-update-slice_fusion.refs_18_.refs_4_), channel_id=1, source_target_pairs={{0,2},{1,5},{2,6},{3,1},{6,10},{7,3},{10,14},{11,7},{14,12},{15,11... | collective-permute-start | bytes 1572872 | tf_op jit(solution)/shard_map/ppermute | solution.py:386
  14.2 10.5 %collective-permute-start.5 = (bf16[2,128,1024]{2,1,0:T(8,128)(2,1)S(1)}, bf16[2,128,1024]{2,1,0:T(8,128)(2,1)S(1)}, u32[]{:S(2)}, u32[]{:S(2)}) collective-permute-start(bf16[2,128,1024]{2,1,0:T(8,128)(2,1)S(1)} %constant_dynamic-update-slice_fusion.refs_18_.refs_4_), channel_id=1, source_target_pairs={{0,1},{1,0},{2,3},{3,2},{4,5},{5,4},{6,7},{7,6},{8,9},{9,8},{10,11... | collective-permute-start | bytes 1572872 | tf_op jit(solution)/shard_map/ppermute | solution.py:389
  14.2 9.8 %copy-start = (f32[1,128,1024]{2,1,0:T(8,128)S(1)}, f32[1,128,1024]{2,1,0:T(8,128)}, u32[]{:S(2)}) copy-start(f32[1,128,1024]{2,1,0:T(8,128)} %param.8) | copy-start | bytes 1572868
  14.2 9.8 %copy-start.1 = (f32[128,128]{1,0:T(8,128)S(1)}, f32[128,128]{1,0:T(8,128)}, u32[]{:S(2)}) copy-start(f32[128,128]{1,0:T(8,128)} %constant.13.clone.cheb_ref) | copy-start | bytes 196612
  14.2 9.8 %copy-start.2 = (f32[16,1024]{1,0:T(8,128)S(1)}, f32[16,1024]{1,0:T(8,128)}, u32[]{:S(2)}) copy-start(f32[16,1024]{1,0:T(8,128)} %pert_ref.1) | copy-start | bytes 196612
  21.4 9.2 %collective-permute-start.4 = (bf16[2,128,1024]{2,1,0:T(8,128)(2,1)S(1)}, bf16[2,128,1024]{2,1,0:T(8,128)(2,1)S(1)}, u32[]{:S(2)}, u32[]{:S(2)}) collective-permute-start(bf16[2,128,1024]{2,1,0:T(8,128)(2,1)S(1)} %collective-permute-done.3.refs_20_.refs_3_), channel_id=1, source_target_pairs={{0,2},{1,5},{2,6},{3,1},{6,10},{7,3},{10,14},{11,7},{14,12},{15,11... | collective-permute-start | bytes 1572872 | tf_op jit(solution)/shard_map/ppermute | solution.py:386
  24.6 8.0 %collective-permute-start.7 = (bf16[2,128,1024]{2,1,0:T(8,128)(2,1)S(1)}, bf16[2,128,1024]{2,1,0:T(8,128)(2,1)S(1)}, u32[]{:S(2)}, u32[]{:S(2)}) collective-permute-start(bf16[2,128,1024]{2,1,0:T(8,128)(2,1)S(1)} %collective-permute-done.3.refs_20_.refs_3_), channel_id=1, source_target_pairs={{0,1},{1,0},{2,3},{3,2},{4,5},{5,4},{6,7},{7,6},{8,9},{9,8},{10,11... | collective-permute-start | bytes 1572872 | tf_op jit(solution)/shard_map/ppermute | solution.py:389
  30.6 2.0 %collective-permute-start.8 = (bf16[2,128,1024]{2,1,0:T(8,128)(2,1)S(1)}, bf16[2,128,1024]{2,1,0:T(8,128)(2,1)S(1)}, u32[]{:S(2)}, u32[]{:S(2)}) collective-permute-start(bf16[2,128,1024]{2,1,0:T(8,128)(2,1)S(1)} %collective-permute-done.4.refs_17_.refs_5_.refs_3_), channel_id=1, source_target_pairs={{0,1},{1,0},{2,3},{3,2},{4,5},{5,4},{6,7},{7,6},{8,9},{9,8},{10,11... | collective-permute-start | bytes 1572872 | tf_op jit(solution)/shard_map/ppermute | solution.py:389
  30.6 6.4 %collective-permute-start.6 = (bf16[1,128,1024]{2,1,0:T(8,128)(2,1)S(1)}, bf16[1,128,1024]{2,1,0:T(8,128)(2,1)S(1)}, u32[]{:S(2)}, u32[]{:S(2)}) collective-permute-start(bf16[1,128,1024]{2,1,0:T(8,128)(2,1)S(1)} %slice.22), channel_id=1, source_target_pairs={{0,2},{1,5},{2,6},{3,1},{6,10},{7,3},{10,14},{11,7},{14,12},{15,11... | collective-permute-start | bytes 786440 | tf_op jit(solution)/shard_map/ppermute | solution.py:386
  36.6 2.0 %copy-start.3 = (f32[1024]{0:T(1024)S(1)}, f32[1024]{0:T(1024)}, u32[]{:S(2)}) copy-start(f32[1024]{0:T(1024)} %param.12) | copy-start | bytes 12292
  36.6 2.0 %copy-start.4 = (f32[1024]{0:T(1024)S(1)}, f32[1024]{0:T(1024)}, u32[]{:S(2)}) copy-start(f32[1024]{0:T(1024)} %param.11) | copy-start | bytes 12292
  37.0 1.5 %collective-permute-start.9 = (bf16[1,128,1024]{2,1,0:T(8,128)(2,1)S(1)}, bf16[1,128,1024]{2,1,0:T(8,128)(2,1)S(1)}, u32[]{:S(2)}, u32[]{:S(2)}) collective-permute-start(bf16[1,128,1024]{2,1,0:T(8,128)(2,1)S(1)} %collective-permute-done.6.refs_16_.refs_5_), channel_id=1, source_target_pairs={{0,1},{1,0},{2,3},{3,2},{4,5},{5,4},{6,7},{7,6},{8,9},{9,8},{10,11... | collective-permute-start | bytes 786440 | tf_op jit(solution)/shard_map/ppermute | solution.py:389
  40.9 1.9 %collective-permute-start.10 = (bf16[1,128,1024]{2,1,0:T(8,128)(2,1)S(1)}, bf16[1,128,1024]{2,1,0:T(8,128)(2,1)S(1)}, u32[]{:S(2)}, u32[]{:S(2)}) collective-permute-start(bf16[1,128,1024]{2,1,0:T(8,128)(2,1)S(1)} %get-tuple-element.120), channel_id=1, source_target_pairs={{0,1},{1,0},{2,3},{3,2},{4,5},{5,4},{6,7},{7,6},{8,9},{9,8},{10,11... | collective-permute-start | bytes 786440 | tf_op jit(solution)/shard_map/ppermute | solution.py:389
  42.8 6.6 %collective-permute-start.12 = (bf16[2,128,1024]{2,1,0:T(8,128)(2,1)S(1)}, bf16[2,128,1024]{2,1,0:T(8,128)(2,1)S(1)}, u32[]{:S(2)}, u32[]{:S(2)}) collective-permute-start(bf16[2,128,1024]{2,1,0:T(8,128)(2,1)S(1)} %get-tuple-element.126), channel_id=1, source_target_pairs={{0,1},{1,0},{2,3},{3,2},{4,5},{5,4},{6,7},{7,6},{8,9},{9,8},{10,11... | collective-permute-start | bytes 1572872 | tf_op jit(solution)/shard_map/ppermute | solution.py:389
  43.1 6.4 %collective-permute-start.11 = (bf16[1,128,1024]{2,1,0:T(8,128)(2,1)S(1)}, bf16[1,128,1024]{2,1,0:T(8,128)(2,1)S(1)}, u32[]{:S(2)}, u32[]{:S(2)}) collective-permute-start(bf16[1,128,1024]{2,1,0:T(8,128)(2,1)S(1)} %add_convert_fusion.2), channel_id=1, source_target_pairs={{0,2},{1,5},{2,6},{3,1},{6,10},{7,3},{10,14},{11,7},{14,12},{15,11... | collective-permute-start | bytes 786440 | tf_op jit(solution)/shard_map/ppermute | solution.py:386
  49.8 9.4 %collective-permute-start.13 = (bf16[2,128,1024]{2,1,0:T(8,128)(2,1)S(1)}, bf16[2,128,1024]{2,1,0:T(8,128)(2,1)S(1)}, u32[]{:S(2)}, u32[]{:S(2)}) collective-permute-start(bf16[2,128,1024]{2,1,0:T(8,128)(2,1)S(1)} %pad_maximum_fusion), channel_id=1, source_target_pairs={{0,2},{1,5},{2,6},{3,1},{6,10},{7,3},{10,14},{11,7},{14,12},{15,11... | collective-permute-start | bytes 1572872 | tf_op jit(solution)/shard_map/ppermute | solution.py:386
  52.0 7.3 %collective-permute-start.15 = (bf16[2,128,1024]{2,1,0:T(8,128)(2,1)S(1)}, bf16[2,128,1024]{2,1,0:T(8,128)(2,1)S(1)}, u32[]{:S(2)}, u32[]{:S(2)}) collective-permute-start(bf16[2,128,1024]{2,1,0:T(8,128)(2,1)S(1)} %get-tuple-element.134), channel_id=1, source_target_pairs={{0,1},{1,0},{2,3},{3,2},{4,5},{5,4},{6,7},{7,6},{8,9},{9,8},{10,11... | collective-permute-start | bytes 1572872 | tf_op jit(solution)/shard_map/ppermute | solution.py:389
  59.5 9.2 %collective-permute-start.16 = (bf16[2,128,1024]{2,1,0:T(8,128)(2,1)S(1)}, bf16[2,128,1024]{2,1,0:T(8,128)(2,1)S(1)}, u32[]{:S(2)}, u32[]{:S(2)}) collective-permute-start(bf16[2,128,1024]{2,1,0:T(8,128)(2,1)S(1)} %add_convert_fusion.1), channel_id=1, source_target_pairs={{0,2},{1,5},{2,6},{3,1},{6,10},{7,3},{10,14},{11,7},{14,12},{15,11... | collective-permute-start | bytes 1572872 | tf_op jit(solution)/shard_map/ppermute | solution.py:386
  61.5 7.3 %collective-permute-start.14 = (bf16[2,128,1024]{2,1,0:T(8,128)(2,1)S(1)}, bf16[2,128,1024]{2,1,0:T(8,128)(2,1)S(1)}, u32[]{:S(2)}, u32[]{:S(2)}) collective-permute-start(bf16[2,128,1024]{2,1,0:T(8,128)(2,1)S(1)} %get-tuple-element.133), channel_id=1, source_target_pairs={{0,1},{1,0},{2,3},{3,2},{4,5},{5,4},{6,7},{7,6},{8,9},{9,8},{10,11... | collective-permute-start | bytes 1572872 | tf_op jit(solution)/shard_map/ppermute | solution.py:389
  68.0 9.2 %collective-permute-start.19 = (bf16[1,128,1024]{2,1,0:T(8,128)(2,1)S(1)}, bf16[1,128,1024]{2,1,0:T(8,128)(2,1)S(1)}, u32[]{:S(2)}, u32[]{:S(2)}) collective-permute-start(bf16[1,128,1024]{2,1,0:T(8,128)(2,1)S(1)} %get-tuple-element.148), channel_id=1, source_target_pairs={{0,1},{1,0},{2,3},{3,2},{4,5},{5,4},{6,7},{7,6},{8,9},{9,8},{10,11... | collective-permute-start | bytes 786440 | tf_op jit(solution)/shard_map/ppermute | solution.py:389
  69.0 8.3 %collective-permute-start.18 = (bf16[1,128,1024]{2,1,0:T(8,128)(2,1)S(1)}, bf16[1,128,1024]{2,1,0:T(8,128)(2,1)S(1)}, u32[]{:S(2)}, u32[]{:S(2)}) collective-permute-start(bf16[1,128,1024]{2,1,0:T(8,128)(2,1)S(1)} %get-tuple-element.155), channel_id=1, source_target_pairs={{0,3},{1,4},{2,7},{3,0},{6,11},{7,2},{10,15},{11,6},{14,13},{15,10... | collective-permute-start | bytes 786440 | tf_op jit(solution)/shard_map/ppermute | solution.py:386
  70.2 8.1 %collective-permute-start.17 = (bf16[1,128,1024]{2,1,0:T(8,128)(2,1)S(1)}, bf16[1,128,1024]{2,1,0:T(8,128)(2,1)S(1)}, u32[]{:S(2)}, u32[]{:S(2)}) collective-permute-start(bf16[1,128,1024]{2,1,0:T(8,128)(2,1)S(1)} %get-tuple-element.156), channel_id=1, source_target_pairs={{0,2},{1,5},{2,6},{3,1},{6,10},{7,3},{10,14},{11,7},{14,12},{15,11... | collective-permute-start | bytes 786440 | tf_op jit(solution)/shard_map/ppermute | solution.py:386
